TPU v7x, 32 devices: a whole 2x2x4 slice. The times are simulated.
32 devices in a mesh: groups: 2 (over y), seq: 4 (over z), mp: 4 (over x, core).
Axes of the slice: x: 2, y: 2, z: 4, core: 2. Of those that a mesh axis runs over, the one named last changes fastest.
Arguments:
- tiles: bfloat16 [1536, 1536], P(('groups', 'seq')), parts along dimension 0, may hold values from -6 to 6
- counts: int32 [8], P(('groups', 'seq')), parts along dimension 0, may hold values from 1 to 192, 576 in all
- dest: int32 [1536, 1], P(('groups', 'seq')), parts along dimension 0, may hold values from 0 to 3; in each aligned block of 192 rows (0 to 191, 192 to 383, ...) at most 64 rows name the same one
- gain_enc: float32 [1536], replicated, may hold values from 0.1 to 1.9
- w_gate: bfloat16 [1536, 4096], P('seq', 'mp'), may hold values from -0.15625 to 0.15625
- w_up: bfloat16 [1536, 4096], P('seq', 'mp'), may hold values from -0.15625 to 0.15625
- w_down: bfloat16 [4096, 1536], P('mp', 'seq'), may hold values from -0.09375 to 0.09375
- gain_slide: float32 [1536], replicated, may hold values from 0.1 to 1.9
- w_qkv: bfloat16 [1536, 2304], P(None, 'mp'), may hold values from -0.15625 to 0.15625
- offsets: int32 [12], P('mp'), may hold values from 0 to 7
Outputs:
- attended: bfloat16 [2048, 768], P(('groups', 'seq'), 'mp'), parts along dimension 0
There are 2 independent parts, one for each index of `groups`. A program takes and returns all parts, laid end to end along the dimension named above; an argument that names none is the same for every part. Nothing has to cross between parts.
Inputs may be any that keep to these rules, and one draw needn't show every extreme that they name: `dest`: among the tiles of one owner, no value is named by more than 64 tiles, a bound that some block reaches of them. `counts`: some owner has all 192 slots live.
All inputs are finite; a program needn't handle non-finite values. No bound on the sum of `counts` on one device may be relied on, other than what follows from the above.
Results may differ from a plain program's by a relative error of at most 0.013.
The roundings to bfloat16 on the way count: a program that leaves them out, or rounds other values in their place, can miss the bound.
Values may be sent and summed in bfloat16 or wider, within the bound.
No kernel may reach another device: no remote copies, remote signals or barrier semaphores. Data moves between devices by JAX's collectives and lax.ppermute only.
A program may use at most 64 MiB of HBM per device.

v0:
```python
import jax
import jax.numpy as jnp
from jax import lax
from jax.sharding import PartitionSpec as P

D_ENC = 1536
HEAD_WIDTH = 64
DILATION_STEP = 8
ENCODER_SLOTS = 256


epsilon = 1e-05


def on_device(tiles, counts, dest, gain_enc, w_gate, w_up, w_down, gain_slide, w_qkv, offsets):
    seq_count = lax.axis_size("seq")
    capacity = ENCODER_SLOTS // seq_count
    tile_rows = tiles.shape[0]
    target = dest[:, 0]
    live_rows = jnp.arange(tile_rows, dtype=jnp.int32) < counts[0]
    chosen = (
        (target[:, None] == jnp.arange(seq_count, dtype=jnp.int32)[None, :]) & live_rows[:, None]
    ).astype(jnp.int32)
    arrival = jnp.sum((jnp.cumsum(chosen, axis=0) - chosen) * chosen, axis=1)
    slot_index = jnp.where(live_rows, target * capacity + arrival, ENCODER_SLOTS)
    outgoing = (
        jnp.zeros((ENCODER_SLOTS, D_ENC), jnp.bfloat16).at[slot_index].set(tiles, mode="drop")
    )
    arrived = lax.all_to_all(outgoing, "seq", split_axis=0, concat_axis=0, tiled=True)
    arrived_f = arrived.astype(jnp.float32)
    inverse = lax.rsqrt(jnp.mean(arrived_f * arrived_f, axis=-1, keepdims=True) + epsilon)
    normed = (arrived_f * inverse * gain_enc).astype(jnp.bfloat16)

    def add_rows(portion):
        return jnp.dot(normed, portion, preferred_element_type=jnp.float32)

    gate_act = add_rows(lax.all_gather(w_gate, "seq", axis=0, tiled=True))
    up_act = add_rows(lax.all_gather(w_up, "seq", axis=0, tiled=True))
    hidden = (jax.nn.silu(gate_act) * up_act).astype(jnp.bfloat16)
    partial_out = jnp.dot(
        hidden,
        lax.all_gather(w_down, "seq", axis=1, tiled=True),
        preferred_element_type=jnp.float32,
    )
    share = lax.psum_scatter(partial_out, "mp", scatter_dimension=1, tiled=True)
    share_width = share.shape[1]
    own_cols = lax.dynamic_slice_in_dim(
        arrived_f, lax.axis_index("mp") * share_width, share_width, 1
    )
    embedded_cols = (own_cols + share).astype(jnp.bfloat16)
    portion_f = lax.all_gather(embedded_cols, "mp", axis=1, tiled=True).astype(jnp.float32)
    accumulated = jnp.dot(
        (portion_f * gain_slide).astype(jnp.bfloat16), w_qkv, preferred_element_type=jnp.float32
    )
    accumulated, squares = (accumulated, jnp.sum(portion_f * portion_f, axis=1))
    projected = accumulated * lax.rsqrt(squares / D_ENC + epsilon)[:, None]
    qkv_act = projected.astype(jnp.bfloat16)
    local_head_output = offsets.shape[0]
    fields = qkv_act.reshape(ENCODER_SLOTS, local_head_output, 3, HEAD_WIDTH)
    query_rows = fields[:, :, 0, :]
    keys_local = fields[:, :, 1, :]
    values_local = fields[:, :, 2, :]
    scale_factor = HEAD_WIDTH ** (-0.5)
    row_selector = (jnp.arange(DILATION_STEP, dtype=jnp.int32)[None, :] == offsets[:, None]).astype(
        jnp.float32
    )
    selected_rows = ENCODER_SLOTS // DILATION_STEP

    def select_rows(slide_field):
        reshaped_rows = slide_field.astype(jnp.float32).reshape(
            selected_rows, DILATION_STEP, local_head_output, HEAD_WIDTH
        )
        return jnp.einsum("rdhe,hd->rhe", reshaped_rows, row_selector).astype(jnp.bfloat16)

    query_sel = select_rows(query_rows)
    package = jnp.concatenate([select_rows(keys_local), select_rows(values_local)], axis=2).reshape(
        selected_rows, local_head_output * 2 * HEAD_WIDTH
    )
    portion = lax.all_gather(package, "seq", axis=0, tiled=True)
    parts_kv = portion.reshape(portion.shape[0], local_head_output, 2, HEAD_WIDTH)
    scores = (
        jnp.einsum(
            "qhe,khe->hqk", query_sel, parts_kv[:, :, 0, :], preferred_element_type=jnp.float32
        )
        * scale_factor
    )
    weights = jnp.exp(scores)
    numer = jnp.einsum(
        "hqk,khe->hqe",
        weights.astype(jnp.bfloat16),
        parts_kv[:, :, 1, :],
        preferred_element_type=jnp.float32,
    )
    remote_den = jnp.sum(weights, axis=-1)
    scores = (
        jnp.einsum("qhe,khe->hqk", query_rows, keys_local, preferred_element_type=jnp.float32)
        * scale_factor
    )
    weights = jnp.exp(scores)
    local_num = jnp.einsum(
        "hqk,khe->hqe",
        weights.astype(jnp.bfloat16),
        values_local,
        preferred_element_type=jnp.float32,
    )
    local_den = jnp.sum(weights, axis=-1)
    spread_num = jnp.einsum("hre,hd->hrde", numer, row_selector).reshape(
        local_head_output, ENCODER_SLOTS, HEAD_WIDTH
    )
    spread_den = jnp.einsum("hr,hd->hrd", remote_den, row_selector).reshape(
        local_head_output, ENCODER_SLOTS
    )
    result = (local_num + spread_num) / (local_den + spread_den)[..., None]
    return (
        jnp.transpose(result, (1, 0, 2))
        .reshape(ENCODER_SLOTS, local_head_output * HEAD_WIDTH)
        .astype(jnp.bfloat16)
    )


def solution(mesh):
    return jax.shard_map(
        on_device,
        mesh=mesh,
        in_specs=(
            P(("groups", "seq"), None),
            P(("groups", "seq")),
            P(("groups", "seq"), None),
            P(),
            P("seq", "mp"),
            P("seq", "mp"),
            P("mp", "seq"),
            P(),
            P(None, "mp"),
            P("mp"),
        ),
        out_specs=P(("groups", "seq"), "mp"),
        check_vma=False,
    )
```

profile of v0, /device:TPU:0, one launch (start us, length us, event | category | flops | bytes accessed | tf_op | source)
XLA Modules:
  0.0 285.4 jit_solution(11303176827611450095)
XLA Ops:
  6.5 0.0 copy-start
  6.5 0.7 all-gather.4.cloned.1.call-update
  7.3 0.0 all-gather.6.cloned.1.call-start
  7.3 0.7 all-gather.6.cloned.1.call-update
  8.0 0.0 all-gather.8.cloned.1.call-start
  8.1 0.7 all-gather.8.cloned.1.call-update
  8.8 0.0 reduce-scatter.2.cloned.1.call-start
  9.5 1.2 reduce-window.6
  10.7 0.1 slice.32
  10.8 0.1 copy.18
  11.0 0.1 copy.19
  11.1 0.1 add_bitcast_fusion
  11.2 2.3 scatter_custom_fusion
  13.4 47.4 %all_to_all.9 = bf16[4,64,1536]{2,1,0:T(8,128)(2,1)S(1)} all-to-all(bf16[4,64,1536]{2,1,0:T(8,128)(2,1)S(1)} %bitcast.103), channel_id=1, replica_groups=mesh['groups'=2,'seq'=4,'mp'=4] {'seq'}, dimensions={0} | all-to-all | bytes 1572864 | tf_op jit(solution)/shard_map/all_to_all | solution.py:29
  60.9 0.2 multiply_reduce_fusion
  61.1 0.1 rsqrt.19
  61.2 1.4 multiply_convert_fusion
  62.6 28.2 %all-gather.4.cloned.1.call-done = bf16[1536,1024]{1,0:T(8,128)(2,1)} async-done(((bf16[384,1024]{1,0:T(8,128)(2,1)}), bf16[1536,1024]{1,0:T(8,128)(2,1)}) %all-gather.4.cloned.1.call-update) | async-done | bytes 3145744 | tf_op jit(solution)/shard_map/all_gather | solution.py:37
  90.8 3.9 %fusion.45 = f32[256,1024]{1,0:T(8,128)} fusion(bf16[256,1536]{1,0:T(8,128)(2,1)S(1)} %get-tuple-element.5, bf16[1536,1024]{1,0:T(8,128)(2,1)} %all-gather.4.cloned.1.call-done), kind=kOutput, calls=%fused_computation.78 | convolution fusion | flops 805306368 | bytes 4980736 | tf_op jit(solution)/shard_map/dot_general | solution.py:35
  94.7 60.2 %all-gather.6.cloned.1.call-done = bf16[1536,1024]{1,0:T(8,128)(2,1)} async-done(((bf16[384,1024]{1,0:T(8,128)(2,1)}), bf16[1536,1024]{1,0:T(8,128)(2,1)}) %all-gather.6.cloned.1.call-update) | async-done | bytes 3145744 | tf_op jit(solution)/shard_map/all_gather | solution.py:38
  155.0 63.6 %all-gather.8.cloned.1.call-done = bf16[1024,1536]{1,0:T(8,128)(2,1)} async-done(((bf16[1024,384]{1,0:T(8,128)(2,1)}), bf16[1024,1536]{1,0:T(8,128)(2,1)}) %all-gather.8.cloned.1.call-update) | async-done | bytes 3145744 | tf_op jit(solution)/shard_map/all_gather | solution.py:42
  218.6 6.2 %fusion.8 = f32[256,1536]{1,0:T(8,128)} fusion(bf16[1024,1536]{1,0:T(8,128)(2,1)} %all-gather.8.cloned.1.call-done, bf16[256,1536]{1,0:T(8,128)(2,1)S(1)} %get-tuple-element.5, bf16[1536,1024]{1,0:T(8,128)(2,1)} %all-gather.6.cloned.1.call-done, f32[256,1024]{1,0:T(8,128)} %fusion.45), kind=kOutput, calls=%fused_computation.18 | convolution fusion | flops 1612185600 | bytes 9699328 | tf_op jit(solution)/shard_map/dot_general | solution.py:40
  224.8 0.0 reduce-scatter.2.cloned.1.call-update
  224.8 0.0 copy-start.4
  224.8 0.1 fusion.41
  224.9 26.8 %reduce-scatter.2.cloned.1.call-done = f32[256,384]{1,0:T(8,128)} async-done(((f32[256,1536]{1,0:T(8,128)}), f32[256,384]{1,0:T(8,128)}) %reduce-scatter.2.cloned.1.call-update) | async-done | bytes 393232 | tf_op jit(solution)/shard_map/reduce_scatter | solution.py:45
  251.7 1.2 add_convert_fusion
  252.9 8.2 %all_gather.18 = bf16[256,1536]{1,0:T(8,128)(2,1)S(1)} all-gather(bf16[256,384]{1,0:T(8,128)(2,1)S(1)} %add_convert_fusion), channel_id=1, replica_groups=mesh['groups'=2,'seq'=4,'mp'=4] {'mp'}, dimensions={1}, use_global_device_ids=true | all-gather | bytes 983040 | tf_op jit(solution)/shard_map/all_gather | solution.py:51
  261.1 0.2 fusion.1
  261.4 0.7 fusion.4
  262.1 0.3 fusion.43
  262.4 0.2 copy.26
  262.6 0.2 copy.25
  262.8 0.2 fusion.15
  263.0 0.2 fusion.17
  263.1 0.1 fusion.28
  263.2 0.1 pad_maximum_fusion
  263.3 13.4 %all_gather.19 = bf16[128,384]{1,0:T(8,128)(2,1)S(1)} all-gather(bf16[32,384]{1,0:T(8,128)(2,1)S(1)} %bitcast.112), channel_id=1, replica_groups=mesh['groups'=2,'seq'=4,'mp'=4] {'seq'}, dimensions={0}, use_global_device_ids=true | all-gather | bytes 122880 | tf_op jit(solution)/shard_map/all_gather | solution.py:79
  276.7 0.1 copy.27
  276.8 0.2 copy.24
  277.0 0.2 fusion.19
  277.2 0.2 fusion.44
  277.4 0.1 broadcast_multiply_fusion
  277.5 0.1 reshape.95
  277.6 0.1 fusion.27
  277.7 0.1 multiply_bitcast_fusion
  277.9 0.1 copy.30
  278.0 0.8 fusion.6
  (23 shorter events, 0.2 us)
Async XLA Ops:
  6.5 254.8 %copy-start = (bf16[1536,576]{0,1:T(8,128)(2,1)S(1)}, bf16[1536,576]{0,1:T(8,128)(2,1)}, u32[]{:S(2)}) copy-start(bf16[1536,576]{0,1:T(8,128)(2,1)} %param.18) | copy-start | bytes 5308420
  6.5 2.9 %copy-start.1 = (s32[192,1]{0,1:T(1,128)S(1)}, s32[192,1]{0,1:T(1,128)}, u32[]{:S(2)}) copy-start(s32[192,1]{0,1:T(1,128)} %param.12) | copy-start | bytes 2308
  6.5 84.3 %all-gather.4.cloned.1.call-start = ((), (), s32[]{:S(2)}) async-start(), calls=%async_computation.2 | async-start | bytes 3932160 | tf_op jit(solution)/shard_map/all_gather | solution.py:37
  7.3 147.7 %all-gather.6.cloned.1.call-start = ((), (), s32[]{:S(2)}) async-start(), calls=%async_computation.3 | async-start | bytes 3932160 | tf_op jit(solution)/shard_map/all_gather | solution.py:38
  8.0 210.5 %all-gather.8.cloned.1.call-start = ((), (), s32[]{:S(2)}) async-start(), calls=%async_computation.4 | async-start | bytes 3932160 | tf_op jit(solution)/shard_map/all_gather | solution.py:42
  8.7 52.5 %copy-start.2 = (f32[1536]{0:T(1024)S(1)}, f32[1536]{0:T(1024)}, u32[]{:S(2)}) copy-start(f32[1536]{0:T(1024)} %param.13) | copy-start | bytes 18436
  8.8 243.0 %reduce-scatter.2.cloned.1.call-start = ((), (), s32[]{:S(2)}) async-start(), calls=%async_computation.5 | async-start | bytes 1966080 | tf_op jit(solution)/shard_map/reduce_scatter | solution.py:45
  94.7 130.1 %copy-start.3 = (s32[3]{0:T(128)S(1)}, s32[3]{0:T(128)}, u32[]{:S(2)}) copy-start(s32[3]{0:T(128)} %param.19) | copy-start | bytes 40
  224.8 36.5 %copy-start.4 = (f32[1536]{0:T(1024)S(1)}, f32[1536]{0:T(1024)}, u32[]{:S(2)}) copy-start(f32[1536]{0:T(1024)} %param.17) | copy-start | bytes 18436
Sparse Core Ops, SparseCore 0:
  8.9 81.8 all-gather.3
  92.4 62.5 all-gather.5
  156.5 61.9 all-gather.7
  224.9 26.7 reduce-scatter.1
where the time goes:
time: 286 us; the launch traced here: 285 us
  waiting for transfers between devices  181 us (63%)
  blocking collectives  69 us (24%)
  between operations  14 us (5%)
  matrix products  12.9 us (5%)
  other arithmetic  4.79 us (2%)
  local copies, waits for them, and re-layouts  3.63 us (1%)
    all_gather x1, waiting for transfers between devices, on_device(): lax.all_gather(w_down, 'seq', axis=1, tiled=True)  63.6 us
    all_gather x1, waiting for transfers between devices, on_device(): up_act = add_rows(lax.all_gather(w_up, 'seq', axis=0, tiled=True))  60.2 us
    all_to_all x1, blocking collectives, on_device(): lax.all_to_all(outgoing, 'seq', split_axis=0, concat_axis=0, tiled=True)  47.4 us
    all_gather x1, waiting for transfers between devices, on_device(): gate_act = add_rows(lax.all_gather(w_gate, 'seq', axis=0, tiled=True))  28.2 us
    reduce_scatter x1, waiting for transfers between devices, on_device(): share = lax.psum_scatter(partial_out, 'mp', scatter_dimension=1, tiled=True)  26.8 us
    all_gather x1, blocking collectives, on_device(): portion = lax.all_gather(package, 'seq', axis=0, tiled=True)  13.4 us
    all_gather x1, blocking collectives, on_device(): lax.all_gather(embedded_cols, 'mp', axis=1, tiled=True).astype(jnp.float32)  8.21 us
    dot_general x1, matrix products, on_device(): jnp.dot(hidden, lax.all_gather(w_down, 'seq', axis=1, tiled=True), prefer...  6.25 us
  transfers between devices with their start and end apart: 4, of which 4 were waited for; matrix products, arithmetic and copies ran while one was open for 3% of the time, Pallas kernels for 0%

commit v1 on v0

--- a/solution.py
+++ b/solution.py
@@ -12,7 +12,14 @@
 epsilon = 1e-05
 
 
-def on_device(tiles, counts, dest, gain_enc, w_gate, w_up, w_down, gain_slide, w_qkv, offsets):
+def gather_seq(package):
+    count = lax.axis_size("seq")
+    if count & (count - 1) == 0 and count <= 4:
+        return jnp.concatenate([package] + [swap(package, "seq", d) for d in range(1, count)])
+    return lax.all_gather(package, "seq", axis=0, tiled=True)
+
+
+def gathered_plan(tiles, counts, dest, gain_enc, w_gate, w_up, w_down, gain_slide, w_qkv, offsets):
     seq_count = lax.axis_size("seq")
     capacity = ENCODER_SLOTS // seq_count
     tile_rows = tiles.shape[0]
@@ -48,7 +55,12 @@
         arrived_f, lax.axis_index("mp") * share_width, share_width, 1
     )
     embedded_cols = (own_cols + share).astype(jnp.bfloat16)
-    portion_f = lax.all_gather(embedded_cols, "mp", axis=1, tiled=True).astype(jnp.float32)
+    embedded = lax.all_gather(embedded_cols, "mp", axis=1, tiled=True)
+    return slide_layer(embedded, gain_slide, w_qkv, offsets)
+
+
+def slide_layer(embedded, gain_slide, w_qkv, offsets):
+    portion_f = embedded.astype(jnp.float32)
     accumulated = jnp.dot(
         (portion_f * gain_slide).astype(jnp.bfloat16), w_qkv, preferred_element_type=jnp.float32
     )
@@ -76,7 +88,7 @@
     package = jnp.concatenate([select_rows(keys_local), select_rows(values_local)], axis=2).reshape(
         selected_rows, local_head_output * 2 * HEAD_WIDTH
     )
-    portion = lax.all_gather(package, "seq", axis=0, tiled=True)
+    portion = gather_seq(package)
     parts_kv = portion.reshape(portion.shape[0], local_head_output, 2, HEAD_WIDTH)
     scores = (
         jnp.einsum(
@@ -116,6 +128,141 @@
         .reshape(ENCODER_SLOTS, local_head_output * HEAD_WIDTH)
         .astype(jnp.bfloat16)
     )
+
+
+def swap(array, axis, distance):
+    size = lax.axis_size(axis)
+    return lax.ppermute(array, axis, [(i, i ^ distance) for i in range(size)])
+
+
+def block_at(array, index, size, axis):
+    return lax.dynamic_slice_in_dim(array, index * size, size, axis)
+
+
+def place_blocks(blocks, owner, axis):
+    size = blocks[0].shape[axis]
+    shape = list(blocks[0].shape)
+    shape[axis] = size * len(blocks)
+    whole = jnp.zeros(shape, blocks[0].dtype)
+    for d, block in enumerate(blocks):
+        whole = lax.dynamic_update_slice_in_dim(whole, block, (owner ^ d) * size, axis)
+    return whole
+
+
+def exchange_weights(block_for, after=None):
+    seq, group = lax.axis_index("seq"), lax.axis_index("groups")
+    count = lax.axis_size("seq")
+    halved = lax.axis_size("groups") == 2
+    outgoing = [block_for(seq ^ d) for d in range(count)]
+    if halved:
+        for d in range(2, count):
+            outgoing[d] = block_at(outgoing[d], group, outgoing[d].shape[0] // 2, 0)
+    if after is not None:
+        outgoing, _ = lax.optimization_barrier((outgoing, after))
+    incoming = [outgoing[0]] + [swap(outgoing[d], "seq", d) for d in range(1, count)]
+    if halved:
+        for d in range(2, count):
+            mine = incoming[d]
+            other = swap(mine, "groups", 1)
+            incoming[d] = jnp.where(
+                group == 0,
+                jnp.concatenate([mine, other], axis=0),
+                jnp.concatenate([other, mine], axis=0),
+            )
+    return incoming
+
+
+def spread_mp(own, axis):
+    blocks = [own]
+    distance = lax.axis_size("mp") // 2
+    found = {0: own}
+    while distance >= 1:
+        keys = sorted(found)
+        sent = jnp.stack([found[k] for k in keys])
+        got = swap(sent, "mp", distance)
+        for i, k in enumerate(keys):
+            found[k ^ distance] = got[i]
+        distance //= 2
+    blocks = [found[d] for d in range(lax.axis_size("mp"))]
+    return place_blocks(blocks, lax.axis_index("mp"), axis)
+
+
+def split_hidden_plan(
+    tiles, counts, dest, gain_enc, w_gate, w_up, w_down, gain_slide, w_qkv, offsets
+):
+    count, mp_size = lax.axis_size("seq"), lax.axis_size("mp")
+    seq, mp = lax.axis_index("seq"), lax.axis_index("mp")
+    capacity = ENCODER_SLOTS // count
+    tile_rows = tiles.shape[0]
+    features = D_ENC // mp_size
+    units = w_gate.shape[1] // count
+
+    target = dest[:, 0]
+    rows = jnp.arange(tile_rows, dtype=jnp.int32)
+    live_rows = rows < counts[0]
+    same = (target[:, None] == target[None, :]) & (rows[None, :] < rows[:, None])
+    arrival = jnp.sum((same & live_rows[None, :]).astype(jnp.int32), axis=1)
+    code = jnp.where(live_rows, target * capacity + arrival, ENCODER_SLOTS)
+
+    own_tiles = block_at(tiles, mp, features, 1)
+    code_row = jnp.pad(code.astype(jnp.bfloat16)[None, :], ((0, 15), (0, features - tile_rows)))
+    package = jnp.concatenate([own_tiles, code_row], axis=0)
+    arrived = [package] + [swap(package, "seq", d) for d in range(1, count)]
+    own_quarter = jnp.concatenate([a[:tile_rows] for a in arrived], axis=0)
+
+    def both_columns(dest_seq):
+        return jnp.concatenate(
+            [block_at(w_gate, dest_seq, units, 1), block_at(w_up, dest_seq, units, 1)], axis=1
+        )
+
+    gate_up_blocks = exchange_weights(both_columns, None)
+    tokens = spread_mp(own_quarter, 1)
+    gate_up = place_blocks(gate_up_blocks, seq, 0)
+
+    down_parts = exchange_weights(
+        lambda dest_seq: block_at(w_down, dest_seq, units, 0), gate_up_blocks[-1]
+    )
+    down_stack = jnp.stack(down_parts)
+    down_rows = []
+    for j in range(mp_size):
+        part = lax.dynamic_index_in_dim(down_stack, seq ^ mp ^ j, 0, False)
+        down_rows.append(swap(part, "mp", j) if j else part)
+    down = place_blocks(down_rows, mp, 0)
+
+    tokens_f = tokens.astype(jnp.float32)
+    inverse = lax.rsqrt(jnp.mean(tokens_f * tokens_f, axis=-1, keepdims=True) + epsilon)
+    normed = (tokens_f * inverse * gain_enc).astype(jnp.bfloat16)
+    acts = jnp.dot(normed, gate_up, preferred_element_type=jnp.float32)
+    hidden_own = (jax.nn.silu(acts[:, :units]) * acts[:, units:]).astype(jnp.bfloat16)
+    hidden = spread_mp(hidden_own, 1)
+    partial_out = jnp.dot(hidden, down, preferred_element_type=jnp.float32).astype(jnp.bfloat16)
+
+    codes = jnp.stack([a[tile_rows, :tile_rows] for a in arrived]).astype(jnp.int32)
+    owners = seq ^ jnp.arange(count, dtype=jnp.int32)[:, None]
+    position = ((codes // capacity) ^ seq) * ENCODER_SLOTS + owners * capacity + codes % capacity
+    position = jnp.where(codes < ENCODER_SLOTS, position, -1).reshape(-1)
+
+    def routed(d, array):
+        chosen = (
+            jnp.arange(ENCODER_SLOTS, dtype=jnp.int32)[:, None] + d * ENCODER_SLOTS
+            == position[None, :]
+        ).astype(jnp.bfloat16)
+        return jnp.dot(chosen, array, preferred_element_type=jnp.float32)
+
+    share = routed(0, own_quarter)
+    sums = [routed(0, partial_out)]
+    for d in range(1, count):
+        sums.append(swap(routed(d, partial_out).astype(jnp.bfloat16), "seq", d).astype(jnp.float32))
+    embedded_cols = (share + sum(sums)).astype(jnp.bfloat16)
+    embedded = spread_mp(embedded_cols, 1)
+    return slide_layer(embedded, gain_slide, w_qkv, offsets)
+
+
+def on_device(*arrays):
+    count, mp_size = lax.axis_size("seq"), lax.axis_size("mp")
+    if count == mp_size and count & (count - 1) == 0 and count <= 4:
+        return split_hidden_plan(*arrays)
+    return gathered_plan(*arrays)
 
 
 def solution(mesh):

time: 286 us -> 149 us (0.52)
  waiting for transfers between devices: 181 us -> 54.5 us
  blocking collectives: 69 us -> 0 us
  starting transfers between devices: 0.12 us -> 39.8 us
  local copies, waits for them, and re-layouts: 3.63 us -> 22.6 us
  other arithmetic: 4.79 us -> 20.9 us
  between operations: 14 us -> 1.33 us
  matrix products: 12.9 us -> 9.37 us
    all_gather x3 -> x0, waiting for transfers between devices: 152 us -> none  [the longest x1 63.6 us: on_device(): lax.all_gather(w_down, 'seq', axis=1, tiled=True)]
    ppermute x0 -> x28, waiting for transfers between devices: none -> 54.5 us  [swap(): return lax.ppermute(array, axis, [(i, i ^ distance) for i in range(size)])]
    all_to_all x1 -> x0, blocking collectives: 47.4 us -> none  [on_device(): lax.all_to_all(outgoing, 'seq', split_axis=0, concat_axis=0, tiled=True)]
    ppermute x0 -> x28, starting transfers between devices: none -> 39.8 us  [swap(): return lax.ppermute(array, axis, [(i, i ^ distance) for i in range(size)])]
    reduce_scatter x1 -> x0, waiting for transfers between devices: 26.8 us -> none  [on_device(): share = lax.psum_scatter(partial_out, 'mp', scatter_dimension=1, tiled=True)]
    all_gather x2 -> x0, blocking collectives: 21.6 us -> none  [the longest x1 13.4 us: on_device(): portion = lax.all_gather(package, 'seq', axis=0, tiled=True)]
    dynamic_update_slice x0 -> x14, local copies, waits for them, and re-layouts: none -> 8.09 us  [place_blocks(): lax.dynamic_update_slice_in_dim(whole, block, (owner ^ d) * size, axis)]
    dynamic_slice x0 -> x4, local copies, waits for them, and re-layouts: none -> 5.77 us  [block_at(): return lax.dynamic_slice_in_dim(array, index * size, size, axis)]
  transfers between devices with their start and end apart: 4 -> 28, of which waited for: 4 -> 17; matrix products, arithmetic and copies ran while one was open for 3% -> 26% of each run, Pallas kernels for 0% -> 0%
where the time goes in v1:
time: 149 us
  waiting for transfers between devices  54.5 us (37%)
  starting transfers between devices  39.8 us (27%)
  local copies, waits for them, and re-layouts  22.6 us (15%)
  other arithmetic  20.9 us (14%)
  matrix products  9.37 us (6%)
    ppermute x28, waiting for transfers between devices, swap(): return lax.ppermute(array, axis, [(i, i ^ distance) for i in range(size)])  54.5 us
    ppermute x28, starting transfers between devices, swap(): return lax.ppermute(array, axis, [(i, i ^ distance) for i in range(size)])  39.8 us
    dynamic_update_slice x14, local copies, waits for them, and re-layouts, place_blocks(): lax.dynamic_update_slice_in_dim(whole, block, (owner ^ d) * size, axis)  8.09 us
    dynamic_slice x4, local copies, waits for them, and re-layouts, block_at(): return lax.dynamic_slice_in_dim(array, index * size, size, axis)  5.77 us
    dynamic_update_slice x4, other arithmetic, place_blocks(): lax.dynamic_update_slice_in_dim(whole, block, (owner ^ d) * size, axis)  5.69 us
    concatenate x3, other arithmetic, both_columns(): jnp.concatenate([block_at(w_gate, dest_seq, units, 1), block_at(w_up, des...  4.06 us
    dot_general x1, matrix products, split_hidden_plan(): acts = jnp.dot(normed, gate_up, preferred_element_type=jnp.float32)  3.55 us
    another operation x4, other arithmetic, spread_mp(): sent = jnp.stack([found[k] for k in keys])  3.36 us
  transfers between devices with their start and end apart: 28, of which 17 were waited for; matrix products, arithmetic and copies ran while one was open for 26% of the time, Pallas kernels for 0%

profile of v1, /device:TPU:0, one launch (start us, length us, event | category | flops | bytes accessed | tf_op | source)
XLA Modules:
  0.0 148.5 jit_solution(10904240097411643251)
XLA Ops:
  3.4 3.1 %collective-permute-start = (bf16[208,384]{1,0:T(8,128)(2,1)S(1)}, bf16[208,384]{1,0:T(8,128)(2,1)S(1)}, u32[]{:S(2)}, u32[]{:S(2)}) collective-permute-start(bf16[208,384]{1,0:T(8,128)(2,1)S(1)} %fusion.49), channel_id=1, source_target_pairs={{0,4},{4,0},{8,12},{12,8},{1,5},{5,1},{9,13},{13,9},{2,6},{6,2},{1... | collective-permute-start | bytes 479240 | tf_op jit(solution)/shard_map/ppermute | solution.py:135
  6.5 2.6 %collective-permute-start.1 = (bf16[208,384]{1,0:T(8,128)(2,1)S(1)}, bf16[208,384]{1,0:T(8,128)(2,1)S(1)}, u32[]{:S(2)}, u32[]{:S(2)}) collective-permute-start(bf16[208,384]{1,0:T(8,128)(2,1)S(1)} %fusion.49), channel_id=1, source_target_pairs={{0,8},{4,12},{8,0},{12,4},{1,9},{5,13},{9,1},{13,5},{2,10},{6,14},... | collective-permute-start | bytes 479240 | tf_op jit(solution)/shard_map/ppermute | solution.py:135
  9.1 3.9 %collective-permute-done = bf16[208,384]{1,0:T(8,128)(2,1)S(1)} collective-permute-done((bf16[208,384]{1,0:T(8,128)(2,1)S(1)}, bf16[208,384]{1,0:T(8,128)(2,1)S(1)}, u32[]{:S(2)}, u32[]{:S(2)}) %collective-permute-start) | collective-permute-done | bytes 159776 | tf_op jit(solution)/shard_map/ppermute | solution.py:135
  13.0 8.3 %collective-permute-done.1 = bf16[208,384]{1,0:T(8,128)(2,1)S(1)} collective-permute-done((bf16[208,384]{1,0:T(8,128)(2,1)S(1)}, bf16[208,384]{1,0:T(8,128)(2,1)S(1)}, u32[]{:S(2)}, u32[]{:S(2)}) %collective-permute-start.1) | collective-permute-done | bytes 159776 | tf_op jit(solution)/shard_map/ppermute | solution.py:135
  22.6 1.6 %broadcast_in_dim.19 = bf16[768,1536]{1,0:T(8,128)(2,1)} broadcast(bf16[]{:T(256)} %constant.93.clone.1), dimensions={} | broadcast | bytes 2359298 | tf_op jit(solution)/shard_map/broadcast_in_dim | solution.py:146
  25.2 1.6 %collective-permute-start.3 = (bf16[1,768,384]{2,1,0:T(8,128)(2,1)S(1)}, bf16[1,768,384]{2,1,0:T(8,128)(2,1)S(1)}, u32[]{:S(2)}, u32[]{:S(2)}) collective-permute-start(bf16[1,768,384]{2,1,0:T(8,128)(2,1)S(1)} %get-tuple-element.32), channel_id=1, source_target_pairs={{0,2},{1,3},{2,0},{3,1},{4,6},{5,7},{6,4},{7,5},{8,10},{9,11},{10,... | collective-permute-start | bytes 1769480 | tf_op jit(solution)/shard_map/ppermute | solution.py:135
  26.8 2.4 %constant_dynamic-slice_fusion.4 = (bf16[384,256]{1,0:T(8,128)(2,1)}, bf16[384,256]{1,0:T(8,128)(2,1)S(1)}, bf16[384,256]{1,0:T(8,128)(2,1)S(1)}, bf16[384,256]{...) fusion(bf16[384,1024]{1,0:T(8,128)(2,1)} %param.15, ...), kind=kLoop, calls=%fused_computation.128 | loop fusion | bytes 3145744 | tf_op jit(solution)/shard_map/dynamic_slice | solution.py:139
  30.0 1.9 %collective-permute-start.5 = (bf16[384,512]{1,0:T(8,128)(2,1)}, bf16[384,512]{1,0:T(8,128)(2,1)}, u32[]{:S(2)}, u32[]{:S(2)}) collective-permute-start(bf16[384,512]{1,0:T(8,128)(2,1)} %pad_maximum_fusion.4), channel_id=1, source_target_pairs={{0,4},{4,0},{8,12},{12,8},{1,5},{5,1},{9,13},{13,9},{2,6},{6,2},{1... | collective-permute-start | bytes 1179656 | tf_op jit(solution)/shard_map/ppermute | solution.py:135
  31.9 1.6 %fusion.38 = bf16[192,512]{1,0:T(8,128)(2,1)} fusion(s32[]{:T(128)S(6)} %select_n.183, bf16[384,256]{1,0:T(8,128)(2,1)} %get-tuple-element.45, bf16[384,256]{1,0:T(8,128)(2,1)} %get-tuple-element.27), kind=kLoop, calls=%fused_computation.72 | loop fusion | flops 393216 | bytes 589828 | tf_op jit(solution)/shard_map/concatenate | solution.py:214
  34.5 1.6 %fusion.37 = bf16[192,512]{1,0:T(8,128)(2,1)} fusion(s32[]{:T(128)S(6)} %select_n.183, bf16[384,256]{1,0:T(8,128)(2,1)} %get-tuple-element.48, bf16[384,256]{1,0:T(8,128)(2,1)} %get-tuple-element.24), kind=kLoop, calls=%fused_computation.71 | loop fusion | flops 393216 | bytes 589828 | tf_op jit(solution)/shard_map/concatenate | solution.py:214
  36.2 1.5 collective-permute-start.8
  37.7 1.2 pad_maximum_fusion
  39.8 1.2 broadcast_in_dim.20
  42.0 1.6 %constant_dynamic-slice_fusion = (bf16[128,384]{1,0:T(8,128)(2,1)}, bf16[128,384]{1,0:T(8,128)(2,1)S(1)}) fusion(bf16[1024,384]{1,0:T(8,128)(2,1)} %param.16, s32[]{:T(128)S(6)} %dynamic_slice.81, s32[]{:T(128)S(6)} %dynamic_slice.79), kind=kLoop, calls=%fused_computation.122 | loop fusion | bytes 393224 | tf_op jit(solution)/shard_map/dynamic_slice | solution.py:139
  43.6 1.9 %collective-permute-done.6 = bf16[192,512]{1,0:T(8,128)(2,1)} collective-permute-done((bf16[192,512]{1,0:T(8,128)(2,1)}, bf16[192,512]{1,0:T(8,128)(2,1)}, u32[]{:S(2)}, u32[]{:S(2)}) %collective-permute-start.6) | collective-permute-done | bytes 196640 | tf_op jit(solution)/shard_map/ppermute | solution.py:135
  45.5 1.5 %collective-permute-start.7 = (bf16[192,512]{1,0:T(8,128)(2,1)}, bf16[192,512]{1,0:T(8,128)(2,1)S(1)}, u32[]{:S(2)}, u32[]{:S(2)}) collective-permute-start(bf16[192,512]{1,0:T(8,128)(2,1)} %collective-permute-done.6), channel_id=1, source_target_pairs={{0,16},{16,0},{1,17},{17,1},{2,18},{18,2},{3,19},{19,3},{4,20},{20... | collective-permute-start | bytes 589832 | tf_op jit(solution)/shard_map/ppermute | solution.py:135
  47.0 3.8 %collective-permute-done.8 = bf16[192,512]{1,0:T(8,128)(2,1)} collective-permute-done((bf16[192,512]{1,0:T(8,128)(2,1)}, bf16[192,512]{1,0:T(8,128)(2,1)}, u32[]{:S(2)}, u32[]{:S(2)}) %collective-permute-start.8) | collective-permute-done | bytes 196640 | tf_op jit(solution)/shard_map/ppermute | solution.py:135
  50.7 1.5 %collective-permute-start.9 = (bf16[192,512]{1,0:T(8,128)(2,1)}, bf16[192,512]{1,0:T(8,128)(2,1)S(1)}, u32[]{:S(2)}, u32[]{:S(2)}) collective-permute-start(bf16[192,512]{1,0:T(8,128)(2,1)} %collective-permute-done.8), channel_id=1, source_target_pairs={{0,16},{16,0},{1,17},{17,1},{2,18},{18,2},{3,19},{19,3},{4,20},{20... | collective-permute-start | bytes 589832 | tf_op jit(solution)/shard_map/ppermute | solution.py:135
  52.3 1.8 %constant_dynamic-update-slice_fusion.6 = bf16[1536,512]{1,0:T(8,128)(2,1)} fusion(bf16[1536,512]{1,0:T(8,128)(2,1)} %maximum_dynamic-update-slice_fusion, bf16[384,512]{1,0:T(8,128)(2,1)} %collective-permute-done.5, s32[]{:T(128)S(6)} %select_n.180), kind=kLoop, calls=%fused_computation.132 | loop fusion | bytes 786436 | tf_op jit(solution)/shard_map/dynamic_update_slice | solution.py:148
  54.0 1.9 %fusion.26 = bf16[1536,512]{1,0:T(8,128)(2,1)} fusion(bf16[1536,512]{1,0:T(8,128)(2,1)} %constant_dynamic-update-slice_fusion.6, s32[]{:T(128)S(6)} %select_n.185, bf16[192,512]{1,0:T(8,128)(2,1)S(1)} %collective-permute-done.7, bf16[192,512]{1,0:T(8,128)(2,1)} %collective-permute-done.6, pred[]{:T(512)S(6)} %eq.43), kind=kLoop, calls=%fused_computation.53 | loop fusion | flops 1769472 | bytes 786437 | tf_op jit(solution)/shard_map/dynamic_update_slice | solution.py:148
  56.6 2.0 %constant_dynamic-update-slice_fusion.5 = bf16[1536,512]{1,0:T(8,128)(2,1)} fusion(bf16[1536,512]{1,0:T(8,128)(2,1)} %fusion.26, s32[]{:T(128)S(6)} %select_n.188, bf16[192,512]{1,0:T(8,128)(2,1)} %collective-permute-done.8, bf16[192,512]{1,0:T(8,128)(2,1)S(1)} %collective-permute-done.9, pred[]{:T(512)S(6)} %eq.43), kind=kLoop, calls=%fused_computation.127 | loop fusion | flops 1769472 | bytes 786437 | tf_op jit(solution)/shard_map/dynamic_update_slice | solution.py:148
  58.6 3.3 %collective-permute-start.13 = (bf16[128,384]{1,0:T(8,128)(2,1)S(1)}, bf16[128,384]{1,0:T(8,128)(2,1)}, u32[]{:S(2)}, u32[]{:S(2)}) collective-permute-start(bf16[128,384]{1,0:T(8,128)(2,1)S(1)} %get-tuple-element.11), channel_id=1, source_target_pairs={{0,8},{4,12},{8,0},{12,4},{1,9},{5,13},{9,1},{13,5},{2,10},{6,14},... | collective-permute-start | bytes 294920 | tf_op jit(solution)/shard_map/ppermute | solution.py:135
  64.0 2.6 %collective-permute-start.15 = (bf16[128,384]{1,0:T(8,128)(2,1)}, bf16[128,384]{1,0:T(8,128)(2,1)}, u32[]{:S(2)}, u32[]{:S(2)}) collective-permute-start(bf16[128,384]{1,0:T(8,128)(2,1)} %get-tuple-element.12), channel_id=1, source_target_pairs={{0,12},{4,8},{8,4},{12,0},{1,13},{5,9},{9,5},{13,1},{2,14},{6,10},... | collective-permute-start | bytes 294920 | tf_op jit(solution)/shard_map/ppermute | solution.py:135
  66.5 1.7 %collective-permute-done.13 = bf16[128,384]{1,0:T(8,128)(2,1)} collective-permute-done((bf16[128,384]{1,0:T(8,128)(2,1)S(1)}, bf16[128,384]{1,0:T(8,128)(2,1)}, u32[]{:S(2)}, u32[]{:S(2)}) %collective-permute-start.13) | collective-permute-done | bytes 98336 | tf_op jit(solution)/shard_map/ppermute | solution.py:135
  68.3 1.5 %collective-permute-start.14 = (bf16[128,384]{1,0:T(8,128)(2,1)}, bf16[128,384]{1,0:T(8,128)(2,1)}, u32[]{:S(2)}, u32[]{:S(2)}) collective-permute-start(bf16[128,384]{1,0:T(8,128)(2,1)} %collective-permute-done.13), channel_id=1, source_target_pairs={{0,16},{16,0},{1,17},{17,1},{2,18},{18,2},{3,19},{19,3},{4,20},{20... | collective-permute-start | bytes 294920 | tf_op jit(solution)/shard_map/ppermute | solution.py:135
  69.8 2.0 %fusion.23 = bf16[768,1536]{1,0:T(8,128)(2,1)} fusion(bf16[768,1536]{1,0:T(8,128)(2,1)} %get-tuple-element.33, s32[]{:T(128)S(6)} %select_n.174, bf16[2,768,384]{2,1,0:T(8,128)(2,1)} %collective-permute-done.4), kind=kLoop, calls=%fused_computation.41 | loop fusion | bytes 1179652 | tf_op jit(solution)/shard_map/dynamic_update_slice | solution.py:148
  72.7 2.0 %fusion.22 = bf16[768,1536]{1,0:T(8,128)(2,1)} fusion(bf16[768,1536]{1,0:T(8,128)(2,1)} %bitcast_dynamic-update-slice_fusion, s32[]{:T(128)S(6)} %select_n.176, bf16[2,768,384]{2,1,0:T(8,128)(2,1)} %collective-permute-done.4), kind=kLoop, calls=%fused_computation.39 | loop fusion | bytes 1179652 | tf_op jit(solution)/shard_map/dynamic_update_slice | solution.py:148
  74.7 2.2 %fusion = f32[768]{0:T(1024)S(1)} fusion(bf16[768,1536]{1,0:T(8,128)(2,1)} %fusion.22), kind=kLoop, calls=%fused_computation.2 | loop fusion | flops 3538176 | bytes 2362368 | tf_op jit(solution)/shard_map/reduce_sum | solution.py:233
  76.9 3.5 %fusion.3 = f32[768,512]{1,0:T(8,128)S(1)} fusion(bf16[1536,512]{1,0:T(8,128)(2,1)} %constant_dynamic-update-slice_fusion.5, bf16[768,1536]{1,0:T(8,128)(2,1)} %fusion.22, f32[1536]{0:T(1024)S(1)} %copy-done.12, f32[768]{0:T(1024)S(1)} %add_rsqrt_fusion), kind=kOutput, calls=%fused_computation.5 | convolution fusion | flops 1212678144 | bytes 5514240 | tf_op jit(solution)/shard_map/dot_general | solution.py:235
  83.1 1.1 maximum_select_fusion.2
  84.2 3.2 %collective-permute-done.16 = bf16[128,384]{1,0:T(8,128)(2,1)S(1)} collective-permute-done((bf16[128,384]{1,0:T(8,128)(2,1)}, bf16[128,384]{1,0:T(8,128)(2,1)S(1)}, u32[]{:S(2)}, u32[]{:S(2)}) %collective-permute-start.16) | collective-permute-done | bytes 98336 | tf_op jit(solution)/shard_map/ppermute | solution.py:135
  88.5 1.1 pad_maximum_fusion.2
  89.8 1.2 pad_maximum_fusion.1
  91.7 1.5 %collective-permute-start.18 = (bf16[256,384]{1,0:T(8,128)(2,1)S(1)}, bf16[256,384]{1,0:T(8,128)(2,1)S(1)}, u32[]{:S(2)}, u32[]{:S(2)}) collective-permute-start(bf16[256,384]{1,0:T(8,128)(2,1)S(1)} %get-tuple-element.18), channel_id=1, source_target_pairs={{0,2},{1,3},{2,0},{3,1},{4,6},{5,7},{6,4},{7,5},{8,10},{9,11},{10,... | collective-permute-start | bytes 589832 | tf_op jit(solution)/shard_map/ppermute | solution.py:135
  93.6 5.9 %collective-permute-done.18 = bf16[256,384]{1,0:T(8,128)(2,1)S(1)} collective-permute-done((bf16[256,384]{1,0:T(8,128)(2,1)S(1)}, bf16[256,384]{1,0:T(8,128)(2,1)S(1)}, u32[]{:S(2)}, u32[]{:S(2)}) %collective-permute-start.18) | collective-permute-done | bytes 196640 | tf_op jit(solution)/shard_map/ppermute | solution.py:135
  99.6 2.3 %collective-permute-done.19 = bf16[256,384]{1,0:T(8,128)(2,1)S(1)} collective-permute-done((bf16[256,384]{1,0:T(8,128)(2,1)S(1)}, bf16[256,384]{1,0:T(8,128)(2,1)S(1)}, u32[]{:S(2)}, u32[]{:S(2)}) %collective-permute-start.19) | collective-permute-done | bytes 196640 | tf_op jit(solution)/shard_map/ppermute | solution.py:135
  104.5 1.6 %collective-permute-start.20 = (bf16[256,384]{1,0:T(8,128)(2,1)S(1)}, bf16[256,384]{1,0:T(8,128)(2,1)S(1)}, u32[]{:S(2)}, u32[]{:S(2)}) collective-permute-start(bf16[256,384]{1,0:T(8,128)(2,1)S(1)} %convolution_convert_fusion.3), channel_id=1, source_target_pairs={{0,4},{4,0},{8,12},{12,8},{1,5},{5,1},{9,13},{13,9},{2,6},{6,2},{1... | collective-permute-start | bytes 589832 | tf_op jit(solution)/shard_map/ppermute | solution.py:135
  106.6 1.8 %collective-permute-start.21 = (bf16[256,384]{1,0:T(8,128)(2,1)S(1)}, bf16[256,384]{1,0:T(8,128)(2,1)S(1)}, u32[]{:S(2)}, u32[]{:S(2)}) collective-permute-start(bf16[256,384]{1,0:T(8,128)(2,1)S(1)} %convolution_convert_fusion.2), channel_id=1, source_target_pairs={{0,8},{4,12},{8,0},{12,4},{1,9},{5,13},{9,1},{13,5},{2,10},{6,14},... | collective-permute-start | bytes 589832 | tf_op jit(solution)/shard_map/ppermute | solution.py:135
  108.8 1.5 collective-permute-start.22
  110.7 5.4 %collective-permute-done.20 = bf16[256,384]{1,0:T(8,128)(2,1)S(1)} collective-permute-done((bf16[256,384]{1,0:T(8,128)(2,1)S(1)}, bf16[256,384]{1,0:T(8,128)(2,1)S(1)}, u32[]{:S(2)}, u32[]{:S(2)}) %collective-permute-start.20) | collective-permute-done | bytes 196640 | tf_op jit(solution)/shard_map/ppermute | solution.py:135
  116.1 7.7 %collective-permute-done.21 = bf16[256,384]{1,0:T(8,128)(2,1)S(1)} collective-permute-done((bf16[256,384]{1,0:T(8,128)(2,1)S(1)}, bf16[256,384]{1,0:T(8,128)(2,1)S(1)}, u32[]{:S(2)}, u32[]{:S(2)}) %collective-permute-start.21) | collective-permute-done | bytes 196640 | tf_op jit(solution)/shard_map/ppermute | solution.py:135
  124.3 1.4 collective-permute-start.23
  125.8 4.8 %collective-permute-done.23 = bf16[1,256,384]{2,1,0:T(8,128)(2,1)S(1)} collective-permute-done((bf16[1,256,384]{2,1,0:T(8,128)(2,1)S(1)}, bf16[1,256,384]{2,1,0:T(8,128)(2,1)S(1)}, u32[]{:S(2)}, u32[]{:S(2)}) %collective-permute-start.23) | collective-permute-done | bytes 196640 | tf_op jit(solution)/shard_map/ppermute | solution.py:135
  130.8 1.6 %collective-permute-done.24 = bf16[2,256,384]{2,1,0:T(8,128)(2,1)S(1)} collective-permute-done((bf16[2,256,384]{2,1,0:T(8,128)(2,1)S(1)}, bf16[2,256,384]{2,1,0:T(8,128)(2,1)S(1)}, u32[]{:S(2)}, u32[]{:S(2)}) %collective-permute-start.24) | collective-permute-done | bytes 393248 | tf_op jit(solution)/shard_map/ppermute | solution.py:135
  134.5 4.4 %collective-permute-start.25 = (bf16[32,384]{1,0:T(8,128)(2,1)S(1)}, bf16[32,384]{1,0:T(8,128)(2,1)S(1)}, u32[]{:S(2)}, u32[]{:S(2)}) collective-permute-start(bf16[32,384]{1,0:T(8,128)(2,1)S(1)} %bitcast.155), channel_id=1, source_target_pairs={{0,4},{4,0},{8,12},{12,8},{1,5},{5,1},{9,13},{13,9},{2,6},{6,2},{1... | collective-permute-start | bytes 73736 | tf_op jit(solution)/shard_map/ppermute | solution.py:135
  138.9 2.0 %collective-permute-start.26 = (bf16[32,384]{1,0:T(8,128)(2,1)S(1)}, bf16[32,384]{1,0:T(8,128)(2,1)S(1)}, u32[]{:S(2)}, u32[]{:S(2)}) collective-permute-start(bf16[32,384]{1,0:T(8,128)(2,1)S(1)} %bitcast.156), channel_id=1, source_target_pairs={{0,8},{4,12},{8,0},{12,4},{1,9},{5,13},{9,1},{13,5},{2,10},{6,14},... | collective-permute-start | bytes 73736 | tf_op jit(solution)/shard_map/ppermute | solution.py:135
  140.8 1.4 collective-permute-start.27
  144.0 2.5 %collective-permute-done.27 = bf16[32,384]{1,0:T(8,128)(2,1)S(1)} collective-permute-done((bf16[32,384]{1,0:T(8,128)(2,1)S(1)}, bf16[32,384]{1,0:T(8,128)(2,1)S(1)}, u32[]{:S(2)}, u32[]{:S(2)}) %collective-permute-start.27) | collective-permute-done | bytes 24608 | tf_op jit(solution)/shard_map/ppermute | solution.py:135
  (135 shorter events, 27.4 us)
Async XLA Ops:
  0.0 132.8 %copy-start = (bf16[1536,576]{0,1:T(8,128)(2,1)S(1)}, bf16[1536,576]{0,1:T(8,128)(2,1)}, u32[]{:S(2)}) copy-start(bf16[1536,576]{0,1:T(8,128)(2,1)} %param.18) | copy-start | bytes 5308420
  3.4 9.6 %collective-permute-start = (bf16[208,384]{1,0:T(8,128)(2,1)S(1)}, bf16[208,384]{1,0:T(8,128)(2,1)S(1)}, u32[]{:S(2)}, u32[]{:S(2)}) collective-permute-start(bf16[208,384]{1,0:T(8,128)(2,1)S(1)} %fusion.49), channel_id=1, source_target_pairs={{0,4},{4,0},{8,12},{12,8},{1,5},{5,1},{9,13},{13,9},{2,6},{6,2},{1... | collective-permute-start | bytes 479240 | tf_op jit(solution)/shard_map/ppermute | solution.py:135
  6.5 14.8 %collective-permute-start.1 = (bf16[208,384]{1,0:T(8,128)(2,1)S(1)}, bf16[208,384]{1,0:T(8,128)(2,1)S(1)}, u32[]{:S(2)}, u32[]{:S(2)}) collective-permute-start(bf16[208,384]{1,0:T(8,128)(2,1)S(1)} %fusion.49), channel_id=1, source_target_pairs={{0,8},{4,12},{8,0},{12,4},{1,9},{5,13},{9,1},{13,5},{2,10},{6,14},... | collective-permute-start | bytes 479240 | tf_op jit(solution)/shard_map/ppermute | solution.py:135
  9.1 12.2 %collective-permute-start.2 = (bf16[208,384]{1,0:T(8,128)(2,1)S(1)}, bf16[208,384]{1,0:T(8,128)(2,1)S(1)}, u32[]{:S(2)}, u32[]{:S(2)}) collective-permute-start(bf16[208,384]{1,0:T(8,128)(2,1)S(1)} %fusion.49), channel_id=1, source_target_pairs={{0,12},{4,8},{8,4},{12,0},{1,13},{5,9},{9,5},{13,1},{2,14},{6,10},... | collective-permute-start | bytes 479240 | tf_op jit(solution)/shard_map/ppermute | solution.py:135
  12.9 8.4 %copy-start.8 = (bf16[208,384]{1,0:T(8,128)(2,1)}, bf16[208,384]{1,0:T(8,128)(2,1)S(1)}, u32[]{:S(2)}) copy-start(bf16[208,384]{1,0:T(8,128)(2,1)S(1)} %collective-permute-done) | copy-start | bytes 479236
  13.0 12.2 %copy-start.1 = (bf16[192,384]{1,0:T(8,128)(2,1)}, bf16[192,384]{1,0:T(8,128)(2,1)S(1)}, u32[]{:S(2)}) copy-start(bf16[192,384]{1,0:T(8,128)(2,1)S(1)} %slice.80) | copy-start | bytes 442372
  21.3 0.7 copy-start.9
  21.3 3.9 %copy-start.3 = (bf16[192,384]{1,0:T(8,128)(2,1)}, bf16[192,384]{1,0:T(8,128)(2,1)S(1)}, u32[]{:S(2)}) copy-start(bf16[192,384]{1,0:T(8,128)(2,1)S(1)} %slice.81) | copy-start | bytes 442372
  21.9 0.7 copy-start.10
  22.6 2.6 %copy-start.5 = (bf16[192,384]{1,0:T(8,128)(2,1)}, bf16[192,384]{1,0:T(8,128)(2,1)S(1)}, u32[]{:S(2)}) copy-start(bf16[192,384]{1,0:T(8,128)(2,1)S(1)} %slice.82) | copy-start | bytes 442372
  25.2 12.5 %collective-permute-start.3 = (bf16[1,768,384]{2,1,0:T(8,128)(2,1)S(1)}, bf16[1,768,384]{2,1,0:T(8,128)(2,1)S(1)}, u32[]{:S(2)}, u32[]{:S(2)}) collective-permute-start(bf16[1,768,384]{2,1,0:T(8,128)(2,1)S(1)} %get-tuple-element.32), channel_id=1, source_target_pairs={{0,2},{1,3},{2,0},{3,1},{4,6},{5,7},{6,4},{7,5},{8,10},{9,11},{10,... | collective-permute-start | bytes 1769480 | tf_op jit(solution)/shard_map/ppermute | solution.py:135
  30.0 22.3 %collective-permute-start.5 = (bf16[384,512]{1,0:T(8,128)(2,1)}, bf16[384,512]{1,0:T(8,128)(2,1)}, u32[]{:S(2)}, u32[]{:S(2)}) collective-permute-start(bf16[384,512]{1,0:T(8,128)(2,1)} %pad_maximum_fusion.4), channel_id=1, source_target_pairs={{0,4},{4,0},{8,12},{12,8},{1,5},{5,1},{9,13},{13,9},{2,6},{6,2},{1... | collective-permute-start | bytes 1179656 | tf_op jit(solution)/shard_map/ppermute | solution.py:135
  33.5 11.9 %collective-permute-start.6 = (bf16[192,512]{1,0:T(8,128)(2,1)}, bf16[192,512]{1,0:T(8,128)(2,1)}, u32[]{:S(2)}, u32[]{:S(2)}) collective-permute-start(bf16[192,512]{1,0:T(8,128)(2,1)} %fusion.38), channel_id=1, source_target_pairs={{0,8},{4,12},{8,0},{12,4},{1,9},{5,13},{9,1},{13,5},{2,10},{6,14},... | collective-permute-start | bytes 589832 | tf_op jit(solution)/shard_map/ppermute | solution.py:135
  36.2 14.6 %collective-permute-start.8 = (bf16[192,512]{1,0:T(8,128)(2,1)}, bf16[192,512]{1,0:T(8,128)(2,1)}, u32[]{:S(2)}, u32[]{:S(2)}) collective-permute-start(bf16[192,512]{1,0:T(8,128)(2,1)} %fusion.37), channel_id=1, source_target_pairs={{0,12},{4,8},{8,4},{12,0},{1,13},{5,9},{9,5},{13,1},{2,14},{6,10},... | collective-permute-start | bytes 589832 | tf_op jit(solution)/shard_map/ppermute | solution.py:135
  37.7 1.3 copy-start.7
  38.8 31.0 %collective-permute-start.4 = (bf16[2,768,384]{2,1,0:T(8,128)(2,1)}, bf16[2,768,384]{2,1,0:T(8,128)(2,1)}, u32[]{:S(2)}, u32[]{:S(2)}) collective-permute-start(bf16[2,768,384]{2,1,0:T(8,128)(2,1)} %pad_maximum_fusion), channel_id=1, source_target_pairs={{0,1},{1,0},{2,3},{3,2},{4,5},{5,4},{6,7},{7,6},{8,9},{9,8},{10,11... | collective-permute-start | bytes 3538952 | tf_op jit(solution)/shard_map/ppermute | solution.py:135
  45.5 8.6 %collective-permute-start.7 = (bf16[192,512]{1,0:T(8,128)(2,1)}, bf16[192,512]{1,0:T(8,128)(2,1)S(1)}, u32[]{:S(2)}, u32[]{:S(2)}) collective-permute-start(bf16[192,512]{1,0:T(8,128)(2,1)} %collective-permute-done.6), channel_id=1, source_target_pairs={{0,16},{16,0},{1,17},{17,1},{2,18},{18,2},{3,19},{19,3},{4,20},{20... | collective-permute-start | bytes 589832 | tf_op jit(solution)/shard_map/ppermute | solution.py:135
  50.7 5.9 %collective-permute-start.9 = (bf16[192,512]{1,0:T(8,128)(2,1)}, bf16[192,512]{1,0:T(8,128)(2,1)S(1)}, u32[]{:S(2)}, u32[]{:S(2)}) collective-permute-start(bf16[192,512]{1,0:T(8,128)(2,1)} %collective-permute-done.8), channel_id=1, source_target_pairs={{0,16},{16,0},{1,17},{17,1},{2,18},{18,2},{3,19},{19,3},{4,20},{20... | collective-permute-start | bytes 589832 | tf_op jit(solution)/shard_map/ppermute | solution.py:135
  58.6 9.7 %collective-permute-start.13 = (bf16[128,384]{1,0:T(8,128)(2,1)S(1)}, bf16[128,384]{1,0:T(8,128)(2,1)}, u32[]{:S(2)}, u32[]{:S(2)}) collective-permute-start(bf16[128,384]{1,0:T(8,128)(2,1)S(1)} %get-tuple-element.11), channel_id=1, source_target_pairs={{0,8},{4,12},{8,0},{12,4},{1,9},{5,13},{9,1},{13,5},{2,10},{6,14},... | collective-permute-start | bytes 294920 | tf_op jit(solution)/shard_map/ppermute | solution.py:135
  64.0 18.7 %collective-permute-start.15 = (bf16[128,384]{1,0:T(8,128)(2,1)}, bf16[128,384]{1,0:T(8,128)(2,1)}, u32[]{:S(2)}, u32[]{:S(2)}) collective-permute-start(bf16[128,384]{1,0:T(8,128)(2,1)} %get-tuple-element.12), channel_id=1, source_target_pairs={{0,12},{4,8},{8,4},{12,0},{1,13},{5,9},{9,5},{13,1},{2,14},{6,10},... | collective-permute-start | bytes 294920 | tf_op jit(solution)/shard_map/ppermute | solution.py:135
  68.3 14.9 %collective-permute-start.14 = (bf16[128,384]{1,0:T(8,128)(2,1)}, bf16[128,384]{1,0:T(8,128)(2,1)}, u32[]{:S(2)}, u32[]{:S(2)}) collective-permute-start(bf16[128,384]{1,0:T(8,128)(2,1)} %collective-permute-done.13), channel_id=1, source_target_pairs={{0,16},{16,0},{1,17},{17,1},{2,18},{18,2},{3,19},{19,3},{4,20},{20... | collective-permute-start | bytes 294920 | tf_op jit(solution)/shard_map/ppermute | solution.py:135
  72.7 4.2 %copy-start.12 = (f32[1536]{0:T(1024)S(1)}, f32[1536]{0:T(1024)}, u32[]{:S(2)}) copy-start(f32[1536]{0:T(1024)} %param.13) | copy-start | bytes 18436
  81.7 8.1 %collective-permute-start.10 = (bf16[1,768,256]{2,1,0:T(8,128)(2,1)}, bf16[1,768,256]{2,1,0:T(8,128)(2,1)}, u32[]{:S(2)}, u32[]{:S(2)}) collective-permute-start(bf16[1,768,256]{2,1,0:T(8,128)(2,1)} %bitcast.8), channel_id=1, source_target_pairs={{0,2},{1,3},{2,0},{3,1},{4,6},{5,7},{6,4},{7,5},{8,10},{9,11},{10,... | collective-permute-start | bytes 1179656 | tf_op jit(solution)/shard_map/ppermute | solution.py:135
  81.8 6.7 %collective-permute-start.12 = (bf16[256,384]{1,0:T(8,128)(2,1)}, bf16[256,384]{1,0:T(8,128)(2,1)S(1)}, u32[]{:S(2)}, u32[]{:S(2)}) collective-permute-start(bf16[256,384]{1,0:T(8,128)(2,1)} %get-tuple-element.10), channel_id=1, source_target_pairs={{0,4},{4,0},{8,12},{12,8},{1,5},{5,1},{9,13},{13,9},{2,6},{6,2},{1... | collective-permute-start | bytes 589832 | tf_op jit(solution)/shard_map/ppermute | solution.py:135
  82.6 4.8 %collective-permute-start.16 = (bf16[128,384]{1,0:T(8,128)(2,1)}, bf16[128,384]{1,0:T(8,128)(2,1)S(1)}, u32[]{:S(2)}, u32[]{:S(2)}) collective-permute-start(bf16[128,384]{1,0:T(8,128)(2,1)} %collective-permute-done.15), channel_id=1, source_target_pairs={{0,16},{16,0},{1,17},{17,1},{2,18},{18,2},{3,19},{19,3},{4,20},{20... | collective-permute-start | bytes 294920 | tf_op jit(solution)/shard_map/ppermute | solution.py:135
  91.0 10.9 %collective-permute-start.11 = (bf16[2,768,256]{2,1,0:T(8,128)(2,1)S(1)}, bf16[2,768,256]{2,1,0:T(8,128)(2,1)S(1)}, u32[]{:S(2)}, u32[]{:S(2)}) collective-permute-start(bf16[2,768,256]{2,1,0:T(8,128)(2,1)S(1)} %pad_maximum_fusion.1), channel_id=1, source_target_pairs={{0,1},{1,0},{2,3},{3,2},{4,5},{5,4},{6,7},{7,6},{8,9},{9,8},{10,11... | collective-permute-start | bytes 2359304 | tf_op jit(solution)/shard_map/ppermute | solution.py:135
  91.1 2.5 %collective-permute-start.17 = (bf16[256,384]{1,0:T(8,128)(2,1)S(1)}, bf16[256,384]{1,0:T(8,128)(2,1)S(1)}, u32[]{:S(2)}, u32[]{:S(2)}) collective-permute-start(bf16[256,384]{1,0:T(8,128)(2,1)S(1)} %get-tuple-element.19), channel_id=1, source_target_pairs={{0,1},{1,0},{2,3},{3,2},{4,5},{5,4},{6,7},{7,6},{8,9},{9,8},{10,11... | collective-permute-start | bytes 589832 | tf_op jit(solution)/shard_map/ppermute | solution.py:135
  91.7 7.8 %collective-permute-start.18 = (bf16[256,384]{1,0:T(8,128)(2,1)S(1)}, bf16[256,384]{1,0:T(8,128)(2,1)S(1)}, u32[]{:S(2)}, u32[]{:S(2)}) collective-permute-start(bf16[256,384]{1,0:T(8,128)(2,1)S(1)} %get-tuple-element.18), channel_id=1, source_target_pairs={{0,2},{1,3},{2,0},{3,1},{4,6},{5,7},{6,4},{7,5},{8,10},{9,11},{10,... | collective-permute-start | bytes 589832 | tf_op jit(solution)/shard_map/ppermute | solution.py:135
  93.2 8.6 %collective-permute-start.19 = (bf16[256,384]{1,0:T(8,128)(2,1)S(1)}, bf16[256,384]{1,0:T(8,128)(2,1)S(1)}, u32[]{:S(2)}, u32[]{:S(2)}) collective-permute-start(bf16[256,384]{1,0:T(8,128)(2,1)S(1)} %get-tuple-element.17), channel_id=1, source_target_pairs={{0,3},{1,2},{2,1},{3,0},{4,7},{5,6},{6,5},{7,4},{8,11},{9,10},{10,... | collective-permute-start | bytes 589832 | tf_op jit(solution)/shard_map/ppermute | solution.py:135
  104.5 11.6 %collective-permute-start.20 = (bf16[256,384]{1,0:T(8,128)(2,1)S(1)}, bf16[256,384]{1,0:T(8,128)(2,1)S(1)}, u32[]{:S(2)}, u32[]{:S(2)}) collective-permute-start(bf16[256,384]{1,0:T(8,128)(2,1)S(1)} %convolution_convert_fusion.3), channel_id=1, source_target_pairs={{0,4},{4,0},{8,12},{12,8},{1,5},{5,1},{9,13},{13,9},{2,6},{6,2},{1... | collective-permute-start | bytes 589832 | tf_op jit(solution)/shard_map/ppermute | solution.py:135
  106.6 17.3 %copy-start.2 = (bf16[192,384]{1,0:T(8,128)(2,1)S(1)}, bf16[192,384]{1,0:T(8,128)(2,1)}, u32[]{:S(2)}) copy-start(bf16[192,384]{1,0:T(8,128)(2,1)} %copy-done.1) | copy-start | bytes 442372
  106.6 17.3 %copy-start.4 = (bf16[192,384]{1,0:T(8,128)(2,1)S(1)}, bf16[192,384]{1,0:T(8,128)(2,1)}, u32[]{:S(2)}) copy-start(bf16[192,384]{1,0:T(8,128)(2,1)} %copy-done.3) | copy-start | bytes 442372
  106.6 17.3 %copy-start.6 = (bf16[192,384]{1,0:T(8,128)(2,1)S(1)}, bf16[192,384]{1,0:T(8,128)(2,1)}, u32[]{:S(2)}) copy-start(bf16[192,384]{1,0:T(8,128)(2,1)} %copy-done.5) | copy-start | bytes 442372
  106.6 17.2 %collective-permute-start.21 = (bf16[256,384]{1,0:T(8,128)(2,1)S(1)}, bf16[256,384]{1,0:T(8,128)(2,1)S(1)}, u32[]{:S(2)}, u32[]{:S(2)}) collective-permute-start(bf16[256,384]{1,0:T(8,128)(2,1)S(1)} %convolution_convert_fusion.2), channel_id=1, source_target_pairs={{0,8},{4,12},{8,0},{12,4},{1,9},{5,13},{9,1},{13,5},{2,10},{6,14},... | collective-permute-start | bytes 589832 | tf_op jit(solution)/shard_map/ppermute | solution.py:135
  108.8 14.9 %collective-permute-start.22 = (bf16[256,384]{1,0:T(8,128)(2,1)S(1)}, bf16[256,384]{1,0:T(8,128)(2,1)S(1)}, u32[]{:S(2)}, u32[]{:S(2)}) collective-permute-start(bf16[256,384]{1,0:T(8,128)(2,1)S(1)} %convolution_convert_fusion.1), channel_id=1, source_target_pairs={{0,12},{4,8},{8,4},{12,0},{1,13},{5,9},{9,5},{13,1},{2,14},{6,10},... | collective-permute-start | bytes 589832 | tf_op jit(solution)/shard_map/ppermute | solution.py:135
  123.9 6.9 %copy-start.11 = (s32[3]{0:T(128)S(1)}, s32[3]{0:T(128)}, u32[]{:S(2)}) copy-start(s32[3]{0:T(128)} %param.19) | copy-start | bytes 40
  124.3 8.5 %copy-start.13 = (f32[1536]{0:T(1024)S(1)}, f32[1536]{0:T(1024)}, u32[]{:S(2)}) copy-start(f32[1536]{0:T(1024)} %param.17) | copy-start | bytes 18436
  124.3 6.3 %collective-permute-start.23 = (bf16[1,256,384]{2,1,0:T(8,128)(2,1)S(1)}, bf16[1,256,384]{2,1,0:T(8,128)(2,1)S(1)}, u32[]{:S(2)}, u32[]{:S(2)}) collective-permute-start(bf16[1,256,384]{2,1,0:T(8,128)(2,1)S(1)} %bitcast.149), channel_id=1, source_target_pairs={{0,2},{1,3},{2,0},{3,1},{4,6},{5,7},{6,4},{7,5},{8,10},{9,11},{10,... | collective-permute-start | bytes 589832 | tf_op jit(solution)/shard_map/ppermute | solution.py:135
  130.7 1.8 %collective-permute-start.24 = (bf16[2,256,384]{2,1,0:T(8,128)(2,1)S(1)}, bf16[2,256,384]{2,1,0:T(8,128)(2,1)S(1)}, u32[]{:S(2)}, u32[]{:S(2)}) collective-permute-start(bf16[2,256,384]{2,1,0:T(8,128)(2,1)S(1)} %pad_maximum_fusion.5), channel_id=1, source_target_pairs={{0,1},{1,0},{2,3},{3,2},{4,5},{5,4},{6,7},{7,6},{8,9},{9,8},{10,11... | collective-permute-start | bytes 1179656 | tf_op jit(solution)/shard_map/ppermute | solution.py:135
  134.5 8.7 %collective-permute-start.25 = (bf16[32,384]{1,0:T(8,128)(2,1)S(1)}, bf16[32,384]{1,0:T(8,128)(2,1)S(1)}, u32[]{:S(2)}, u32[]{:S(2)}) collective-permute-start(bf16[32,384]{1,0:T(8,128)(2,1)S(1)} %bitcast.155), channel_id=1, source_target_pairs={{0,4},{4,0},{8,12},{12,8},{1,5},{5,1},{9,13},{13,9},{2,6},{6,2},{1... | collective-permute-start | bytes 73736 | tf_op jit(solution)/shard_map/ppermute | solution.py:135
  138.9 4.9 %collective-permute-start.26 = (bf16[32,384]{1,0:T(8,128)(2,1)S(1)}, bf16[32,384]{1,0:T(8,128)(2,1)S(1)}, u32[]{:S(2)}, u32[]{:S(2)}) collective-permute-start(bf16[32,384]{1,0:T(8,128)(2,1)S(1)} %bitcast.156), channel_id=1, source_target_pairs={{0,8},{4,12},{8,0},{12,4},{1,9},{5,13},{9,1},{13,5},{2,10},{6,14},... | collective-permute-start | bytes 73736 | tf_op jit(solution)/shard_map/ppermute | solution.py:135
  140.8 5.6 %collective-permute-start.27 = (bf16[32,384]{1,0:T(8,128)(2,1)S(1)}, bf16[32,384]{1,0:T(8,128)(2,1)S(1)}, u32[]{:S(2)}, u32[]{:S(2)}) collective-permute-start(bf16[32,384]{1,0:T(8,128)(2,1)S(1)} %bitcast.157), channel_id=1, source_target_pairs={{0,12},{4,8},{8,4},{12,0},{1,13},{5,9},{9,5},{13,1},{2,14},{6,10},... | collective-permute-start | bytes 73736 | tf_op jit(solution)/shard_map/ppermute | solution.py:135

commit v2 on v0

--- a/solution.py
+++ b/solution.py
@@ -1,6 +1,10 @@
+import functools
+
 import jax
 import jax.numpy as jnp
 from jax import lax
+from jax.experimental import pallas as pl
+from jax.experimental.pallas import tpu as pltpu
 from jax.sharding import PartitionSpec as P
 
 D_ENC = 1536
@@ -12,7 +16,14 @@
 epsilon = 1e-05
 
 
-def on_device(tiles, counts, dest, gain_enc, w_gate, w_up, w_down, gain_slide, w_qkv, offsets):
+def gather_seq(package):
+    count = lax.axis_size("seq")
+    if count & (count - 1) == 0 and count <= 4:
+        return jnp.concatenate([package] + [swap(package, "seq", d) for d in range(1, count)])
+    return lax.all_gather(package, "seq", axis=0, tiled=True)
+
+
+def gathered_plan(tiles, counts, dest, gain_enc, w_gate, w_up, w_down, gain_slide, w_qkv, offsets):
     seq_count = lax.axis_size("seq")
     capacity = ENCODER_SLOTS // seq_count
     tile_rows = tiles.shape[0]
@@ -48,7 +59,12 @@
         arrived_f, lax.axis_index("mp") * share_width, share_width, 1
     )
     embedded_cols = (own_cols + share).astype(jnp.bfloat16)
-    portion_f = lax.all_gather(embedded_cols, "mp", axis=1, tiled=True).astype(jnp.float32)
+    embedded = lax.all_gather(embedded_cols, "mp", axis=1, tiled=True)
+    return slide_layer(embedded, gain_slide, w_qkv, offsets)
+
+
+def slide_layer(embedded, gain_slide, w_qkv, offsets):
+    portion_f = embedded.astype(jnp.float32)
     accumulated = jnp.dot(
         (portion_f * gain_slide).astype(jnp.bfloat16), w_qkv, preferred_element_type=jnp.float32
     )
@@ -76,7 +92,7 @@
     package = jnp.concatenate([select_rows(keys_local), select_rows(values_local)], axis=2).reshape(
         selected_rows, local_head_output * 2 * HEAD_WIDTH
     )
-    portion = lax.all_gather(package, "seq", axis=0, tiled=True)
+    portion = gather_seq(package)
     parts_kv = portion.reshape(portion.shape[0], local_head_output, 2, HEAD_WIDTH)
     scores = (
         jnp.einsum(
@@ -116,6 +132,322 @@
         .reshape(ENCODER_SLOTS, local_head_output * HEAD_WIDTH)
         .astype(jnp.bfloat16)
     )
+
+
+def swap(array, axis, distance):
+    size = lax.axis_size(axis)
+    return lax.ppermute(array, axis, [(i, i ^ distance) for i in range(size)])
+
+
+def block_at(array, index, size, axis):
+    return lax.dynamic_slice_in_dim(array, index * size, size, axis)
+
+
+def copy_all(pairs, sems):
+    copies = [pltpu.make_async_copy(a, b, sems.at[i]) for i, (a, b) in enumerate(pairs)]
+    for copy in copies:
+        copy.start()
+    for copy in copies:
+        copy.wait()
+
+
+def call(body, outs, inputs, ids, copies=0, scratch=(), spaces=None, cost=None):
+    vmem, anywhere = pltpu.VMEM, pl.ANY
+    spaces = spaces or [vmem] * len(inputs)
+    in_specs = [pl.BlockSpec(memory_space=pltpu.SMEM)]
+    in_specs += [pl.BlockSpec(memory_space=space) for space in spaces]
+    out_space = anywhere if cost == "copies" else vmem
+    scratch = list(scratch)
+    if copies:
+        scratch.append(pltpu.SemaphoreType.DMA((copies,)))
+    return pl.pallas_call(
+        body,
+        out_shape=[jax.ShapeDtypeStruct(shape, kind) for shape, kind in outs],
+        in_specs=in_specs,
+        out_specs=[pl.BlockSpec(memory_space=out_space)] * len(outs),
+        scratch_shapes=scratch,
+        compiler_params=pltpu.CompilerParams(vmem_limit_bytes=40 * 1024 * 1024),
+    )(ids, *inputs)
+
+
+def at(index, size):
+    return pl.ds(pl.multiple_of(index * size, size), size)
+
+
+def cut_body(count, ids, tiles, w_gate, w_up, w_down, quarter, *outs_and_sems):
+    outs, sems = outs_and_sems[:-1], outs_and_sems[-1]
+    seq, mp, group = ids[0], ids[1], ids[2]
+    depth = w_gate.shape[0]
+    units = w_gate.shape[1] // count
+    pairs = [(tiles.at[:, at(mp, quarter.shape[1])], quarter)]
+    for d in range(1, count):
+        target = outs[d - 1]
+        rows = pl.ds(0, depth)
+        if target.shape[0] != depth:
+            rows = at(group, depth // 2)
+        for i, weight in enumerate((w_gate, w_up)):
+            pairs.append(
+                (weight.at[rows, at(seq ^ d, units)], target.at[:, pl.ds(i * units, units)])
+            )
+    for e in range(count):
+        target = outs[count - 1 + e]
+        half = target.shape[0]
+        pairs.append((w_down.at[at((e ^ mp) * 2 + group, half), :], target))
+    copy_all(pairs, sems)
+
+
+def hidden_body(count, ids, gain, tiles, w_gate, w_up, *refs):
+    (own, far, near, near_far) = refs[: count - 1], *refs[count - 1 : count + 2]
+    blocks = refs[count + 2 : count + 7]
+    first, second, weights, sems = refs[count + 7 :]
+    seq, mp, group = ids[0], ids[1], ids[2]
+    depth = w_gate.shape[0]
+    units = w_gate.shape[1] // count
+    half = depth // 2
+    pairs = []
+    for i, weight in enumerate((w_gate, w_up)):
+        pairs.append(
+            (weight.at[:, at(seq, units)], weights.at[at(seq, depth), pl.ds(i * units, units)])
+        )
+    pairs.append((blocks[0], weights.at[at(seq ^ 1, depth), :]))
+    for d in (2, 3):
+        mine, other = blocks[2 * d - 3], blocks[2 * d - 2]
+        pairs.append((mine, weights.at[at((seq ^ d) * 2 + group, half), :]))
+        pairs.append((other, weights.at[at((seq ^ d) * 2 + 1 - group, half), :]))
+    copy_all(pairs, sems)
+
+    def gated(pieces):
+        values = [piece.astype(jnp.float32) for piece, _ in pieces]
+        squares = sum(jnp.sum(v * v, axis=1, keepdims=True) for v in values)
+        inverse = lax.rsqrt(squares * (1.0 / D_ENC) + epsilon)
+        acts = 0.0
+        for v, (_, index) in zip(values, pieces):
+            normed = (v * inverse * gain[:, at(index, depth)]).astype(jnp.bfloat16)
+            acts += jnp.dot(normed, weights[at(index, depth), :], preferred_element_type=jnp.float32)
+        gate_act = acts[:, :units]
+        return (gate_act * jax.nn.sigmoid(gate_act) * acts[:, units:]).astype(jnp.bfloat16)
+
+    rows = tiles.shape[0]
+    for d in (2, 3, 1, 0):
+        if d == 0:
+            pieces = [(tiles[:, pl.ds(q * depth, depth)], q) for q in range(count)]
+        else:
+            pieces = [(own[d - 1][...], mp), (far[d - 1], mp ^ 2)]
+            pieces += [(near[d - 1], mp ^ 1), (near_far[d - 1], mp ^ 3)]
+        out = first if d >= 2 else second
+        out[pl.ds((d % 2) * rows, rows), :] = gated(pieces)
+
+
+def down_body(count, keep, ids, own, far, near, near_far, *refs):
+    parts = refs[: 2 * count]
+    low, high, weights, sems = refs[2 * count :]
+    seq, mp, group = ids[0], ids[1], ids[2]
+    units = own.shape[1]
+    half = units // 2
+    pairs = []
+    for e in range(count):
+        pairs.append((parts[2 * e], weights.at[at((e ^ seq) * 2 + group, half), :]))
+        pairs.append((parts[2 * e + 1], weights.at[at((e ^ seq) * 2 + 1 - group, half), :]))
+    copy_all(pairs, sems)
+    rows = low.shape[0]
+    for i, out in enumerate((low, high)):
+        span = pl.ds(i * rows, rows)
+        total = 0.0
+        for piece, index in ((own, mp), (far, mp ^ 2), (near, mp ^ 1), (near_far, mp ^ 3)):
+            total += jnp.dot(
+                piece[span, :], weights[at(index, units), :], preferred_element_type=jnp.float32
+            )
+        out[...] = total.astype(out.dtype)
+
+
+def project_body(count, ids, gain, code, w_qkv, own, far, near, near_far, *outs):
+    seq, mp = ids[0], ids[1]
+    features = own.shape[1]
+    capacity = outs[0].shape[0]
+    heads = w_qkv.shape[1] // (3 * HEAD_WIDTH)
+    squares, total = 0.0, 0.0
+    for piece, index in ((own, mp), (far, mp ^ 2), (near, mp ^ 1), (near_far, mp ^ 3)):
+        v = piece[...].astype(jnp.float32)
+        squares += jnp.sum(v * v, axis=1, keepdims=True)
+        scaled = (v * gain[:, at(index, features)]).astype(jnp.bfloat16)
+        total += jnp.dot(
+            scaled, w_qkv[at(index, features), :], preferred_element_type=jnp.float32
+        )
+    projected = (total * lax.rsqrt(squares / D_ENC + epsilon)).astype(jnp.bfloat16)
+    codes = code[...]
+    rows = codes.shape[1]
+    slot = lax.broadcasted_iota(jnp.int32, (capacity, rows), 0)
+
+    def pick(wanted, array):
+        chosen = jnp.where(codes == wanted, 1.0, 0.0).astype(jnp.bfloat16)
+        return jnp.dot(chosen, array, preferred_element_type=jnp.float32).astype(jnp.bfloat16)
+
+    spread = []
+    per_block = capacity // DILATION_STEP
+    index = lax.broadcasted_iota(jnp.int32, (count * per_block, rows), 0)
+    for h in range(heads):
+        wanted = (index // per_block) * capacity + (index % per_block) * DILATION_STEP + ids[4 + h]
+        start = (3 * h + 1) * HEAD_WIDTH
+        both = pick(wanted, projected[:, start : start + 2 * HEAD_WIDTH])
+        spread.append(
+            jnp.concatenate([both[:, :HEAD_WIDTH], both[:, HEAD_WIDTH:]], axis=0)
+        )
+    width = projected.shape[1]
+    beside = jnp.concatenate(spread, axis=1)
+    for d, out in enumerate(outs):
+        out[:, :width] = pick((seq ^ d) * capacity + slot, projected)
+        out[:, width:] = beside
+
+
+def attend_body(count, ids, *refs):
+    packages, out, rows = refs[:count], refs[count], refs[count + 1]
+    seq = ids[0]
+    capacity = packages[0].shape[0]
+    heads = out.shape[1] // HEAD_WIDTH
+    width = heads * 3 * HEAD_WIDTH
+    for d, package in enumerate(packages):
+        rows[at(seq ^ d, capacity), :] = package[:, :width]
+    far = [package[:, width:] for package in packages]
+    half = capacity // 2
+    far_keys = jnp.concatenate([f[:half] for f in far], axis=0)
+    far_values = jnp.concatenate([f[half:] for f in far], axis=0)
+    residue = lax.broadcasted_iota(jnp.int32, (out.shape[0], 1), 0) % DILATION_STEP
+    scale_factor = HEAD_WIDTH ** (-0.5)
+
+    def branch(query, key, value, mask):
+        scores = lax.dot_general(
+            query, key, (((1,), (1,)), ((), ())), preferred_element_type=jnp.float32
+        )
+        weights = jnp.exp(scores * scale_factor)
+        if mask is not None:
+            weights = jnp.where(mask, weights, 0.0)
+        numer = jnp.dot(
+            weights.astype(jnp.bfloat16), value, preferred_element_type=jnp.float32
+        )
+        return numer, jnp.sum(weights, axis=1, keepdims=True)
+
+    results = []
+    for h in range(heads):
+        query, key, value = (
+            rows[:, pl.ds((3 * h + i) * HEAD_WIDTH, HEAD_WIDTH)] for i in range(3)
+        )
+        span = slice(h * HEAD_WIDTH, (h + 1) * HEAD_WIDTH)
+        near_num, near_den = branch(query, key, value, None)
+        far_num, far_den = branch(query, far_keys[:, span], far_values[:, span], residue == ids[4 + h])
+        results.append((near_num + far_num) / (near_den + far_den))
+    out[...] = jnp.concatenate(results, axis=1).astype(jnp.bfloat16)
+
+
+def spread_mp(own):
+    far = swap(own, "mp", 2)
+    return far, swap(own, "mp", 1), swap(far, "mp", 1)
+
+
+def split_hidden_plan(
+    tiles, counts, dest, gain_enc, w_gate, w_up, w_down, gain_slide, w_qkv, offsets
+):
+    count, mp_size = lax.axis_size("seq"), lax.axis_size("mp")
+    seq, mp, group = (lax.axis_index(name) for name in ("seq", "mp", "groups"))
+    capacity = ENCODER_SLOTS // count
+    tile_rows = tiles.shape[0]
+    features = D_ENC // mp_size
+    depth = w_gate.shape[0]
+    units = w_gate.shape[1] // count
+    bf16 = jnp.bfloat16
+    ids = jnp.concatenate(
+        [jnp.stack([seq, mp, group, counts[0]]).astype(jnp.int32), offsets]
+    )
+    anywhere = pl.ANY
+
+    cut = call(
+        functools.partial(cut_body, count),
+        [((tile_rows, features), bf16), ((depth, 2 * units), bf16)]
+        + [((depth // 2, 2 * units), bf16)] * (count - 2)
+        + [((units // 2, features), bf16)] * count,
+        (tiles, w_gate, w_up, w_down),
+        ids,
+        copies=1 + 2 * (count - 1) + count,
+        spaces=[anywhere] * 4,
+        cost="copies",
+    )
+    quarter, gate_up_out, down_out = cut[0], cut[1:count], cut[count:]
+
+    own = [swap(quarter, "seq", d) for d in range(1, count)]
+    blocks = [swap(gate_up_out[0], "seq", 1)]
+    for d in range(2, count):
+        mine = swap(gate_up_out[d - 1], "seq", d)
+        blocks += [mine, swap(mine, "groups", 1)]
+    spread = spread_mp(jnp.stack(own))
+    first, second = call(
+        functools.partial(hidden_body, count),
+        [((2 * tile_rows, units), bf16)] * 2,
+        (gain_enc[None, :], tiles, w_gate, w_up, *own, *spread, *blocks),
+        ids,
+        copies=7,
+        scratch=[pltpu.VMEM((D_ENC, 2 * units), bf16)],
+        spaces=[pltpu.VMEM] * 2 + [anywhere] * 2 + [pltpu.VMEM] * (count + 2) + [anywhere] * 5,
+    )
+
+    parts = []
+    for e in range(count):
+        send, _ = lax.optimization_barrier((down_out[e], blocks[-2]))
+        perm = []
+        for s in range(count):
+            for m in range(mp_size):
+                perm.append((s * mp_size + m, (e ^ m) * mp_size + s))
+        mine = lax.ppermute(send, ("seq", "mp"), perm)
+        parts.append(mine)
+    others = swap(jnp.stack(parts), "groups", 1)
+    parts = [piece for e in range(count) for piece in (parts[e], others[e])]
+
+    def down(rows_hidden, kinds):
+        return call(
+            functools.partial(down_body, count, None),
+            [((tile_rows, features), kind) for kind in kinds],
+            (rows_hidden, *spread_mp(rows_hidden), *parts),
+            ids,
+            copies=2 * count,
+            scratch=[pltpu.VMEM((count * units, features), bf16)],
+            spaces=[pltpu.VMEM] * 4 + [anywhere] * (2 * count),
+        )
+
+    sum_2, sum_3 = down(first, (bf16, bf16))
+    sum_0, sum_1 = down(second, (jnp.float32, bf16))
+    arrived = [swap(part, "seq", d) for d, part in ((2, sum_2), (3, sum_3), (1, sum_1))]
+    embedded_cols = (
+        block_at(tiles, mp, features, 1).astype(jnp.float32)
+        + (sum_0 + sum(part.astype(jnp.float32) for part in arrived))
+    ).astype(bf16)
+
+    target = dest[:, 0]
+    rows = jnp.arange(tile_rows, dtype=jnp.int32)
+    live_rows = rows < counts[0]
+    same = (target[None, :] == dest) & (rows[:, None] < rows[None, :])
+    arrival = jnp.sum((same & live_rows[:, None]).astype(jnp.int32), axis=0)
+    code = jnp.where(live_rows, target * capacity + arrival, -1)[None, :]
+
+    heads = offsets.shape[0]
+    packages = call(
+        functools.partial(project_body, count),
+        [((capacity, 4 * heads * HEAD_WIDTH), bf16)] * count,
+        (gain_slide[None, :], code, w_qkv, embedded_cols, *spread_mp(embedded_cols)),
+        ids,
+    )
+    packages = [packages[0]] + [swap(packages[d], "seq", d) for d in range(1, count)]
+    return call(
+        functools.partial(attend_body, count),
+        [((ENCODER_SLOTS, heads * HEAD_WIDTH), bf16)],
+        tuple(packages),
+        ids,
+        scratch=[pltpu.VMEM((ENCODER_SLOTS, 3 * heads * HEAD_WIDTH), bf16)],
+    )[0]
+
+
+def on_device(*arrays):
+    sizes = lax.axis_size("groups"), lax.axis_size("seq"), lax.axis_size("mp")
+    if sizes == (2, 4, 4):
+        return split_hidden_plan(*arrays)
+    return gathered_plan(*arrays)
 
 
 def solution(mesh):

time: 286 us -> 123 us (0.43)
  waiting for transfers between devices: 181 us -> 54.7 us
  blocking collectives: 69 us -> 0 us
  starting transfers between devices: 0.12 us -> 43.8 us
  between operations: 14 us -> 0.85 us
  Pallas kernels: 0 us -> 13 us
  matrix products: 12.9 us -> 0 us
  local copies, waits for them, and re-layouts: 3.63 us -> 8.74 us
  other arithmetic: 4.79 us -> 1.28 us
    all_gather x3 -> x0, waiting for transfers between devices: 152 us -> none  [the longest x1 63.6 us: on_device(): lax.all_gather(w_down, 'seq', axis=1, tiled=True)]
    ppermute x0 -> x31, waiting for transfers between devices: none -> 54.7 us  [the longest x27 53.5 us: swap(): return lax.ppermute(array, axis, [(i, i ^ distance) for i in range(size)])]
    all_to_all x1 -> x0, blocking collectives: 47.4 us -> none  [on_device(): lax.all_to_all(outgoing, 'seq', split_axis=0, concat_axis=0, tiled=True)]
    ppermute x0 -> x31, starting transfers between devices: none -> 43.8 us  [the longest x27 33.1 us: swap(): return lax.ppermute(array, axis, [(i, i ^ distance) for i in range(size)])]
    reduce_scatter x1 -> x0, waiting for transfers between devices: 26.8 us -> none  [on_device(): share = lax.psum_scatter(partial_out, 'mp', scatter_dimension=1, tiled=True)]
    all_gather x2 -> x0, blocking collectives: 21.6 us -> none  [the longest x1 13.4 us: on_device(): portion = lax.all_gather(package, 'seq', axis=0, tiled=True)]
    pallas_call x0 -> x6, Pallas kernels: none -> 13 us  [call(): pl.pallas_call(body, out_shape=[jax.ShapeDtypeStruct(shape, kind) for sha...]
    dot_general x10 -> x0, matrix products: 12.9 us -> none  [the longest x1 6.25 us: on_device(): jnp.dot(hidden, lax.all_gather(w_down, 'seq', axis=1, tiled=True), prefer...]
  transfers between devices with their start and end apart: 4 -> 31, of which waited for: 4 -> 15; matrix products, arithmetic and copies ran while one was open for 3% -> 2% of each run, Pallas kernels for 0% -> 7%
where the time goes in v2:
time: 123 us; the launch traced here: 122 us
  waiting for transfers between devices  54.7 us (44%)
  starting transfers between devices  43.8 us (36%)
  Pallas kernels  13 us (11%)
  local copies, waits for them, and re-layouts  8.74 us (7%)
  other arithmetic  1.28 us (1%)
    ppermute x27, waiting for transfers between devices, swap(): return lax.ppermute(array, axis, [(i, i ^ distance) for i in range(size)])  53.5 us
    ppermute x27, starting transfers between devices, swap(): return lax.ppermute(array, axis, [(i, i ^ distance) for i in range(size)])  33.1 us
    pallas_call x6, Pallas kernels, call(): pl.pallas_call(body, out_shape=[jax.ShapeDtypeStruct(shape, kind) for sha...  13 us
    ppermute x4, starting transfers between devices, split_hidden_plan(): mine = lax.ppermute(send, ('seq', 'mp'), perm)  10.8 us
    unnamed x15, local copies, waits for them, and re-layouts  7.21 us
  transfers between devices with their start and end apart: 31, of which 15 were waited for; matrix products, arithmetic and copies ran while one was open for 2% of the time, Pallas kernels for 7%

profile of v2, /device:TPU:0, one launch (start us, length us, event | category | flops | bytes accessed | tf_op | source)
XLA Modules:
  0.0 122.4 jit_solution(7373713436298291330)
XLA Ops:
  0.7 0.7 concatenate.3.ids
  1.4 1.1 copy-done
  2.5 1.1 copy-done.1
  3.7 1.1 copy-done.2
  4.7 1.1 copy-done.3
  5.9 1.4 %shard_map.100 = (bf16[192,384]{1,0:T(8,128)(2,1)S(1)}, bf16[384,512]{1,0:T(8,128)(2,1)S(1)}, bf16[192,512]{1,0:T(8,128)(2,1)S(1)}, bf16[192,512]{1,0:T(8,128)(2...) custom-call(s32[7]{0:T(128)S(1)} %concatenate.3.ids, ...), custom_call_target="tpu_custom_call" | custom-call | tf_op jit(solution)/shard_map/pallas_call | solution.py:163
  7.3 3.1 %collective-permute-start = (bf16[192,384]{1,0:T(8,128)(2,1)S(1)}, bf16[192,384]{1,0:T(8,128)(2,1)S(1)}, u32[]{:S(2)}, u32[]{:S(2)}) collective-permute-start(bf16[192,384]{1,0:T(8,128)(2,1)S(1)} %get-tuple-element.27), channel_id=1, source_target_pairs={{0,4},{4,0},{8,12},{12,8},{1,5},{5,1},{9,13},{13,9},{2,6},{6,2},{1... | collective-permute-start | bytes 442376 | tf_op jit(solution)/shard_map/ppermute | solution.py:139
  10.4 2.6 %collective-permute-start.1 = (bf16[192,384]{1,0:T(8,128)(2,1)S(1)}, bf16[192,384]{1,0:T(8,128)(2,1)S(1)}, u32[]{:S(2)}, u32[]{:S(2)}) collective-permute-start(bf16[192,384]{1,0:T(8,128)(2,1)S(1)} %get-tuple-element.27), channel_id=1, source_target_pairs={{0,8},{4,12},{8,0},{12,4},{1,9},{5,13},{9,1},{13,5},{2,10},{6,14},... | collective-permute-start | bytes 442376 | tf_op jit(solution)/shard_map/ppermute | solution.py:139
  13.0 3.3 %collective-permute-done.refs_0_ = bf16[192,384]{1,0:T(8,128)(2,1)S(1)} collective-permute-done((bf16[192,384]{1,0:T(8,128)(2,1)S(1)}, bf16[192,384]{1,0:T(8,128)(2,1)S(1)}, u32[]{:S(2)}, u32[]{:S(2)}) %collective-permute-start) | collective-permute-done | bytes 147488 | tf_op jit(solution)/shard_map/ppermute | solution.py:139
  16.2 8.1 %collective-permute-done.1.refs_1_ = bf16[192,384]{1,0:T(8,128)(2,1)S(1)} collective-permute-done((bf16[192,384]{1,0:T(8,128)(2,1)S(1)}, bf16[192,384]{1,0:T(8,128)(2,1)S(1)}, u32[]{:S(2)}, u32[]{:S(2)}) %collective-permute-start.1) | collective-permute-done | bytes 147488 | tf_op jit(solution)/shard_map/ppermute | solution.py:139
  24.4 1.6 %collective-permute-start.3 = (bf16[3,192,384]{2,1,0:T(8,128)(2,1)S(1)}, bf16[3,192,384]{2,1,0:T(8,128)(2,1)S(1)}, u32[]{:S(2)}, u32[]{:S(2)}) collective-permute-start(bf16[3,192,384]{2,1,0:T(8,128)(2,1)S(1)} %pad_maximum_fusion), channel_id=1, source_target_pairs={{0,2},{1,3},{2,0},{3,1},{4,6},{5,7},{6,4},{7,5},{8,10},{9,11},{10,... | collective-permute-start | bytes 1327112 | tf_op jit(solution)/shard_map/ppermute | solution.py:139
  26.0 2.3 %collective-permute-start.9 = (bf16[192,512]{1,0:T(8,128)(2,1)S(1)}, bf16[192,512]{1,0:T(8,128)(2,1)S(1)}, u32[]{:S(2)}, u32[]{:S(2)}) collective-permute-start(bf16[192,512]{1,0:T(8,128)(2,1)S(1)} %get-tuple-element.30), channel_id=1, source_target_pairs={{0,12},{4,8},{8,4},{12,0},{1,13},{5,9},{9,5},{13,1},{2,14},{6,10},... | collective-permute-start | bytes 589832 | tf_op jit(solution)/shard_map/ppermute | solution.py:139
  28.3 1.5 %collective-permute-start.7 = (bf16[192,512]{1,0:T(8,128)(2,1)S(1)}, bf16[192,512]{1,0:T(8,128)(2,1)S(1)}, u32[]{:S(2)}, u32[]{:S(2)}) collective-permute-start(bf16[192,512]{1,0:T(8,128)(2,1)S(1)} %get-tuple-element.29), channel_id=1, source_target_pairs={{0,8},{4,12},{8,0},{12,4},{1,9},{5,13},{9,1},{13,5},{2,10},{6,14},... | collective-permute-start | bytes 589832 | tf_op jit(solution)/shard_map/ppermute | solution.py:139
  29.8 5.7 %collective-permute-done.9.refs_9_ = bf16[192,512]{1,0:T(8,128)(2,1)S(1)} collective-permute-done((bf16[192,512]{1,0:T(8,128)(2,1)S(1)}, bf16[192,512]{1,0:T(8,128)(2,1)S(1)}, u32[]{:S(2)}, u32[]{:S(2)}) %collective-permute-start.9) | collective-permute-done | bytes 196640 | tf_op jit(solution)/shard_map/ppermute | solution.py:139
  35.4 0.7 collective-permute-start.14
  36.1 9.3 %collective-permute-start.15 = (bf16[128,384]{1,0:T(8,128)(2,1)S(1)}, bf16[128,384]{1,0:T(8,128)(2,1)S(1)}, u32[]{:S(2)}, u32[]{:S(2)}) collective-permute-start(bf16[128,384]{1,0:T(8,128)(2,1)S(1)} %get-tuple-element.35), channel_id=1, source_target_pairs={{0,4},{1,0},{2,12},{3,8},{4,5},{5,1},{6,13},{7,9},{8,6},{9,2},{10,... | collective-permute-start | bytes 294920 | tf_op jit(solution)/shard_map/ppermute | solution.py:398
  45.4 0.8 collective-permute-start.16
  46.2 3.0 %collective-permute-done.7.refs_7_ = bf16[192,512]{1,0:T(8,128)(2,1)S(1)} collective-permute-done((bf16[192,512]{1,0:T(8,128)(2,1)S(1)}, bf16[192,512]{1,0:T(8,128)(2,1)S(1)}, u32[]{:S(2)}, u32[]{:S(2)}) %collective-permute-start.7) | collective-permute-done | bytes 196640 | tf_op jit(solution)/shard_map/ppermute | solution.py:139
  49.7 1.3 %collective-permute-start.6 = (bf16[384,512]{1,0:T(8,128)(2,1)S(1)}, bf16[384,512]{1,0:T(8,128)(2,1)S(1)}, u32[]{:S(2)}, u32[]{:S(2)}) collective-permute-start(bf16[384,512]{1,0:T(8,128)(2,1)S(1)} %get-tuple-element.28), channel_id=1, source_target_pairs={{0,4},{4,0},{8,12},{12,8},{1,5},{5,1},{9,13},{13,9},{2,6},{6,2},{1... | collective-permute-start | bytes 1179656 | tf_op jit(solution)/shard_map/ppermute | solution.py:139
  51.0 1.5 %collective-permute-start.10 = (bf16[192,512]{1,0:T(8,128)(2,1)S(1)}, bf16[192,512]{1,0:T(8,128)(2,1)S(1)}, u32[]{:S(2)}, u32[]{:S(2)}) collective-permute-start(bf16[192,512]{1,0:T(8,128)(2,1)S(1)} %collective-permute-done.9.refs_9_), channel_id=1, source_target_pairs={{0,16},{16,0},{1,17},{17,1},{2,18},{18,2},{3,19},{19,3},{4,20},{20... | collective-permute-start | bytes 589832 | tf_op jit(solution)/shard_map/ppermute | solution.py:139
  52.5 1.2 collective-permute-done.17.refs_6_
  53.8 1.5 %collective-permute-start.8 = (bf16[192,512]{1,0:T(8,128)(2,1)S(1)}, bf16[192,512]{1,0:T(8,128)(2,1)S(1)}, u32[]{:S(2)}, u32[]{:S(2)}) collective-permute-start(bf16[192,512]{1,0:T(8,128)(2,1)S(1)} %collective-permute-done.7.refs_7_), channel_id=1, source_target_pairs={{0,16},{16,0},{1,17},{17,1},{2,18},{18,2},{3,19},{19,3},{4,20},{20... | collective-permute-start | bytes 589832 | tf_op jit(solution)/shard_map/ppermute | solution.py:139
  55.3 3.1 %collective-permute-done.10.refs_10_ = bf16[192,512]{1,0:T(8,128)(2,1)S(1)} collective-permute-done((bf16[192,512]{1,0:T(8,128)(2,1)S(1)}, bf16[192,512]{1,0:T(8,128)(2,1)S(1)}, u32[]{:S(2)}, u32[]{:S(2)}) %collective-permute-start.10) | collective-permute-done | bytes 196640 | tf_op jit(solution)/shard_map/ppermute | solution.py:139
  58.5 1.5 %collective-permute-start.18 = (bf16[4,128,384]{2,1,0:T(8,128)(2,1)S(1)}, bf16[4,128,384]{2,1,0:T(8,128)(2,1)S(1)}, u32[]{:S(2)}, u32[]{:S(2)}) collective-permute-start(bf16[4,128,384]{2,1,0:T(8,128)(2,1)S(1)} %pad_maximum_fusion.1), channel_id=1, source_target_pairs={{0,16},{16,0},{1,17},{17,1},{2,18},{18,2},{3,19},{19,3},{4,20},{20... | collective-permute-start | bytes 1179656 | tf_op jit(solution)/shard_map/ppermute | solution.py:139
  60.0 1.8 %collective-permute-done.8.refs_8_ = bf16[192,512]{1,0:T(8,128)(2,1)S(1)} collective-permute-done((bf16[192,512]{1,0:T(8,128)(2,1)S(1)}, bf16[192,512]{1,0:T(8,128)(2,1)S(1)}, u32[]{:S(2)}, u32[]{:S(2)}) %collective-permute-start.8) | collective-permute-done | bytes 196640 | tf_op jit(solution)/shard_map/ppermute | solution.py:139
  61.8 3.9 %shard_map.101 = (bf16[384,256]{1,0:T(8,128)(2,1)S(1)}, bf16[384,256]{1,0:T(8,128)(2,1)S(1)}) custom-call(s32[7]{0:T(128)S(1)} %concatenate.3.ids, f32[1,1536]{1,0:T(1,128)S(1)} %broadcast_in_dim.16.gain, bf16[192,1536]{1,0:T(8,128)(2,1)S(1)} %copy-done.2, bf16[384,1024]{1,0:T(8,128)(2,1)S(1)} %copy-done, bf16[384,1024]{1,0:T(8,128)(2,1)S(1)} %copy-done.1, ...), custom_call_target="tpu_custom_call" | custom-call | tf_op jit(solution)/shard_map/pallas_call | solution.py:163
  65.7 6.0 %collective-permute-start.19 = (bf16[384,256]{1,0:T(8,128)(2,1)S(1)}, bf16[384,256]{1,0:T(8,128)(2,1)S(1)}, u32[]{:S(2)}, u32[]{:S(2)}) collective-permute-start(bf16[384,256]{1,0:T(8,128)(2,1)S(1)} %get-tuple-element.41.own), channel_id=1, source_target_pairs={{0,2},{1,3},{2,0},{3,1},{4,6},{5,7},{6,4},{7,5},{8,10},{9,11},{10,... | collective-permute-start | bytes 589832 | tf_op jit(solution)/shard_map/ppermute | solution.py:139
  72.3 5.2 %collective-permute-done.19.far = bf16[384,256]{1,0:T(8,128)(2,1)S(1)} collective-permute-done((bf16[384,256]{1,0:T(8,128)(2,1)S(1)}, bf16[384,256]{1,0:T(8,128)(2,1)S(1)}, u32[]{:S(2)}, u32[]{:S(2)}) %collective-permute-start.19) | collective-permute-done | bytes 196640 | tf_op jit(solution)/shard_map/ppermute | solution.py:139
  77.6 2.3 %collective-permute-done.11.far = bf16[384,256]{1,0:T(8,128)(2,1)S(1)} collective-permute-done((bf16[384,256]{1,0:T(8,128)(2,1)S(1)}, bf16[384,256]{1,0:T(8,128)(2,1)S(1)}, u32[]{:S(2)}, u32[]{:S(2)}) %collective-permute-start.11) | collective-permute-done | bytes 196640 | tf_op jit(solution)/shard_map/ppermute | solution.py:139
  79.9 2.3 %shard_map.103 = (bf16[192,384]{1,0:T(8,128)(2,1)S(1)}, bf16[192,384]{1,0:T(8,128)(2,1)S(1)}) custom-call(s32[7]{0:T(128)S(1)} %concatenate.3.ids, bf16[384,256]{1,0:T(8,128)(2,1)S(1)} %get-tuple-element.41.own, bf16[384,256]{1,0:T(8,128)(2,1)S(1)} %collective-permute-done.19.far, bf16[384,256]{1,0:T(8,128)(2,1)S(1)} %collective-permute-done.20.near, ...), custom_call_target="tpu_custom_call" | custom-call | tf_op jit(solution)/shard_map/pallas_call | solution.py:163
  82.2 2.4 %collective-permute-start.22 = (bf16[192,384]{1,0:T(8,128)(2,1)S(1)}, bf16[192,384]{1,0:T(8,128)(2,1)S(1)}, u32[]{:S(2)}, u32[]{:S(2)}) collective-permute-start(bf16[192,384]{1,0:T(8,128)(2,1)S(1)} %get-tuple-element.42), channel_id=1, source_target_pairs={{0,8},{4,12},{8,0},{12,4},{1,9},{5,13},{9,1},{13,5},{2,10},{6,14},... | collective-permute-start | bytes 442376 | tf_op jit(solution)/shard_map/ppermute | solution.py:139
  84.8 2.3 %shard_map.102 = (f32[192,384]{1,0:T(8,128)S(1)}, bf16[192,384]{1,0:T(8,128)(2,1)S(1)}) custom-call(s32[7]{0:T(128)S(1)} %concatenate.3.ids, bf16[384,256]{1,0:T(8,128)(2,1)S(1)} %get-tuple-element.31.own, bf16[384,256]{1,0:T(8,128)(2,1)S(1)} %collective-permute-done.11.far, bf16[384,256]{1,0:T(8,128)(2,1)S(1)} %collective-permute-done.12.near, ...), custom_call_target="tpu_custom_call" | custom-call | tf_op jit(solution)/shard_map/pallas_call | solution.py:163
  87.1 1.0 collective-permute-start.24
  88.0 7.6 %collective-permute-done.22 = bf16[192,384]{1,0:T(8,128)(2,1)S(1)} collective-permute-done((bf16[192,384]{1,0:T(8,128)(2,1)S(1)}, bf16[192,384]{1,0:T(8,128)(2,1)S(1)}, u32[]{:S(2)}, u32[]{:S(2)}) %collective-permute-start.22) | collective-permute-done | bytes 147488 | tf_op jit(solution)/shard_map/ppermute | solution.py:139
  95.7 3.1 %collective-permute-done.24 = bf16[192,384]{1,0:T(8,128)(2,1)S(1)} collective-permute-done((bf16[192,384]{1,0:T(8,128)(2,1)S(1)}, bf16[192,384]{1,0:T(8,128)(2,1)S(1)}, u32[]{:S(2)}, u32[]{:S(2)}) %collective-permute-start.24) | collective-permute-done | bytes 147488 | tf_op jit(solution)/shard_map/ppermute | solution.py:139
  98.7 1.0 add_convert_fusion.own
  99.8 1.0 collective-permute-start.25
  100.7 2.7 %copy.13.w_qkv = bf16[1536,576]{1,0:T(8,128)(2,1)S(1)} copy(bf16[1536,576]{0,1:T(8,128)(2,1)} %param.18) | data formatting | bytes 3538944 | tf_op args[8]
  103.7 1.9 %collective-permute-done.25.far = bf16[192,384]{1,0:T(8,128)(2,1)S(1)} collective-permute-done((bf16[192,384]{1,0:T(8,128)(2,1)S(1)}, bf16[192,384]{1,0:T(8,128)(2,1)S(1)}, u32[]{:S(2)}, u32[]{:S(2)}) %collective-permute-start.25) | collective-permute-done | bytes 147488 | tf_op jit(solution)/shard_map/ppermute | solution.py:139
  105.7 1.3 %collective-permute-done.27.near_far = bf16[192,384]{1,0:T(8,128)(2,1)S(1)} collective-permute-done((bf16[192,384]{1,0:T(8,128)(2,1)S(1)}, bf16[192,384]{1,0:T(8,128)(2,1)S(1)}, u32[]{:S(2)}, u32[]{:S(2)}) %collective-permute-start.27) | collective-permute-done | bytes 147488 | tf_op jit(solution)/shard_map/ppermute | solution.py:139
  107.0 1.7 %shard_map.104 = (bf16[64,768]{1,0:T(8,128)(2,1)S(1)}, bf16[64,768]{1,0:T(8,128)(2,1)S(1)}, bf16[64,768]{1,0:T(8,128)(2,1)S(1)}, bf16[64,768]{1,0:T(8,128)(2,1)S(1)}) custom-call(s32[7]{0:T(128)S(1)} %concatenate.3.ids, f32[1,1536]{1,0:T(1,128)S(1)} %broadcast_in_dim.14.gain, s32[1,192]{1,0:T(1,128)S(1)} %compare_select_fusion.code, ...), custom_call_target="tpu_custom_call" | custom-call | tf_op jit(solution)/shard_map/pallas_call | solution.py:163
  108.8 0.7 collective-permute-start.28
  109.5 2.5 %collective-permute-start.29 = (bf16[64,768]{1,0:T(8,128)(2,1)S(1)}, bf16[64,768]{1,0:T(8,128)(2,1)S(1)}, u32[]{:S(2)}, u32[]{:S(2)}) collective-permute-start(bf16[64,768]{1,0:T(8,128)(2,1)S(1)} %get-tuple-element.47), channel_id=1, source_target_pairs={{0,8},{4,12},{8,0},{12,4},{1,9},{5,13},{9,1},{13,5},{2,10},{6,14},... | collective-permute-start | bytes 294920 | tf_op jit(solution)/shard_map/ppermute | solution.py:139
  112.0 1.2 %collective-permute-start.30 = (bf16[64,768]{1,0:T(8,128)(2,1)S(1)}, bf16[64,768]{1,0:T(8,128)(2,1)S(1)}, u32[]{:S(2)}, u32[]{:S(2)}) collective-permute-start(bf16[64,768]{1,0:T(8,128)(2,1)S(1)} %get-tuple-element.48), channel_id=1, source_target_pairs={{0,12},{4,8},{8,4},{12,0},{1,13},{5,9},{9,5},{13,1},{2,14},{6,10},... | collective-permute-start | bytes 294920 | tf_op jit(solution)/shard_map/ppermute | solution.py:139
  113.2 1.7 %collective-permute-done.28.refs_1_ = bf16[64,768]{1,0:T(8,128)(2,1)S(1)} collective-permute-done((bf16[64,768]{1,0:T(8,128)(2,1)S(1)}, bf16[64,768]{1,0:T(8,128)(2,1)S(1)}, u32[]{:S(2)}, u32[]{:S(2)}) %collective-permute-start.28) | collective-permute-done | bytes 98336 | tf_op jit(solution)/shard_map/ppermute | solution.py:139
  115.0 5.3 %collective-permute-done.29.refs_2_ = bf16[64,768]{1,0:T(8,128)(2,1)S(1)} collective-permute-done((bf16[64,768]{1,0:T(8,128)(2,1)S(1)}, bf16[64,768]{1,0:T(8,128)(2,1)S(1)}, u32[]{:S(2)}, u32[]{:S(2)}) %collective-permute-start.29) | collective-permute-done | bytes 98336 | tf_op jit(solution)/shard_map/ppermute | solution.py:139
  120.2 1.4 %shard_map.105 = bf16[256,192]{1,0:T(8,128)(2,1)S(1)} custom-call(s32[7]{0:T(128)S(1)} %concatenate.3.ids, bf16[64,768]{1,0:T(8,128)(2,1)S(1)} %get-tuple-element.45.refs_0_, bf16[64,768]{1,0:T(8,128)(2,1)S(1)} %collective-permute-done.28.refs_1_, bf16[64,768]{1,0:T(8,128)(2,1)S(1)} %collective-permute-done.29.refs_2_, ...), custom_call_target="tpu_custom_call" | custom-call | tf_op jit(solution)/shard_map/pallas_call | solution.py:163
  121.7 0.7 copy.14
  (46 shorter events, 1.8 us)
Async XLA Ops:
  1.4 1.1 copy-start
  2.5 1.1 copy-start.1
  3.7 1.1 copy-start.2
  4.7 1.1 copy-start.3
  5.9 54.1 %copy-start.5 = (f32[1536]{0:T(1024)S(1)}, f32[1536]{0:T(1024)}, u32[]{:S(2)}) copy-start(f32[1536]{0:T(1024)} %param.13) | copy-start | bytes 18436
  7.3 8.9 %collective-permute-start = (bf16[192,384]{1,0:T(8,128)(2,1)S(1)}, bf16[192,384]{1,0:T(8,128)(2,1)S(1)}, u32[]{:S(2)}, u32[]{:S(2)}) collective-permute-start(bf16[192,384]{1,0:T(8,128)(2,1)S(1)} %get-tuple-element.27), channel_id=1, source_target_pairs={{0,4},{4,0},{8,12},{12,8},{1,5},{5,1},{9,13},{13,9},{2,6},{6,2},{1... | collective-permute-start | bytes 442376 | tf_op jit(solution)/shard_map/ppermute | solution.py:139
  10.4 14.0 %collective-permute-start.1 = (bf16[192,384]{1,0:T(8,128)(2,1)S(1)}, bf16[192,384]{1,0:T(8,128)(2,1)S(1)}, u32[]{:S(2)}, u32[]{:S(2)}) collective-permute-start(bf16[192,384]{1,0:T(8,128)(2,1)S(1)} %get-tuple-element.27), channel_id=1, source_target_pairs={{0,8},{4,12},{8,0},{12,4},{1,9},{5,13},{9,1},{13,5},{2,10},{6,14},... | collective-permute-start | bytes 442376 | tf_op jit(solution)/shard_map/ppermute | solution.py:139
  13.0 11.4 %collective-permute-start.2 = (bf16[192,384]{1,0:T(8,128)(2,1)S(1)}, bf16[192,384]{1,0:T(8,128)(2,1)S(1)}, u32[]{:S(2)}, u32[]{:S(2)}) collective-permute-start(bf16[192,384]{1,0:T(8,128)(2,1)S(1)} %get-tuple-element.27), channel_id=1, source_target_pairs={{0,12},{4,8},{8,4},{12,0},{1,13},{5,9},{9,5},{13,1},{2,14},{6,10},... | collective-permute-start | bytes 442376 | tf_op jit(solution)/shard_map/ppermute | solution.py:139
  24.4 24.8 %collective-permute-start.3 = (bf16[3,192,384]{2,1,0:T(8,128)(2,1)S(1)}, bf16[3,192,384]{2,1,0:T(8,128)(2,1)S(1)}, u32[]{:S(2)}, u32[]{:S(2)}) collective-permute-start(bf16[3,192,384]{2,1,0:T(8,128)(2,1)S(1)} %pad_maximum_fusion), channel_id=1, source_target_pairs={{0,2},{1,3},{2,0},{3,1},{4,6},{5,7},{6,4},{7,5},{8,10},{9,11},{10,... | collective-permute-start | bytes 1327112 | tf_op jit(solution)/shard_map/ppermute | solution.py:139
  26.0 9.4 %collective-permute-start.9 = (bf16[192,512]{1,0:T(8,128)(2,1)S(1)}, bf16[192,512]{1,0:T(8,128)(2,1)S(1)}, u32[]{:S(2)}, u32[]{:S(2)}) collective-permute-start(bf16[192,512]{1,0:T(8,128)(2,1)S(1)} %get-tuple-element.30), channel_id=1, source_target_pairs={{0,12},{4,8},{8,4},{12,0},{1,13},{5,9},{9,5},{13,1},{2,14},{6,10},... | collective-permute-start | bytes 589832 | tf_op jit(solution)/shard_map/ppermute | solution.py:139
  28.3 20.9 %collective-permute-start.7 = (bf16[192,512]{1,0:T(8,128)(2,1)S(1)}, bf16[192,512]{1,0:T(8,128)(2,1)S(1)}, u32[]{:S(2)}, u32[]{:S(2)}) collective-permute-start(bf16[192,512]{1,0:T(8,128)(2,1)S(1)} %get-tuple-element.29), channel_id=1, source_target_pairs={{0,8},{4,12},{8,0},{12,4},{1,9},{5,13},{9,1},{13,5},{2,10},{6,14},... | collective-permute-start | bytes 589832 | tf_op jit(solution)/shard_map/ppermute | solution.py:139
  35.4 14.3 %collective-permute-start.14 = (bf16[128,384]{1,0:T(8,128)(2,1)S(1)}, bf16[128,384]{1,0:T(8,128)(2,1)S(1)}, u32[]{:S(2)}, u32[]{:S(2)}) collective-permute-start(bf16[128,384]{1,0:T(8,128)(2,1)S(1)} %get-tuple-element.33), channel_id=1, source_target_pairs={{0,0},{1,4},{2,8},{3,12},{4,1},{5,5},{6,9},{7,13},{8,2},{9,6},{10,... | collective-permute-start | bytes 294920 | tf_op jit(solution)/shard_map/ppermute | solution.py:398
  36.1 13.6 %collective-permute-start.15 = (bf16[128,384]{1,0:T(8,128)(2,1)S(1)}, bf16[128,384]{1,0:T(8,128)(2,1)S(1)}, u32[]{:S(2)}, u32[]{:S(2)}) collective-permute-start(bf16[128,384]{1,0:T(8,128)(2,1)S(1)} %get-tuple-element.35), channel_id=1, source_target_pairs={{0,4},{1,0},{2,12},{3,8},{4,5},{5,1},{6,13},{7,9},{8,6},{9,2},{10,... | collective-permute-start | bytes 294920 | tf_op jit(solution)/shard_map/ppermute | solution.py:398
  45.4 5.6 %collective-permute-start.16 = (bf16[128,384]{1,0:T(8,128)(2,1)S(1)}, bf16[128,384]{1,0:T(8,128)(2,1)S(1)}, u32[]{:S(2)}, u32[]{:S(2)}) collective-permute-start(bf16[128,384]{1,0:T(8,128)(2,1)S(1)} %get-tuple-element.37), channel_id=1, source_target_pairs={{0,8},{1,12},{2,0},{3,4},{4,9},{5,13},{6,1},{7,5},{8,10},{9,14},{1... | collective-permute-start | bytes 294920 | tf_op jit(solution)/shard_map/ppermute | solution.py:398
  49.2 12.6 %collective-permute-start.4 = (bf16[3,192,384]{2,1,0:T(8,128)(2,1)S(1)}, bf16[3,192,384]{2,1,0:T(8,128)(2,1)S(1)}, u32[]{:S(2)}, u32[]{:S(2)}) collective-permute-start(bf16[3,192,384]{2,1,0:T(8,128)(2,1)S(1)} %pad_maximum_fusion), channel_id=1, source_target_pairs={{0,1},{1,0},{2,3},{3,2},{4,5},{5,4},{6,7},{7,6},{8,9},{9,8},{10,11... | collective-permute-start | bytes 1327112 | tf_op jit(solution)/shard_map/ppermute | solution.py:139
  49.2 12.6 %collective-permute-start.5 = (bf16[3,192,384]{2,1,0:T(8,128)(2,1)S(1)}, bf16[3,192,384]{2,1,0:T(8,128)(2,1)S(1)}, u32[]{:S(2)}, u32[]{:S(2)}) collective-permute-start(bf16[3,192,384]{2,1,0:T(8,128)(2,1)S(1)} %collective-permute-done.3.refs_3_), channel_id=1, source_target_pairs={{0,1},{1,0},{2,3},{3,2},{4,5},{5,4},{6,7},{7,6},{8,9},{9,8},{10,11... | collective-permute-start | bytes 1327112 | tf_op jit(solution)/shard_map/ppermute | solution.py:139
  49.7 4.0 %collective-permute-start.17 = (bf16[128,384]{1,0:T(8,128)(2,1)S(1)}, bf16[128,384]{1,0:T(8,128)(2,1)S(1)}, u32[]{:S(2)}, u32[]{:S(2)}) collective-permute-start(bf16[128,384]{1,0:T(8,128)(2,1)S(1)} %get-tuple-element.39), channel_id=1, source_target_pairs={{0,12},{1,8},{2,4},{3,0},{4,13},{5,9},{6,5},{7,1},{8,14},{9,10},{1... | collective-permute-start | bytes 294920 | tf_op jit(solution)/shard_map/ppermute | solution.py:398
  49.7 12.1 %collective-permute-start.6 = (bf16[384,512]{1,0:T(8,128)(2,1)S(1)}, bf16[384,512]{1,0:T(8,128)(2,1)S(1)}, u32[]{:S(2)}, u32[]{:S(2)}) collective-permute-start(bf16[384,512]{1,0:T(8,128)(2,1)S(1)} %get-tuple-element.28), channel_id=1, source_target_pairs={{0,4},{4,0},{8,12},{12,8},{1,5},{5,1},{9,13},{13,9},{2,6},{6,2},{1... | collective-permute-start | bytes 1179656 | tf_op jit(solution)/shard_map/ppermute | solution.py:139
  51.0 7.5 %collective-permute-start.10 = (bf16[192,512]{1,0:T(8,128)(2,1)S(1)}, bf16[192,512]{1,0:T(8,128)(2,1)S(1)}, u32[]{:S(2)}, u32[]{:S(2)}) collective-permute-start(bf16[192,512]{1,0:T(8,128)(2,1)S(1)} %collective-permute-done.9.refs_9_), channel_id=1, source_target_pairs={{0,16},{16,0},{1,17},{17,1},{2,18},{18,2},{3,19},{19,3},{4,20},{20... | collective-permute-start | bytes 589832 | tf_op jit(solution)/shard_map/ppermute | solution.py:139
  53.8 8.0 %collective-permute-start.8 = (bf16[192,512]{1,0:T(8,128)(2,1)S(1)}, bf16[192,512]{1,0:T(8,128)(2,1)S(1)}, u32[]{:S(2)}, u32[]{:S(2)}) collective-permute-start(bf16[192,512]{1,0:T(8,128)(2,1)S(1)} %collective-permute-done.7.refs_7_), channel_id=1, source_target_pairs={{0,16},{16,0},{1,17},{17,1},{2,18},{18,2},{3,19},{19,3},{4,20},{20... | collective-permute-start | bytes 589832 | tf_op jit(solution)/shard_map/ppermute | solution.py:139
  58.5 21.3 %collective-permute-start.18 = (bf16[4,128,384]{2,1,0:T(8,128)(2,1)S(1)}, bf16[4,128,384]{2,1,0:T(8,128)(2,1)S(1)}, u32[]{:S(2)}, u32[]{:S(2)}) collective-permute-start(bf16[4,128,384]{2,1,0:T(8,128)(2,1)S(1)} %pad_maximum_fusion.1), channel_id=1, source_target_pairs={{0,16},{16,0},{1,17},{17,1},{2,18},{18,2},{3,19},{19,3},{4,20},{20... | collective-permute-start | bytes 1179656 | tf_op jit(solution)/shard_map/ppermute | solution.py:139
  65.7 11.8 %collective-permute-start.19 = (bf16[384,256]{1,0:T(8,128)(2,1)S(1)}, bf16[384,256]{1,0:T(8,128)(2,1)S(1)}, u32[]{:S(2)}, u32[]{:S(2)}) collective-permute-start(bf16[384,256]{1,0:T(8,128)(2,1)S(1)} %get-tuple-element.41.own), channel_id=1, source_target_pairs={{0,2},{1,3},{2,0},{3,1},{4,6},{5,7},{6,4},{7,5},{8,10},{9,11},{10,... | collective-permute-start | bytes 589832 | tf_op jit(solution)/shard_map/ppermute | solution.py:139
  71.7 8.1 %collective-permute-start.11 = (bf16[384,256]{1,0:T(8,128)(2,1)S(1)}, bf16[384,256]{1,0:T(8,128)(2,1)S(1)}, u32[]{:S(2)}, u32[]{:S(2)}) collective-permute-start(bf16[384,256]{1,0:T(8,128)(2,1)S(1)} %get-tuple-element.31.own), channel_id=1, source_target_pairs={{0,2},{1,3},{2,0},{3,1},{4,6},{5,7},{6,4},{7,5},{8,10},{9,11},{10,... | collective-permute-start | bytes 589832 | tf_op jit(solution)/shard_map/ppermute | solution.py:139
  71.8 8.0 %collective-permute-start.20 = (bf16[384,256]{1,0:T(8,128)(2,1)S(1)}, bf16[384,256]{1,0:T(8,128)(2,1)S(1)}, u32[]{:S(2)}, u32[]{:S(2)}) collective-permute-start(bf16[384,256]{1,0:T(8,128)(2,1)S(1)} %get-tuple-element.41.own), channel_id=1, source_target_pairs={{0,1},{1,0},{2,3},{3,2},{4,5},{5,4},{6,7},{7,6},{8,9},{9,8},{10,11... | collective-permute-start | bytes 589832 | tf_op jit(solution)/shard_map/ppermute | solution.py:139
  71.8 13.0 %collective-permute-start.12 = (bf16[384,256]{1,0:T(8,128)(2,1)S(1)}, bf16[384,256]{1,0:T(8,128)(2,1)S(1)}, u32[]{:S(2)}, u32[]{:S(2)}) collective-permute-start(bf16[384,256]{1,0:T(8,128)(2,1)S(1)} %get-tuple-element.31.own), channel_id=1, source_target_pairs={{0,1},{1,0},{2,3},{3,2},{4,5},{5,4},{6,7},{7,6},{8,9},{9,8},{10,11... | collective-permute-start | bytes 589832 | tf_op jit(solution)/shard_map/ppermute | solution.py:139
  77.6 2.3 %collective-permute-start.21 = (bf16[384,256]{1,0:T(8,128)(2,1)S(1)}, bf16[384,256]{1,0:T(8,128)(2,1)S(1)}, u32[]{:S(2)}, u32[]{:S(2)}) collective-permute-start(bf16[384,256]{1,0:T(8,128)(2,1)S(1)} %collective-permute-done.19.far), channel_id=1, source_target_pairs={{0,1},{1,0},{2,3},{3,2},{4,5},{5,4},{6,7},{7,6},{8,9},{9,8},{10,11... | collective-permute-start | bytes 589832 | tf_op jit(solution)/shard_map/ppermute | solution.py:139
  79.8 5.0 %collective-permute-start.13 = (bf16[384,256]{1,0:T(8,128)(2,1)S(1)}, bf16[384,256]{1,0:T(8,128)(2,1)S(1)}, u32[]{:S(2)}, u32[]{:S(2)}) collective-permute-start(bf16[384,256]{1,0:T(8,128)(2,1)S(1)} %collective-permute-done.11.far), channel_id=1, source_target_pairs={{0,1},{1,0},{2,3},{3,2},{4,5},{5,4},{6,7},{7,6},{8,9},{9,8},{10,11... | collective-permute-start | bytes 589832 | tf_op jit(solution)/shard_map/ppermute | solution.py:139
  82.2 13.5 %collective-permute-start.22 = (bf16[192,384]{1,0:T(8,128)(2,1)S(1)}, bf16[192,384]{1,0:T(8,128)(2,1)S(1)}, u32[]{:S(2)}, u32[]{:S(2)}) collective-permute-start(bf16[192,384]{1,0:T(8,128)(2,1)S(1)} %get-tuple-element.42), channel_id=1, source_target_pairs={{0,8},{4,12},{8,0},{12,4},{1,9},{5,13},{9,1},{13,5},{2,10},{6,14},... | collective-permute-start | bytes 442376 | tf_op jit(solution)/shard_map/ppermute | solution.py:139
  84.5 11.1 %collective-permute-start.23 = (bf16[192,384]{1,0:T(8,128)(2,1)S(1)}, bf16[192,384]{1,0:T(8,128)(2,1)S(1)}, u32[]{:S(2)}, u32[]{:S(2)}) collective-permute-start(bf16[192,384]{1,0:T(8,128)(2,1)S(1)} %get-tuple-element.43), channel_id=1, source_target_pairs={{0,12},{4,8},{8,4},{12,0},{1,13},{5,9},{9,5},{13,1},{2,14},{6,10},... | collective-permute-start | bytes 442376 | tf_op jit(solution)/shard_map/ppermute | solution.py:139
  87.1 11.7 %collective-permute-start.24 = (bf16[192,384]{1,0:T(8,128)(2,1)S(1)}, bf16[192,384]{1,0:T(8,128)(2,1)S(1)}, u32[]{:S(2)}, u32[]{:S(2)}) collective-permute-start(bf16[192,384]{1,0:T(8,128)(2,1)S(1)} %get-tuple-element.44), channel_id=1, source_target_pairs={{0,4},{4,0},{8,12},{12,8},{1,5},{5,1},{9,13},{13,9},{2,6},{6,2},{1... | collective-permute-start | bytes 442376 | tf_op jit(solution)/shard_map/ppermute | solution.py:139
  99.8 3.7 %copy-start.6 = (f32[1536]{0:T(1024)S(1)}, f32[1536]{0:T(1024)}, u32[]{:S(2)}) copy-start(f32[1536]{0:T(1024)} %param.17) | copy-start | bytes 18436
  99.8 3.7 %copy-start.4 = (s32[192,1]{0,1:T(1,128)S(1)}, s32[192,1]{0,1:T(1,128)}, u32[]{:S(2)}) copy-start(s32[192,1]{0,1:T(1,128)} %param.12) | copy-start | bytes 2308
  99.8 5.9 %collective-permute-start.25 = (bf16[192,384]{1,0:T(8,128)(2,1)S(1)}, bf16[192,384]{1,0:T(8,128)(2,1)S(1)}, u32[]{:S(2)}, u32[]{:S(2)}) collective-permute-start(bf16[192,384]{1,0:T(8,128)(2,1)S(1)} %add_convert_fusion.own), channel_id=1, source_target_pairs={{0,2},{1,3},{2,0},{3,1},{4,6},{5,7},{6,4},{7,5},{8,10},{9,11},{10,... | collective-permute-start | bytes 442376 | tf_op jit(solution)/shard_map/ppermute | solution.py:139
  103.7 2.0 %collective-permute-start.26 = (bf16[192,384]{1,0:T(8,128)(2,1)S(1)}, bf16[192,384]{1,0:T(8,128)(2,1)S(1)}, u32[]{:S(2)}, u32[]{:S(2)}) collective-permute-start(bf16[192,384]{1,0:T(8,128)(2,1)S(1)} %add_convert_fusion.own), channel_id=1, source_target_pairs={{0,1},{1,0},{2,3},{3,2},{4,5},{5,4},{6,7},{7,6},{8,9},{9,8},{10,11... | collective-permute-start | bytes 442376 | tf_op jit(solution)/shard_map/ppermute | solution.py:139
  105.6 1.4 %collective-permute-start.27 = (bf16[192,384]{1,0:T(8,128)(2,1)S(1)}, bf16[192,384]{1,0:T(8,128)(2,1)S(1)}, u32[]{:S(2)}, u32[]{:S(2)}) collective-permute-start(bf16[192,384]{1,0:T(8,128)(2,1)S(1)} %collective-permute-done.25.far), channel_id=1, source_target_pairs={{0,1},{1,0},{2,3},{3,2},{4,5},{5,4},{6,7},{7,6},{8,9},{9,8},{10,11... | collective-permute-start | bytes 442376 | tf_op jit(solution)/shard_map/ppermute | solution.py:139
  108.8 6.2 %collective-permute-start.28 = (bf16[64,768]{1,0:T(8,128)(2,1)S(1)}, bf16[64,768]{1,0:T(8,128)(2,1)S(1)}, u32[]{:S(2)}, u32[]{:S(2)}) collective-permute-start(bf16[64,768]{1,0:T(8,128)(2,1)S(1)} %get-tuple-element.46), channel_id=1, source_target_pairs={{0,4},{4,0},{8,12},{12,8},{1,5},{5,1},{9,13},{13,9},{2,6},{6,2},{1... | collective-permute-start | bytes 294920 | tf_op jit(solution)/shard_map/ppermute | solution.py:139
  109.5 10.8 %collective-permute-start.29 = (bf16[64,768]{1,0:T(8,128)(2,1)S(1)}, bf16[64,768]{1,0:T(8,128)(2,1)S(1)}, u32[]{:S(2)}, u32[]{:S(2)}) collective-permute-start(bf16[64,768]{1,0:T(8,128)(2,1)S(1)} %get-tuple-element.47), channel_id=1, source_target_pairs={{0,8},{4,12},{8,0},{12,4},{1,9},{5,13},{9,1},{13,5},{2,10},{6,14},... | collective-permute-start | bytes 294920 | tf_op jit(solution)/shard_map/ppermute | solution.py:139
  112.0 8.2 %collective-permute-start.30 = (bf16[64,768]{1,0:T(8,128)(2,1)S(1)}, bf16[64,768]{1,0:T(8,128)(2,1)S(1)}, u32[]{:S(2)}, u32[]{:S(2)}) collective-permute-start(bf16[64,768]{1,0:T(8,128)(2,1)S(1)} %get-tuple-element.48), channel_id=1, source_target_pairs={{0,12},{4,8},{8,4},{12,0},{1,13},{5,9},{9,5},{13,1},{2,14},{6,10},... | collective-permute-start | bytes 294920 | tf_op jit(solution)/shard_map/ppermute | solution.py:139

commit v3 on v0

--- a/solution.py
+++ b/solution.py
@@ -1,6 +1,10 @@
+import functools
+
 import jax
 import jax.numpy as jnp
 from jax import lax
+from jax.experimental import pallas as pl
+from jax.experimental.pallas import tpu as pltpu
 from jax.sharding import PartitionSpec as P
 
 D_ENC = 1536
@@ -12,7 +16,14 @@
 epsilon = 1e-05
 
 
-def on_device(tiles, counts, dest, gain_enc, w_gate, w_up, w_down, gain_slide, w_qkv, offsets):
+def gather_seq(package):
+    count = lax.axis_size("seq")
+    if count & (count - 1) == 0 and count <= 4:
+        return jnp.concatenate([package] + [swap(package, "seq", d) for d in range(1, count)])
+    return lax.all_gather(package, "seq", axis=0, tiled=True)
+
+
+def gathered_plan(tiles, counts, dest, gain_enc, w_gate, w_up, w_down, gain_slide, w_qkv, offsets):
     seq_count = lax.axis_size("seq")
     capacity = ENCODER_SLOTS // seq_count
     tile_rows = tiles.shape[0]
@@ -48,7 +59,12 @@
         arrived_f, lax.axis_index("mp") * share_width, share_width, 1
     )
     embedded_cols = (own_cols + share).astype(jnp.bfloat16)
-    portion_f = lax.all_gather(embedded_cols, "mp", axis=1, tiled=True).astype(jnp.float32)
+    embedded = lax.all_gather(embedded_cols, "mp", axis=1, tiled=True)
+    return slide_layer(embedded, gain_slide, w_qkv, offsets)
+
+
+def slide_layer(embedded, gain_slide, w_qkv, offsets):
+    portion_f = embedded.astype(jnp.float32)
     accumulated = jnp.dot(
         (portion_f * gain_slide).astype(jnp.bfloat16), w_qkv, preferred_element_type=jnp.float32
     )
@@ -76,7 +92,7 @@
     package = jnp.concatenate([select_rows(keys_local), select_rows(values_local)], axis=2).reshape(
         selected_rows, local_head_output * 2 * HEAD_WIDTH
     )
-    portion = lax.all_gather(package, "seq", axis=0, tiled=True)
+    portion = gather_seq(package)
     parts_kv = portion.reshape(portion.shape[0], local_head_output, 2, HEAD_WIDTH)
     scores = (
         jnp.einsum(
@@ -116,6 +132,356 @@
         .reshape(ENCODER_SLOTS, local_head_output * HEAD_WIDTH)
         .astype(jnp.bfloat16)
     )
+
+
+def swap(array, axis, distance):
+    size = lax.axis_size(axis)
+    return lax.ppermute(array, axis, [(i, i ^ distance) for i in range(size)])
+
+
+def block_at(array, index, size, axis):
+    return lax.dynamic_slice_in_dim(array, index * size, size, axis)
+
+
+def call(body, outs, inputs, spaces=None, scratch=(), copies=0, megabytes=40):
+    spaces = spaces or [pltpu.VMEM] * len(inputs)
+    out_space = pl.ANY if copies else pltpu.VMEM
+    scratch = list(scratch)
+    if copies:
+        scratch.append(pltpu.SemaphoreType.DMA((copies,)))
+    return pl.pallas_call(
+        body,
+        out_shape=[jax.ShapeDtypeStruct(shape, kind) for shape, kind in outs],
+        in_specs=[pl.BlockSpec(memory_space=space) for space in spaces],
+        out_specs=[pl.BlockSpec(memory_space=out_space)] * len(outs),
+        scratch_shapes=scratch,
+        compiler_params=pltpu.CompilerParams(vmem_limit_bytes=megabytes * 1024 * 1024),
+    )(*inputs)
+
+
+def at(index, size):
+    return pl.ds(pl.multiple_of(index * size, size), size)
+
+
+def place():
+    return tuple(lax.axis_index(name) for name in ("seq", "mp", "groups"))
+
+
+def column_block(seq, mp):
+    step = jnp.where(mp == 2, seq + 1, seq + 3) & 3
+    return jnp.where(mp < 2, seq ^ (2 * mp), step)
+
+
+def column_user(seq, mp):
+    step = jnp.where(mp == 2, seq + 3, seq + 1) & 3
+    return jnp.where(mp < 2, seq ^ (2 * mp), step)
+
+
+def cut_body(
+    count, tiles, w_gate, w_up, w_down, quarter, mixed, third, next_block, kept, *downs_and_sems
+):
+    downs, sems = downs_and_sems[:-1], downs_and_sems[-1]
+    seq, mp, group = place()
+    depth, units = w_gate.shape[0], w_gate.shape[1] // count
+    half, features = depth // 2, quarter.shape[1]
+    copies = []
+
+    def copy(source, target, other=None):
+        started = pltpu.make_async_copy(source, target, sems.at[len(copies)])
+        if other is None:
+            started.start()
+        else:
+            second = pltpu.make_async_copy(other, target, sems.at[len(copies)])
+            pl.when(group == 0)(started.start)
+            pl.when(group != 0)(second.start)
+        copies.append(started)
+
+    own_columns = tiles.at[:, at(mp, features)]
+    copy(own_columns, quarter)
+    copy(own_columns, mixed.at[:, pl.ds(0, features)])
+    for owner, target, start in ((seq ^ 2, mixed, features), (seq ^ 3, third, 0)):
+        for i in range(2):
+            span = pl.ds(i * half, half), at(owner, units)
+            copy(w_gate.at[span], target.at[:, pl.ds(start + i * units, units)], w_up.at[span])
+    for owner, target in ((seq ^ 1, next_block), (seq, kept)):
+        for i, weight in enumerate((w_gate, w_up)):
+            copy(weight.at[:, at(owner, units)], target.at[:, pl.ds(i * units, units)])
+    for j, down in enumerate(downs):
+        copy(w_down.at[at(column_user(seq, mp ^ j), units), :], down)
+    for started in copies:
+        started.wait()
+
+
+def restack_body(first, mixed, third, stacked, columns):
+    features = first.shape[1]
+    stacked[0] = first[...]
+    stacked[1] = mixed[:, :features]
+    stacked[2] = third[...]
+    columns[...] = mixed[:, features:]
+
+
+def code_body(capacity, counts, dest, dest_row, code):
+    rows = dest_row.shape[1]
+    later = lax.broadcasted_iota(jnp.int32, (rows, rows), 1)
+    earlier = lax.broadcasted_iota(jnp.int32, (rows, rows), 0)
+    same = (dest[...] == dest_row[...]) & (earlier < later)
+    rank = jnp.sum(jnp.where(same, 1, 0), axis=0, keepdims=True)
+    live = lax.broadcasted_iota(jnp.int32, (1, rows), 1) < counts[0]
+    code[...] = jnp.where(live, dest_row[...] * capacity + rank, -1)
+
+
+def hidden_body(
+    count, gain, tiles, own, far, near, near_far, kept, next_block, *refs
+):
+    halves, (first, second, normed, weights) = refs[:4], refs[4:]
+    seq, mp, group = place()
+    depth, units = weights.shape[1:]
+    half = depth // 2
+    rows = tiles.shape[0]
+    for i, piece in enumerate(halves):
+        weights[i, :half, :] = piece[:, :units]
+        weights[i, half:, :] = piece[:, units:]
+
+    def gated(d):
+        if d == 0:
+            pieces = [(tiles[:, pl.ds(q * depth, depth)], q) for q in range(count)]
+        else:
+            pieces = [(own[d - 1], mp), (far[d - 1], mp ^ 2)]
+            pieces += [(near[d - 1], mp ^ 1), (near_far[d - 1], mp ^ 3)]
+        values = [piece.astype(jnp.float32) for piece, _ in pieces]
+        squares = sum(jnp.sum(v * v, axis=1, keepdims=True) for v in values)
+        inverse = lax.rsqrt(squares * (1.0 / D_ENC) + epsilon)
+        for v, (_, index) in zip(values, pieces):
+            normed[index] = (v * inverse * gain[:, at(index, depth)]).astype(jnp.bfloat16)
+        dot = functools.partial(jnp.dot, preferred_element_type=jnp.float32)
+        both = dot(normed[seq], kept[...]) + dot(normed[seq ^ 1], next_block[...])
+        mine = dot(normed[seq ^ 2], weights[0]) + dot(normed[seq ^ 3], weights[2])
+        other = dot(normed[seq ^ 2], weights[1]) + dot(normed[seq ^ 3], weights[3])
+        gate_act = both[:, :units] + jnp.where(group == 0, mine, other)
+        up_act = both[:, units:] + jnp.where(group == 0, other, mine)
+        return (gate_act * jax.nn.sigmoid(gate_act) * up_act).astype(jnp.bfloat16)
+
+    for d in range(count - 1, -1, -1):
+        out = first if d >= 2 else second
+        out[pl.ds((d % 2) * rows, rows), :] = gated(d)
+
+
+def down_body(own, far, near, near_far, weights, low, high):
+    rows = low.shape[0]
+    for i, out in enumerate((low, high)):
+        total = 0.0
+        for j, piece in enumerate((own, near, far, near_far)):
+            total += jnp.dot(
+                piece[pl.ds(i * rows, rows), :], weights[j], preferred_element_type=jnp.float32
+            )
+        out[...] = total.astype(out.dtype)
+
+
+def project_body(count, offsets, gain, code, w_qkv_t, own, far, near, near_far, *outs):
+    seq, mp, _ = place()
+    features = own.shape[1]
+    capacity = outs[0].shape[0]
+    heads = offsets.shape[0]
+    squares, total = 0.0, 0.0
+    for j, piece in enumerate((own, near, far, near_far)):
+        index = column_block(seq, mp ^ j)
+        v = piece[...].astype(jnp.float32)
+        squares += jnp.sum(v * v, axis=1, keepdims=True)
+        scaled = (v * gain[:, at(index, features)]).astype(jnp.bfloat16)
+        total += lax.dot_general(
+            scaled,
+            w_qkv_t[:, at(index, features)],
+            (((1,), (1,)), ((), ())),
+            preferred_element_type=jnp.float32,
+        )
+    projected = (total * lax.rsqrt(squares * (1.0 / D_ENC) + epsilon)).astype(jnp.bfloat16)
+    codes = code[...]
+    rows = codes.shape[1]
+
+    def pick(wanted, array):
+        chosen = jnp.where(codes == wanted, 1.0, 0.0).astype(jnp.bfloat16)
+        return jnp.dot(chosen, array, preferred_element_type=jnp.float32).astype(jnp.bfloat16)
+
+    spread = []
+    per_block = capacity // DILATION_STEP
+    index = lax.broadcasted_iota(jnp.int32, (count * per_block, rows), 0)
+    for h in range(heads):
+        wanted = (index // per_block) * capacity + (index % per_block) * DILATION_STEP + offsets[h]
+        start = (3 * h + 1) * HEAD_WIDTH
+        both = pick(wanted, projected[:, start : start + 2 * HEAD_WIDTH])
+        spread.append(jnp.concatenate([both[:, :HEAD_WIDTH], both[:, HEAD_WIDTH:]], axis=0))
+    width = projected.shape[1]
+    beside = jnp.concatenate(spread, axis=1)
+    slot = lax.broadcasted_iota(jnp.int32, (capacity, rows), 0)
+    for d, out in enumerate(outs):
+        out[:, :width] = pick((seq ^ d) * capacity + slot, projected)
+        out[:, width:] = beside
+
+
+def attend_body(count, offsets, *refs):
+    packages, out, rows = refs[:count], refs[count], refs[count + 1]
+    seq, _, _ = place()
+    capacity = packages[0].shape[0]
+    heads = offsets.shape[0]
+    width = heads * 3 * HEAD_WIDTH
+    for d, package in enumerate(packages):
+        rows[at(seq ^ d, capacity), :] = package[:, :width]
+    far = [package[:, width:] for package in packages]
+    half = capacity // 2
+    far_keys = jnp.concatenate([f[:half] for f in far], axis=0)
+    far_values = jnp.concatenate([f[half:] for f in far], axis=0)
+    residue = lax.broadcasted_iota(jnp.int32, (1, out.shape[1]), 1) % DILATION_STEP
+    scale_factor = HEAD_WIDTH ** (-0.5)
+
+    def branch(query, key, value, mask):
+        scores = lax.dot_general(
+            key, query, (((1,), (1,)), ((), ())), preferred_element_type=jnp.float32
+        )
+        weights = jnp.exp(scores * scale_factor)
+        if mask is not None:
+            weights = jnp.where(mask, weights, 0.0)
+        numer = lax.dot_general(
+            value,
+            weights.astype(jnp.bfloat16),
+            (((0,), (0,)), ((), ())),
+            preferred_element_type=jnp.float32,
+        )
+        return numer, jnp.sum(weights, axis=0, keepdims=True)
+
+    for h in range(heads):
+        query, key, value = (
+            rows[:, pl.ds((3 * h + i) * HEAD_WIDTH, HEAD_WIDTH)] for i in range(3)
+        )
+        span = slice(h * HEAD_WIDTH, (h + 1) * HEAD_WIDTH)
+        near_num, near_den = branch(query, key, value, None)
+        mask = residue == offsets[h]
+        far_num, far_den = branch(query, far_keys[:, span], far_values[:, span], mask)
+        out[span, :] = ((near_num + far_num) / (near_den + far_den)).astype(jnp.bfloat16)
+
+
+def spread_mp(own, after=None):
+    far = swap(own, "mp", 2)
+    near = swap(own, "mp", 1)
+    relayed = far
+    if after is not None:
+        relayed, _ = lax.optimization_barrier((far, after))
+    return far, near, swap(relayed, "mp", 1)
+
+
+def split_hidden_plan(
+    tiles, counts, dest, gain_enc, w_gate, w_up, w_down, gain_slide, w_qkv, offsets
+):
+    count, mp_size = lax.axis_size("seq"), lax.axis_size("mp")
+    seq, mp = lax.axis_index("seq"), lax.axis_index("mp")
+    capacity = ENCODER_SLOTS // count
+    tile_rows = tiles.shape[0]
+    features = D_ENC // mp_size
+    depth = w_gate.shape[0]
+    units = w_gate.shape[1] // count
+    heads = offsets.shape[0]
+    bf16 = jnp.bfloat16
+    vmem, smem = pltpu.VMEM, pltpu.SMEM
+
+    quarter, mixed, third, next_block, kept, *downs = call(
+        functools.partial(cut_body, count),
+        [
+            ((tile_rows, features), bf16),
+            ((depth // 2, features + 2 * units), bf16),
+            ((depth // 2, 2 * units), bf16),
+            ((depth, 2 * units), bf16),
+            ((depth, 2 * units), bf16),
+        ]
+        + [((units, features), bf16)] * mp_size,
+        (tiles, w_gate, w_up, w_down),
+        spaces=[pltpu.HBM] * 4,
+        copies=10 + mp_size,
+        megabytes=60,
+    )
+    code = call(
+        functools.partial(code_body, capacity),
+        [((1, tile_rows), jnp.int32)],
+        (counts, dest, dest.reshape(1, tile_rows)),
+        spaces=[smem, vmem, vmem],
+    )[0]
+
+    own_1, mixed_in, own_3 = swap(quarter, "seq", 1), swap(mixed, "seq", 2), swap(quarter, "seq", 3)
+    downs = [downs[0]] + [swap(downs[j], "mp", j) for j in range(1, mp_size)]
+    own_1, mixed_in, own_3, downs, code = lax.optimization_barrier(
+        (own_1, mixed_in, own_3, downs, code)
+    )
+    own, columns = call(
+        restack_body,
+        [((count - 1, tile_rows, features), bf16), (third.shape, bf16)],
+        (own_1, mixed_in, own_3),
+    )
+    third, next_block, _ = lax.optimization_barrier((third, next_block, own))
+    third_in, next_in = swap(third, "seq", 3), swap(next_block, "seq", 1)
+    halves = [columns, swap(columns, "groups", 1), third_in, swap(third_in, "groups", 1)]
+    spread = spread_mp(own)
+    first, second = call(
+        functools.partial(hidden_body, count),
+        [((2 * tile_rows, units), bf16)] * 2,
+        (gain_enc[None, :], tiles, own, *spread, kept, next_in, *halves),
+        scratch=[
+            pltpu.VMEM((count, tile_rows, depth), bf16),
+            pltpu.VMEM((len(halves), depth, units), bf16),
+        ],
+    )
+
+    down_send, _ = lax.optimization_barrier((jnp.stack(downs), (third_in, next_in)))
+    perm = []
+    for s in range(count):
+        for m in range(mp_size):
+            user = (s ^ 2 * m) if m < 2 else (s + 2 * m - 5) % count
+            perm.append((s * mp_size + m, user * mp_size + m))
+    down_in = lax.ppermute(down_send, ("seq", "mp"), perm)
+
+    def down(rows_hidden, kinds, after):
+        return call(
+            down_body,
+            [((tile_rows, features), kind) for kind in kinds],
+            (rows_hidden, *spread_mp(rows_hidden, after), down_in),
+        )
+
+    sum_2, sum_3 = down(first, (bf16, bf16), None)
+    sum_0, sum_1 = down(second, (jnp.float32, bf16), sum_2)
+    holder = [0, 2, 1, 3]
+
+    def to_owner(part, d):
+        perm = []
+        for s in range(count):
+            for m in range(mp_size):
+                owner = s ^ d
+                perm.append((s * mp_size + m, owner * mp_size + holder[(s + holder[m] - owner) % count]))
+        return lax.ppermute(part, ("seq", "mp"), perm)
+
+    arrived = [to_owner(part, d) for d, part in ((2, sum_2), (3, sum_3), (1, sum_1))]
+    embedded_cols = (
+        block_at(tiles, column_block(seq, mp), features, 1).astype(jnp.float32)
+        + (sum_0 + sum(part.astype(jnp.float32) for part in arrived))
+    ).astype(bf16)
+
+    packages = call(
+        functools.partial(project_body, count),
+        [((capacity, 4 * heads * HEAD_WIDTH), bf16)] * count,
+        (offsets, gain_slide[None, :], code, w_qkv.T, embedded_cols, *spread_mp(embedded_cols)),
+        spaces=[smem] + [vmem] * 7,
+    )
+    packages = [packages[0]] + [swap(packages[d], "seq", d) for d in range(1, count)]
+    return call(
+        functools.partial(attend_body, count),
+        [((heads * HEAD_WIDTH, ENCODER_SLOTS), bf16)],
+        (offsets, *packages),
+        spaces=[smem] + [vmem] * count,
+        scratch=[pltpu.VMEM((ENCODER_SLOTS, 3 * heads * HEAD_WIDTH), bf16)],
+    )[0].T
+
+
+def on_device(*arrays):
+    sizes = lax.axis_size("groups"), lax.axis_size("seq"), lax.axis_size("mp")
+    if sizes == (2, 4, 4):
+        return split_hidden_plan(*arrays)
+    return gathered_plan(*arrays)
 
 
 def solution(mesh):

time: 286 us -> 181 us (0.63)
  waiting for transfers between devices: 181 us -> 70.4 us
  Pallas kernels: 0 us -> 77.5 us
  blocking collectives: 69 us -> 0 us
  starting transfers between devices: 0.12 us -> 30.9 us
  between operations: 14 us -> 0.81 us
  matrix products: 12.9 us -> 0 us
  other arithmetic: 4.79 us -> 1.15 us
  local copies, waits for them, and re-layouts: 3.63 us -> 0.16 us
    all_gather x3 -> x0, waiting for transfers between devices: 152 us -> none  [the longest x1 63.6 us: on_device(): lax.all_gather(w_down, 'seq', axis=1, tiled=True)]
    pallas_call x0 -> x8, Pallas kernels: none -> 77.5 us  [call(): pl.pallas_call(body, out_shape=[jax.ShapeDtypeStruct(shape, kind) for sha...]
    ppermute x0 -> x29, waiting for transfers between devices: none -> 70.4 us  [the longest x25 59 us: swap(): return lax.ppermute(array, axis, [(i, i ^ distance) for i in range(size)])]
    all_to_all x1 -> x0, blocking collectives: 47.4 us -> none  [on_device(): lax.all_to_all(outgoing, 'seq', split_axis=0, concat_axis=0, tiled=True)]
    ppermute x0 -> x29, starting transfers between devices: none -> 30.9 us  [the longest x25 26.3 us: swap(): return lax.ppermute(array, axis, [(i, i ^ distance) for i in range(size)])]
    reduce_scatter x1 -> x0, waiting for transfers between devices: 26.8 us -> none  [on_device(): share = lax.psum_scatter(partial_out, 'mp', scatter_dimension=1, tiled=True)]
    all_gather x2 -> x0, blocking collectives: 21.6 us -> none  [the longest x1 13.4 us: on_device(): portion = lax.all_gather(package, 'seq', axis=0, tiled=True)]
    dot_general x10 -> x0, matrix products: 12.9 us -> none  [the longest x1 6.25 us: on_device(): jnp.dot(hidden, lax.all_gather(w_down, 'seq', axis=1, tiled=True), prefer...]
  transfers between devices with their start and end apart: 4 -> 29, of which waited for: 4 -> 16; matrix products, arithmetic and copies ran while one was open for 3% -> 1% of each run, Pallas kernels for 0% -> 2%
where the time goes in v3:
time: 181 us
  Pallas kernels  77.5 us (43%)
  waiting for transfers between devices  70.4 us (39%)
  starting transfers between devices  30.9 us (17%)
    pallas_call x8, Pallas kernels, call(): pl.pallas_call(body, out_shape=[jax.ShapeDtypeStruct(shape, kind) for sha...  77.5 us
    ppermute x25, waiting for transfers between devices, swap(): return lax.ppermute(array, axis, [(i, i ^ distance) for i in range(size)])  59 us
    ppermute x25, starting transfers between devices, swap(): return lax.ppermute(array, axis, [(i, i ^ distance) for i in range(size)])  26.3 us
    ppermute x3, waiting for transfers between devices, to_owner(): return lax.ppermute(part, ('seq', 'mp'), perm)  11.4 us
    ppermute x3, starting transfers between devices, to_owner(): return lax.ppermute(part, ('seq', 'mp'), perm)  3.9 us
  transfers between devices with their start and end apart: 29, of which 16 were waited for; matrix products, arithmetic and copies ran while one was open for 1% of the time, Pallas kernels for 2%

profile of v3, /device:TPU:0, one launch (start us, length us, event | category | flops | bytes accessed | tf_op | source)
XLA Modules:
  0.0 180.9 jit_solution(12173879712308876216)
XLA Ops:
  0.0 69.7 %shard_map.100 = (bf16[192,384]{1,0:T(8,128)(2,1)}, bf16[192,896]{1,0:T(8,128)(2,1)}, bf16[192,512]{1,0:T(8,128)(2,1)}, bf16[384,512]{1,0:T(8,128)(2,1)}, bf16[3...) custom-call(bf16[192,1536]{1,0:T(8,128)(2,1)} %tiles.3, ...), custom_call_target="tpu_custom_call" | custom-call | tf_op jit(solution)/shard_map/pallas_call | solution.py:152
  69.7 0.0 copy-start
  69.8 4.1 %collective-permute-start.1 = (bf16[192,896]{1,0:T(8,128)(2,1)}, bf16[192,896]{1,0:T(8,128)(2,1)S(1)}, u32[]{:S(2)}, u32[]{:S(2)}) collective-permute-start(bf16[192,896]{1,0:T(8,128)(2,1)} %get-tuple-element.39), channel_id=1, source_target_pairs={{0,8},{4,12},{8,0},{12,4},{1,9},{5,13},{9,1},{13,5},{2,10},{6,14},... | collective-permute-start | bytes 1032200 | tf_op jit(solution)/shard_map/ppermute | solution.py:139
  73.9 1.6 collective-permute-start
  75.4 1.5 collective-permute-start.4
  76.9 0.4 collective-permute-start.5
  77.3 7.4 %collective-permute-done.first = bf16[192,384]{1,0:T(8,128)(2,1)S(1)} collective-permute-done((bf16[192,384]{1,0:T(8,128)(2,1)}, bf16[192,384]{1,0:T(8,128)(2,1)S(1)}, u32[]{:S(2)}, u32[]{:S(2)}) %collective-permute-start) | collective-permute-done | bytes 147488 | tf_op jit(solution)/shard_map/ppermute | solution.py:139
  84.7 1.4 collective-permute-start.2
  86.1 0.1 copy.11.dest
  86.8 0.1 shard_map.101.code
  86.9 4.9 %collective-permute-done.2.third = bf16[192,384]{1,0:T(8,128)(2,1)S(1)} collective-permute-done((bf16[192,384]{1,0:T(8,128)(2,1)}, bf16[192,384]{1,0:T(8,128)(2,1)S(1)}, u32[]{:S(2)}, u32[]{:S(2)}) %collective-permute-start.2) | collective-permute-done | bytes 147488 | tf_op jit(solution)/shard_map/ppermute | solution.py:139
  91.9 1.6 collective-permute-done.1.mixed
  93.5 0.1 shard_map.102
  93.6 1.9 %collective-permute-start.6 = (bf16[3,192,384]{2,1,0:T(8,128)(2,1)S(1)}, bf16[3,192,384]{2,1,0:T(8,128)(2,1)S(1)}, u32[]{:S(2)}, u32[]{:S(2)}) collective-permute-start(bf16[3,192,384]{2,1,0:T(8,128)(2,1)S(1)} %get-tuple-element.48.own), channel_id=1, source_target_pairs={{0,2},{1,3},{2,0},{3,1},{4,6},{5,7},{6,4},{7,5},{8,10},{9,11},{10,... | collective-permute-start | bytes 1327112 | tf_op jit(solution)/shard_map/ppermute | solution.py:139
  95.5 2.8 %collective-permute-start.9 = (bf16[384,512]{1,0:T(8,128)(2,1)}, bf16[384,512]{1,0:T(8,128)(2,1)S(1)}, u32[]{:S(2)}, u32[]{:S(2)}) collective-permute-start(bf16[384,512]{1,0:T(8,128)(2,1)} %get-tuple-element.52), channel_id=1, source_target_pairs={{0,4},{4,0},{8,12},{12,8},{1,5},{5,1},{9,13},{13,9},{2,6},{6,2},{1... | collective-permute-start | bytes 1179656 | tf_op jit(solution)/shard_map/ppermute | solution.py:139
  98.3 3.3 %collective-permute-start.11 = (bf16[192,512]{1,0:T(8,128)(2,1)}, bf16[192,512]{1,0:T(8,128)(2,1)S(1)}, u32[]{:S(2)}, u32[]{:S(2)}) collective-permute-start(bf16[192,512]{1,0:T(8,128)(2,1)} %get-tuple-element.54), channel_id=1, source_target_pairs={{0,12},{4,8},{8,4},{12,0},{1,13},{5,9},{9,5},{13,1},{2,14},{6,10},... | collective-permute-start | bytes 589832 | tf_op jit(solution)/shard_map/ppermute | solution.py:139
  101.6 1.0 collective-permute-done.6.far
  102.6 1.0 pad_maximum_fusion
  103.6 11.1 %collective-permute-done.11.refs_2_ = bf16[192,512]{1,0:T(8,128)(2,1)S(1)} collective-permute-done((bf16[192,512]{1,0:T(8,128)(2,1)}, bf16[192,512]{1,0:T(8,128)(2,1)S(1)}, u32[]{:S(2)}, u32[]{:S(2)}) %collective-permute-start.11) | collective-permute-done | bytes 196640 | tf_op jit(solution)/shard_map/ppermute | solution.py:139
  114.7 0.7 collective-permute-start.18
  115.4 1.6 collective-permute-start.10
  117.0 0.5 collective-permute-start.12
  117.5 5.7 %collective-permute-done.10.refs_1_ = bf16[192,512]{1,0:T(8,128)(2,1)S(1)} collective-permute-done((bf16[192,512]{1,0:T(8,128)(2,1)S(1)}, bf16[192,512]{1,0:T(8,128)(2,1)S(1)}, u32[]{:S(2)}, u32[]{:S(2)}) %collective-permute-start.10) | collective-permute-done | bytes 196640 | tf_op jit(solution)/shard_map/ppermute | solution.py:139
  123.3 3.3 %collective-permute-done.12.refs_3_ = bf16[192,512]{1,0:T(8,128)(2,1)S(1)} collective-permute-done((bf16[192,512]{1,0:T(8,128)(2,1)S(1)}, bf16[192,512]{1,0:T(8,128)(2,1)S(1)}, u32[]{:S(2)}, u32[]{:S(2)}) %collective-permute-start.12) | collective-permute-done | bytes 196640 | tf_op jit(solution)/shard_map/ppermute | solution.py:139
  126.6 2.5 %shard_map.103 = (bf16[384,256]{1,0:T(8,128)(2,1)S(1)}, bf16[384,256]{1,0:T(8,128)(2,1)S(1)}) custom-call(f32[1,1536]{1,0:T(1,128)S(1)} %broadcast_in_dim.7.gain, bf16[192,1536]{1,0:T(8,128)(2,1)S(1)} %copy-done, bf16[3,192,384]{2,1,0:T(8,128)(2,1)S(1)} %get-tuple-element.48.own, bf16[3,192,384]{2,1,0:T(8,128)(2,1)S(1)} %collective-permute-done.6.far, ...), custom_call_target="tpu_custom_call" | custom-call | tf_op jit(solution)/shard_map/pallas_call | solution.py:152
  129.1 0.6 collective-permute-start.15
  129.8 5.5 %collective-permute-done.15.far = bf16[384,256]{1,0:T(8,128)(2,1)S(1)} collective-permute-done((bf16[384,256]{1,0:T(8,128)(2,1)S(1)}, bf16[384,256]{1,0:T(8,128)(2,1)S(1)}, u32[]{:S(2)}, u32[]{:S(2)}) %collective-permute-start.15) | collective-permute-done | bytes 196640 | tf_op jit(solution)/shard_map/ppermute | solution.py:139
  135.3 0.4 collective-permute-start.13
  135.6 0.2 collective-permute-start.14
  135.8 0.8 collective-permute-done.17.near_far
  136.7 0.6 shard_map.104
  137.3 5.3 %collective-permute-done.13.far = bf16[384,256]{1,0:T(8,128)(2,1)S(1)} collective-permute-done((bf16[384,256]{1,0:T(8,128)(2,1)S(1)}, bf16[384,256]{1,0:T(8,128)(2,1)S(1)}, u32[]{:S(2)}, u32[]{:S(2)}) %collective-permute-start.13) | collective-permute-done | bytes 196640 | tf_op jit(solution)/shard_map/ppermute | solution.py:139
  142.6 3.5 %collective-permute-start.21 = (bf16[192,384]{1,0:T(8,128)(2,1)S(1)}, bf16[192,384]{1,0:T(8,128)(2,1)S(1)}, u32[]{:S(2)}, u32[]{:S(2)}) collective-permute-start(bf16[192,384]{1,0:T(8,128)(2,1)S(1)} %get-tuple-element.65), channel_id=1, source_target_pairs={{0,14},{1,15},{2,13},{3,12},{4,11},{5,10},{6,8},{7,9},{8,6},{9,7},... | collective-permute-start | bytes 442376 | tf_op jit(solution)/shard_map/ppermute | solution.py:456
  146.1 0.6 shard_map.105
  146.7 0.4 collective-permute-start.22
  147.1 8.7 %collective-permute-done.20 = bf16[192,384]{1,0:T(8,128)(2,1)S(1)} collective-permute-done((bf16[192,384]{1,0:T(8,128)(2,1)S(1)}, bf16[192,384]{1,0:T(8,128)(2,1)S(1)}, u32[]{:S(2)}, u32[]{:S(2)}) %collective-permute-start.20) | collective-permute-done | bytes 147488 | tf_op jit(solution)/shard_map/ppermute | solution.py:456
  155.8 2.7 %collective-permute-done.22 = bf16[192,384]{1,0:T(8,128)(2,1)S(1)} collective-permute-done((bf16[192,384]{1,0:T(8,128)(2,1)S(1)}, bf16[192,384]{1,0:T(8,128)(2,1)S(1)}, u32[]{:S(2)}, u32[]{:S(2)}) %collective-permute-start.22) | collective-permute-done | bytes 147488 | tf_op jit(solution)/shard_map/ppermute | solution.py:456
  158.5 0.1 add_convert_fusion.own
  158.6 1.6 collective-permute-start.23
  160.2 4.3 %collective-permute-done.23.far = bf16[192,384]{1,0:T(8,128)(2,1)S(1)} collective-permute-done((bf16[192,384]{1,0:T(8,128)(2,1)S(1)}, bf16[192,384]{1,0:T(8,128)(2,1)S(1)}, u32[]{:S(2)}, u32[]{:S(2)}) %collective-permute-start.23) | collective-permute-done | bytes 147488 | tf_op jit(solution)/shard_map/ppermute | solution.py:139
  164.5 1.3 collective-permute-done.25.near_far
  165.9 1.9 %shard_map.106 = (bf16[64,768]{1,0:T(8,128)(2,1)S(1)}, bf16[64,768]{1,0:T(8,128)(2,1)S(1)}, bf16[64,768]{1,0:T(8,128)(2,1)S(1)}, bf16[64,768]{1,0:T(8,128)(2,1)S(1)}) custom-call(s32[3]{0:T(128)S(1)} %copy-done.4, f32[1,1536]{1,0:T(1,128)S(1)} %broadcast_in_dim.6.gain, s32[1,192]{1,0:T(1,128)S(1)} %shard_map.101.code, bf16[576,1536]{1,0:T(8,128)(2,1)S(1)} %bitcast.7, ...), custom_call_target="tpu_custom_call" | custom-call | tf_op jit(solution)/shard_map/pallas_call | solution.py:152
  167.8 0.8 collective-permute-start.26
  168.5 1.9 %collective-permute-start.27 = (bf16[64,768]{1,0:T(8,128)(2,1)S(1)}, bf16[64,768]{1,0:T(8,128)(2,1)S(1)}, u32[]{:S(2)}, u32[]{:S(2)}) collective-permute-start(bf16[64,768]{1,0:T(8,128)(2,1)S(1)} %get-tuple-element.69), channel_id=1, source_target_pairs={{0,8},{4,12},{8,0},{12,4},{1,9},{5,13},{9,1},{13,5},{2,10},{6,14},... | collective-permute-start | bytes 294920 | tf_op jit(solution)/shard_map/ppermute | solution.py:139
  170.4 1.8 collective-permute-start.28
  172.2 2.3 %collective-permute-done.26.refs_1_ = bf16[64,768]{1,0:T(8,128)(2,1)S(1)} collective-permute-done((bf16[64,768]{1,0:T(8,128)(2,1)S(1)}, bf16[64,768]{1,0:T(8,128)(2,1)S(1)}, u32[]{:S(2)}, u32[]{:S(2)}) %collective-permute-start.26) | collective-permute-done | bytes 98336 | tf_op jit(solution)/shard_map/ppermute | solution.py:139
  174.5 4.3 %collective-permute-done.27.refs_2_ = bf16[64,768]{1,0:T(8,128)(2,1)S(1)} collective-permute-done((bf16[64,768]{1,0:T(8,128)(2,1)S(1)}, bf16[64,768]{1,0:T(8,128)(2,1)S(1)}, u32[]{:S(2)}, u32[]{:S(2)}) %collective-permute-start.27) | collective-permute-done | bytes 98336 | tf_op jit(solution)/shard_map/ppermute | solution.py:139
  178.8 2.1 %shard_map.107 = bf16[192,256]{1,0:T(8,128)(2,1)} custom-call(s32[3]{0:T(128)S(1)} %copy-done.4, bf16[64,768]{1,0:T(8,128)(2,1)S(1)} %get-tuple-element.67.refs_0_, bf16[64,768]{1,0:T(8,128)(2,1)S(1)} %collective-permute-done.26.refs_1_, bf16[64,768]{1,0:T(8,128)(2,1)S(1)} %collective-permute-done.27.refs_2_, bf16[64,768]{1,0:T(8,128)(2,1)S(1)} %collective-permute-done.28.refs_3_), custom_call_target="tpu_custom_call" | custom-call | tf_op jit(solution)/shard_map/pallas_call | solution.py:152
  (37 shorter events, 0.1 us)
Async XLA Ops:
  0.0 86.1 %copy-start.3 = (s32[192,1]{0,1:T(1,128)S(1)}, s32[192,1]{0,1:T(1,128)}, u32[]{:S(2)}) copy-start(s32[192,1]{0,1:T(1,128)} %param.12) | copy-start | bytes 2308
  69.7 47.8 %copy-start.5 = (f32[1536]{0:T(1024)S(1)}, f32[1536]{0:T(1024)}, u32[]{:S(2)}) copy-start(f32[1536]{0:T(1024)} %param.13) | copy-start | bytes 18436
  69.7 56.9 %copy-start = (bf16[192,1536]{1,0:T(8,128)(2,1)S(1)}, bf16[192,1536]{1,0:T(8,128)(2,1)}, u32[]{:S(2)}) copy-start(bf16[192,1536]{1,0:T(8,128)(2,1)} %tiles.3) | copy-start | bytes 1769476
  69.8 56.8 %copy-start.2 = (bf16[384,512]{1,0:T(8,128)(2,1)S(1)}, bf16[384,512]{1,0:T(8,128)(2,1)}, u32[]{:S(2)}) copy-start(bf16[384,512]{1,0:T(8,128)(2,1)} %get-tuple-element.49.kept) | copy-start | bytes 1179652
  69.8 23.7 %collective-permute-start.1 = (bf16[192,896]{1,0:T(8,128)(2,1)}, bf16[192,896]{1,0:T(8,128)(2,1)S(1)}, u32[]{:S(2)}, u32[]{:S(2)}) collective-permute-start(bf16[192,896]{1,0:T(8,128)(2,1)} %get-tuple-element.39), channel_id=1, source_target_pairs={{0,8},{4,12},{8,0},{12,4},{1,9},{5,13},{9,1},{13,5},{2,10},{6,14},... | collective-permute-start | bytes 1032200 | tf_op jit(solution)/shard_map/ppermute | solution.py:139
  73.9 10.8 %collective-permute-start = (bf16[192,384]{1,0:T(8,128)(2,1)}, bf16[192,384]{1,0:T(8,128)(2,1)S(1)}, u32[]{:S(2)}, u32[]{:S(2)}) collective-permute-start(bf16[192,384]{1,0:T(8,128)(2,1)} %get-tuple-element.38), channel_id=1, source_target_pairs={{0,4},{4,0},{8,12},{12,8},{1,5},{5,1},{9,13},{13,9},{2,6},{6,2},{1... | collective-permute-start | bytes 442376 | tf_op jit(solution)/shard_map/ppermute | solution.py:139
  75.4 16.4 %collective-permute-start.3 = (bf16[256,384]{1,0:T(8,128)(2,1)}, bf16[256,384]{1,0:T(8,128)(2,1)S(1)}, u32[]{:S(2)}, u32[]{:S(2)}) collective-permute-start(bf16[256,384]{1,0:T(8,128)(2,1)} %get-tuple-element.41), channel_id=1, source_target_pairs={{0,1},{1,0},{2,3},{3,2},{4,5},{5,4},{6,7},{7,6},{8,9},{9,8},{10,11... | collective-permute-start | bytes 589832 | tf_op jit(solution)/shard_map/ppermute | solution.py:139
  75.4 16.4 %collective-permute-start.4 = (bf16[256,384]{1,0:T(8,128)(2,1)}, bf16[256,384]{1,0:T(8,128)(2,1)S(1)}, u32[]{:S(2)}, u32[]{:S(2)}) collective-permute-start(bf16[256,384]{1,0:T(8,128)(2,1)} %get-tuple-element.42), channel_id=1, source_target_pairs={{0,2},{1,3},{2,0},{3,1},{4,6},{5,7},{6,4},{7,5},{8,10},{9,11},{10,... | collective-permute-start | bytes 589832 | tf_op jit(solution)/shard_map/ppermute | solution.py:139
  76.9 14.9 %collective-permute-start.5 = (bf16[256,384]{1,0:T(8,128)(2,1)}, bf16[256,384]{1,0:T(8,128)(2,1)S(1)}, u32[]{:S(2)}, u32[]{:S(2)}) collective-permute-start(bf16[256,384]{1,0:T(8,128)(2,1)} %get-tuple-element.43), channel_id=1, source_target_pairs={{0,3},{1,2},{2,1},{3,0},{4,7},{5,6},{6,5},{7,4},{8,11},{9,10},{10,... | collective-permute-start | bytes 589832 | tf_op jit(solution)/shard_map/ppermute | solution.py:139
  84.7 7.2 %collective-permute-start.2 = (bf16[192,384]{1,0:T(8,128)(2,1)}, bf16[192,384]{1,0:T(8,128)(2,1)S(1)}, u32[]{:S(2)}, u32[]{:S(2)}) collective-permute-start(bf16[192,384]{1,0:T(8,128)(2,1)} %get-tuple-element.38), channel_id=1, source_target_pairs={{0,12},{4,8},{8,4},{12,0},{1,13},{5,9},{9,5},{13,1},{2,14},{6,10},... | collective-permute-start | bytes 442376 | tf_op jit(solution)/shard_map/ppermute | solution.py:139
  93.6 9.0 %collective-permute-start.6 = (bf16[3,192,384]{2,1,0:T(8,128)(2,1)S(1)}, bf16[3,192,384]{2,1,0:T(8,128)(2,1)S(1)}, u32[]{:S(2)}, u32[]{:S(2)}) collective-permute-start(bf16[3,192,384]{2,1,0:T(8,128)(2,1)S(1)} %get-tuple-element.48.own), channel_id=1, source_target_pairs={{0,2},{1,3},{2,0},{3,1},{4,6},{5,7},{6,4},{7,5},{8,10},{9,11},{10,... | collective-permute-start | bytes 1327112 | tf_op jit(solution)/shard_map/ppermute | solution.py:139
  95.5 19.3 %collective-permute-start.9 = (bf16[384,512]{1,0:T(8,128)(2,1)}, bf16[384,512]{1,0:T(8,128)(2,1)S(1)}, u32[]{:S(2)}, u32[]{:S(2)}) collective-permute-start(bf16[384,512]{1,0:T(8,128)(2,1)} %get-tuple-element.52), channel_id=1, source_target_pairs={{0,4},{4,0},{8,12},{12,8},{1,5},{5,1},{9,13},{13,9},{2,6},{6,2},{1... | collective-permute-start | bytes 1179656 | tf_op jit(solution)/shard_map/ppermute | solution.py:139
  98.3 16.4 %collective-permute-start.11 = (bf16[192,512]{1,0:T(8,128)(2,1)}, bf16[192,512]{1,0:T(8,128)(2,1)S(1)}, u32[]{:S(2)}, u32[]{:S(2)}) collective-permute-start(bf16[192,512]{1,0:T(8,128)(2,1)} %get-tuple-element.54), channel_id=1, source_target_pairs={{0,12},{4,8},{8,4},{12,0},{1,13},{5,9},{9,5},{13,1},{2,14},{6,10},... | collective-permute-start | bytes 589832 | tf_op jit(solution)/shard_map/ppermute | solution.py:139
  101.6 25.0 %collective-permute-start.7 = (bf16[3,192,384]{2,1,0:T(8,128)(2,1)S(1)}, bf16[3,192,384]{2,1,0:T(8,128)(2,1)S(1)}, u32[]{:S(2)}, u32[]{:S(2)}) collective-permute-start(bf16[3,192,384]{2,1,0:T(8,128)(2,1)S(1)} %get-tuple-element.48.own), channel_id=1, source_target_pairs={{0,1},{1,0},{2,3},{3,2},{4,5},{5,4},{6,7},{7,6},{8,9},{9,8},{10,11... | collective-permute-start | bytes 1327112 | tf_op jit(solution)/shard_map/ppermute | solution.py:139
  102.6 24.0 %collective-permute-start.8 = (bf16[3,192,384]{2,1,0:T(8,128)(2,1)S(1)}, bf16[3,192,384]{2,1,0:T(8,128)(2,1)S(1)}, u32[]{:S(2)}, u32[]{:S(2)}) collective-permute-start(bf16[3,192,384]{2,1,0:T(8,128)(2,1)S(1)} %collective-permute-done.6.far), channel_id=1, source_target_pairs={{0,1},{1,0},{2,3},{3,2},{4,5},{5,4},{6,7},{7,6},{8,9},{9,8},{10,11... | collective-permute-start | bytes 1327112 | tf_op jit(solution)/shard_map/ppermute | solution.py:139
  114.7 21.1 %collective-permute-start.18 = (bf16[4,256,384]{2,1,0:T(8,128)(2,1)S(1)}, bf16[4,256,384]{2,1,0:T(8,128)(2,1)S(1)}, u32[]{:S(2)}, u32[]{:S(2)}) collective-permute-start(bf16[4,256,384]{2,1,0:T(8,128)(2,1)S(1)} %pad_maximum_fusion), channel_id=1, source_target_pairs={{0,0},{1,9},{2,14},{3,7},{4,4},{5,13},{6,2},{7,11},{8,8},{9,1},{10... | collective-permute-start | bytes 2359304 | tf_op jit(solution)/shard_map/ppermute | solution.py:437
  115.4 7.8 %collective-permute-start.10 = (bf16[192,512]{1,0:T(8,128)(2,1)S(1)}, bf16[192,512]{1,0:T(8,128)(2,1)S(1)}, u32[]{:S(2)}, u32[]{:S(2)}) collective-permute-start(bf16[192,512]{1,0:T(8,128)(2,1)S(1)} %get-tuple-element.53.refs_0_), channel_id=1, source_target_pairs={{0,16},{16,0},{1,17},{17,1},{2,18},{18,2},{3,19},{19,3},{4,20},{20... | collective-permute-start | bytes 589832 | tf_op jit(solution)/shard_map/ppermute | solution.py:139
  117.0 9.6 %collective-permute-start.12 = (bf16[192,512]{1,0:T(8,128)(2,1)S(1)}, bf16[192,512]{1,0:T(8,128)(2,1)S(1)}, u32[]{:S(2)}, u32[]{:S(2)}) collective-permute-start(bf16[192,512]{1,0:T(8,128)(2,1)S(1)} %collective-permute-done.11.refs_2_), channel_id=1, source_target_pairs={{0,16},{16,0},{1,17},{17,1},{2,18},{18,2},{3,19},{19,3},{4,20},{20... | collective-permute-start | bytes 589832 | tf_op jit(solution)/shard_map/ppermute | solution.py:139
  129.1 6.1 %collective-permute-start.15 = (bf16[384,256]{1,0:T(8,128)(2,1)S(1)}, bf16[384,256]{1,0:T(8,128)(2,1)S(1)}, u32[]{:S(2)}, u32[]{:S(2)}) collective-permute-start(bf16[384,256]{1,0:T(8,128)(2,1)S(1)} %get-tuple-element.56.own), channel_id=1, source_target_pairs={{0,2},{1,3},{2,0},{3,1},{4,6},{5,7},{6,4},{7,5},{8,10},{9,11},{10,... | collective-permute-start | bytes 589832 | tf_op jit(solution)/shard_map/ppermute | solution.py:139
  129.8 6.1 %collective-permute-start.16 = (bf16[384,256]{1,0:T(8,128)(2,1)S(1)}, bf16[384,256]{1,0:T(8,128)(2,1)S(1)}, u32[]{:S(2)}, u32[]{:S(2)}) collective-permute-start(bf16[384,256]{1,0:T(8,128)(2,1)S(1)} %get-tuple-element.56.own), channel_id=1, source_target_pairs={{0,1},{1,0},{2,3},{3,2},{4,5},{5,4},{6,7},{7,6},{8,9},{9,8},{10,11... | collective-permute-start | bytes 589832 | tf_op jit(solution)/shard_map/ppermute | solution.py:139
  135.2 1.4 collective-permute-start.17
  135.2 29.3 %copy-start.6 = (f32[1536]{0:T(1024)S(1)}, f32[1536]{0:T(1024)}, u32[]{:S(2)}) copy-start(f32[1536]{0:T(1024)} %param.17) | copy-start | bytes 18436
  135.2 30.6 %copy-start.1 = (bf16[1536,576]{0,1:T(8,128)(2,1)S(1)}, bf16[1536,576]{0,1:T(8,128)(2,1)}, u32[]{:S(2)}) copy-start(bf16[1536,576]{0,1:T(8,128)(2,1)} %param.18) | copy-start | bytes 5308420
  135.2 30.6 %copy-start.4 = (s32[3]{0:T(128)S(1)}, s32[3]{0:T(128)}, u32[]{:S(2)}) copy-start(s32[3]{0:T(128)} %offsets.3) | copy-start | bytes 40
  135.3 7.3 %collective-permute-start.13 = (bf16[384,256]{1,0:T(8,128)(2,1)S(1)}, bf16[384,256]{1,0:T(8,128)(2,1)S(1)}, u32[]{:S(2)}, u32[]{:S(2)}) collective-permute-start(bf16[384,256]{1,0:T(8,128)(2,1)S(1)} %get-tuple-element.55.own), channel_id=1, source_target_pairs={{0,2},{1,3},{2,0},{3,1},{4,6},{5,7},{6,4},{7,5},{8,10},{9,11},{10,... | collective-permute-start | bytes 589832 | tf_op jit(solution)/shard_map/ppermute | solution.py:139
  135.6 10.5 %collective-permute-start.14 = (bf16[384,256]{1,0:T(8,128)(2,1)S(1)}, bf16[384,256]{1,0:T(8,128)(2,1)S(1)}, u32[]{:S(2)}, u32[]{:S(2)}) collective-permute-start(bf16[384,256]{1,0:T(8,128)(2,1)S(1)} %get-tuple-element.55.own), channel_id=1, source_target_pairs={{0,1},{1,0},{2,3},{3,2},{4,5},{5,4},{6,7},{7,6},{8,9},{9,8},{10,11... | collective-permute-start | bytes 589832 | tf_op jit(solution)/shard_map/ppermute | solution.py:139
  142.6 3.6 %collective-permute-start.19 = (bf16[384,256]{1,0:T(8,128)(2,1)S(1)}, bf16[384,256]{1,0:T(8,128)(2,1)S(1)}, u32[]{:S(2)}, u32[]{:S(2)}) collective-permute-start(bf16[384,256]{1,0:T(8,128)(2,1)S(1)} %collective-permute-done.13.far), channel_id=1, source_target_pairs={{0,1},{1,0},{2,3},{3,2},{4,5},{5,4},{6,7},{7,6},{8,9},{9,8},{10,11... | collective-permute-start | bytes 589832 | tf_op jit(solution)/shard_map/ppermute | solution.py:139
  142.6 13.2 %collective-permute-start.20 = (bf16[192,384]{1,0:T(8,128)(2,1)S(1)}, bf16[192,384]{1,0:T(8,128)(2,1)S(1)}, u32[]{:S(2)}, u32[]{:S(2)}) collective-permute-start(bf16[192,384]{1,0:T(8,128)(2,1)S(1)} %get-tuple-element.62), channel_id=1, source_target_pairs={{0,9},{1,8},{2,11},{3,10},{4,13},{5,12},{6,15},{7,14},{8,1},{9,0},... | collective-permute-start | bytes 442376 | tf_op jit(solution)/shard_map/ppermute | solution.py:456
  142.6 13.2 %collective-permute-start.21 = (bf16[192,384]{1,0:T(8,128)(2,1)S(1)}, bf16[192,384]{1,0:T(8,128)(2,1)S(1)}, u32[]{:S(2)}, u32[]{:S(2)}) collective-permute-start(bf16[192,384]{1,0:T(8,128)(2,1)S(1)} %get-tuple-element.65), channel_id=1, source_target_pairs={{0,14},{1,15},{2,13},{3,12},{4,11},{5,10},{6,8},{7,9},{8,6},{9,7},... | collective-permute-start | bytes 442376 | tf_op jit(solution)/shard_map/ppermute | solution.py:456
  146.7 11.8 %collective-permute-start.22 = (bf16[192,384]{1,0:T(8,128)(2,1)S(1)}, bf16[192,384]{1,0:T(8,128)(2,1)S(1)}, u32[]{:S(2)}, u32[]{:S(2)}) collective-permute-start(bf16[192,384]{1,0:T(8,128)(2,1)S(1)} %get-tuple-element.66), channel_id=1, source_target_pairs={{0,7},{1,6},{2,4},{3,5},{4,2},{5,3},{6,1},{7,0},{8,15},{9,14},{10,... | collective-permute-start | bytes 442376 | tf_op jit(solution)/shard_map/ppermute | solution.py:456
  158.6 5.9 %collective-permute-start.23 = (bf16[192,384]{1,0:T(8,128)(2,1)S(1)}, bf16[192,384]{1,0:T(8,128)(2,1)S(1)}, u32[]{:S(2)}, u32[]{:S(2)}) collective-permute-start(bf16[192,384]{1,0:T(8,128)(2,1)S(1)} %add_convert_fusion.own), channel_id=1, source_target_pairs={{0,2},{1,3},{2,0},{3,1},{4,6},{5,7},{6,4},{7,5},{8,10},{9,11},{10,... | collective-permute-start | bytes 442376 | tf_op jit(solution)/shard_map/ppermute | solution.py:139
  160.2 4.3 %collective-permute-start.24 = (bf16[192,384]{1,0:T(8,128)(2,1)S(1)}, bf16[192,384]{1,0:T(8,128)(2,1)S(1)}, u32[]{:S(2)}, u32[]{:S(2)}) collective-permute-start(bf16[192,384]{1,0:T(8,128)(2,1)S(1)} %add_convert_fusion.own), channel_id=1, source_target_pairs={{0,1},{1,0},{2,3},{3,2},{4,5},{5,4},{6,7},{7,6},{8,9},{9,8},{10,11... | collective-permute-start | bytes 442376 | tf_op jit(solution)/shard_map/ppermute | solution.py:139
  164.5 1.4 collective-permute-start.25
  167.8 6.7 %collective-permute-start.26 = (bf16[64,768]{1,0:T(8,128)(2,1)S(1)}, bf16[64,768]{1,0:T(8,128)(2,1)S(1)}, u32[]{:S(2)}, u32[]{:S(2)}) collective-permute-start(bf16[64,768]{1,0:T(8,128)(2,1)S(1)} %get-tuple-element.68), channel_id=1, source_target_pairs={{0,4},{4,0},{8,12},{12,8},{1,5},{5,1},{9,13},{13,9},{2,6},{6,2},{1... | collective-permute-start | bytes 294920 | tf_op jit(solution)/shard_map/ppermute | solution.py:139
  168.5 10.3 %collective-permute-start.27 = (bf16[64,768]{1,0:T(8,128)(2,1)S(1)}, bf16[64,768]{1,0:T(8,128)(2,1)S(1)}, u32[]{:S(2)}, u32[]{:S(2)}) collective-permute-start(bf16[64,768]{1,0:T(8,128)(2,1)S(1)} %get-tuple-element.69), channel_id=1, source_target_pairs={{0,8},{4,12},{8,0},{12,4},{1,9},{5,13},{9,1},{13,5},{2,10},{6,14},... | collective-permute-start | bytes 294920 | tf_op jit(solution)/shard_map/ppermute | solution.py:139
  170.4 8.4 %collective-permute-start.28 = (bf16[64,768]{1,0:T(8,128)(2,1)S(1)}, bf16[64,768]{1,0:T(8,128)(2,1)S(1)}, u32[]{:S(2)}, u32[]{:S(2)}) collective-permute-start(bf16[64,768]{1,0:T(8,128)(2,1)S(1)} %get-tuple-element.70), channel_id=1, source_target_pairs={{0,12},{4,8},{8,4},{12,0},{1,13},{5,9},{9,5},{13,1},{2,14},{6,10},... | collective-permute-start | bytes 294920 | tf_op jit(solution)/shard_map/ppermute | solution.py:139

commit v4 on v3

--- a/solution.py
+++ b/solution.py
@@ -145,7 +145,6 @@
 
 def call(body, outs, inputs, spaces=None, scratch=(), copies=0, megabytes=40):
     spaces = spaces or [pltpu.VMEM] * len(inputs)
-    out_space = pl.ANY if copies else pltpu.VMEM
     scratch = list(scratch)
     if copies:
         scratch.append(pltpu.SemaphoreType.DMA((copies,)))
@@ -153,7 +152,7 @@
         body,
         out_shape=[jax.ShapeDtypeStruct(shape, kind) for shape, kind in outs],
         in_specs=[pl.BlockSpec(memory_space=space) for space in spaces],
-        out_specs=[pl.BlockSpec(memory_space=out_space)] * len(outs),
+        out_specs=[pl.BlockSpec(memory_space=pltpu.VMEM)] * len(outs),
         scratch_shapes=scratch,
         compiler_params=pltpu.CompilerParams(vmem_limit_bytes=megabytes * 1024 * 1024),
     )(*inputs)
@@ -178,12 +177,11 @@
 
 
 def cut_body(
-    count, tiles, w_gate, w_up, w_down, quarter, mixed, third, next_block, kept, *downs_and_sems
+    count, tiles, w_gate, w_up, w_down, next_out, second_out, third_out, kept, near, far, sems
 ):
-    downs, sems = downs_and_sems[:-1], downs_and_sems[-1]
     seq, mp, group = place()
     depth, units = w_gate.shape[0], w_gate.shape[1] // count
-    half, features = depth // 2, quarter.shape[1]
+    half, features = depth // 2, near.shape[2]
     copies = []
 
     def copy(source, target, other=None):
@@ -196,28 +194,32 @@
             pl.when(group != 0)(second.start)
         copies.append(started)
 
-    own_columns = tiles.at[:, at(mp, features)]
-    copy(own_columns, quarter)
-    copy(own_columns, mixed.at[:, pl.ds(0, features)])
-    for owner, target, start in ((seq ^ 2, mixed, features), (seq ^ 3, third, 0)):
+    for d, target in ((1, next_out), (2, second_out), (3, third_out)):
+        copy(tiles.at[:, at(mp, features)], target.at[:, pl.ds(0, features)])
         for i in range(2):
-            span = pl.ds(i * half, half), at(owner, units)
-            copy(w_gate.at[span], target.at[:, pl.ds(start + i * units, units)], w_up.at[span])
-    for owner, target in ((seq ^ 1, next_block), (seq, kept)):
-        for i, weight in enumerate((w_gate, w_up)):
-            copy(weight.at[:, at(owner, units)], target.at[:, pl.ds(i * units, units)])
-    for j, down in enumerate(downs):
-        copy(w_down.at[at(column_user(seq, mp ^ j), units), :], down)
+            span = pl.ds(i * half, half), at(seq ^ d, units)
+            if d == 1:
+                for k, weight in enumerate((w_gate, w_up)):
+                    columns = pl.ds(features + (2 * i + k) * units, units)
+                    copy(weight.at[span], target.at[:, columns])
+            else:
+                columns = pl.ds(features + i * units, units)
+                copy(w_gate.at[span], target.at[:, columns], w_up.at[span])
+    for i, weight in enumerate((w_gate, w_up)):
+        copy(weight.at[:, at(seq, units)], kept.at[:, pl.ds(i * units, units)])
+    for j in range(4):
+        rows = at(column_user(seq, mp ^ j), units)
+        copy(w_down.at[rows, :], (far if j >= 2 else near).at[j % 2])
     for started in copies:
         started.wait()
 
 
-def restack_body(first, mixed, third, stacked, columns):
-    features = first.shape[1]
-    stacked[0] = first[...]
-    stacked[1] = mixed[:, :features]
-    stacked[2] = third[...]
-    columns[...] = mixed[:, features:]
+def restack_body(first, second, third, stacked, columns):
+    features = stacked.shape[2]
+    for i, package in enumerate((first, second, third)):
+        stacked[i] = package[:, :features]
+    columns[0] = second[:, features:]
+    columns[1] = third[:, features:]
 
 
 def code_body(capacity, counts, dest, dest_row, code):
@@ -231,16 +233,20 @@
 
 
 def hidden_body(
-    count, gain, tiles, own, far, near, near_far, kept, next_block, *refs
+    count, gain, tiles, own, far, near, near_far, kept, next_in, columns, others, out, *scratch
 ):
-    halves, (first, second, normed, weights) = refs[:4], refs[4:]
+    normed, weights, next_weights = scratch
     seq, mp, group = place()
     depth, units = weights.shape[1:]
     half = depth // 2
-    rows = tiles.shape[0]
-    for i, piece in enumerate(halves):
-        weights[i, :half, :] = piece[:, :units]
-        weights[i, half:, :] = piece[:, units:]
+    rows, features = tiles.shape[0], own.shape[2]
+    for i in range(2):
+        span = pl.ds(i * half, half)
+        for k in range(2):
+            weights[2 * k, span, :] = columns[k, :, i * units : (i + 1) * units]
+            weights[2 * k + 1, span, :] = others[k, :, i * units : (i + 1) * units]
+        start = features + 2 * i * units
+        next_weights[span, :] = next_in[:, start : start + 2 * units]
 
     def gated(d):
         if d == 0:
@@ -252,27 +258,27 @@
         squares = sum(jnp.sum(v * v, axis=1, keepdims=True) for v in values)
         inverse = lax.rsqrt(squares * (1.0 / D_ENC) + epsilon)
         for v, (_, index) in zip(values, pieces):
-            normed[index] = (v * inverse * gain[:, at(index, depth)]).astype(jnp.bfloat16)
+            normed[d, index] = (v * inverse * gain[:, at(index, depth)]).astype(jnp.bfloat16)
         dot = functools.partial(jnp.dot, preferred_element_type=jnp.float32)
-        both = dot(normed[seq], kept[...]) + dot(normed[seq ^ 1], next_block[...])
-        mine = dot(normed[seq ^ 2], weights[0]) + dot(normed[seq ^ 3], weights[2])
-        other = dot(normed[seq ^ 2], weights[1]) + dot(normed[seq ^ 3], weights[3])
+        both = dot(normed[d, seq], kept[...]) + dot(normed[d, seq ^ 1], next_weights[...])
+        mine = dot(normed[d, seq ^ 2], weights[0]) + dot(normed[d, seq ^ 3], weights[2])
+        other = dot(normed[d, seq ^ 2], weights[1]) + dot(normed[d, seq ^ 3], weights[3])
         gate_act = both[:, :units] + jnp.where(group == 0, mine, other)
         up_act = both[:, units:] + jnp.where(group == 0, other, mine)
         return (gate_act * jax.nn.sigmoid(gate_act) * up_act).astype(jnp.bfloat16)
 
     for d in range(count - 1, -1, -1):
-        out = first if d >= 2 else second
-        out[pl.ds((d % 2) * rows, rows), :] = gated(d)
-
-
-def down_body(own, far, near, near_far, weights, low, high):
-    rows = low.shape[0]
-    for i, out in enumerate((low, high)):
+        out[pl.ds(d * rows, rows), :] = gated(d)
+
+
+def down_body(own, far, near, near_far, even, odd, *outs):
+    rows = outs[0].shape[0]
+    for i, out in enumerate(outs):
         total = 0.0
-        for j, piece in enumerate((own, near, far, near_far)):
+        pairs = ((own, even[0]), (near, odd[0]), (far, even[1]), (near_far, odd[1]))
+        for piece, weights in pairs:
             total += jnp.dot(
-                piece[pl.ds(i * rows, rows), :], weights[j], preferred_element_type=jnp.float32
+                piece[pl.ds(i * rows, rows), :], weights, preferred_element_type=jnp.float32
             )
         out[...] = total.astype(out.dtype)
 
@@ -359,13 +365,10 @@
         out[span, :] = ((near_num + far_num) / (near_den + far_den)).astype(jnp.bfloat16)
 
 
-def spread_mp(own, after=None):
+def spread_mp(own, beside=None):
     far = swap(own, "mp", 2)
-    near = swap(own, "mp", 1)
-    relayed = far
-    if after is not None:
-        relayed, _ = lax.optimization_barrier((far, after))
-    return far, near, swap(relayed, "mp", 1)
+    relayed = far if beside is None else lax.optimization_barrier((far, beside))[0]
+    return far, swap(own, "mp", 1), swap(relayed, "mp", 1)
 
 
 def split_hidden_plan(
@@ -382,20 +385,20 @@
     bf16 = jnp.bfloat16
     vmem, smem = pltpu.VMEM, pltpu.SMEM
 
-    quarter, mixed, third, next_block, kept, *downs = call(
+    *packages, kept, down_near, down_far = call(
         functools.partial(cut_body, count),
         [
-            ((tile_rows, features), bf16),
-            ((depth // 2, features + 2 * units), bf16),
-            ((depth // 2, 2 * units), bf16),
+            ((tile_rows, features + 4 * units), bf16),
+            ((tile_rows, features + 2 * units), bf16),
+            ((tile_rows, features + 2 * units), bf16),
             ((depth, 2 * units), bf16),
-            ((depth, 2 * units), bf16),
-        ]
-        + [((units, features), bf16)] * mp_size,
+            ((2, units, features), bf16),
+            ((2, units, features), bf16),
+        ],
         (tiles, w_gate, w_up, w_down),
         spaces=[pltpu.HBM] * 4,
-        copies=10 + mp_size,
-        megabytes=60,
+        copies=17,
+        megabytes=57,
     )
     code = call(
         functools.partial(code_body, capacity),
@@ -404,47 +407,45 @@
         spaces=[smem, vmem, vmem],
     )[0]
 
-    own_1, mixed_in, own_3 = swap(quarter, "seq", 1), swap(mixed, "seq", 2), swap(quarter, "seq", 3)
-    downs = [downs[0]] + [swap(downs[j], "mp", j) for j in range(1, mp_size)]
-    own_1, mixed_in, own_3, downs, code = lax.optimization_barrier(
-        (own_1, mixed_in, own_3, downs, code)
-    )
+    packages = [swap(packages[d - 1], "seq", d) for d in range(1, count)]
+    from_far = swap(down_far, "mp", 2)
+    down_send = [jnp.stack([down_near[j], from_far[j]]) for j in range(2)]
+    packages, down_send, code = lax.optimization_barrier((packages, down_send, code))
     own, columns = call(
         restack_body,
-        [((count - 1, tile_rows, features), bf16), (third.shape, bf16)],
-        (own_1, mixed_in, own_3),
-    )
-    third, next_block, _ = lax.optimization_barrier((third, next_block, own))
-    third_in, next_in = swap(third, "seq", 3), swap(next_block, "seq", 1)
-    halves = [columns, swap(columns, "groups", 1), third_in, swap(third_in, "groups", 1)]
-    spread = spread_mp(own)
-    first, second = call(
+        [
+            ((count - 1, tile_rows, features), bf16),
+            ((count - 2, tile_rows, 2 * units), bf16),
+        ],
+        packages,
+    )
+    others = swap(columns, "groups", 1)
+    down_send, _ = lax.optimization_barrier((down_send, own))
+    down_in = []
+    for j in range(2):
+        perm = []
+        for s in range(count):
+            for m in range(mp_size):
+                k = m ^ j
+                user = (s ^ 2 * k) if k < 2 else (s + 2 * k - 5) % count
+                perm.append((s * mp_size + m, user * mp_size + k))
+        down_in.append(lax.ppermute(down_send[j], ("seq", "mp"), perm))
+    spread = spread_mp(own, (others, down_in[0]))
+    hidden = call(
         functools.partial(hidden_body, count),
-        [((2 * tile_rows, units), bf16)] * 2,
-        (gain_enc[None, :], tiles, own, *spread, kept, next_in, *halves),
+        [((count * tile_rows, units), bf16)],
+        (gain_enc[None, :], tiles, own, *spread, kept, packages[0], columns, others),
         scratch=[
-            pltpu.VMEM((count, tile_rows, depth), bf16),
-            pltpu.VMEM((len(halves), depth, units), bf16),
+            pltpu.VMEM((count, count, tile_rows, depth), bf16),
+            pltpu.VMEM((4, depth, units), bf16),
+            pltpu.VMEM((depth, 2 * units), bf16),
         ],
-    )
-
-    down_send, _ = lax.optimization_barrier((jnp.stack(downs), (third_in, next_in)))
-    perm = []
-    for s in range(count):
-        for m in range(mp_size):
-            user = (s ^ 2 * m) if m < 2 else (s + 2 * m - 5) % count
-            perm.append((s * mp_size + m, user * mp_size + m))
-    down_in = lax.ppermute(down_send, ("seq", "mp"), perm)
-
-    def down(rows_hidden, kinds, after):
-        return call(
-            down_body,
-            [((tile_rows, features), kind) for kind in kinds],
-            (rows_hidden, *spread_mp(rows_hidden, after), down_in),
-        )
-
-    sum_2, sum_3 = down(first, (bf16, bf16), None)
-    sum_0, sum_1 = down(second, (jnp.float32, bf16), sum_2)
+    )[0]
+    sums = call(
+        down_body,
+        [((tile_rows, features), kind) for kind in (jnp.float32, bf16, bf16, bf16)],
+        (hidden, *spread_mp(hidden), *down_in),
+    )
     holder = [0, 2, 1, 3]
 
     def to_owner(part, d):
@@ -455,10 +456,10 @@
                 perm.append((s * mp_size + m, owner * mp_size + holder[(s + holder[m] - owner) % count]))
         return lax.ppermute(part, ("seq", "mp"), perm)
 
-    arrived = [to_owner(part, d) for d, part in ((2, sum_2), (3, sum_3), (1, sum_1))]
+    arrived = [to_owner(sums[d], d) for d in (2, 3, 1)]
     embedded_cols = (
         block_at(tiles, column_block(seq, mp), features, 1).astype(jnp.float32)
-        + (sum_0 + sum(part.astype(jnp.float32) for part in arrived))
+        + (sums[0] + sum(part.astype(jnp.float32) for part in arrived))
     ).astype(bf16)
 
     packages = call(

time: 181 us -> 111 us (0.61)
  Pallas kernels: 77.5 us -> 11.2 us
  waiting for transfers between devices: 70.4 us -> 66.5 us
    pallas_call x8 -> x7, Pallas kernels: 77.5 us -> 11.2 us  [call(): pl.pallas_call(body, out_shape=[jax.ShapeDtypeStruct(shape, kind) for sha...]
    ppermute x25 -> x17, waiting for transfers between devices: 59 us -> 54.5 us  [swap(): return lax.ppermute(array, axis, [(i, i ^ distance) for i in range(size)])]
    ppermute x25 -> x17, starting transfers between devices: 26.3 us -> 24.5 us  [swap(): return lax.ppermute(array, axis, [(i, i ^ distance) for i in range(size)])]
  transfers between devices with their start and end apart: 29 -> 22, of which waited for: 16 -> 15; matrix products, arithmetic and copies ran while one was open for 1% -> 1% of each run, Pallas kernels for 2% -> 0%
where the time goes in v4:
time: 111 us
  waiting for transfers between devices  66.5 us (60%)
  starting transfers between devices  30.8 us (28%)
  Pallas kernels  11.2 us (10%)
  local copies, waits for them, and re-layouts  1.27 us (1%)
    ppermute x17, waiting for transfers between devices, swap(): return lax.ppermute(array, axis, [(i, i ^ distance) for i in range(size)])  54.5 us
    ppermute x17, starting transfers between devices, swap(): return lax.ppermute(array, axis, [(i, i ^ distance) for i in range(size)])  24.5 us
    ppermute x3, waiting for transfers between devices, to_owner(): return lax.ppermute(part, ('seq', 'mp'), perm)  12 us
    pallas_call x7, Pallas kernels, call(): pl.pallas_call(body, out_shape=[jax.ShapeDtypeStruct(shape, kind) for sha...  11.2 us
    ppermute x3, starting transfers between devices, to_owner(): return lax.ppermute(part, ('seq', 'mp'), perm)  4.93 us
  transfers between devices with their start and end apart: 22, of which 15 were waited for; matrix products, arithmetic and copies ran while one was open for 1% of the time, Pallas kernels for 0%

profile of v4, /device:TPU:0, one launch (start us, length us, event | category | flops | bytes accessed | tf_op | source)
XLA Modules:
  0.0 110.8 jit_solution(11441162419011346186)
XLA Ops:
  0.0 3.3 %shard_map.100 = (bf16[192,1408]{1,0:T(8,128)(2,1)}, bf16[192,896]{1,0:T(8,128)(2,1)}, bf16[192,896]{1,0:T(8,128)(2,1)}, bf16[384,512]{1,0:T(8,128)(2,1)}, bf16[...) custom-call(bf16[192,1536]{1,0:T(8,128)(2,1)} %tiles.3, bf16[384,1024]{1,0:T(8,128)(2,1)} %w_gate.1, ...), custom_call_target="tpu_custom_call" | custom-call | tf_op jit(solution)/shard_map/pallas_call | solution.py:151
  3.3 3.0 %collective-permute-start.3 = (bf16[2,256,384]{2,1,0:T(8,128)(2,1)}, bf16[2,256,384]{2,1,0:T(8,128)(2,1)S(1)}, u32[]{:S(2)}, u32[]{:S(2)}) collective-permute-start(bf16[2,256,384]{2,1,0:T(8,128)(2,1)} %get-tuple-element.34), channel_id=1, source_target_pairs={{0,2},{1,3},{2,0},{3,1},{4,6},{5,7},{6,4},{7,5},{8,10},{9,11},{10,... | collective-permute-start | bytes 1179656 | tf_op jit(solution)/shard_map/ppermute | solution.py:139
  6.3 1.6 %collective-permute-start = (bf16[192,1408]{1,0:T(8,128)(2,1)}, bf16[192,1408]{1,0:T(8,128)(2,1)S(1)}, u32[]{:S(2)}, u32[]{:S(2)}) collective-permute-start(bf16[192,1408]{1,0:T(8,128)(2,1)} %get-tuple-element.30), channel_id=1, source_target_pairs={{0,4},{4,0},{8,12},{12,8},{1,5},{5,1},{9,13},{13,9},{2,6},{6,2},{1... | collective-permute-start | bytes 1622024 | tf_op jit(solution)/shard_map/ppermute | solution.py:139
  7.9 2.6 %collective-permute-start.1 = (bf16[192,896]{1,0:T(8,128)(2,1)}, bf16[192,896]{1,0:T(8,128)(2,1)S(1)}, u32[]{:S(2)}, u32[]{:S(2)}) collective-permute-start(bf16[192,896]{1,0:T(8,128)(2,1)} %get-tuple-element.31), channel_id=1, source_target_pairs={{0,8},{4,12},{8,0},{12,4},{1,9},{5,13},{9,1},{13,5},{2,10},{6,14},... | collective-permute-start | bytes 1032200 | tf_op jit(solution)/shard_map/ppermute | solution.py:139
  10.5 0.2 collective-permute-start.2
  10.7 0.1 copy.11.dest
  11.5 0.1 shard_map.101.code
  11.6 1.1 fusion
  12.7 0.0 copy-start.5
  12.7 0.0 copy-start
  12.7 2.9 %collective-permute-done.3 = bf16[2,256,384]{2,1,0:T(8,128)(2,1)S(1)} collective-permute-done((bf16[2,256,384]{2,1,0:T(8,128)(2,1)}, bf16[2,256,384]{2,1,0:T(8,128)(2,1)S(1)}, u32[]{:S(2)}, u32[]{:S(2)}) %collective-permute-start.3) | collective-permute-done | bytes 393248 | tf_op jit(solution)/shard_map/ppermute | solution.py:139
  15.7 0.1 pad_maximum_fusion
  15.8 12.6 %collective-permute-done.1.second = bf16[192,896]{1,0:T(8,128)(2,1)S(1)} collective-permute-done((bf16[192,896]{1,0:T(8,128)(2,1)}, bf16[192,896]{1,0:T(8,128)(2,1)S(1)}, u32[]{:S(2)}, u32[]{:S(2)}) %collective-permute-start.1) | collective-permute-done | bytes 344096 | tf_op jit(solution)/shard_map/ppermute | solution.py:139
  28.4 8.8 %collective-permute-done.2.third = bf16[192,896]{1,0:T(8,128)(2,1)S(1)} collective-permute-done((bf16[192,896]{1,0:T(8,128)(2,1)}, bf16[192,896]{1,0:T(8,128)(2,1)S(1)}, u32[]{:S(2)}, u32[]{:S(2)}) %collective-permute-start.2) | collective-permute-done | bytes 344096 | tf_op jit(solution)/shard_map/ppermute | solution.py:139
  37.2 0.1 shard_map.102
  37.2 0.6 collective-permute-start.4
  37.8 0.7 collective-permute-start.7
  38.5 1.6 %collective-permute-start.6 = (bf16[2,192,512]{2,1,0:T(8,128)(2,1)S(1)}, bf16[2,192,512]{2,1,0:T(8,128)(2,1)S(1)}, u32[]{:S(2)}, u32[]{:S(2)}) collective-permute-start(bf16[2,192,512]{2,1,0:T(8,128)(2,1)S(1)} %get-tuple-element.40.columns), channel_id=1, source_target_pairs={{0,16},{16,0},{1,17},{17,1},{2,18},{18,2},{3,19},{19,3},{4,20},{20... | collective-permute-start | bytes 1179656 | tf_op jit(solution)/shard_map/ppermute | solution.py:139
  40.1 3.6 %collective-permute-start.5 = (bf16[3,192,384]{2,1,0:T(8,128)(2,1)S(1)}, bf16[3,192,384]{2,1,0:T(8,128)(2,1)S(1)}, u32[]{:S(2)}, u32[]{:S(2)}) collective-permute-start(bf16[3,192,384]{2,1,0:T(8,128)(2,1)S(1)} %get-tuple-element.39.own), channel_id=1, source_target_pairs={{0,1},{1,0},{2,3},{3,2},{4,5},{5,4},{6,7},{7,6},{8,9},{9,8},{10,11... | collective-permute-start | bytes 1327112 | tf_op jit(solution)/shard_map/ppermute | solution.py:139
  43.7 3.8 %collective-permute-done.6.others = bf16[2,192,512]{2,1,0:T(8,128)(2,1)S(1)} collective-permute-done((bf16[2,192,512]{2,1,0:T(8,128)(2,1)S(1)}, bf16[2,192,512]{2,1,0:T(8,128)(2,1)S(1)}, u32[]{:S(2)}, u32[]{:S(2)}) %collective-permute-start.6) | collective-permute-done | bytes 393248 | tf_op jit(solution)/shard_map/ppermute | solution.py:139
  47.6 0.4 collective-permute-done.4.far
  48.0 3.8 %collective-permute-start.8 = (bf16[3,192,384]{2,1,0:T(8,128)(2,1)S(1)}, bf16[3,192,384]{2,1,0:T(8,128)(2,1)S(1)}, u32[]{:S(2)}, u32[]{:S(2)}) collective-permute-start(bf16[3,192,384]{2,1,0:T(8,128)(2,1)S(1)} %collective-permute-done.4.far), channel_id=1, source_target_pairs={{0,1},{1,0},{2,3},{3,2},{4,5},{5,4},{6,7},{7,6},{8,9},{9,8},{10,11... | collective-permute-start | bytes 1327112 | tf_op jit(solution)/shard_map/ppermute | solution.py:139
  51.8 1.4 %collective-permute-done.8.near_far = bf16[3,192,384]{2,1,0:T(8,128)(2,1)S(1)} collective-permute-done((bf16[3,192,384]{2,1,0:T(8,128)(2,1)S(1)}, bf16[3,192,384]{2,1,0:T(8,128)(2,1)S(1)}, u32[]{:S(2)}, u32[]{:S(2)}) %collective-permute-start.8) | collective-permute-done | bytes 442400 | tf_op jit(solution)/shard_map/ppermute | solution.py:139
  53.2 2.7 %shard_map.103.own = bf16[768,256]{1,0:T(8,128)(2,1)S(1)} custom-call(f32[1,1536]{1,0:T(1,128)S(1)} %broadcast_in_dim.7.gain, bf16[192,1536]{1,0:T(8,128)(2,1)S(1)} %copy-done, bf16[3,192,384]{2,1,0:T(8,128)(2,1)S(1)} %get-tuple-element.39.own, bf16[3,192,384]{2,1,0:T(8,128)(2,1)S(1)} %collective-permute-done.4.far, ...), custom_call_target="tpu_custom_call" | custom-call | tf_op jit(solution)/shard_map/pallas_call | solution.py:151
  56.0 0.0 copy-start.6
  56.0 0.0 copy-start.1
  56.0 0.0 copy-start.4
  56.0 2.6 %collective-permute-start.9 = (bf16[768,256]{1,0:T(8,128)(2,1)S(1)}, bf16[768,256]{1,0:T(8,128)(2,1)S(1)}, u32[]{:S(2)}, u32[]{:S(2)}) collective-permute-start(bf16[768,256]{1,0:T(8,128)(2,1)S(1)} %shard_map.103.own), channel_id=1, source_target_pairs={{0,2},{1,3},{2,0},{3,1},{4,6},{5,7},{6,4},{7,5},{8,10},{9,11},{10,... | collective-permute-start | bytes 1179656 | tf_op jit(solution)/shard_map/ppermute | solution.py:139
  58.6 0.8 collective-permute-start.12
  59.4 8.6 %collective-permute-done.9.far = bf16[768,256]{1,0:T(8,128)(2,1)S(1)} collective-permute-done((bf16[768,256]{1,0:T(8,128)(2,1)S(1)}, bf16[768,256]{1,0:T(8,128)(2,1)S(1)}, u32[]{:S(2)}, u32[]{:S(2)}) %collective-permute-start.9) | collective-permute-done | bytes 393248 | tf_op jit(solution)/shard_map/ppermute | solution.py:139
  68.1 1.7 %collective-permute-done.11.near_far = bf16[768,256]{1,0:T(8,128)(2,1)S(1)} collective-permute-done((bf16[768,256]{1,0:T(8,128)(2,1)S(1)}, bf16[768,256]{1,0:T(8,128)(2,1)S(1)}, u32[]{:S(2)}, u32[]{:S(2)}) %collective-permute-start.11) | collective-permute-done | bytes 393248 | tf_op jit(solution)/shard_map/ppermute | solution.py:139
  69.8 1.0 shard_map.104
  70.8 1.4 %collective-permute-start.13 = (bf16[192,384]{1,0:T(8,128)(2,1)S(1)}, bf16[192,384]{1,0:T(8,128)(2,1)S(1)}, u32[]{:S(2)}, u32[]{:S(2)}) collective-permute-start(bf16[192,384]{1,0:T(8,128)(2,1)S(1)} %get-tuple-element.48), channel_id=1, source_target_pairs={{0,9},{1,8},{2,11},{3,10},{4,13},{5,12},{6,15},{7,14},{8,1},{9,0},... | collective-permute-start | bytes 442376 | tf_op jit(solution)/shard_map/ppermute | solution.py:457
  72.1 3.6 %collective-permute-start.14 = (bf16[192,384]{1,0:T(8,128)(2,1)S(1)}, bf16[192,384]{1,0:T(8,128)(2,1)S(1)}, u32[]{:S(2)}, u32[]{:S(2)}) collective-permute-start(bf16[192,384]{1,0:T(8,128)(2,1)S(1)} %get-tuple-element.49), channel_id=1, source_target_pairs={{0,14},{1,15},{2,13},{3,12},{4,11},{5,10},{6,8},{7,9},{8,6},{9,7},... | collective-permute-start | bytes 442376 | tf_op jit(solution)/shard_map/ppermute | solution.py:457
  75.7 7.5 %collective-permute-done.13 = bf16[192,384]{1,0:T(8,128)(2,1)S(1)} collective-permute-done((bf16[192,384]{1,0:T(8,128)(2,1)S(1)}, bf16[192,384]{1,0:T(8,128)(2,1)S(1)}, u32[]{:S(2)}, u32[]{:S(2)}) %collective-permute-start.13) | collective-permute-done | bytes 147488 | tf_op jit(solution)/shard_map/ppermute | solution.py:457
  83.2 0.5 collective-permute-done.14
  83.7 4.0 %collective-permute-done.15 = bf16[192,384]{1,0:T(8,128)(2,1)S(1)} collective-permute-done((bf16[192,384]{1,0:T(8,128)(2,1)S(1)}, bf16[192,384]{1,0:T(8,128)(2,1)S(1)}, u32[]{:S(2)}, u32[]{:S(2)}) %collective-permute-start.15) | collective-permute-done | bytes 147488 | tf_op jit(solution)/shard_map/ppermute | solution.py:457
  87.7 0.1 add_convert_fusion.own
  87.8 0.3 collective-permute-start.16
  88.1 5.6 %collective-permute-done.16.far = bf16[192,384]{1,0:T(8,128)(2,1)S(1)} collective-permute-done((bf16[192,384]{1,0:T(8,128)(2,1)S(1)}, bf16[192,384]{1,0:T(8,128)(2,1)S(1)}, u32[]{:S(2)}, u32[]{:S(2)}) %collective-permute-start.16) | collective-permute-done | bytes 147488 | tf_op jit(solution)/shard_map/ppermute | solution.py:139
  93.8 1.3 %collective-permute-done.18.near_far = bf16[192,384]{1,0:T(8,128)(2,1)S(1)} collective-permute-done((bf16[192,384]{1,0:T(8,128)(2,1)S(1)}, bf16[192,384]{1,0:T(8,128)(2,1)S(1)}, u32[]{:S(2)}, u32[]{:S(2)}) %collective-permute-start.18) | collective-permute-done | bytes 147488 | tf_op jit(solution)/shard_map/ppermute | solution.py:139
  95.1 1.9 %shard_map.105 = (bf16[64,768]{1,0:T(8,128)(2,1)S(1)}, bf16[64,768]{1,0:T(8,128)(2,1)S(1)}, bf16[64,768]{1,0:T(8,128)(2,1)S(1)}, bf16[64,768]{1,0:T(8,128)(2,1)S(1)}) custom-call(s32[3]{0:T(128)S(1)} %copy-done.4, f32[1,1536]{1,0:T(1,128)S(1)} %broadcast_in_dim.6.gain, s32[1,192]{1,0:T(1,128)S(1)} %shard_map.101.code, bf16[576,1536]{1,0:T(8,128)(2,1)S(1)} %bitcast.3, ...), custom_call_target="tpu_custom_call" | custom-call | tf_op jit(solution)/shard_map/pallas_call | solution.py:151
  97.0 1.2 %collective-permute-start.19 = (bf16[64,768]{1,0:T(8,128)(2,1)S(1)}, bf16[64,768]{1,0:T(8,128)(2,1)S(1)}, u32[]{:S(2)}, u32[]{:S(2)}) collective-permute-start(bf16[64,768]{1,0:T(8,128)(2,1)S(1)} %get-tuple-element.52), channel_id=1, source_target_pairs={{0,4},{4,0},{8,12},{12,8},{1,5},{5,1},{9,13},{13,9},{2,6},{6,2},{1... | collective-permute-start | bytes 294920 | tf_op jit(solution)/shard_map/ppermute | solution.py:139
  98.2 1.4 %collective-permute-start.20 = (bf16[64,768]{1,0:T(8,128)(2,1)S(1)}, bf16[64,768]{1,0:T(8,128)(2,1)S(1)}, u32[]{:S(2)}, u32[]{:S(2)}) collective-permute-start(bf16[64,768]{1,0:T(8,128)(2,1)S(1)} %get-tuple-element.53), channel_id=1, source_target_pairs={{0,8},{4,12},{8,0},{12,4},{1,9},{5,13},{9,1},{13,5},{2,10},{6,14},... | collective-permute-start | bytes 294920 | tf_op jit(solution)/shard_map/ppermute | solution.py:139
  99.6 1.9 %collective-permute-start.21 = (bf16[64,768]{1,0:T(8,128)(2,1)S(1)}, bf16[64,768]{1,0:T(8,128)(2,1)S(1)}, u32[]{:S(2)}, u32[]{:S(2)}) collective-permute-start(bf16[64,768]{1,0:T(8,128)(2,1)S(1)} %get-tuple-element.54), channel_id=1, source_target_pairs={{0,12},{4,8},{8,4},{12,0},{1,13},{5,9},{9,5},{13,1},{2,14},{6,10},... | collective-permute-start | bytes 294920 | tf_op jit(solution)/shard_map/ppermute | solution.py:139
  101.5 1.9 %collective-permute-done.19.refs_1_ = bf16[64,768]{1,0:T(8,128)(2,1)S(1)} collective-permute-done((bf16[64,768]{1,0:T(8,128)(2,1)S(1)}, bf16[64,768]{1,0:T(8,128)(2,1)S(1)}, u32[]{:S(2)}, u32[]{:S(2)}) %collective-permute-start.19) | collective-permute-done | bytes 98336 | tf_op jit(solution)/shard_map/ppermute | solution.py:139
  103.3 5.4 %collective-permute-done.20.refs_2_ = bf16[64,768]{1,0:T(8,128)(2,1)S(1)} collective-permute-done((bf16[64,768]{1,0:T(8,128)(2,1)S(1)}, bf16[64,768]{1,0:T(8,128)(2,1)S(1)}, u32[]{:S(2)}, u32[]{:S(2)}) %collective-permute-start.20) | collective-permute-done | bytes 98336 | tf_op jit(solution)/shard_map/ppermute | solution.py:139
  108.7 2.1 %shard_map.106 = bf16[192,256]{1,0:T(8,128)(2,1)} custom-call(s32[3]{0:T(128)S(1)} %copy-done.4, bf16[64,768]{1,0:T(8,128)(2,1)S(1)} %get-tuple-element.51.refs_0_, bf16[64,768]{1,0:T(8,128)(2,1)S(1)} %collective-permute-done.19.refs_1_, bf16[64,768]{1,0:T(8,128)(2,1)S(1)} %collective-permute-done.20.refs_2_, bf16[64,768]{1,0:T(8,128)(2,1)S(1)} %collective-permute-done.21.refs_3_), custom_call_target="tpu_custom_call" | custom-call | tf_op jit(solution)/shard_map/pallas_call | solution.py:151
  (24 shorter events, 0.1 us)
Async XLA Ops:
  0.0 10.7 %copy-start.3 = (s32[192,1]{0,1:T(1,128)S(1)}, s32[192,1]{0,1:T(1,128)}, u32[]{:S(2)}) copy-start(s32[192,1]{0,1:T(1,128)} %param.12) | copy-start | bytes 2308
  3.3 12.3 %collective-permute-start.3 = (bf16[2,256,384]{2,1,0:T(8,128)(2,1)}, bf16[2,256,384]{2,1,0:T(8,128)(2,1)S(1)}, u32[]{:S(2)}, u32[]{:S(2)}) collective-permute-start(bf16[2,256,384]{2,1,0:T(8,128)(2,1)} %get-tuple-element.34), channel_id=1, source_target_pairs={{0,2},{1,3},{2,0},{3,1},{4,6},{5,7},{6,4},{7,5},{8,10},{9,11},{10,... | collective-permute-start | bytes 1179656 | tf_op jit(solution)/shard_map/ppermute | solution.py:139
  6.3 30.8 %collective-permute-start = (bf16[192,1408]{1,0:T(8,128)(2,1)}, bf16[192,1408]{1,0:T(8,128)(2,1)S(1)}, u32[]{:S(2)}, u32[]{:S(2)}) collective-permute-start(bf16[192,1408]{1,0:T(8,128)(2,1)} %get-tuple-element.30), channel_id=1, source_target_pairs={{0,4},{4,0},{8,12},{12,8},{1,5},{5,1},{9,13},{13,9},{2,6},{6,2},{1... | collective-permute-start | bytes 1622024 | tf_op jit(solution)/shard_map/ppermute | solution.py:139
  7.9 20.5 %collective-permute-start.1 = (bf16[192,896]{1,0:T(8,128)(2,1)}, bf16[192,896]{1,0:T(8,128)(2,1)S(1)}, u32[]{:S(2)}, u32[]{:S(2)}) collective-permute-start(bf16[192,896]{1,0:T(8,128)(2,1)} %get-tuple-element.31), channel_id=1, source_target_pairs={{0,8},{4,12},{8,0},{12,4},{1,9},{5,13},{9,1},{13,5},{2,10},{6,14},... | collective-permute-start | bytes 1032200 | tf_op jit(solution)/shard_map/ppermute | solution.py:139
  10.5 26.7 %collective-permute-start.2 = (bf16[192,896]{1,0:T(8,128)(2,1)}, bf16[192,896]{1,0:T(8,128)(2,1)S(1)}, u32[]{:S(2)}, u32[]{:S(2)}) collective-permute-start(bf16[192,896]{1,0:T(8,128)(2,1)} %get-tuple-element.32), channel_id=1, source_target_pairs={{0,12},{4,8},{8,4},{12,0},{1,13},{5,9},{9,5},{13,1},{2,14},{6,10},... | collective-permute-start | bytes 1032200 | tf_op jit(solution)/shard_map/ppermute | solution.py:139
  12.7 39.1 %copy-start.5 = (f32[1536]{0:T(1024)S(1)}, f32[1536]{0:T(1024)}, u32[]{:S(2)}) copy-start(f32[1536]{0:T(1024)} %param.13) | copy-start | bytes 18436
  12.7 40.5 %copy-start = (bf16[192,1536]{1,0:T(8,128)(2,1)S(1)}, bf16[192,1536]{1,0:T(8,128)(2,1)}, u32[]{:S(2)}) copy-start(bf16[192,1536]{1,0:T(8,128)(2,1)} %tiles.3) | copy-start | bytes 1769476
  12.7 40.5 %copy-start.2 = (bf16[384,512]{1,0:T(8,128)(2,1)S(1)}, bf16[384,512]{1,0:T(8,128)(2,1)}, u32[]{:S(2)}) copy-start(bf16[384,512]{1,0:T(8,128)(2,1)} %get-tuple-element.45.kept) | copy-start | bytes 1179652
  37.2 10.7 %collective-permute-start.4 = (bf16[3,192,384]{2,1,0:T(8,128)(2,1)S(1)}, bf16[3,192,384]{2,1,0:T(8,128)(2,1)S(1)}, u32[]{:S(2)}, u32[]{:S(2)}) collective-permute-start(bf16[3,192,384]{2,1,0:T(8,128)(2,1)S(1)} %get-tuple-element.39.own), channel_id=1, source_target_pairs={{0,2},{1,3},{2,0},{3,1},{4,6},{5,7},{6,4},{7,5},{8,10},{9,11},{10,... | collective-permute-start | bytes 1327112 | tf_op jit(solution)/shard_map/ppermute | solution.py:139
  37.8 5.9 %collective-permute-start.7 = (bf16[2,256,384]{2,1,0:T(8,128)(2,1)S(1)}, bf16[2,256,384]{2,1,0:T(8,128)(2,1)S(1)}, u32[]{:S(2)}, u32[]{:S(2)}) collective-permute-start(bf16[2,256,384]{2,1,0:T(8,128)(2,1)S(1)} %get-tuple-element.43), channel_id=1, source_target_pairs={{0,0},{1,9},{2,14},{3,7},{4,4},{5,13},{6,2},{7,11},{8,8},{9,1},{10... | collective-permute-start | bytes 1179656 | tf_op jit(solution)/shard_map/ppermute | solution.py:432
  38.5 9.1 %collective-permute-start.6 = (bf16[2,192,512]{2,1,0:T(8,128)(2,1)S(1)}, bf16[2,192,512]{2,1,0:T(8,128)(2,1)S(1)}, u32[]{:S(2)}, u32[]{:S(2)}) collective-permute-start(bf16[2,192,512]{2,1,0:T(8,128)(2,1)S(1)} %get-tuple-element.40.columns), channel_id=1, source_target_pairs={{0,16},{16,0},{1,17},{17,1},{2,18},{18,2},{3,19},{19,3},{4,20},{20... | collective-permute-start | bytes 1179656 | tf_op jit(solution)/shard_map/ppermute | solution.py:139
  40.1 11.7 %collective-permute-start.5 = (bf16[3,192,384]{2,1,0:T(8,128)(2,1)S(1)}, bf16[3,192,384]{2,1,0:T(8,128)(2,1)S(1)}, u32[]{:S(2)}, u32[]{:S(2)}) collective-permute-start(bf16[3,192,384]{2,1,0:T(8,128)(2,1)S(1)} %get-tuple-element.39.own), channel_id=1, source_target_pairs={{0,1},{1,0},{2,3},{3,2},{4,5},{5,4},{6,7},{7,6},{8,9},{9,8},{10,11... | collective-permute-start | bytes 1327112 | tf_op jit(solution)/shard_map/ppermute | solution.py:139
  48.0 5.3 %collective-permute-start.8 = (bf16[3,192,384]{2,1,0:T(8,128)(2,1)S(1)}, bf16[3,192,384]{2,1,0:T(8,128)(2,1)S(1)}, u32[]{:S(2)}, u32[]{:S(2)}) collective-permute-start(bf16[3,192,384]{2,1,0:T(8,128)(2,1)S(1)} %collective-permute-done.4.far), channel_id=1, source_target_pairs={{0,1},{1,0},{2,3},{3,2},{4,5},{5,4},{6,7},{7,6},{8,9},{9,8},{10,11... | collective-permute-start | bytes 1327112 | tf_op jit(solution)/shard_map/ppermute | solution.py:139
  56.0 37.8 %copy-start.6 = (f32[1536]{0:T(1024)S(1)}, f32[1536]{0:T(1024)}, u32[]{:S(2)}) copy-start(f32[1536]{0:T(1024)} %param.17) | copy-start | bytes 18436
  56.0 39.1 %copy-start.1 = (bf16[1536,576]{0,1:T(8,128)(2,1)S(1)}, bf16[1536,576]{0,1:T(8,128)(2,1)}, u32[]{:S(2)}) copy-start(bf16[1536,576]{0,1:T(8,128)(2,1)} %param.18) | copy-start | bytes 5308420
  56.0 39.1 %copy-start.4 = (s32[3]{0:T(128)S(1)}, s32[3]{0:T(128)}, u32[]{:S(2)}) copy-start(s32[3]{0:T(128)} %offsets.3) | copy-start | bytes 40
  56.0 12.1 %collective-permute-start.9 = (bf16[768,256]{1,0:T(8,128)(2,1)S(1)}, bf16[768,256]{1,0:T(8,128)(2,1)S(1)}, u32[]{:S(2)}, u32[]{:S(2)}) collective-permute-start(bf16[768,256]{1,0:T(8,128)(2,1)S(1)} %shard_map.103.own), channel_id=1, source_target_pairs={{0,2},{1,3},{2,0},{3,1},{4,6},{5,7},{6,4},{7,5},{8,10},{9,11},{10,... | collective-permute-start | bytes 1179656 | tf_op jit(solution)/shard_map/ppermute | solution.py:139
  58.6 9.4 %collective-permute-start.12 = (bf16[2,256,384]{2,1,0:T(8,128)(2,1)S(1)}, bf16[2,256,384]{2,1,0:T(8,128)(2,1)S(1)}, u32[]{:S(2)}, u32[]{:S(2)}) collective-permute-start(bf16[2,256,384]{2,1,0:T(8,128)(2,1)S(1)} %get-tuple-element.46), channel_id=1, source_target_pairs={{0,9},{1,0},{2,7},{3,14},{4,13},{5,4},{6,11},{7,2},{8,1},{9,8},{10... | collective-permute-start | bytes 1179656 | tf_op jit(solution)/shard_map/ppermute | solution.py:432
  59.4 8.7 %collective-permute-start.10 = (bf16[768,256]{1,0:T(8,128)(2,1)S(1)}, bf16[768,256]{1,0:T(8,128)(2,1)S(1)}, u32[]{:S(2)}, u32[]{:S(2)}) collective-permute-start(bf16[768,256]{1,0:T(8,128)(2,1)S(1)} %shard_map.103.own), channel_id=1, source_target_pairs={{0,1},{1,0},{2,3},{3,2},{4,5},{5,4},{6,7},{7,6},{8,9},{9,8},{10,11... | collective-permute-start | bytes 1179656 | tf_op jit(solution)/shard_map/ppermute | solution.py:139
  68.1 1.7 %collective-permute-start.11 = (bf16[768,256]{1,0:T(8,128)(2,1)S(1)}, bf16[768,256]{1,0:T(8,128)(2,1)S(1)}, u32[]{:S(2)}, u32[]{:S(2)}) collective-permute-start(bf16[768,256]{1,0:T(8,128)(2,1)S(1)} %collective-permute-done.9.far), channel_id=1, source_target_pairs={{0,1},{1,0},{2,3},{3,2},{4,5},{5,4},{6,7},{7,6},{8,9},{9,8},{10,11... | collective-permute-start | bytes 1179656 | tf_op jit(solution)/shard_map/ppermute | solution.py:139
  70.8 12.4 %collective-permute-start.13 = (bf16[192,384]{1,0:T(8,128)(2,1)S(1)}, bf16[192,384]{1,0:T(8,128)(2,1)S(1)}, u32[]{:S(2)}, u32[]{:S(2)}) collective-permute-start(bf16[192,384]{1,0:T(8,128)(2,1)S(1)} %get-tuple-element.48), channel_id=1, source_target_pairs={{0,9},{1,8},{2,11},{3,10},{4,13},{5,12},{6,15},{7,14},{8,1},{9,0},... | collective-permute-start | bytes 442376 | tf_op jit(solution)/shard_map/ppermute | solution.py:457
  72.1 11.6 %collective-permute-start.14 = (bf16[192,384]{1,0:T(8,128)(2,1)S(1)}, bf16[192,384]{1,0:T(8,128)(2,1)S(1)}, u32[]{:S(2)}, u32[]{:S(2)}) collective-permute-start(bf16[192,384]{1,0:T(8,128)(2,1)S(1)} %get-tuple-element.49), channel_id=1, source_target_pairs={{0,14},{1,15},{2,13},{3,12},{4,11},{5,10},{6,8},{7,9},{8,6},{9,7},... | collective-permute-start | bytes 442376 | tf_op jit(solution)/shard_map/ppermute | solution.py:457
  75.7 12.0 %collective-permute-start.15 = (bf16[192,384]{1,0:T(8,128)(2,1)S(1)}, bf16[192,384]{1,0:T(8,128)(2,1)S(1)}, u32[]{:S(2)}, u32[]{:S(2)}) collective-permute-start(bf16[192,384]{1,0:T(8,128)(2,1)S(1)} %get-tuple-element.50), channel_id=1, source_target_pairs={{0,7},{1,6},{2,4},{3,5},{4,2},{5,3},{6,1},{7,0},{8,15},{9,14},{10,... | collective-permute-start | bytes 442376 | tf_op jit(solution)/shard_map/ppermute | solution.py:457
  87.8 5.9 %collective-permute-start.16 = (bf16[192,384]{1,0:T(8,128)(2,1)S(1)}, bf16[192,384]{1,0:T(8,128)(2,1)S(1)}, u32[]{:S(2)}, u32[]{:S(2)}) collective-permute-start(bf16[192,384]{1,0:T(8,128)(2,1)S(1)} %add_convert_fusion.own), channel_id=1, source_target_pairs={{0,2},{1,3},{2,0},{3,1},{4,6},{5,7},{6,4},{7,5},{8,10},{9,11},{10,... | collective-permute-start | bytes 442376 | tf_op jit(solution)/shard_map/ppermute | solution.py:139
  88.1 5.6 %collective-permute-start.17 = (bf16[192,384]{1,0:T(8,128)(2,1)S(1)}, bf16[192,384]{1,0:T(8,128)(2,1)S(1)}, u32[]{:S(2)}, u32[]{:S(2)}) collective-permute-start(bf16[192,384]{1,0:T(8,128)(2,1)S(1)} %add_convert_fusion.own), channel_id=1, source_target_pairs={{0,1},{1,0},{2,3},{3,2},{4,5},{5,4},{6,7},{7,6},{8,9},{9,8},{10,11... | collective-permute-start | bytes 442376 | tf_op jit(solution)/shard_map/ppermute | solution.py:139
  93.8 1.4 %collective-permute-start.18 = (bf16[192,384]{1,0:T(8,128)(2,1)S(1)}, bf16[192,384]{1,0:T(8,128)(2,1)S(1)}, u32[]{:S(2)}, u32[]{:S(2)}) collective-permute-start(bf16[192,384]{1,0:T(8,128)(2,1)S(1)} %collective-permute-done.16.far), channel_id=1, source_target_pairs={{0,1},{1,0},{2,3},{3,2},{4,5},{5,4},{6,7},{7,6},{8,9},{9,8},{10,11... | collective-permute-start | bytes 442376 | tf_op jit(solution)/shard_map/ppermute | solution.py:139
  97.0 6.3 %collective-permute-start.19 = (bf16[64,768]{1,0:T(8,128)(2,1)S(1)}, bf16[64,768]{1,0:T(8,128)(2,1)S(1)}, u32[]{:S(2)}, u32[]{:S(2)}) collective-permute-start(bf16[64,768]{1,0:T(8,128)(2,1)S(1)} %get-tuple-element.52), channel_id=1, source_target_pairs={{0,4},{4,0},{8,12},{12,8},{1,5},{5,1},{9,13},{13,9},{2,6},{6,2},{1... | collective-permute-start | bytes 294920 | tf_op jit(solution)/shard_map/ppermute | solution.py:139
  98.2 10.5 %collective-permute-start.20 = (bf16[64,768]{1,0:T(8,128)(2,1)S(1)}, bf16[64,768]{1,0:T(8,128)(2,1)S(1)}, u32[]{:S(2)}, u32[]{:S(2)}) collective-permute-start(bf16[64,768]{1,0:T(8,128)(2,1)S(1)} %get-tuple-element.53), channel_id=1, source_target_pairs={{0,8},{4,12},{8,0},{12,4},{1,9},{5,13},{9,1},{13,5},{2,10},{6,14},... | collective-permute-start | bytes 294920 | tf_op jit(solution)/shard_map/ppermute | solution.py:139
  99.6 9.1 %collective-permute-start.21 = (bf16[64,768]{1,0:T(8,128)(2,1)S(1)}, bf16[64,768]{1,0:T(8,128)(2,1)S(1)}, u32[]{:S(2)}, u32[]{:S(2)}) collective-permute-start(bf16[64,768]{1,0:T(8,128)(2,1)S(1)} %get-tuple-element.54), channel_id=1, source_target_pairs={{0,12},{4,8},{8,4},{12,0},{1,13},{5,9},{9,5},{13,1},{2,14},{6,10},... | collective-permute-start | bytes 294920 | tf_op jit(solution)/shard_map/ppermute | solution.py:139

commit v5 on v4

--- a/solution.py
+++ b/solution.py
@@ -176,12 +176,7 @@
     return jnp.where(mp < 2, seq ^ (2 * mp), step)
 
 
-def cut_body(
-    count, tiles, w_gate, w_up, w_down, next_out, second_out, third_out, kept, near, far, sems
-):
-    seq, mp, group = place()
-    depth, units = w_gate.shape[0], w_gate.shape[1] // count
-    half, features = depth // 2, near.shape[2]
+def copier(sems, group):
     copies = []
 
     def copy(source, target, other=None):
@@ -194,32 +189,58 @@
             pl.when(group != 0)(second.start)
         copies.append(started)
 
-    for d, target in ((1, next_out), (2, second_out), (3, third_out)):
-        copy(tiles.at[:, at(mp, features)], target.at[:, pl.ds(0, features)])
-        for i in range(2):
-            span = pl.ds(i * half, half), at(seq ^ d, units)
-            if d == 1:
-                for k, weight in enumerate((w_gate, w_up)):
-                    columns = pl.ds(features + (2 * i + k) * units, units)
-                    copy(weight.at[span], target.at[:, columns])
-            else:
-                columns = pl.ds(features + i * units, units)
-                copy(w_gate.at[span], target.at[:, columns], w_up.at[span])
+    return copies, copy
+
+
+def cut_first_body(count, tiles, w_gate, w_up, first_out, second_out, quarter, sems):
+    seq, mp, group = place()
+    copies, copy = copier(sems, group)
+    half, units = w_gate.shape[0] // 2, w_gate.shape[1] // count
+    features = quarter.shape[1]
+    own_columns = tiles.at[:, at(mp, features)]
+    for i in range(2):
+        span = pl.ds(i * half, half), at(seq ^ 2, units)
+        columns = pl.ds(features + i * units, units)
+        copy(w_gate.at[span], second_out.at[:, columns], w_up.at[span])
+        span = pl.ds(i * half, half), at(seq ^ 1, units)
+        for k, weight in enumerate((w_gate, w_up)):
+            columns = pl.ds(features + (2 * i + k) * units, units)
+            copy(weight.at[span], first_out.at[:, columns])
+    for target in (second_out.at[:, pl.ds(0, features)], first_out.at[:, pl.ds(0, features)]):
+        copy(own_columns, target)
+    copy(own_columns, quarter)
+    for started in copies:
+        started.wait()
+
+
+def cut_second_body(count, w_gate, w_up, w_down, third_out, kept, near, far, sems):
+    seq, mp, group = place()
+    copies, copy = copier(sems, group)
+    half, units = w_gate.shape[0] // 2, w_gate.shape[1] // count
+    part = units // 2
+    for j, target in ((2, far), (0, near)):
+        rows = at(column_user(seq, mp ^ j) * 2 + group, part)
+        copy(w_down.at[rows, :], target.at[pl.ds(0, part), :])
+        rows = at(column_user(seq, mp ^ (j + 1)), units)
+        copy(w_down.at[rows, :], target.at[pl.ds(part, units), :])
+    for i in range(2):
+        span = pl.ds(i * half, half), at(seq ^ 3, units)
+        copy(w_gate.at[span], third_out.at[:, pl.ds(i * units, units)], w_up.at[span])
     for i, weight in enumerate((w_gate, w_up)):
         copy(weight.at[:, at(seq, units)], kept.at[:, pl.ds(i * units, units)])
-    for j in range(4):
-        rows = at(column_user(seq, mp ^ j), units)
-        copy(w_down.at[rows, :], (far if j >= 2 else near).at[j % 2])
     for started in copies:
         started.wait()
 
 
-def restack_body(first, second, third, stacked, columns):
+def restack_body(first, second, third, near, far, stacked, columns, even, odd):
     features = stacked.shape[2]
-    for i, package in enumerate((first, second, third)):
-        stacked[i] = package[:, :features]
-    columns[0] = second[:, features:]
-    columns[1] = third[:, features:]
+    stacked[0] = first[:, :features]
+    stacked[1] = second[:, :features]
+    stacked[2] = third[...]
+    columns[...] = second[:, features:]
+    for i, rows in enumerate((near, far)):
+        even[i] = rows[: even.shape[1], :]
+        odd[i] = rows[even.shape[1] :, :]
 
 
 def code_body(capacity, counts, dest, dest_row, code):
@@ -233,20 +254,19 @@
 
 
 def hidden_body(
-    count, gain, tiles, own, far, near, near_far, kept, next_in, columns, others, out, *scratch
+    count, gain, tiles, own, far, near, near_far, kept, next_in, *refs
 ):
-    normed, weights, next_weights = scratch
+    halves, (out, normed, weights, next_weights) = refs[:4], refs[4:]
     seq, mp, group = place()
     depth, units = weights.shape[1:]
     half = depth // 2
-    rows, features = tiles.shape[0], own.shape[2]
+    rows = tiles.shape[0]
+    for i, piece in enumerate(halves):
+        weights[i, :half, :] = piece[:, :units]
+        weights[i, half:, :] = piece[:, units:]
     for i in range(2):
-        span = pl.ds(i * half, half)
-        for k in range(2):
-            weights[2 * k, span, :] = columns[k, :, i * units : (i + 1) * units]
-            weights[2 * k + 1, span, :] = others[k, :, i * units : (i + 1) * units]
-        start = features + 2 * i * units
-        next_weights[span, :] = next_in[:, start : start + 2 * units]
+        start = own.shape[2] + 2 * i * units
+        next_weights[i * half : (i + 1) * half, :] = next_in[:, start : start + 2 * units]
 
     def gated(d):
         if d == 0:
@@ -271,14 +291,19 @@
         out[pl.ds(d * rows, rows), :] = gated(d)
 
 
-def down_body(own, far, near, near_far, even, odd, *outs):
+def down_body(own, far, near, near_far, even, even_other, odd, *outs):
+    _, _, group = place()
     rows = outs[0].shape[0]
+    weights = [None, odd[0], None, odd[1]]
+    for j in range(2):
+        mine, other = even[j], even_other[j]
+        low, high = jnp.where(group == 0, mine, other), jnp.where(group == 0, other, mine)
+        weights[2 * j] = jnp.concatenate([low, high], axis=0)
     for i, out in enumerate(outs):
         total = 0.0
-        pairs = ((own, even[0]), (near, odd[0]), (far, even[1]), (near_far, odd[1]))
-        for piece, weights in pairs:
+        for j, piece in enumerate((own, near, far, near_far)):
             total += jnp.dot(
-                piece[pl.ds(i * rows, rows), :], weights, preferred_element_type=jnp.float32
+                piece[pl.ds(i * rows, rows), :], weights[j], preferred_element_type=jnp.float32
             )
         out[...] = total.astype(out.dtype)
 
@@ -385,19 +410,29 @@
     bf16 = jnp.bfloat16
     vmem, smem = pltpu.VMEM, pltpu.SMEM
 
-    *packages, kept, down_near, down_far = call(
-        functools.partial(cut_body, count),
+    first_out, second_out, quarter = call(
+        functools.partial(cut_first_body, count),
         [
             ((tile_rows, features + 4 * units), bf16),
             ((tile_rows, features + 2 * units), bf16),
-            ((tile_rows, features + 2 * units), bf16),
+            ((tile_rows, features), bf16),
+        ],
+        (tiles, w_gate, w_up),
+        spaces=[pltpu.HBM] * 3,
+        copies=9,
+        megabytes=57,
+    )
+    third_out, kept, down_near, down_far = call(
+        functools.partial(cut_second_body, count),
+        [
+            ((tile_rows, 2 * units), bf16),
             ((depth, 2 * units), bf16),
-            ((2, units, features), bf16),
-            ((2, units, features), bf16),
+            ((3 * units // 2, features), bf16),
+            ((3 * units // 2, features), bf16),
         ],
-        (tiles, w_gate, w_up, w_down),
-        spaces=[pltpu.HBM] * 4,
-        copies=17,
+        (w_gate, w_up, w_down),
+        spaces=[pltpu.HBM] * 3,
+        copies=8,
         megabytes=57,
     )
     code = call(
@@ -407,21 +442,32 @@
         spaces=[smem, vmem, vmem],
     )[0]
 
-    packages = [swap(packages[d - 1], "seq", d) for d in range(1, count)]
+    arrived = swap(first_out, "seq", 1), swap(second_out, "seq", 2), swap(quarter, "seq", 3)
     from_far = swap(down_far, "mp", 2)
-    down_send = [jnp.stack([down_near[j], from_far[j]]) for j in range(2)]
-    packages, down_send, code = lax.optimization_barrier((packages, down_send, code))
-    own, columns = call(
+    arrived, from_far, code = lax.optimization_barrier((arrived, from_far, code))
+    own, columns, *down_send = call(
         restack_body,
         [
             ((count - 1, tile_rows, features), bf16),
-            ((count - 2, tile_rows, 2 * units), bf16),
+            ((tile_rows, 2 * units), bf16),
+            ((2, units // 2, features), bf16),
+            ((2, units, features), bf16),
         ],
-        packages,
-    )
-    others = swap(columns, "groups", 1)
-    down_send, _ = lax.optimization_barrier((down_send, own))
-    down_in = []
+        (*arrived, down_near, from_far),
+    )
+    third_out, _ = lax.optimization_barrier((third_out, own))
+    third, others, far, near = lax.optimization_barrier(
+        (
+            swap(third_out, "seq", 3),
+            swap(columns, "groups", 1),
+            swap(own, "mp", 2),
+            swap(own, "mp", 1),
+        )
+    )
+    halves = columns, others, third, swap(third, "groups", 1)
+    spread = far, near, swap(far, "mp", 1)
+    down_send, _ = lax.optimization_barrier((down_send, far))
+    parts = []
     for j in range(2):
         perm = []
         for s in range(count):
@@ -429,22 +475,24 @@
                 k = m ^ j
                 user = (s ^ 2 * k) if k < 2 else (s + 2 * k - 5) % count
                 perm.append((s * mp_size + m, user * mp_size + k))
-        down_in.append(lax.ppermute(down_send[j], ("seq", "mp"), perm))
-    spread = spread_mp(own, (others, down_in[0]))
+        parts.append(lax.ppermute(down_send[j], ("seq", "mp"), perm))
+    (tiles, *spread), parts[0] = lax.optimization_barrier(((tiles, *spread), parts[0]))
     hidden = call(
         functools.partial(hidden_body, count),
         [((count * tile_rows, units), bf16)],
-        (gain_enc[None, :], tiles, own, *spread, kept, packages[0], columns, others),
+        (gain_enc[None, :], tiles, own, *spread, kept, arrived[0], *halves),
         scratch=[
             pltpu.VMEM((count, count, tile_rows, depth), bf16),
             pltpu.VMEM((4, depth, units), bf16),
             pltpu.VMEM((depth, 2 * units), bf16),
         ],
     )[0]
+    even, odd = parts
+    even_other = swap(even, "groups", 1)
     sums = call(
         down_body,
         [((tile_rows, features), kind) for kind in (jnp.float32, bf16, bf16, bf16)],
-        (hidden, *spread_mp(hidden), *down_in),
+        (hidden, *spread_mp(hidden, even_other), even, even_other, odd),
     )
     holder = [0, 2, 1, 3]
 

time: 111 us -> 110 us (level)
  waiting for transfers between devices: 66.5 us -> 64.3 us
  Pallas kernels: 11.2 us -> 12.8 us
    ppermute x17 -> x20, waiting for transfers between devices: 54.5 us -> 51.8 us  [swap(): return lax.ppermute(array, axis, [(i, i ^ distance) for i in range(size)])]
    pallas_call x7 -> x8, Pallas kernels: 11.2 us -> 12.8 us  [call(): pl.pallas_call(body, out_shape=[jax.ShapeDtypeStruct(shape, kind) for sha...]
    ppermute x17 -> x20, starting transfers between devices: 24.5 us -> 25.1 us  [swap(): return lax.ppermute(array, axis, [(i, i ^ distance) for i in range(size)])]
  transfers between devices with their start and end apart: 22 -> 25, of which waited for: 15 -> 13; matrix products, arithmetic and copies ran while one was open for 1% -> 0% of each run, Pallas kernels for 0% -> 2%
where the time goes in v5:
time: 110 us
  waiting for transfers between devices  64.3 us (58%)
  starting transfers between devices  30.9 us (28%)
  Pallas kernels  12.8 us (12%)
  local copies, waits for them, and re-layouts  1.12 us (1%)
    ppermute x20, waiting for transfers between devices, swap(): return lax.ppermute(array, axis, [(i, i ^ distance) for i in range(size)])  51.8 us
    ppermute x20, starting transfers between devices, swap(): return lax.ppermute(array, axis, [(i, i ^ distance) for i in range(size)])  25.1 us
    pallas_call x8, Pallas kernels, call(): pl.pallas_call(body, out_shape=[jax.ShapeDtypeStruct(shape, kind) for sha...  12.8 us
    ppermute x3, waiting for transfers between devices, to_owner(): return lax.ppermute(part, ('seq', 'mp'), perm)  12.5 us
    ppermute x3, starting transfers between devices, to_owner(): return lax.ppermute(part, ('seq', 'mp'), perm)  4.62 us
  transfers between devices with their start and end apart: 25, of which 13 were waited for; matrix products, arithmetic and copies ran while one was open for 0% of the time, Pallas kernels for 2%

profile of v5, /device:TPU:0, one launch (start us, length us, event | category | flops | bytes accessed | tf_op | source)
XLA Modules:
  0.0 110.0 jit_solution(8172100197320110351)
XLA Ops:
  0.0 2.4 %shard_map.100 = (bf16[192,1408]{1,0:T(8,128)(2,1)}, bf16[192,896]{1,0:T(8,128)(2,1)}, bf16[192,384]{1,0:T(8,128)(2,1)}) custom-call(bf16[192,1536]{1,0:T(8,128)(2,1)} %tiles.2, bf16[384,1024]{1,0:T(8,128)(2,1)} %w_gate.3, bf16[384,1024]{1,0:T(8,128)(2,1)} %w_up.3), custom_call_target="tpu_custom_call" | custom-call | tf_op jit(solution)/shard_map/pallas_call | solution.py:151
  2.4 3.1 %collective-permute-start = (bf16[192,1408]{1,0:T(8,128)(2,1)}, bf16[192,1408]{1,0:T(8,128)(2,1)S(1)}, u32[]{:S(2)}, u32[]{:S(2)}) collective-permute-start(bf16[192,1408]{1,0:T(8,128)(2,1)} %get-tuple-element.42), channel_id=1, source_target_pairs={{0,4},{4,0},{8,12},{12,8},{1,5},{5,1},{9,13},{13,9},{2,6},{6,2},{1... | collective-permute-start | bytes 1622024 | tf_op jit(solution)/shard_map/ppermute | solution.py:139
  5.5 2.6 %collective-permute-start.1 = (bf16[192,896]{1,0:T(8,128)(2,1)}, bf16[192,896]{1,0:T(8,128)(2,1)S(1)}, u32[]{:S(2)}, u32[]{:S(2)}) collective-permute-start(bf16[192,896]{1,0:T(8,128)(2,1)} %get-tuple-element.43), channel_id=1, source_target_pairs={{0,8},{4,12},{8,0},{12,4},{1,9},{5,13},{9,1},{13,5},{2,10},{6,14},... | collective-permute-start | bytes 1032200 | tf_op jit(solution)/shard_map/ppermute | solution.py:139
  8.1 2.5 %shard_map.101 = (bf16[192,512]{1,0:T(8,128)(2,1)}, bf16[384,512]{1,0:T(8,128)(2,1)}, bf16[384,384]{1,0:T(8,128)(2,1)}, bf16[384,384]{1,0:T(8,128)(2,1)}) custom-call(bf16[384,1024]{1,0:T(8,128)(2,1)} %w_gate.3, bf16[384,1024]{1,0:T(8,128)(2,1)} %w_up.3, bf16[1024,384]{1,0:T(8,128)(2,1)} %w_down.1), custom_call_target="tpu_custom_call" | custom-call | tf_op jit(solution)/shard_map/pallas_call | solution.py:151
  10.6 1.6 %collective-permute-start.3 = (bf16[384,384]{1,0:T(8,128)(2,1)}, bf16[384,384]{1,0:T(8,128)(2,1)S(1)}, u32[]{:S(2)}, u32[]{:S(2)}) collective-permute-start(bf16[384,384]{1,0:T(8,128)(2,1)} %get-tuple-element.45), channel_id=1, source_target_pairs={{0,2},{1,3},{2,0},{3,1},{4,6},{5,7},{6,4},{7,5},{8,10},{9,11},{10,... | collective-permute-start | bytes 884744 | tf_op jit(solution)/shard_map/ppermute | solution.py:139
  12.1 0.2 collective-permute-start.2
  12.3 0.1 copy.11.dest
  13.1 0.1 shard_map.102.code
  13.2 17.5 %collective-permute-done.2.third = bf16[192,384]{1,0:T(8,128)(2,1)S(1)} collective-permute-done((bf16[192,384]{1,0:T(8,128)(2,1)S(1)}, bf16[192,384]{1,0:T(8,128)(2,1)S(1)}, u32[]{:S(2)}, u32[]{:S(2)}) %collective-permute-start.2) | collective-permute-done | bytes 147488 | tf_op jit(solution)/shard_map/ppermute | solution.py:139
  30.7 1.0 copy-done.3
  31.7 0.1 shard_map.103
  31.8 1.6 %collective-permute-start.6 = (bf16[3,192,384]{2,1,0:T(8,128)(2,1)S(1)}, bf16[3,192,384]{2,1,0:T(8,128)(2,1)S(1)}, u32[]{:S(2)}, u32[]{:S(2)}) collective-permute-start(bf16[3,192,384]{2,1,0:T(8,128)(2,1)S(1)} %get-tuple-element.53.own), channel_id=1, source_target_pairs={{0,2},{1,3},{2,0},{3,1},{4,6},{5,7},{6,4},{7,5},{8,10},{9,11},{10,... | collective-permute-start | bytes 1327112 | tf_op jit(solution)/shard_map/ppermute | solution.py:139
  33.3 1.6 %collective-permute-start.4 = (bf16[192,512]{1,0:T(8,128)(2,1)}, bf16[192,512]{1,0:T(8,128)(2,1)S(1)}, u32[]{:S(2)}, u32[]{:S(2)}) collective-permute-start(bf16[192,512]{1,0:T(8,128)(2,1)} %get-tuple-element.54), channel_id=1, source_target_pairs={{0,12},{4,8},{8,4},{12,0},{1,13},{5,9},{9,5},{13,1},{2,14},{6,10},... | collective-permute-start | bytes 589832 | tf_op jit(solution)/shard_map/ppermute | solution.py:139
  34.9 1.5 %collective-permute-start.5 = (bf16[192,512]{1,0:T(8,128)(2,1)S(1)}, bf16[192,512]{1,0:T(8,128)(2,1)S(1)}, u32[]{:S(2)}, u32[]{:S(2)}) collective-permute-start(bf16[192,512]{1,0:T(8,128)(2,1)S(1)} %get-tuple-element.55.refs_0_), channel_id=1, source_target_pairs={{0,16},{16,0},{1,17},{17,1},{2,18},{18,2},{3,19},{19,3},{4,20},{20... | collective-permute-start | bytes 589832 | tf_op jit(solution)/shard_map/ppermute | solution.py:139
  36.4 6.3 %collective-permute-done.4.refs_2_ = bf16[192,512]{1,0:T(8,128)(2,1)S(1)} collective-permute-done((bf16[192,512]{1,0:T(8,128)(2,1)}, bf16[192,512]{1,0:T(8,128)(2,1)S(1)}, u32[]{:S(2)}, u32[]{:S(2)}) %collective-permute-start.4) | collective-permute-done | bytes 196640 | tf_op jit(solution)/shard_map/ppermute | solution.py:139
  42.8 0.1 collective-permute-done.6.far
  42.9 0.7 collective-permute-start.9
  43.5 1.6 %collective-permute-start.10 = (bf16[192,512]{1,0:T(8,128)(2,1)S(1)}, bf16[192,512]{1,0:T(8,128)(2,1)S(1)}, u32[]{:S(2)}, u32[]{:S(2)}) collective-permute-start(bf16[192,512]{1,0:T(8,128)(2,1)S(1)} %collective-permute-done.4.refs_2_), channel_id=1, source_target_pairs={{0,16},{16,0},{1,17},{17,1},{2,18},{18,2},{3,19},{19,3},{4,20},{20... | collective-permute-start | bytes 589832 | tf_op jit(solution)/shard_map/ppermute | solution.py:139
  45.2 4.1 %collective-permute-done.10.refs_3_ = bf16[192,512]{1,0:T(8,128)(2,1)S(1)} collective-permute-done((bf16[192,512]{1,0:T(8,128)(2,1)S(1)}, bf16[192,512]{1,0:T(8,128)(2,1)S(1)}, u32[]{:S(2)}, u32[]{:S(2)}) %collective-permute-start.10) | collective-permute-done | bytes 196640 | tf_op jit(solution)/shard_map/ppermute | solution.py:139
  49.3 2.8 %shard_map.104.own = bf16[768,256]{1,0:T(8,128)(2,1)S(1)} custom-call(f32[1,1536]{1,0:T(1,128)S(1)} %broadcast_in_dim.7.gain, bf16[192,1536]{1,0:T(8,128)(2,1)S(1)} %copy-done, bf16[3,192,384]{2,1,0:T(8,128)(2,1)S(1)} %get-tuple-element.53.own, bf16[3,192,384]{2,1,0:T(8,128)(2,1)S(1)} %collective-permute-done.6.far, ...), custom_call_target="tpu_custom_call" | custom-call | tf_op jit(solution)/shard_map/pallas_call | solution.py:151
  52.1 0.0 copy-start.7
  52.1 0.0 copy-start.1
  52.1 0.0 copy-start.5
  52.1 5.0 %collective-permute-start.11 = (bf16[768,256]{1,0:T(8,128)(2,1)S(1)}, bf16[768,256]{1,0:T(8,128)(2,1)S(1)}, u32[]{:S(2)}, u32[]{:S(2)}) collective-permute-start(bf16[768,256]{1,0:T(8,128)(2,1)S(1)} %shard_map.104.own), channel_id=1, source_target_pairs={{0,2},{1,3},{2,0},{3,1},{4,6},{5,7},{6,4},{7,5},{8,10},{9,11},{10,... | collective-permute-start | bytes 1179656 | tf_op jit(solution)/shard_map/ppermute | solution.py:139
  57.1 1.5 %collective-permute-start.13 = (bf16[2,128,384]{2,1,0:T(8,128)(2,1)S(1)}, bf16[2,128,384]{2,1,0:T(8,128)(2,1)S(1)}, u32[]{:S(2)}, u32[]{:S(2)}) collective-permute-start(bf16[2,128,384]{2,1,0:T(8,128)(2,1)S(1)} %collective-permute-done.9.even), channel_id=1, source_target_pairs={{0,16},{16,0},{1,17},{17,1},{2,18},{18,2},{3,19},{19,3},{4,20},{20... | collective-permute-start | bytes 589832 | tf_op jit(solution)/shard_map/ppermute | solution.py:139
  58.7 0.6 collective-permute-start.15
  59.2 5.2 %collective-permute-done.13.even_other = bf16[2,128,384]{2,1,0:T(8,128)(2,1)S(1)} collective-permute-done((bf16[2,128,384]{2,1,0:T(8,128)(2,1)S(1)}, bf16[2,128,384]{2,1,0:T(8,128)(2,1)S(1)}, u32[]{:S(2)}, u32[]{:S(2)}) %collective-permute-start.13) | collective-permute-done | bytes 196640 | tf_op jit(solution)/shard_map/ppermute | solution.py:139
  64.4 2.6 %collective-permute-done.11.far = bf16[768,256]{1,0:T(8,128)(2,1)S(1)} collective-permute-done((bf16[768,256]{1,0:T(8,128)(2,1)S(1)}, bf16[768,256]{1,0:T(8,128)(2,1)S(1)}, u32[]{:S(2)}, u32[]{:S(2)}) %collective-permute-start.11) | collective-permute-done | bytes 393248 | tf_op jit(solution)/shard_map/ppermute | solution.py:139
  67.0 0.1 collective-permute-start.14
  67.1 1.6 %collective-permute-done.14.near_far = bf16[768,256]{1,0:T(8,128)(2,1)S(1)} collective-permute-done((bf16[768,256]{1,0:T(8,128)(2,1)S(1)}, bf16[768,256]{1,0:T(8,128)(2,1)S(1)}, u32[]{:S(2)}, u32[]{:S(2)}) %collective-permute-start.14) | collective-permute-done | bytes 393248 | tf_op jit(solution)/shard_map/ppermute | solution.py:139
  68.7 1.0 shard_map.105
  69.7 0.9 collective-permute-start.16
  70.7 3.5 %collective-permute-start.17 = (bf16[192,384]{1,0:T(8,128)(2,1)S(1)}, bf16[192,384]{1,0:T(8,128)(2,1)S(1)}, u32[]{:S(2)}, u32[]{:S(2)}) collective-permute-start(bf16[192,384]{1,0:T(8,128)(2,1)S(1)} %get-tuple-element.73), channel_id=1, source_target_pairs={{0,14},{1,15},{2,13},{3,12},{4,11},{5,10},{6,8},{7,9},{8,6},{9,7},... | collective-permute-start | bytes 442376 | tf_op jit(solution)/shard_map/ppermute | solution.py:505
  74.2 0.1 collective-permute-start.18
  74.3 7.9 %collective-permute-done.16 = bf16[192,384]{1,0:T(8,128)(2,1)S(1)} collective-permute-done((bf16[192,384]{1,0:T(8,128)(2,1)S(1)}, bf16[192,384]{1,0:T(8,128)(2,1)S(1)}, u32[]{:S(2)}, u32[]{:S(2)}) %collective-permute-start.16) | collective-permute-done | bytes 147488 | tf_op jit(solution)/shard_map/ppermute | solution.py:505
  82.2 4.6 %collective-permute-done.18 = bf16[192,384]{1,0:T(8,128)(2,1)S(1)} collective-permute-done((bf16[192,384]{1,0:T(8,128)(2,1)S(1)}, bf16[192,384]{1,0:T(8,128)(2,1)S(1)}, u32[]{:S(2)}, u32[]{:S(2)}) %collective-permute-start.18) | collective-permute-done | bytes 147488 | tf_op jit(solution)/shard_map/ppermute | solution.py:505
  86.8 0.1 add_convert_fusion.own
  86.9 0.1 collective-permute-start.19
  87.0 0.2 collective-permute-start.20
  87.2 5.7 %collective-permute-done.19.far = bf16[192,384]{1,0:T(8,128)(2,1)S(1)} collective-permute-done((bf16[192,384]{1,0:T(8,128)(2,1)S(1)}, bf16[192,384]{1,0:T(8,128)(2,1)S(1)}, u32[]{:S(2)}, u32[]{:S(2)}) %collective-permute-start.19) | collective-permute-done | bytes 147488 | tf_op jit(solution)/shard_map/ppermute | solution.py:139
  92.9 1.3 %collective-permute-done.21.near_far = bf16[192,384]{1,0:T(8,128)(2,1)S(1)} collective-permute-done((bf16[192,384]{1,0:T(8,128)(2,1)S(1)}, bf16[192,384]{1,0:T(8,128)(2,1)S(1)}, u32[]{:S(2)}, u32[]{:S(2)}) %collective-permute-start.21) | collective-permute-done | bytes 147488 | tf_op jit(solution)/shard_map/ppermute | solution.py:139
  94.3 1.9 %shard_map.106 = (bf16[64,768]{1,0:T(8,128)(2,1)S(1)}, bf16[64,768]{1,0:T(8,128)(2,1)S(1)}, bf16[64,768]{1,0:T(8,128)(2,1)S(1)}, bf16[64,768]{1,0:T(8,128)(2,1)S(1)}) custom-call(s32[3]{0:T(128)S(1)} %copy-done.5, f32[1,1536]{1,0:T(1,128)S(1)} %broadcast_in_dim.6.gain, s32[1,192]{1,0:T(1,128)S(1)} %shard_map.102.code, bf16[576,1536]{1,0:T(8,128)(2,1)S(1)} %bitcast.3, ...), custom_call_target="tpu_custom_call" | custom-call | tf_op jit(solution)/shard_map/pallas_call | solution.py:151
  96.1 1.2 %collective-permute-start.22 = (bf16[64,768]{1,0:T(8,128)(2,1)S(1)}, bf16[64,768]{1,0:T(8,128)(2,1)S(1)}, u32[]{:S(2)}, u32[]{:S(2)}) collective-permute-start(bf16[64,768]{1,0:T(8,128)(2,1)S(1)} %get-tuple-element.76), channel_id=1, source_target_pairs={{0,4},{4,0},{8,12},{12,8},{1,5},{5,1},{9,13},{13,9},{2,6},{6,2},{1... | collective-permute-start | bytes 294920 | tf_op jit(solution)/shard_map/ppermute | solution.py:139
  97.3 0.7 collective-permute-start.23
  98.0 2.6 %collective-permute-start.24 = (bf16[64,768]{1,0:T(8,128)(2,1)S(1)}, bf16[64,768]{1,0:T(8,128)(2,1)S(1)}, u32[]{:S(2)}, u32[]{:S(2)}) collective-permute-start(bf16[64,768]{1,0:T(8,128)(2,1)S(1)} %get-tuple-element.78), channel_id=1, source_target_pairs={{0,12},{4,8},{8,4},{12,0},{1,13},{5,9},{9,5},{13,1},{2,14},{6,10},... | collective-permute-start | bytes 294920 | tf_op jit(solution)/shard_map/ppermute | solution.py:139
  100.6 1.5 %collective-permute-done.22.refs_1_ = bf16[64,768]{1,0:T(8,128)(2,1)S(1)} collective-permute-done((bf16[64,768]{1,0:T(8,128)(2,1)S(1)}, bf16[64,768]{1,0:T(8,128)(2,1)S(1)}, u32[]{:S(2)}, u32[]{:S(2)}) %collective-permute-start.22) | collective-permute-done | bytes 98336 | tf_op jit(solution)/shard_map/ppermute | solution.py:139
  102.1 5.8 %collective-permute-done.23.refs_2_ = bf16[64,768]{1,0:T(8,128)(2,1)S(1)} collective-permute-done((bf16[64,768]{1,0:T(8,128)(2,1)S(1)}, bf16[64,768]{1,0:T(8,128)(2,1)S(1)}, u32[]{:S(2)}, u32[]{:S(2)}) %collective-permute-start.23) | collective-permute-done | bytes 98336 | tf_op jit(solution)/shard_map/ppermute | solution.py:139
  107.9 2.1 %shard_map.107 = bf16[192,256]{1,0:T(8,128)(2,1)} custom-call(s32[3]{0:T(128)S(1)} %copy-done.5, bf16[64,768]{1,0:T(8,128)(2,1)S(1)} %get-tuple-element.75.refs_0_, bf16[64,768]{1,0:T(8,128)(2,1)S(1)} %collective-permute-done.22.refs_1_, bf16[64,768]{1,0:T(8,128)(2,1)S(1)} %collective-permute-done.23.refs_2_, bf16[64,768]{1,0:T(8,128)(2,1)S(1)} %collective-permute-done.24.refs_3_), custom_call_target="tpu_custom_call" | custom-call | tf_op jit(solution)/shard_map/pallas_call | solution.py:151
  (32 shorter events, 0.1 us)
Async XLA Ops:
  0.0 12.3 %copy-start.4 = (s32[192,1]{0,1:T(1,128)S(1)}, s32[192,1]{0,1:T(1,128)}, u32[]{:S(2)}) copy-start(s32[192,1]{0,1:T(1,128)} %param.12) | copy-start | bytes 2308
  2.4 9.7 %copy-start.8 = (bf16[192,384]{1,0:T(8,128)(2,1)S(1)}, bf16[192,384]{1,0:T(8,128)(2,1)}, u32[]{:S(2)}) copy-start(bf16[192,384]{1,0:T(8,128)(2,1)} %get-tuple-element.44) | copy-start | bytes 442372
  2.4 28.3 %collective-permute-start = (bf16[192,1408]{1,0:T(8,128)(2,1)}, bf16[192,1408]{1,0:T(8,128)(2,1)S(1)}, u32[]{:S(2)}, u32[]{:S(2)}) collective-permute-start(bf16[192,1408]{1,0:T(8,128)(2,1)} %get-tuple-element.42), channel_id=1, source_target_pairs={{0,4},{4,0},{8,12},{12,8},{1,5},{5,1},{9,13},{13,9},{2,6},{6,2},{1... | collective-permute-start | bytes 1622024 | tf_op jit(solution)/shard_map/ppermute | solution.py:139
  5.5 39.6 %copy-start.6 = (f32[1536]{0:T(1024)S(1)}, f32[1536]{0:T(1024)}, u32[]{:S(2)}) copy-start(f32[1536]{0:T(1024)} %param.13) | copy-start | bytes 18436
  5.5 43.8 %copy-start = (bf16[192,1536]{1,0:T(8,128)(2,1)S(1)}, bf16[192,1536]{1,0:T(8,128)(2,1)}, u32[]{:S(2)}) copy-start(bf16[192,1536]{1,0:T(8,128)(2,1)} %tiles.2) | copy-start | bytes 1769476
  5.5 25.2 %collective-permute-start.1 = (bf16[192,896]{1,0:T(8,128)(2,1)}, bf16[192,896]{1,0:T(8,128)(2,1)S(1)}, u32[]{:S(2)}, u32[]{:S(2)}) collective-permute-start(bf16[192,896]{1,0:T(8,128)(2,1)} %get-tuple-element.43), channel_id=1, source_target_pairs={{0,8},{4,12},{8,0},{12,4},{1,9},{5,13},{9,1},{13,5},{2,10},{6,14},... | collective-permute-start | bytes 1032200 | tf_op jit(solution)/shard_map/ppermute | solution.py:139
  10.5 38.7 %copy-start.2 = (bf16[384,512]{1,0:T(8,128)(2,1)S(1)}, bf16[384,512]{1,0:T(8,128)(2,1)}, u32[]{:S(2)}) copy-start(bf16[384,512]{1,0:T(8,128)(2,1)} %get-tuple-element.65.kept) | copy-start | bytes 1179652
  10.6 20.1 %collective-permute-start.3 = (bf16[384,384]{1,0:T(8,128)(2,1)}, bf16[384,384]{1,0:T(8,128)(2,1)S(1)}, u32[]{:S(2)}, u32[]{:S(2)}) collective-permute-start(bf16[384,384]{1,0:T(8,128)(2,1)} %get-tuple-element.45), channel_id=1, source_target_pairs={{0,2},{1,3},{2,0},{3,1},{4,6},{5,7},{6,4},{7,5},{8,10},{9,11},{10,... | collective-permute-start | bytes 884744 | tf_op jit(solution)/shard_map/ppermute | solution.py:139
  12.1 18.6 %collective-permute-start.2 = (bf16[192,384]{1,0:T(8,128)(2,1)S(1)}, bf16[192,384]{1,0:T(8,128)(2,1)S(1)}, u32[]{:S(2)}, u32[]{:S(2)}) collective-permute-start(bf16[192,384]{1,0:T(8,128)(2,1)S(1)} %copy-done.8), channel_id=1, source_target_pairs={{0,12},{4,8},{8,4},{12,0},{1,13},{5,9},{9,5},{13,1},{2,14},{6,10},... | collective-permute-start | bytes 442376 | tf_op jit(solution)/shard_map/ppermute | solution.py:139
  30.7 1.0 copy-start.3
  31.8 11.1 %collective-permute-start.6 = (bf16[3,192,384]{2,1,0:T(8,128)(2,1)S(1)}, bf16[3,192,384]{2,1,0:T(8,128)(2,1)S(1)}, u32[]{:S(2)}, u32[]{:S(2)}) collective-permute-start(bf16[3,192,384]{2,1,0:T(8,128)(2,1)S(1)} %get-tuple-element.53.own), channel_id=1, source_target_pairs={{0,2},{1,3},{2,0},{3,1},{4,6},{5,7},{6,4},{7,5},{8,10},{9,11},{10,... | collective-permute-start | bytes 1327112 | tf_op jit(solution)/shard_map/ppermute | solution.py:139
  33.3 9.5 %collective-permute-start.7 = (bf16[3,192,384]{2,1,0:T(8,128)(2,1)S(1)}, bf16[3,192,384]{2,1,0:T(8,128)(2,1)S(1)}, u32[]{:S(2)}, u32[]{:S(2)}) collective-permute-start(bf16[3,192,384]{2,1,0:T(8,128)(2,1)S(1)} %get-tuple-element.53.own), channel_id=1, source_target_pairs={{0,1},{1,0},{2,3},{3,2},{4,5},{5,4},{6,7},{7,6},{8,9},{9,8},{10,11... | collective-permute-start | bytes 1327112 | tf_op jit(solution)/shard_map/ppermute | solution.py:139
  33.3 9.4 %collective-permute-start.4 = (bf16[192,512]{1,0:T(8,128)(2,1)}, bf16[192,512]{1,0:T(8,128)(2,1)S(1)}, u32[]{:S(2)}, u32[]{:S(2)}) collective-permute-start(bf16[192,512]{1,0:T(8,128)(2,1)} %get-tuple-element.54), channel_id=1, source_target_pairs={{0,12},{4,8},{8,4},{12,0},{1,13},{5,9},{9,5},{13,1},{2,14},{6,10},... | collective-permute-start | bytes 589832 | tf_op jit(solution)/shard_map/ppermute | solution.py:139
  34.9 7.9 %collective-permute-start.5 = (bf16[192,512]{1,0:T(8,128)(2,1)S(1)}, bf16[192,512]{1,0:T(8,128)(2,1)S(1)}, u32[]{:S(2)}, u32[]{:S(2)}) collective-permute-start(bf16[192,512]{1,0:T(8,128)(2,1)S(1)} %get-tuple-element.55.refs_0_), channel_id=1, source_target_pairs={{0,16},{16,0},{1,17},{17,1},{2,18},{18,2},{3,19},{19,3},{4,20},{20... | collective-permute-start | bytes 589832 | tf_op jit(solution)/shard_map/ppermute | solution.py:139
  42.9 2.3 %collective-permute-start.8 = (bf16[3,192,384]{2,1,0:T(8,128)(2,1)S(1)}, bf16[3,192,384]{2,1,0:T(8,128)(2,1)S(1)}, u32[]{:S(2)}, u32[]{:S(2)}) collective-permute-start(bf16[3,192,384]{2,1,0:T(8,128)(2,1)S(1)} %collective-permute-done.6.far), channel_id=1, source_target_pairs={{0,1},{1,0},{2,3},{3,2},{4,5},{5,4},{6,7},{7,6},{8,9},{9,8},{10,11... | collective-permute-start | bytes 1327112 | tf_op jit(solution)/shard_map/ppermute | solution.py:139
  42.9 2.3 %collective-permute-start.9 = (bf16[2,128,384]{2,1,0:T(8,128)(2,1)S(1)}, bf16[2,128,384]{2,1,0:T(8,128)(2,1)S(1)}, u32[]{:S(2)}, u32[]{:S(2)}) collective-permute-start(bf16[2,128,384]{2,1,0:T(8,128)(2,1)S(1)} %get-tuple-element.60), channel_id=1, source_target_pairs={{0,0},{1,9},{2,14},{3,7},{4,4},{5,13},{6,2},{7,11},{8,8},{9,1},{10... | collective-permute-start | bytes 589832 | tf_op jit(solution)/shard_map/ppermute | solution.py:478
  43.5 5.7 %collective-permute-start.10 = (bf16[192,512]{1,0:T(8,128)(2,1)S(1)}, bf16[192,512]{1,0:T(8,128)(2,1)S(1)}, u32[]{:S(2)}, u32[]{:S(2)}) collective-permute-start(bf16[192,512]{1,0:T(8,128)(2,1)S(1)} %collective-permute-done.4.refs_2_), channel_id=1, source_target_pairs={{0,16},{16,0},{1,17},{17,1},{2,18},{18,2},{3,19},{19,3},{4,20},{20... | collective-permute-start | bytes 589832 | tf_op jit(solution)/shard_map/ppermute | solution.py:139
  52.1 40.8 %copy-start.7 = (f32[1536]{0:T(1024)S(1)}, f32[1536]{0:T(1024)}, u32[]{:S(2)}) copy-start(f32[1536]{0:T(1024)} %param.17) | copy-start | bytes 18436
  52.1 42.2 %copy-start.1 = (bf16[1536,576]{0,1:T(8,128)(2,1)S(1)}, bf16[1536,576]{0,1:T(8,128)(2,1)}, u32[]{:S(2)}) copy-start(bf16[1536,576]{0,1:T(8,128)(2,1)} %param.18) | copy-start | bytes 5308420
  52.1 42.2 %copy-start.5 = (s32[3]{0:T(128)S(1)}, s32[3]{0:T(128)}, u32[]{:S(2)}) copy-start(s32[3]{0:T(128)} %offsets.3) | copy-start | bytes 40
  52.1 14.9 %collective-permute-start.11 = (bf16[768,256]{1,0:T(8,128)(2,1)S(1)}, bf16[768,256]{1,0:T(8,128)(2,1)S(1)}, u32[]{:S(2)}, u32[]{:S(2)}) collective-permute-start(bf16[768,256]{1,0:T(8,128)(2,1)S(1)} %shard_map.104.own), channel_id=1, source_target_pairs={{0,2},{1,3},{2,0},{3,1},{4,6},{5,7},{6,4},{7,5},{8,10},{9,11},{10,... | collective-permute-start | bytes 1179656 | tf_op jit(solution)/shard_map/ppermute | solution.py:139
  57.1 7.3 %collective-permute-start.13 = (bf16[2,128,384]{2,1,0:T(8,128)(2,1)S(1)}, bf16[2,128,384]{2,1,0:T(8,128)(2,1)S(1)}, u32[]{:S(2)}, u32[]{:S(2)}) collective-permute-start(bf16[2,128,384]{2,1,0:T(8,128)(2,1)S(1)} %collective-permute-done.9.even), channel_id=1, source_target_pairs={{0,16},{16,0},{1,17},{17,1},{2,18},{18,2},{3,19},{19,3},{4,20},{20... | collective-permute-start | bytes 589832 | tf_op jit(solution)/shard_map/ppermute | solution.py:139
  58.7 8.5 %collective-permute-start.15 = (bf16[2,256,384]{2,1,0:T(8,128)(2,1)S(1)}, bf16[2,256,384]{2,1,0:T(8,128)(2,1)S(1)}, u32[]{:S(2)}, u32[]{:S(2)}) collective-permute-start(bf16[2,256,384]{2,1,0:T(8,128)(2,1)S(1)} %get-tuple-element.70), channel_id=1, source_target_pairs={{0,9},{1,0},{2,7},{3,14},{4,13},{5,4},{6,11},{7,2},{8,1},{9,8},{10... | collective-permute-start | bytes 1179656 | tf_op jit(solution)/shard_map/ppermute | solution.py:478
  59.2 7.9 %collective-permute-start.12 = (bf16[768,256]{1,0:T(8,128)(2,1)S(1)}, bf16[768,256]{1,0:T(8,128)(2,1)S(1)}, u32[]{:S(2)}, u32[]{:S(2)}) collective-permute-start(bf16[768,256]{1,0:T(8,128)(2,1)S(1)} %shard_map.104.own), channel_id=1, source_target_pairs={{0,1},{1,0},{2,3},{3,2},{4,5},{5,4},{6,7},{7,6},{8,9},{9,8},{10,11... | collective-permute-start | bytes 1179656 | tf_op jit(solution)/shard_map/ppermute | solution.py:139
  67.0 1.7 %collective-permute-start.14 = (bf16[768,256]{1,0:T(8,128)(2,1)S(1)}, bf16[768,256]{1,0:T(8,128)(2,1)S(1)}, u32[]{:S(2)}, u32[]{:S(2)}) collective-permute-start(bf16[768,256]{1,0:T(8,128)(2,1)S(1)} %collective-permute-done.11.far), channel_id=1, source_target_pairs={{0,1},{1,0},{2,3},{3,2},{4,5},{5,4},{6,7},{7,6},{8,9},{9,8},{10,11... | collective-permute-start | bytes 1179656 | tf_op jit(solution)/shard_map/ppermute | solution.py:139
  69.7 12.5 %collective-permute-start.16 = (bf16[192,384]{1,0:T(8,128)(2,1)S(1)}, bf16[192,384]{1,0:T(8,128)(2,1)S(1)}, u32[]{:S(2)}, u32[]{:S(2)}) collective-permute-start(bf16[192,384]{1,0:T(8,128)(2,1)S(1)} %get-tuple-element.72), channel_id=1, source_target_pairs={{0,9},{1,8},{2,11},{3,10},{4,13},{5,12},{6,15},{7,14},{8,1},{9,0},... | collective-permute-start | bytes 442376 | tf_op jit(solution)/shard_map/ppermute | solution.py:505
  70.7 11.5 %collective-permute-start.17 = (bf16[192,384]{1,0:T(8,128)(2,1)S(1)}, bf16[192,384]{1,0:T(8,128)(2,1)S(1)}, u32[]{:S(2)}, u32[]{:S(2)}) collective-permute-start(bf16[192,384]{1,0:T(8,128)(2,1)S(1)} %get-tuple-element.73), channel_id=1, source_target_pairs={{0,14},{1,15},{2,13},{3,12},{4,11},{5,10},{6,8},{7,9},{8,6},{9,7},... | collective-permute-start | bytes 442376 | tf_op jit(solution)/shard_map/ppermute | solution.py:505
  74.2 12.6 %collective-permute-start.18 = (bf16[192,384]{1,0:T(8,128)(2,1)S(1)}, bf16[192,384]{1,0:T(8,128)(2,1)S(1)}, u32[]{:S(2)}, u32[]{:S(2)}) collective-permute-start(bf16[192,384]{1,0:T(8,128)(2,1)S(1)} %get-tuple-element.74), channel_id=1, source_target_pairs={{0,7},{1,6},{2,4},{3,5},{4,2},{5,3},{6,1},{7,0},{8,15},{9,14},{10,... | collective-permute-start | bytes 442376 | tf_op jit(solution)/shard_map/ppermute | solution.py:505
  86.9 5.9 %collective-permute-start.19 = (bf16[192,384]{1,0:T(8,128)(2,1)S(1)}, bf16[192,384]{1,0:T(8,128)(2,1)S(1)}, u32[]{:S(2)}, u32[]{:S(2)}) collective-permute-start(bf16[192,384]{1,0:T(8,128)(2,1)S(1)} %add_convert_fusion.own), channel_id=1, source_target_pairs={{0,2},{1,3},{2,0},{3,1},{4,6},{5,7},{6,4},{7,5},{8,10},{9,11},{10,... | collective-permute-start | bytes 442376 | tf_op jit(solution)/shard_map/ppermute | solution.py:139
  87.0 5.9 %collective-permute-start.20 = (bf16[192,384]{1,0:T(8,128)(2,1)S(1)}, bf16[192,384]{1,0:T(8,128)(2,1)S(1)}, u32[]{:S(2)}, u32[]{:S(2)}) collective-permute-start(bf16[192,384]{1,0:T(8,128)(2,1)S(1)} %add_convert_fusion.own), channel_id=1, source_target_pairs={{0,1},{1,0},{2,3},{3,2},{4,5},{5,4},{6,7},{7,6},{8,9},{9,8},{10,11... | collective-permute-start | bytes 442376 | tf_op jit(solution)/shard_map/ppermute | solution.py:139
  92.9 1.4 %collective-permute-start.21 = (bf16[192,384]{1,0:T(8,128)(2,1)S(1)}, bf16[192,384]{1,0:T(8,128)(2,1)S(1)}, u32[]{:S(2)}, u32[]{:S(2)}) collective-permute-start(bf16[192,384]{1,0:T(8,128)(2,1)S(1)} %collective-permute-done.19.far), channel_id=1, source_target_pairs={{0,1},{1,0},{2,3},{3,2},{4,5},{5,4},{6,7},{7,6},{8,9},{9,8},{10,11... | collective-permute-start | bytes 442376 | tf_op jit(solution)/shard_map/ppermute | solution.py:139
  96.1 6.0 %collective-permute-start.22 = (bf16[64,768]{1,0:T(8,128)(2,1)S(1)}, bf16[64,768]{1,0:T(8,128)(2,1)S(1)}, u32[]{:S(2)}, u32[]{:S(2)}) collective-permute-start(bf16[64,768]{1,0:T(8,128)(2,1)S(1)} %get-tuple-element.76), channel_id=1, source_target_pairs={{0,4},{4,0},{8,12},{12,8},{1,5},{5,1},{9,13},{13,9},{2,6},{6,2},{1... | collective-permute-start | bytes 294920 | tf_op jit(solution)/shard_map/ppermute | solution.py:139
  97.3 10.6 %collective-permute-start.23 = (bf16[64,768]{1,0:T(8,128)(2,1)S(1)}, bf16[64,768]{1,0:T(8,128)(2,1)S(1)}, u32[]{:S(2)}, u32[]{:S(2)}) collective-permute-start(bf16[64,768]{1,0:T(8,128)(2,1)S(1)} %get-tuple-element.77), channel_id=1, source_target_pairs={{0,8},{4,12},{8,0},{12,4},{1,9},{5,13},{9,1},{13,5},{2,10},{6,14},... | collective-permute-start | bytes 294920 | tf_op jit(solution)/shard_map/ppermute | solution.py:139
  98.0 9.9 %collective-permute-start.24 = (bf16[64,768]{1,0:T(8,128)(2,1)S(1)}, bf16[64,768]{1,0:T(8,128)(2,1)S(1)}, u32[]{:S(2)}, u32[]{:S(2)}) collective-permute-start(bf16[64,768]{1,0:T(8,128)(2,1)S(1)} %get-tuple-element.78), channel_id=1, source_target_pairs={{0,12},{4,8},{8,4},{12,0},{1,13},{5,9},{9,5},{13,1},{2,14},{6,10},... | collective-permute-start | bytes 294920 | tf_op jit(solution)/shard_map/ppermute | solution.py:139

commit v6 on v5

--- a/solution.py
+++ b/solution.py
@@ -177,27 +177,30 @@
 
 
 def copier(sems, group):
-    copies = []
+    copies, used = [], [0]
 
     def copy(source, target, other=None):
-        started = pltpu.make_async_copy(source, target, sems.at[len(copies)])
+        started = pltpu.make_async_copy(source, target, sems.at[used[0]])
         if other is None:
             started.start()
         else:
-            second = pltpu.make_async_copy(other, target, sems.at[len(copies)])
+            second = pltpu.make_async_copy(other, target, sems.at[used[0]])
             pl.when(group == 0)(started.start)
             pl.when(group != 0)(second.start)
         copies.append(started)
+        used[0] += 1
 
     return copies, copy
 
 
-def cut_first_body(count, tiles, w_gate, w_up, first_out, second_out, quarter, sems):
+def cut_first_body(
+    count, tiles, w_gate, w_up, gain, first_out, second_out, quarter, normed, held, sems
+):
     seq, mp, group = place()
     copies, copy = copier(sems, group)
     half, units = w_gate.shape[0] // 2, w_gate.shape[1] // count
     features = quarter.shape[1]
-    own_columns = tiles.at[:, at(mp, features)]
+    copy(tiles, held)
     for i in range(2):
         span = pl.ds(i * half, half), at(seq ^ 2, units)
         columns = pl.ds(features + i * units, units)
@@ -206,9 +209,17 @@
         for k, weight in enumerate((w_gate, w_up)):
             columns = pl.ds(features + (2 * i + k) * units, units)
             copy(weight.at[span], first_out.at[:, columns])
-    for target in (second_out.at[:, pl.ds(0, features)], first_out.at[:, pl.ds(0, features)]):
-        copy(own_columns, target)
-    copy(own_columns, quarter)
+    copies.pop(0).wait()
+    values = held[...].astype(jnp.float32)
+    squares = jnp.sum(values * values, axis=1, keepdims=True)
+    inverse = lax.rsqrt(squares * (1.0 / D_ENC) + epsilon)
+    normed[...] = (values * inverse * gain[...]).astype(jnp.bfloat16)
+    columns = at(mp, features)
+    values = held[:, columns].astype(jnp.float32)
+    own_columns = (values * inverse * gain[:, columns]).astype(jnp.bfloat16)
+    second_out[:, :features] = own_columns
+    first_out[:, :features] = own_columns
+    quarter[...] = own_columns
     for started in copies:
         started.wait()
 
@@ -232,63 +243,77 @@
         started.wait()
 
 
-def restack_body(first, second, third, near, far, stacked, columns, even, odd):
+def restack_body(first, second, third, stacked, columns):
     features = stacked.shape[2]
     stacked[0] = first[:, :features]
     stacked[1] = second[:, :features]
     stacked[2] = third[...]
     columns[...] = second[:, features:]
+
+
+def pair_body(near, far, even, odd):
     for i, rows in enumerate((near, far)):
         even[i] = rows[: even.shape[1], :]
         odd[i] = rows[even.shape[1] :, :]
 
 
-def code_body(capacity, counts, dest, dest_row, code):
+def routes_body(count, counts, offsets, dest, dest_row, routes):
+    seq, _, _ = place()
     rows = dest_row.shape[1]
+    capacity = ENCODER_SLOTS // count
     later = lax.broadcasted_iota(jnp.int32, (rows, rows), 1)
     earlier = lax.broadcasted_iota(jnp.int32, (rows, rows), 0)
     same = (dest[...] == dest_row[...]) & (earlier < later)
     rank = jnp.sum(jnp.where(same, 1, 0), axis=0, keepdims=True)
     live = lax.broadcasted_iota(jnp.int32, (1, rows), 1) < counts[0]
-    code[...] = jnp.where(live, dest_row[...] * capacity + rank, -1)
-
-
-def hidden_body(
-    count, gain, tiles, own, far, near, near_far, kept, next_in, *refs
-):
-    halves, (out, normed, weights, next_weights) = refs[:4], refs[4:]
+    codes = jnp.where(live, dest_row[...] * capacity + rank, -1)
+
+    def chosen(wanted):
+        return jnp.where(codes == wanted, 1.0, 0.0).astype(jnp.bfloat16)
+
+    slot = lax.broadcasted_iota(jnp.int32, (capacity, rows), 0)
+    for d in range(count):
+        routes[pl.ds(d * capacity, capacity), :] = chosen((seq ^ d) * capacity + slot)
+    per_block = capacity // DILATION_STEP
+    spread = count * per_block
+    index = lax.broadcasted_iota(jnp.int32, (spread, rows), 0)
+    wanted = (index // per_block) * capacity + (index % per_block) * DILATION_STEP
+    for h in range(offsets.shape[0]):
+        routes[pl.ds(count * capacity + h * spread, spread), :] = chosen(wanted + offsets[h])
+
+
+def hidden_body(count, normed, own, far, near, near_far, kept, next_in, *refs):
+    (second, second_other, third, third_other), (out, weights) = refs[:4], refs[4:]
     seq, mp, group = place()
-    depth, units = weights.shape[1:]
+    depth, units = weights.shape[2:]
     half = depth // 2
-    rows = tiles.shape[0]
-    for i, piece in enumerate(halves):
-        weights[i, :half, :] = piece[:, :units]
-        weights[i, half:, :] = piece[:, units:]
-    for i in range(2):
-        start = own.shape[2] + 2 * i * units
-        next_weights[i * half : (i + 1) * half, :] = next_in[:, start : start + 2 * units]
-
-    def gated(d):
+    rows = normed.shape[0]
+    for k in range(2):
+        weights[k, seq] = kept[:, k * units : (k + 1) * units]
+        for i in range(2):
+            start = own.shape[2] + (2 * i + k) * units
+            span = pl.ds(i * half, half)
+            weights[k, seq ^ 1, span, :] = next_in[:, start : start + units]
+    for d, mine, other in ((2, second, second_other), (3, third, third_other)):
+        for i in range(2):
+            span, columns = pl.ds(i * half, half), slice(i * units, (i + 1) * units)
+            weights[group, seq ^ d, span, :] = mine[:, columns]
+            weights[1 - group, seq ^ d, span, :] = other[:, columns]
+    for d in range(count):
         if d == 0:
-            pieces = [(tiles[:, pl.ds(q * depth, depth)], q) for q in range(count)]
+            pieces = [(normed[:, q * depth : (q + 1) * depth], q) for q in range(count)]
         else:
-            pieces = [(own[d - 1], mp), (far[d - 1], mp ^ 2)]
-            pieces += [(near[d - 1], mp ^ 1), (near_far[d - 1], mp ^ 3)]
-        values = [piece.astype(jnp.float32) for piece, _ in pieces]
-        squares = sum(jnp.sum(v * v, axis=1, keepdims=True) for v in values)
-        inverse = lax.rsqrt(squares * (1.0 / D_ENC) + epsilon)
-        for v, (_, index) in zip(values, pieces):
-            normed[d, index] = (v * inverse * gain[:, at(index, depth)]).astype(jnp.bfloat16)
-        dot = functools.partial(jnp.dot, preferred_element_type=jnp.float32)
-        both = dot(normed[d, seq], kept[...]) + dot(normed[d, seq ^ 1], next_weights[...])
-        mine = dot(normed[d, seq ^ 2], weights[0]) + dot(normed[d, seq ^ 3], weights[2])
-        other = dot(normed[d, seq ^ 2], weights[1]) + dot(normed[d, seq ^ 3], weights[3])
-        gate_act = both[:, :units] + jnp.where(group == 0, mine, other)
-        up_act = both[:, units:] + jnp.where(group == 0, other, mine)
-        return (gate_act * jax.nn.sigmoid(gate_act) * up_act).astype(jnp.bfloat16)
-
-    for d in range(count - 1, -1, -1):
-        out[pl.ds(d * rows, rows), :] = gated(d)
+            pieces = [(own[d - 1], mp), (near[d - 1], mp ^ 1)]
+            pieces += [(far[d - 1], mp ^ 2), (near_far[d - 1], mp ^ 3)]
+        gate_act, up_act = (
+            sum(
+                jnp.dot(piece, weights[k, index], preferred_element_type=jnp.float32)
+                for piece, index in pieces
+            )
+            for k in range(2)
+        )
+        gated = gate_act * jax.nn.sigmoid(gate_act) * up_act
+        out[pl.ds(d * rows, rows), :] = gated.astype(jnp.bfloat16)
 
 
 def down_body(own, far, near, near_far, even, even_other, odd, *outs):
@@ -308,11 +333,11 @@
         out[...] = total.astype(out.dtype)
 
 
-def project_body(count, offsets, gain, code, w_qkv_t, own, far, near, near_far, *outs):
+def project_body(count, gain, routes, w_qkv_t, own, far, near, near_far, *outs):
     seq, mp, _ = place()
     features = own.shape[1]
     capacity = outs[0].shape[0]
-    heads = offsets.shape[0]
+    heads = w_qkv_t.shape[0] // (3 * HEAD_WIDTH)
     squares, total = 0.0, 0.0
     for j, piece in enumerate((own, near, far, near_far)):
         index = column_block(seq, mp ^ j)
@@ -326,27 +351,20 @@
             preferred_element_type=jnp.float32,
         )
     projected = (total * lax.rsqrt(squares * (1.0 / D_ENC) + epsilon)).astype(jnp.bfloat16)
-    codes = code[...]
-    rows = codes.shape[1]
-
-    def pick(wanted, array):
-        chosen = jnp.where(codes == wanted, 1.0, 0.0).astype(jnp.bfloat16)
-        return jnp.dot(chosen, array, preferred_element_type=jnp.float32).astype(jnp.bfloat16)
-
-    spread = []
-    per_block = capacity // DILATION_STEP
-    index = lax.broadcasted_iota(jnp.int32, (count * per_block, rows), 0)
+    routed = jnp.dot(routes[...], projected, preferred_element_type=jnp.float32)
+    routed = routed.astype(jnp.bfloat16)
+    width = projected.shape[1]
+    spread = capacity // 2
+    for d, out in enumerate(outs):
+        out[:, :width] = routed[d * capacity : (d + 1) * capacity]
     for h in range(heads):
-        wanted = (index // per_block) * capacity + (index % per_block) * DILATION_STEP + offsets[h]
-        start = (3 * h + 1) * HEAD_WIDTH
-        both = pick(wanted, projected[:, start : start + 2 * HEAD_WIDTH])
-        spread.append(jnp.concatenate([both[:, :HEAD_WIDTH], both[:, HEAD_WIDTH:]], axis=0))
-    width = projected.shape[1]
-    beside = jnp.concatenate(spread, axis=1)
-    slot = lax.broadcasted_iota(jnp.int32, (capacity, rows), 0)
-    for d, out in enumerate(outs):
-        out[:, :width] = pick((seq ^ d) * capacity + slot, projected)
-        out[:, width:] = beside
+        first = count * capacity + h * spread
+        for i in range(2):
+            start = (3 * h + 1 + i) * HEAD_WIDTH
+            piece = routed[first : first + spread, start : start + HEAD_WIDTH]
+            for out in outs:
+                span = slice(width + h * HEAD_WIDTH, width + (h + 1) * HEAD_WIDTH)
+                out[i * spread : (i + 1) * spread, span] = piece
 
 
 def attend_body(count, offsets, *refs):
@@ -364,30 +382,28 @@
     residue = lax.broadcasted_iota(jnp.int32, (1, out.shape[1]), 1) % DILATION_STEP
     scale_factor = HEAD_WIDTH ** (-0.5)
 
-    def branch(query, key, value, mask):
+    local = out.shape[1]
+    for h in range(heads):
+        query, key, value = (
+            rows[:, pl.ds((3 * h + i) * HEAD_WIDTH, HEAD_WIDTH)] for i in range(3)
+        )
+        span = slice(h * HEAD_WIDTH, (h + 1) * HEAD_WIDTH)
+        keys = jnp.concatenate([key, far_keys[:, span]], axis=0)
+        values = jnp.concatenate([value, far_values[:, span]], axis=0)
         scores = lax.dot_general(
-            key, query, (((1,), (1,)), ((), ())), preferred_element_type=jnp.float32
+            keys, query, (((1,), (1,)), ((), ())), preferred_element_type=jnp.float32
         )
         weights = jnp.exp(scores * scale_factor)
-        if mask is not None:
-            weights = jnp.where(mask, weights, 0.0)
+        dilated = jnp.where(residue == offsets[h], weights[local:], 0.0)
+        weights = jnp.concatenate([weights[:local], dilated], axis=0)
         numer = lax.dot_general(
-            value,
+            values,
             weights.astype(jnp.bfloat16),
             (((0,), (0,)), ((), ())),
             preferred_element_type=jnp.float32,
         )
-        return numer, jnp.sum(weights, axis=0, keepdims=True)
-
-    for h in range(heads):
-        query, key, value = (
-            rows[:, pl.ds((3 * h + i) * HEAD_WIDTH, HEAD_WIDTH)] for i in range(3)
-        )
-        span = slice(h * HEAD_WIDTH, (h + 1) * HEAD_WIDTH)
-        near_num, near_den = branch(query, key, value, None)
-        mask = residue == offsets[h]
-        far_num, far_den = branch(query, far_keys[:, span], far_values[:, span], mask)
-        out[span, :] = ((near_num + far_num) / (near_den + far_den)).astype(jnp.bfloat16)
+        denom = jnp.sum(weights, axis=0, keepdims=True)
+        out[span, :] = (numer / denom).astype(jnp.bfloat16)
 
 
 def spread_mp(own, beside=None):
@@ -410,16 +426,18 @@
     bf16 = jnp.bfloat16
     vmem, smem = pltpu.VMEM, pltpu.SMEM
 
-    first_out, second_out, quarter = call(
+    first_out, second_out, quarter, normed = call(
         functools.partial(cut_first_body, count),
         [
             ((tile_rows, features + 4 * units), bf16),
             ((tile_rows, features + 2 * units), bf16),
             ((tile_rows, features), bf16),
+            ((tile_rows, D_ENC), bf16),
         ],
-        (tiles, w_gate, w_up),
-        spaces=[pltpu.HBM] * 3,
-        copies=9,
+        (tiles, w_gate, w_up, gain_enc[None, :]),
+        spaces=[pltpu.HBM] * 3 + [vmem],
+        copies=7,
+        scratch=[pltpu.VMEM((tile_rows, D_ENC), bf16)],
         megabytes=57,
     )
     third_out, kept, down_near, down_far = call(
@@ -435,38 +453,41 @@
         copies=8,
         megabytes=57,
     )
-    code = call(
-        functools.partial(code_body, capacity),
-        [((1, tile_rows), jnp.int32)],
-        (counts, dest, dest.reshape(1, tile_rows)),
-        spaces=[smem, vmem, vmem],
+    routes = call(
+        functools.partial(routes_body, count),
+        [((ENCODER_SLOTS + heads * ENCODER_SLOTS // DILATION_STEP, tile_rows), bf16)],
+        (counts, offsets, dest, dest.reshape(1, tile_rows)),
+        spaces=[smem, smem, vmem, vmem],
     )[0]
 
     arrived = swap(first_out, "seq", 1), swap(second_out, "seq", 2), swap(quarter, "seq", 3)
     from_far = swap(down_far, "mp", 2)
-    arrived, from_far, code = lax.optimization_barrier((arrived, from_far, code))
-    own, columns, *down_send = call(
+    arrived, from_far, routes = lax.optimization_barrier((arrived, from_far, routes))
+    own, columns = call(
         restack_body,
         [
             ((count - 1, tile_rows, features), bf16),
             ((tile_rows, 2 * units), bf16),
-            ((2, units // 2, features), bf16),
-            ((2, units, features), bf16),
         ],
-        (*arrived, down_near, from_far),
-    )
-    third_out, _ = lax.optimization_barrier((third_out, own))
-    third, others, far, near = lax.optimization_barrier(
+        arrived,
+    )
+    third_out, down_near, _ = lax.optimization_barrier((third_out, down_near, own))
+    down_send = call(
+        pair_body,
+        [((2, units // 2, features), bf16), ((2, units, features), bf16)],
+        (down_near, from_far),
+    )
+    third, others, far, near, down_send = lax.optimization_barrier(
         (
             swap(third_out, "seq", 3),
             swap(columns, "groups", 1),
             swap(own, "mp", 2),
             swap(own, "mp", 1),
+            down_send,
         )
     )
     halves = columns, others, third, swap(third, "groups", 1)
     spread = far, near, swap(far, "mp", 1)
-    down_send, _ = lax.optimization_barrier((down_send, far))
     parts = []
     for j in range(2):
         perm = []
@@ -476,15 +497,13 @@
                 user = (s ^ 2 * k) if k < 2 else (s + 2 * k - 5) % count
                 perm.append((s * mp_size + m, user * mp_size + k))
         parts.append(lax.ppermute(down_send[j], ("seq", "mp"), perm))
-    (tiles, *spread), parts[0] = lax.optimization_barrier(((tiles, *spread), parts[0]))
+    spread, parts[0] = lax.optimization_barrier((spread, parts[0]))
     hidden = call(
         functools.partial(hidden_body, count),
         [((count * tile_rows, units), bf16)],
-        (gain_enc[None, :], tiles, own, *spread, kept, arrived[0], *halves),
+        (normed, own, *spread, kept, arrived[0], *halves),
         scratch=[
-            pltpu.VMEM((count, count, tile_rows, depth), bf16),
-            pltpu.VMEM((4, depth, units), bf16),
-            pltpu.VMEM((depth, 2 * units), bf16),
+            pltpu.VMEM((2, count, depth, units), bf16),
         ],
     )[0]
     even, odd = parts
@@ -513,8 +532,7 @@
     packages = call(
         functools.partial(project_body, count),
         [((capacity, 4 * heads * HEAD_WIDTH), bf16)] * count,
-        (offsets, gain_slide[None, :], code, w_qkv.T, embedded_cols, *spread_mp(embedded_cols)),
-        spaces=[smem] + [vmem] * 7,
+        (gain_slide[None, :], routes, w_qkv.T, embedded_cols, *spread_mp(embedded_cols)),
     )
     packages = [packages[0]] + [swap(packages[d], "seq", d) for d in range(1, count)]
     return call(

time: 110 us -> 111 us (level)
  waiting for transfers between devices: 64.3 us -> 62.8 us
  local copies, waits for them, and re-layouts: 1.12 us -> 2.41 us
    ppermute x20, waiting for transfers between devices: 51.8 us -> 50.3 us  [swap(): return lax.ppermute(array, axis, [(i, i ^ distance) for i in range(size)])]
    broadcast_in_dim x1, local copies, waits for them, and re-layouts: 0.01 us -> 1.29 us  [split_hidden_plan(): gain_enc[None, :]]
    pallas_call x8 -> x9, Pallas kernels: 12.8 us -> 12.8 us  [call(): pl.pallas_call(body, out_shape=[jax.ShapeDtypeStruct(shape, kind) for sha...]
  transfers between devices with their start and end apart: 25 -> 25, of which waited for: 13 -> 13; matrix products, arithmetic and copies ran while one was open for 0% -> 0% of each run, Pallas kernels for 2% -> 3%
where the time goes in v6:
time: 111 us
  waiting for transfers between devices  62.8 us (57%)
  starting transfers between devices  30.8 us (28%)
  Pallas kernels  12.8 us (12%)
  local copies, waits for them, and re-layouts  2.41 us (2%)
    ppermute x20, waiting for transfers between devices, swap(): return lax.ppermute(array, axis, [(i, i ^ distance) for i in range(size)])  50.3 us
    ppermute x20, starting transfers between devices, swap(): return lax.ppermute(array, axis, [(i, i ^ distance) for i in range(size)])  25 us
    pallas_call x9, Pallas kernels, call(): pl.pallas_call(body, out_shape=[jax.ShapeDtypeStruct(shape, kind) for sha...  12.8 us
    ppermute x3, waiting for transfers between devices, to_owner(): return lax.ppermute(part, ('seq', 'mp'), perm)  12.5 us
    ppermute x3, starting transfers between devices, to_owner(): return lax.ppermute(part, ('seq', 'mp'), perm)  4.59 us
  transfers between devices with their start and end apart: 25, of which 13 were waited for; matrix products, arithmetic and copies ran while one was open for 0% of the time, Pallas kernels for 3%

profile of v6, /device:TPU:0, one launch (start us, length us, event | category | flops | bytes accessed | tf_op | source)
XLA Modules:
  0.0 110.7 jit_solution(8562756225125220014)
XLA Ops:
  0.0 1.3 %broadcast_in_dim.7.gain = f32[1,1536]{1,0:T(1,128)} reshape(f32[1536]{0:T(1024)} %param.13) | data formatting | bytes 12288 | tf_op jit(solution)/shard_map/broadcast_in_dim | solution.py:437
  1.3 3.3 %shard_map.100 = (bf16[192,1408]{1,0:T(8,128)(2,1)}, bf16[192,896]{1,0:T(8,128)(2,1)}, bf16[192,384]{1,0:T(8,128)(2,1)}, bf16[192,1536]{1,0:T(8,128)(2,1)}) custom-call(bf16[192,1536]{1,0:T(8,128)(2,1)} %tiles.1, bf16[384,1024]{1,0:T(8,128)(2,1)} %w_gate.3, bf16[384,1024]{1,0:T(8,128)(2,1)} %w_up.3, f32[1,1536]{1,0:T(1,128)} %broadcast_in_dim.7.gain), custom_call_target="tpu_custom_call" | custom-call | tf_op jit(solution)/shard_map/pallas_call | solution.py:151
  4.6 3.1 %collective-permute-start = (bf16[192,1408]{1,0:T(8,128)(2,1)}, bf16[192,1408]{1,0:T(8,128)(2,1)S(1)}, u32[]{:S(2)}, u32[]{:S(2)}) collective-permute-start(bf16[192,1408]{1,0:T(8,128)(2,1)} %get-tuple-element.43), channel_id=1, source_target_pairs={{0,4},{4,0},{8,12},{12,8},{1,5},{5,1},{9,13},{13,9},{2,6},{6,2},{1... | collective-permute-start | bytes 1622024 | tf_op jit(solution)/shard_map/ppermute | solution.py:139
  7.7 2.6 %collective-permute-start.1 = (bf16[192,896]{1,0:T(8,128)(2,1)}, bf16[192,896]{1,0:T(8,128)(2,1)S(1)}, u32[]{:S(2)}, u32[]{:S(2)}) collective-permute-start(bf16[192,896]{1,0:T(8,128)(2,1)} %get-tuple-element.44), channel_id=1, source_target_pairs={{0,8},{4,12},{8,0},{12,4},{1,9},{5,13},{9,1},{13,5},{2,10},{6,14},... | collective-permute-start | bytes 1032200 | tf_op jit(solution)/shard_map/ppermute | solution.py:139
  10.3 2.4 %shard_map.101 = (bf16[192,512]{1,0:T(8,128)(2,1)}, bf16[384,512]{1,0:T(8,128)(2,1)}, bf16[384,384]{1,0:T(8,128)(2,1)}, bf16[384,384]{1,0:T(8,128)(2,1)}) custom-call(bf16[384,1024]{1,0:T(8,128)(2,1)} %w_gate.3, bf16[384,1024]{1,0:T(8,128)(2,1)} %w_up.3, bf16[1024,384]{1,0:T(8,128)(2,1)} %w_down.1), custom_call_target="tpu_custom_call" | custom-call | tf_op jit(solution)/shard_map/pallas_call | solution.py:151
  12.8 1.6 %collective-permute-start.3 = (bf16[384,384]{1,0:T(8,128)(2,1)}, bf16[384,384]{1,0:T(8,128)(2,1)S(1)}, u32[]{:S(2)}, u32[]{:S(2)}) collective-permute-start(bf16[384,384]{1,0:T(8,128)(2,1)} %get-tuple-element.46), channel_id=1, source_target_pairs={{0,2},{1,3},{2,0},{3,1},{4,6},{5,7},{6,4},{7,5},{8,10},{9,11},{10,... | collective-permute-start | bytes 884744 | tf_op jit(solution)/shard_map/ppermute | solution.py:139
  14.3 0.2 collective-permute-start.2
  14.5 0.1 copy.11.dest
  15.3 0.7 shard_map.102.routes
  16.0 16.9 %collective-permute-done.2.third = bf16[192,384]{1,0:T(8,128)(2,1)S(1)} collective-permute-done((bf16[192,384]{1,0:T(8,128)(2,1)S(1)}, bf16[192,384]{1,0:T(8,128)(2,1)S(1)}, u32[]{:S(2)}, u32[]{:S(2)}) %collective-permute-start.2) | collective-permute-done | bytes 147488 | tf_op jit(solution)/shard_map/ppermute | solution.py:139
  32.9 0.1 shard_map.103
  33.0 1.6 %collective-permute-start.6 = (bf16[3,192,384]{2,1,0:T(8,128)(2,1)S(1)}, bf16[3,192,384]{2,1,0:T(8,128)(2,1)S(1)}, u32[]{:S(2)}, u32[]{:S(2)}) collective-permute-start(bf16[3,192,384]{2,1,0:T(8,128)(2,1)S(1)} %get-tuple-element.52.own), channel_id=1, source_target_pairs={{0,2},{1,3},{2,0},{3,1},{4,6},{5,7},{6,4},{7,5},{8,10},{9,11},{10,... | collective-permute-start | bytes 1327112 | tf_op jit(solution)/shard_map/ppermute | solution.py:139
  34.6 1.6 %collective-permute-start.4 = (bf16[192,512]{1,0:T(8,128)(2,1)}, bf16[192,512]{1,0:T(8,128)(2,1)S(1)}, u32[]{:S(2)}, u32[]{:S(2)}) collective-permute-start(bf16[192,512]{1,0:T(8,128)(2,1)} %get-tuple-element.55), channel_id=1, source_target_pairs={{0,12},{4,8},{8,4},{12,0},{1,13},{5,9},{9,5},{13,1},{2,14},{6,10},... | collective-permute-start | bytes 589832 | tf_op jit(solution)/shard_map/ppermute | solution.py:139
  36.1 1.5 %collective-permute-start.5 = (bf16[192,512]{1,0:T(8,128)(2,1)S(1)}, bf16[192,512]{1,0:T(8,128)(2,1)S(1)}, u32[]{:S(2)}, u32[]{:S(2)}) collective-permute-start(bf16[192,512]{1,0:T(8,128)(2,1)S(1)} %get-tuple-element.56.refs_0_), channel_id=1, source_target_pairs={{0,16},{16,0},{1,17},{17,1},{2,18},{18,2},{3,19},{19,3},{4,20},{20... | collective-permute-start | bytes 589832 | tf_op jit(solution)/shard_map/ppermute | solution.py:139
  37.6 1.0 copy-done.3
  38.6 0.1 shard_map.104
  38.7 5.3 %collective-permute-done.4.refs_2_ = bf16[192,512]{1,0:T(8,128)(2,1)S(1)} collective-permute-done((bf16[192,512]{1,0:T(8,128)(2,1)}, bf16[192,512]{1,0:T(8,128)(2,1)S(1)}, u32[]{:S(2)}, u32[]{:S(2)}) %collective-permute-start.4) | collective-permute-done | bytes 196640 | tf_op jit(solution)/shard_map/ppermute | solution.py:139
  44.0 0.1 collective-permute-done.6.far
  44.1 0.7 collective-permute-start.9
  44.8 1.6 %collective-permute-start.10 = (bf16[192,512]{1,0:T(8,128)(2,1)S(1)}, bf16[192,512]{1,0:T(8,128)(2,1)S(1)}, u32[]{:S(2)}, u32[]{:S(2)}) collective-permute-start(bf16[192,512]{1,0:T(8,128)(2,1)S(1)} %collective-permute-done.4.refs_2_), channel_id=1, source_target_pairs={{0,16},{16,0},{1,17},{17,1},{2,18},{18,2},{3,19},{19,3},{4,20},{20... | collective-permute-start | bytes 589832 | tf_op jit(solution)/shard_map/ppermute | solution.py:139
  46.4 4.1 %collective-permute-done.10.refs_3_ = bf16[192,512]{1,0:T(8,128)(2,1)S(1)} collective-permute-done((bf16[192,512]{1,0:T(8,128)(2,1)S(1)}, bf16[192,512]{1,0:T(8,128)(2,1)S(1)}, u32[]{:S(2)}, u32[]{:S(2)}) %collective-permute-start.10) | collective-permute-done | bytes 196640 | tf_op jit(solution)/shard_map/ppermute | solution.py:139
  50.5 1.9 %shard_map.105.own = bf16[768,256]{1,0:T(8,128)(2,1)S(1)} custom-call(bf16[192,1536]{1,0:T(8,128)(2,1)S(1)} %copy-done.1, bf16[3,192,384]{2,1,0:T(8,128)(2,1)S(1)} %get-tuple-element.52.own, bf16[3,192,384]{2,1,0:T(8,128)(2,1)S(1)} %collective-permute-done.6.far, bf16[3,192,384]{2,1,0:T(8,128)(2,1)S(1)} %collective-permute-done.7.near, ...), custom_call_target="tpu_custom_call" | custom-call | tf_op jit(solution)/shard_map/pallas_call | solution.py:151
  52.4 0.0 copy-start.6
  52.5 5.0 %collective-permute-start.11 = (bf16[768,256]{1,0:T(8,128)(2,1)S(1)}, bf16[768,256]{1,0:T(8,128)(2,1)S(1)}, u32[]{:S(2)}, u32[]{:S(2)}) collective-permute-start(bf16[768,256]{1,0:T(8,128)(2,1)S(1)} %shard_map.105.own), channel_id=1, source_target_pairs={{0,2},{1,3},{2,0},{3,1},{4,6},{5,7},{6,4},{7,5},{8,10},{9,11},{10,... | collective-permute-start | bytes 1179656 | tf_op jit(solution)/shard_map/ppermute | solution.py:139
  57.5 1.5 %collective-permute-start.13 = (bf16[2,128,384]{2,1,0:T(8,128)(2,1)S(1)}, bf16[2,128,384]{2,1,0:T(8,128)(2,1)S(1)}, u32[]{:S(2)}, u32[]{:S(2)}) collective-permute-start(bf16[2,128,384]{2,1,0:T(8,128)(2,1)S(1)} %collective-permute-done.9.even), channel_id=1, source_target_pairs={{0,16},{16,0},{1,17},{17,1},{2,18},{18,2},{3,19},{19,3},{4,20},{20... | collective-permute-start | bytes 589832 | tf_op jit(solution)/shard_map/ppermute | solution.py:139
  59.0 0.5 collective-permute-start.15
  59.6 5.2 %collective-permute-done.13.even_other = bf16[2,128,384]{2,1,0:T(8,128)(2,1)S(1)} collective-permute-done((bf16[2,128,384]{2,1,0:T(8,128)(2,1)S(1)}, bf16[2,128,384]{2,1,0:T(8,128)(2,1)S(1)}, u32[]{:S(2)}, u32[]{:S(2)}) %collective-permute-start.13) | collective-permute-done | bytes 196640 | tf_op jit(solution)/shard_map/ppermute | solution.py:139
  64.8 2.6 %collective-permute-done.11.far = bf16[768,256]{1,0:T(8,128)(2,1)S(1)} collective-permute-done((bf16[768,256]{1,0:T(8,128)(2,1)S(1)}, bf16[768,256]{1,0:T(8,128)(2,1)S(1)}, u32[]{:S(2)}, u32[]{:S(2)}) %collective-permute-start.11) | collective-permute-done | bytes 393248 | tf_op jit(solution)/shard_map/ppermute | solution.py:139
  67.4 0.1 collective-permute-start.14
  67.5 1.6 %collective-permute-done.14.near_far = bf16[768,256]{1,0:T(8,128)(2,1)S(1)} collective-permute-done((bf16[768,256]{1,0:T(8,128)(2,1)S(1)}, bf16[768,256]{1,0:T(8,128)(2,1)S(1)}, u32[]{:S(2)}, u32[]{:S(2)}) %collective-permute-start.14) | collective-permute-done | bytes 393248 | tf_op jit(solution)/shard_map/ppermute | solution.py:139
  69.1 1.0 shard_map.106
  70.1 0.9 collective-permute-start.16
  71.0 3.5 %collective-permute-start.17 = (bf16[192,384]{1,0:T(8,128)(2,1)S(1)}, bf16[192,384]{1,0:T(8,128)(2,1)S(1)}, u32[]{:S(2)}, u32[]{:S(2)}) collective-permute-start(bf16[192,384]{1,0:T(8,128)(2,1)S(1)} %get-tuple-element.75), channel_id=1, source_target_pairs={{0,14},{1,15},{2,13},{3,12},{4,11},{5,10},{6,8},{7,9},{8,6},{9,7},... | collective-permute-start | bytes 442376 | tf_op jit(solution)/shard_map/ppermute | solution.py:524
  74.6 0.1 collective-permute-start.18
  74.7 7.9 %collective-permute-done.16 = bf16[192,384]{1,0:T(8,128)(2,1)S(1)} collective-permute-done((bf16[192,384]{1,0:T(8,128)(2,1)S(1)}, bf16[192,384]{1,0:T(8,128)(2,1)S(1)}, u32[]{:S(2)}, u32[]{:S(2)}) %collective-permute-start.16) | collective-permute-done | bytes 147488 | tf_op jit(solution)/shard_map/ppermute | solution.py:524
  82.6 4.6 %collective-permute-done.18 = bf16[192,384]{1,0:T(8,128)(2,1)S(1)} collective-permute-done((bf16[192,384]{1,0:T(8,128)(2,1)S(1)}, bf16[192,384]{1,0:T(8,128)(2,1)S(1)}, u32[]{:S(2)}, u32[]{:S(2)}) %collective-permute-start.18) | collective-permute-done | bytes 147488 | tf_op jit(solution)/shard_map/ppermute | solution.py:524
  87.2 1.0 add_convert_fusion.own
  88.2 0.1 collective-permute-start.19
  88.3 0.2 collective-permute-start.20
  88.5 5.7 %collective-permute-done.19.far = bf16[192,384]{1,0:T(8,128)(2,1)S(1)} collective-permute-done((bf16[192,384]{1,0:T(8,128)(2,1)S(1)}, bf16[192,384]{1,0:T(8,128)(2,1)S(1)}, u32[]{:S(2)}, u32[]{:S(2)}) %collective-permute-start.19) | collective-permute-done | bytes 147488 | tf_op jit(solution)/shard_map/ppermute | solution.py:139
  94.2 1.3 %collective-permute-done.21.near_far = bf16[192,384]{1,0:T(8,128)(2,1)S(1)} collective-permute-done((bf16[192,384]{1,0:T(8,128)(2,1)S(1)}, bf16[192,384]{1,0:T(8,128)(2,1)S(1)}, u32[]{:S(2)}, u32[]{:S(2)}) %collective-permute-start.21) | collective-permute-done | bytes 147488 | tf_op jit(solution)/shard_map/ppermute | solution.py:139
  95.5 1.3 %shard_map.107 = (bf16[64,768]{1,0:T(8,128)(2,1)S(1)}, bf16[64,768]{1,0:T(8,128)(2,1)S(1)}, bf16[64,768]{1,0:T(8,128)(2,1)S(1)}, bf16[64,768]{1,0:T(8,128)(2,1)S(1)}) custom-call(f32[1,1536]{1,0:T(1,128)S(1)} %broadcast_in_dim.6.gain, bf16[352,192]{1,0:T(8,128)(2,1)S(1)} %shard_map.102.routes, bf16[576,1536]{1,0:T(8,128)(2,1)S(1)} %bitcast.3, ...), custom_call_target="tpu_custom_call" | custom-call | tf_op jit(solution)/shard_map/pallas_call | solution.py:151
  96.8 1.2 %collective-permute-start.22 = (bf16[64,768]{1,0:T(8,128)(2,1)S(1)}, bf16[64,768]{1,0:T(8,128)(2,1)S(1)}, u32[]{:S(2)}, u32[]{:S(2)}) collective-permute-start(bf16[64,768]{1,0:T(8,128)(2,1)S(1)} %get-tuple-element.78), channel_id=1, source_target_pairs={{0,4},{4,0},{8,12},{12,8},{1,5},{5,1},{9,13},{13,9},{2,6},{6,2},{1... | collective-permute-start | bytes 294920 | tf_op jit(solution)/shard_map/ppermute | solution.py:139
  98.0 0.7 collective-permute-start.23
  98.6 2.6 %collective-permute-start.24 = (bf16[64,768]{1,0:T(8,128)(2,1)S(1)}, bf16[64,768]{1,0:T(8,128)(2,1)S(1)}, u32[]{:S(2)}, u32[]{:S(2)}) collective-permute-start(bf16[64,768]{1,0:T(8,128)(2,1)S(1)} %get-tuple-element.80), channel_id=1, source_target_pairs={{0,12},{4,8},{8,4},{12,0},{1,13},{5,9},{9,5},{13,1},{2,14},{6,10},... | collective-permute-start | bytes 294920 | tf_op jit(solution)/shard_map/ppermute | solution.py:139
  101.2 1.5 %collective-permute-done.22.refs_1_ = bf16[64,768]{1,0:T(8,128)(2,1)S(1)} collective-permute-done((bf16[64,768]{1,0:T(8,128)(2,1)S(1)}, bf16[64,768]{1,0:T(8,128)(2,1)S(1)}, u32[]{:S(2)}, u32[]{:S(2)}) %collective-permute-start.22) | collective-permute-done | bytes 98336 | tf_op jit(solution)/shard_map/ppermute | solution.py:139
  102.7 5.9 %collective-permute-done.23.refs_2_ = bf16[64,768]{1,0:T(8,128)(2,1)S(1)} collective-permute-done((bf16[64,768]{1,0:T(8,128)(2,1)S(1)}, bf16[64,768]{1,0:T(8,128)(2,1)S(1)}, u32[]{:S(2)}, u32[]{:S(2)}) %collective-permute-start.23) | collective-permute-done | bytes 98336 | tf_op jit(solution)/shard_map/ppermute | solution.py:139
  108.6 2.2 %shard_map.108 = bf16[192,256]{1,0:T(8,128)(2,1)} custom-call(s32[3]{0:T(128)S(1)} %copy-done.5, bf16[64,768]{1,0:T(8,128)(2,1)S(1)} %get-tuple-element.77.refs_0_, bf16[64,768]{1,0:T(8,128)(2,1)S(1)} %collective-permute-done.22.refs_1_, bf16[64,768]{1,0:T(8,128)(2,1)S(1)} %collective-permute-done.23.refs_2_, bf16[64,768]{1,0:T(8,128)(2,1)S(1)} %collective-permute-done.24.refs_3_), custom_call_target="tpu_custom_call" | custom-call | tf_op jit(solution)/shard_map/pallas_call | solution.py:151
  (31 shorter events, 0.1 us)
Async XLA Ops:
  1.3 13.2 %copy-start.4 = (s32[192,1]{0,1:T(1,128)S(1)}, s32[192,1]{0,1:T(1,128)}, u32[]{:S(2)}) copy-start(s32[192,1]{0,1:T(1,128)} %param.12) | copy-start | bytes 2308
  4.6 9.7 %copy-start.7 = (bf16[192,384]{1,0:T(8,128)(2,1)S(1)}, bf16[192,384]{1,0:T(8,128)(2,1)}, u32[]{:S(2)}) copy-start(bf16[192,384]{1,0:T(8,128)(2,1)} %get-tuple-element.45) | copy-start | bytes 442372
  4.6 10.7 %copy-start.5 = (s32[3]{0:T(128)S(1)}, s32[3]{0:T(128)}, u32[]{:S(2)}) copy-start(s32[3]{0:T(128)} %offsets.3) | copy-start | bytes 40
  4.6 28.3 %collective-permute-start = (bf16[192,1408]{1,0:T(8,128)(2,1)}, bf16[192,1408]{1,0:T(8,128)(2,1)S(1)}, u32[]{:S(2)}, u32[]{:S(2)}) collective-permute-start(bf16[192,1408]{1,0:T(8,128)(2,1)} %get-tuple-element.43), channel_id=1, source_target_pairs={{0,4},{4,0},{8,12},{12,8},{1,5},{5,1},{9,13},{13,9},{2,6},{6,2},{1... | collective-permute-start | bytes 1622024 | tf_op jit(solution)/shard_map/ppermute | solution.py:139
  7.7 42.8 %copy-start.1 = (bf16[192,1536]{1,0:T(8,128)(2,1)S(1)}, bf16[192,1536]{1,0:T(8,128)(2,1)}, u32[]{:S(2)}) copy-start(bf16[192,1536]{1,0:T(8,128)(2,1)} %get-tuple-element.48.normed) | copy-start | bytes 1769476
  7.7 25.2 %collective-permute-start.1 = (bf16[192,896]{1,0:T(8,128)(2,1)}, bf16[192,896]{1,0:T(8,128)(2,1)S(1)}, u32[]{:S(2)}, u32[]{:S(2)}) collective-permute-start(bf16[192,896]{1,0:T(8,128)(2,1)} %get-tuple-element.44), channel_id=1, source_target_pairs={{0,8},{4,12},{8,0},{12,4},{1,9},{5,13},{9,1},{13,5},{2,10},{6,14},... | collective-permute-start | bytes 1032200 | tf_op jit(solution)/shard_map/ppermute | solution.py:139
  12.7 37.8 %copy-start.2 = (bf16[384,512]{1,0:T(8,128)(2,1)S(1)}, bf16[384,512]{1,0:T(8,128)(2,1)}, u32[]{:S(2)}) copy-start(bf16[384,512]{1,0:T(8,128)(2,1)} %get-tuple-element.67.kept) | copy-start | bytes 1179652
  12.8 20.2 %collective-permute-start.3 = (bf16[384,384]{1,0:T(8,128)(2,1)}, bf16[384,384]{1,0:T(8,128)(2,1)S(1)}, u32[]{:S(2)}, u32[]{:S(2)}) collective-permute-start(bf16[384,384]{1,0:T(8,128)(2,1)} %get-tuple-element.46), channel_id=1, source_target_pairs={{0,2},{1,3},{2,0},{3,1},{4,6},{5,7},{6,4},{7,5},{8,10},{9,11},{10,... | collective-permute-start | bytes 884744 | tf_op jit(solution)/shard_map/ppermute | solution.py:139
  14.3 18.6 %collective-permute-start.2 = (bf16[192,384]{1,0:T(8,128)(2,1)S(1)}, bf16[192,384]{1,0:T(8,128)(2,1)S(1)}, u32[]{:S(2)}, u32[]{:S(2)}) collective-permute-start(bf16[192,384]{1,0:T(8,128)(2,1)S(1)} %copy-done.7), channel_id=1, source_target_pairs={{0,12},{4,8},{8,4},{12,0},{1,13},{5,9},{9,5},{13,1},{2,14},{6,10},... | collective-permute-start | bytes 442376 | tf_op jit(solution)/shard_map/ppermute | solution.py:139
  33.0 11.1 %collective-permute-start.6 = (bf16[3,192,384]{2,1,0:T(8,128)(2,1)S(1)}, bf16[3,192,384]{2,1,0:T(8,128)(2,1)S(1)}, u32[]{:S(2)}, u32[]{:S(2)}) collective-permute-start(bf16[3,192,384]{2,1,0:T(8,128)(2,1)S(1)} %get-tuple-element.52.own), channel_id=1, source_target_pairs={{0,2},{1,3},{2,0},{3,1},{4,6},{5,7},{6,4},{7,5},{8,10},{9,11},{10,... | collective-permute-start | bytes 1327112 | tf_op jit(solution)/shard_map/ppermute | solution.py:139
  34.6 9.5 %collective-permute-start.7 = (bf16[3,192,384]{2,1,0:T(8,128)(2,1)S(1)}, bf16[3,192,384]{2,1,0:T(8,128)(2,1)S(1)}, u32[]{:S(2)}, u32[]{:S(2)}) collective-permute-start(bf16[3,192,384]{2,1,0:T(8,128)(2,1)S(1)} %get-tuple-element.52.own), channel_id=1, source_target_pairs={{0,1},{1,0},{2,3},{3,2},{4,5},{5,4},{6,7},{7,6},{8,9},{9,8},{10,11... | collective-permute-start | bytes 1327112 | tf_op jit(solution)/shard_map/ppermute | solution.py:139
  34.6 9.4 %collective-permute-start.4 = (bf16[192,512]{1,0:T(8,128)(2,1)}, bf16[192,512]{1,0:T(8,128)(2,1)S(1)}, u32[]{:S(2)}, u32[]{:S(2)}) collective-permute-start(bf16[192,512]{1,0:T(8,128)(2,1)} %get-tuple-element.55), channel_id=1, source_target_pairs={{0,12},{4,8},{8,4},{12,0},{1,13},{5,9},{9,5},{13,1},{2,14},{6,10},... | collective-permute-start | bytes 589832 | tf_op jit(solution)/shard_map/ppermute | solution.py:139
  36.1 7.9 %collective-permute-start.5 = (bf16[192,512]{1,0:T(8,128)(2,1)S(1)}, bf16[192,512]{1,0:T(8,128)(2,1)S(1)}, u32[]{:S(2)}, u32[]{:S(2)}) collective-permute-start(bf16[192,512]{1,0:T(8,128)(2,1)S(1)} %get-tuple-element.56.refs_0_), channel_id=1, source_target_pairs={{0,16},{16,0},{1,17},{17,1},{2,18},{18,2},{3,19},{19,3},{4,20},{20... | collective-permute-start | bytes 589832 | tf_op jit(solution)/shard_map/ppermute | solution.py:139
  37.6 1.0 copy-start.3
  44.1 2.3 %collective-permute-start.8 = (bf16[3,192,384]{2,1,0:T(8,128)(2,1)S(1)}, bf16[3,192,384]{2,1,0:T(8,128)(2,1)S(1)}, u32[]{:S(2)}, u32[]{:S(2)}) collective-permute-start(bf16[3,192,384]{2,1,0:T(8,128)(2,1)S(1)} %collective-permute-done.6.far), channel_id=1, source_target_pairs={{0,1},{1,0},{2,3},{3,2},{4,5},{5,4},{6,7},{7,6},{8,9},{9,8},{10,11... | collective-permute-start | bytes 1327112 | tf_op jit(solution)/shard_map/ppermute | solution.py:139
  44.1 2.3 %collective-permute-start.9 = (bf16[2,128,384]{2,1,0:T(8,128)(2,1)S(1)}, bf16[2,128,384]{2,1,0:T(8,128)(2,1)S(1)}, u32[]{:S(2)}, u32[]{:S(2)}) collective-permute-start(bf16[2,128,384]{2,1,0:T(8,128)(2,1)S(1)} %get-tuple-element.63), channel_id=1, source_target_pairs={{0,0},{1,9},{2,14},{3,7},{4,4},{5,13},{6,2},{7,11},{8,8},{9,1},{10... | collective-permute-start | bytes 589832 | tf_op jit(solution)/shard_map/ppermute | solution.py:499
  44.8 5.7 %collective-permute-start.10 = (bf16[192,512]{1,0:T(8,128)(2,1)S(1)}, bf16[192,512]{1,0:T(8,128)(2,1)S(1)}, u32[]{:S(2)}, u32[]{:S(2)}) collective-permute-start(bf16[192,512]{1,0:T(8,128)(2,1)S(1)} %collective-permute-done.4.refs_2_), channel_id=1, source_target_pairs={{0,16},{16,0},{1,17},{17,1},{2,18},{18,2},{3,19},{19,3},{4,20},{20... | collective-permute-start | bytes 589832 | tf_op jit(solution)/shard_map/ppermute | solution.py:139
  52.4 41.7 %copy-start.6 = (f32[1536]{0:T(1024)S(1)}, f32[1536]{0:T(1024)}, u32[]{:S(2)}) copy-start(f32[1536]{0:T(1024)} %param.17) | copy-start | bytes 18436
  52.5 43.1 %copy-start = (bf16[1536,576]{0,1:T(8,128)(2,1)S(1)}, bf16[1536,576]{0,1:T(8,128)(2,1)}, u32[]{:S(2)}) copy-start(bf16[1536,576]{0,1:T(8,128)(2,1)} %param.18) | copy-start | bytes 5308420
  52.5 14.9 %collective-permute-start.11 = (bf16[768,256]{1,0:T(8,128)(2,1)S(1)}, bf16[768,256]{1,0:T(8,128)(2,1)S(1)}, u32[]{:S(2)}, u32[]{:S(2)}) collective-permute-start(bf16[768,256]{1,0:T(8,128)(2,1)S(1)} %shard_map.105.own), channel_id=1, source_target_pairs={{0,2},{1,3},{2,0},{3,1},{4,6},{5,7},{6,4},{7,5},{8,10},{9,11},{10,... | collective-permute-start | bytes 1179656 | tf_op jit(solution)/shard_map/ppermute | solution.py:139
  57.5 7.3 %collective-permute-start.13 = (bf16[2,128,384]{2,1,0:T(8,128)(2,1)S(1)}, bf16[2,128,384]{2,1,0:T(8,128)(2,1)S(1)}, u32[]{:S(2)}, u32[]{:S(2)}) collective-permute-start(bf16[2,128,384]{2,1,0:T(8,128)(2,1)S(1)} %collective-permute-done.9.even), channel_id=1, source_target_pairs={{0,16},{16,0},{1,17},{17,1},{2,18},{18,2},{3,19},{19,3},{4,20},{20... | collective-permute-start | bytes 589832 | tf_op jit(solution)/shard_map/ppermute | solution.py:139
  59.0 8.5 %collective-permute-start.15 = (bf16[2,256,384]{2,1,0:T(8,128)(2,1)S(1)}, bf16[2,256,384]{2,1,0:T(8,128)(2,1)S(1)}, u32[]{:S(2)}, u32[]{:S(2)}) collective-permute-start(bf16[2,256,384]{2,1,0:T(8,128)(2,1)S(1)} %get-tuple-element.72), channel_id=1, source_target_pairs={{0,9},{1,0},{2,7},{3,14},{4,13},{5,4},{6,11},{7,2},{8,1},{9,8},{10... | collective-permute-start | bytes 1179656 | tf_op jit(solution)/shard_map/ppermute | solution.py:499
  59.6 7.9 %collective-permute-start.12 = (bf16[768,256]{1,0:T(8,128)(2,1)S(1)}, bf16[768,256]{1,0:T(8,128)(2,1)S(1)}, u32[]{:S(2)}, u32[]{:S(2)}) collective-permute-start(bf16[768,256]{1,0:T(8,128)(2,1)S(1)} %shard_map.105.own), channel_id=1, source_target_pairs={{0,1},{1,0},{2,3},{3,2},{4,5},{5,4},{6,7},{7,6},{8,9},{9,8},{10,11... | collective-permute-start | bytes 1179656 | tf_op jit(solution)/shard_map/ppermute | solution.py:139
  67.4 1.7 %collective-permute-start.14 = (bf16[768,256]{1,0:T(8,128)(2,1)S(1)}, bf16[768,256]{1,0:T(8,128)(2,1)S(1)}, u32[]{:S(2)}, u32[]{:S(2)}) collective-permute-start(bf16[768,256]{1,0:T(8,128)(2,1)S(1)} %collective-permute-done.11.far), channel_id=1, source_target_pairs={{0,1},{1,0},{2,3},{3,2},{4,5},{5,4},{6,7},{7,6},{8,9},{9,8},{10,11... | collective-permute-start | bytes 1179656 | tf_op jit(solution)/shard_map/ppermute | solution.py:139
  70.1 12.5 %collective-permute-start.16 = (bf16[192,384]{1,0:T(8,128)(2,1)S(1)}, bf16[192,384]{1,0:T(8,128)(2,1)S(1)}, u32[]{:S(2)}, u32[]{:S(2)}) collective-permute-start(bf16[192,384]{1,0:T(8,128)(2,1)S(1)} %get-tuple-element.74), channel_id=1, source_target_pairs={{0,9},{1,8},{2,11},{3,10},{4,13},{5,12},{6,15},{7,14},{8,1},{9,0},... | collective-permute-start | bytes 442376 | tf_op jit(solution)/shard_map/ppermute | solution.py:524
  71.0 11.6 %collective-permute-start.17 = (bf16[192,384]{1,0:T(8,128)(2,1)S(1)}, bf16[192,384]{1,0:T(8,128)(2,1)S(1)}, u32[]{:S(2)}, u32[]{:S(2)}) collective-permute-start(bf16[192,384]{1,0:T(8,128)(2,1)S(1)} %get-tuple-element.75), channel_id=1, source_target_pairs={{0,14},{1,15},{2,13},{3,12},{4,11},{5,10},{6,8},{7,9},{8,6},{9,7},... | collective-permute-start | bytes 442376 | tf_op jit(solution)/shard_map/ppermute | solution.py:524
  74.6 12.6 %collective-permute-start.18 = (bf16[192,384]{1,0:T(8,128)(2,1)S(1)}, bf16[192,384]{1,0:T(8,128)(2,1)S(1)}, u32[]{:S(2)}, u32[]{:S(2)}) collective-permute-start(bf16[192,384]{1,0:T(8,128)(2,1)S(1)} %get-tuple-element.76), channel_id=1, source_target_pairs={{0,7},{1,6},{2,4},{3,5},{4,2},{5,3},{6,1},{7,0},{8,15},{9,14},{10,... | collective-permute-start | bytes 442376 | tf_op jit(solution)/shard_map/ppermute | solution.py:524
  88.2 5.9 %collective-permute-start.19 = (bf16[192,384]{1,0:T(8,128)(2,1)S(1)}, bf16[192,384]{1,0:T(8,128)(2,1)S(1)}, u32[]{:S(2)}, u32[]{:S(2)}) collective-permute-start(bf16[192,384]{1,0:T(8,128)(2,1)S(1)} %add_convert_fusion.own), channel_id=1, source_target_pairs={{0,2},{1,3},{2,0},{3,1},{4,6},{5,7},{6,4},{7,5},{8,10},{9,11},{10,... | collective-permute-start | bytes 442376 | tf_op jit(solution)/shard_map/ppermute | solution.py:139
  88.3 5.9 %collective-permute-start.20 = (bf16[192,384]{1,0:T(8,128)(2,1)S(1)}, bf16[192,384]{1,0:T(8,128)(2,1)S(1)}, u32[]{:S(2)}, u32[]{:S(2)}) collective-permute-start(bf16[192,384]{1,0:T(8,128)(2,1)S(1)} %add_convert_fusion.own), channel_id=1, source_target_pairs={{0,1},{1,0},{2,3},{3,2},{4,5},{5,4},{6,7},{7,6},{8,9},{9,8},{10,11... | collective-permute-start | bytes 442376 | tf_op jit(solution)/shard_map/ppermute | solution.py:139
  94.1 1.4 %collective-permute-start.21 = (bf16[192,384]{1,0:T(8,128)(2,1)S(1)}, bf16[192,384]{1,0:T(8,128)(2,1)S(1)}, u32[]{:S(2)}, u32[]{:S(2)}) collective-permute-start(bf16[192,384]{1,0:T(8,128)(2,1)S(1)} %collective-permute-done.19.far), channel_id=1, source_target_pairs={{0,1},{1,0},{2,3},{3,2},{4,5},{5,4},{6,7},{7,6},{8,9},{9,8},{10,11... | collective-permute-start | bytes 442376 | tf_op jit(solution)/shard_map/ppermute | solution.py:139
  96.8 5.9 %collective-permute-start.22 = (bf16[64,768]{1,0:T(8,128)(2,1)S(1)}, bf16[64,768]{1,0:T(8,128)(2,1)S(1)}, u32[]{:S(2)}, u32[]{:S(2)}) collective-permute-start(bf16[64,768]{1,0:T(8,128)(2,1)S(1)} %get-tuple-element.78), channel_id=1, source_target_pairs={{0,4},{4,0},{8,12},{12,8},{1,5},{5,1},{9,13},{13,9},{2,6},{6,2},{1... | collective-permute-start | bytes 294920 | tf_op jit(solution)/shard_map/ppermute | solution.py:139
  98.0 10.6 %collective-permute-start.23 = (bf16[64,768]{1,0:T(8,128)(2,1)S(1)}, bf16[64,768]{1,0:T(8,128)(2,1)S(1)}, u32[]{:S(2)}, u32[]{:S(2)}) collective-permute-start(bf16[64,768]{1,0:T(8,128)(2,1)S(1)} %get-tuple-element.79), channel_id=1, source_target_pairs={{0,8},{4,12},{8,0},{12,4},{1,9},{5,13},{9,1},{13,5},{2,10},{6,14},... | collective-permute-start | bytes 294920 | tf_op jit(solution)/shard_map/ppermute | solution.py:139
  98.6 10.0 %collective-permute-start.24 = (bf16[64,768]{1,0:T(8,128)(2,1)S(1)}, bf16[64,768]{1,0:T(8,128)(2,1)S(1)}, u32[]{:S(2)}, u32[]{:S(2)}) collective-permute-start(bf16[64,768]{1,0:T(8,128)(2,1)S(1)} %get-tuple-element.80), channel_id=1, source_target_pairs={{0,12},{4,8},{8,4},{12,0},{1,13},{5,9},{9,5},{13,1},{2,14},{6,10},... | collective-permute-start | bytes 294920 | tf_op jit(solution)/shard_map/ppermute | solution.py:139

commit v7 on v6

--- a/solution.py
+++ b/solution.py
@@ -193,8 +193,15 @@
     return copies, copy
 
 
+def normalise(rows, part, gain):
+    values = rows[...].astype(jnp.float32)
+    squares = jnp.sum(values * values, axis=1, keepdims=True)
+    inverse = lax.rsqrt(squares * (1.0 / D_ENC) + epsilon)
+    return (part.astype(jnp.float32) * inverse * gain[None, :]).astype(jnp.bfloat16)
+
+
 def cut_first_body(
-    count, tiles, w_gate, w_up, gain, first_out, second_out, quarter, normed, held, sems
+    count, tiles, w_gate, w_up, gain, first_out, second_out, quarter, held, sems
 ):
     seq, mp, group = place()
     copies, copy = copier(sems, group)
@@ -210,13 +217,8 @@
             columns = pl.ds(features + (2 * i + k) * units, units)
             copy(weight.at[span], first_out.at[:, columns])
     copies.pop(0).wait()
-    values = held[...].astype(jnp.float32)
-    squares = jnp.sum(values * values, axis=1, keepdims=True)
-    inverse = lax.rsqrt(squares * (1.0 / D_ENC) + epsilon)
-    normed[...] = (values * inverse * gain[...]).astype(jnp.bfloat16)
     columns = at(mp, features)
-    values = held[:, columns].astype(jnp.float32)
-    own_columns = (values * inverse * gain[:, columns]).astype(jnp.bfloat16)
+    own_columns = normalise(held, held[:, columns], gain[columns])
     second_out[:, :features] = own_columns
     first_out[:, :features] = own_columns
     quarter[...] = own_columns
@@ -224,10 +226,13 @@
         started.wait()
 
 
-def cut_second_body(count, w_gate, w_up, w_down, third_out, kept, near, far, sems):
+def cut_second_body(
+    count, tiles, w_gate, w_up, w_down, gain, third_out, kept, near, far, normed, residual, held, sems
+):
     seq, mp, group = place()
     copies, copy = copier(sems, group)
     half, units = w_gate.shape[0] // 2, w_gate.shape[1] // count
+    copy(tiles, held)
     part = units // 2
     for j, target in ((2, far), (0, near)):
         rows = at(column_user(seq, mp ^ j) * 2 + group, part)
@@ -239,6 +244,9 @@
         copy(w_gate.at[span], third_out.at[:, pl.ds(i * units, units)], w_up.at[span])
     for i, weight in enumerate((w_gate, w_up)):
         copy(weight.at[:, at(seq, units)], kept.at[:, pl.ds(i * units, units)])
+    copies.pop(0).wait()
+    normed[...] = normalise(held, held[...], gain[...])
+    residual[...] = held[:, at(column_block(seq, mp), residual.shape[1])]
     for started in copies:
         started.wait()
 
@@ -316,7 +324,7 @@
         out[pl.ds(d * rows, rows), :] = gated.astype(jnp.bfloat16)
 
 
-def down_body(own, far, near, near_far, even, even_other, odd, *outs):
+def down_body(residual, own, far, near, near_far, even, even_other, odd, *outs):
     _, _, group = place()
     rows = outs[0].shape[0]
     weights = [None, odd[0], None, odd[1]]
@@ -325,12 +333,18 @@
         low, high = jnp.where(group == 0, mine, other), jnp.where(group == 0, other, mine)
         weights[2 * j] = jnp.concatenate([low, high], axis=0)
     for i, out in enumerate(outs):
-        total = 0.0
+        total = residual[...].astype(jnp.float32) if i == 0 else 0.0
         for j, piece in enumerate((own, near, far, near_far)):
             total += jnp.dot(
                 piece[pl.ds(i * rows, rows), :], weights[j], preferred_element_type=jnp.float32
             )
         out[...] = total.astype(out.dtype)
+
+
+def sum_body(own, *refs):
+    parts, out = refs[:-1], refs[-1]
+    total = own[...] + sum(part[...].astype(jnp.float32) for part in parts)
+    out[...] = total.astype(out.dtype)
 
 
 def project_body(count, gain, routes, w_qkv_t, own, far, near, near_far, *outs):
@@ -426,31 +440,33 @@
     bf16 = jnp.bfloat16
     vmem, smem = pltpu.VMEM, pltpu.SMEM
 
-    first_out, second_out, quarter, normed = call(
+    first_out, second_out, quarter = call(
         functools.partial(cut_first_body, count),
         [
             ((tile_rows, features + 4 * units), bf16),
             ((tile_rows, features + 2 * units), bf16),
             ((tile_rows, features), bf16),
-            ((tile_rows, D_ENC), bf16),
         ],
-        (tiles, w_gate, w_up, gain_enc[None, :]),
+        (tiles, w_gate, w_up, gain_enc),
         spaces=[pltpu.HBM] * 3 + [vmem],
         copies=7,
         scratch=[pltpu.VMEM((tile_rows, D_ENC), bf16)],
         megabytes=57,
     )
-    third_out, kept, down_near, down_far = call(
+    third_out, kept, down_near, down_far, normed, residual = call(
         functools.partial(cut_second_body, count),
         [
             ((tile_rows, 2 * units), bf16),
             ((depth, 2 * units), bf16),
             ((3 * units // 2, features), bf16),
             ((3 * units // 2, features), bf16),
+            ((tile_rows, D_ENC), bf16),
+            ((tile_rows, features), bf16),
         ],
-        (w_gate, w_up, w_down),
-        spaces=[pltpu.HBM] * 3,
-        copies=8,
+        (tiles, w_gate, w_up, w_down, gain_enc),
+        spaces=[pltpu.HBM] * 4 + [vmem],
+        scratch=[pltpu.VMEM((tile_rows, D_ENC), bf16)],
+        copies=9,
         megabytes=57,
     )
     routes = call(
@@ -460,7 +476,8 @@
         spaces=[smem, smem, vmem, vmem],
     )[0]
 
-    arrived = swap(first_out, "seq", 1), swap(second_out, "seq", 2), swap(quarter, "seq", 3)
+    second_in, third_in = swap(second_out, "seq", 2), swap(quarter, "seq", 3)
+    arrived = swap(first_out, "seq", 1), second_in, third_in
     from_far = swap(down_far, "mp", 2)
     arrived, from_far, routes = lax.optimization_barrier((arrived, from_far, routes))
     own, columns = call(
@@ -511,7 +528,7 @@
     sums = call(
         down_body,
         [((tile_rows, features), kind) for kind in (jnp.float32, bf16, bf16, bf16)],
-        (hidden, *spread_mp(hidden, even_other), even, even_other, odd),
+        (residual, hidden, *spread_mp(hidden, even_other), even, even_other, odd),
     )
     holder = [0, 2, 1, 3]
 
@@ -524,10 +541,9 @@
         return lax.ppermute(part, ("seq", "mp"), perm)
 
     arrived = [to_owner(sums[d], d) for d in (2, 3, 1)]
-    embedded_cols = (
-        block_at(tiles, column_block(seq, mp), features, 1).astype(jnp.float32)
-        + (sums[0] + sum(part.astype(jnp.float32) for part in arrived))
-    ).astype(bf16)
+    embedded_cols = call(
+        sum_body, [((tile_rows, features), bf16)], (sums[0], *arrived)
+    )[0]
 
     packages = call(
         functools.partial(project_body, count),

time: 111 us -> 108 us (0.973)
  local copies, waits for them, and re-layouts: 2.41 us -> 1.12 us
    broadcast_in_dim x1 -> x0, local copies, waits for them, and re-layouts: 1.29 us -> none  [split_hidden_plan(): gain_enc[None, :]]
    pallas_call x9 -> x10, Pallas kernels: 12.8 us -> 13.6 us  [call(): pl.pallas_call(body, out_shape=[jax.ShapeDtypeStruct(shape, kind) for sha...]
  transfers between devices with their start and end apart: 25 -> 25, of which waited for: 13 -> 13; matrix products, arithmetic and copies ran while one was open for 0% -> 0% of each run, Pallas kernels for 3% -> 4%
where the time goes in v7:
time: 108 us
  waiting for transfers between devices  61.8 us (57%)
  starting transfers between devices  30.9 us (29%)
  Pallas kernels  13.6 us (13%)
  local copies, waits for them, and re-layouts  1.12 us (1%)
    ppermute x20, waiting for transfers between devices, swap(): return lax.ppermute(array, axis, [(i, i ^ distance) for i in range(size)])  49.3 us
    ppermute x20, starting transfers between devices, swap(): return lax.ppermute(array, axis, [(i, i ^ distance) for i in range(size)])  25 us
    pallas_call x10, Pallas kernels, call(): pl.pallas_call(body, out_shape=[jax.ShapeDtypeStruct(shape, kind) for sha...  13.6 us
    ppermute x3, waiting for transfers between devices, to_owner(): return lax.ppermute(part, ('seq', 'mp'), perm)  12.5 us
    ppermute x3, starting transfers between devices, to_owner(): return lax.ppermute(part, ('seq', 'mp'), perm)  4.63 us
  transfers between devices with their start and end apart: 25, of which 13 were waited for; matrix products, arithmetic and copies ran while one was open for 0% of the time, Pallas kernels for 4%

profile of v7, /device:TPU:0, one launch (start us, length us, event | category | flops | bytes accessed | tf_op | source)
XLA Modules:
  0.0 108.2 jit_solution(6737062560604040614)
XLA Ops:
  0.0 3.0 %shard_map.100 = (bf16[192,1408]{1,0:T(8,128)(2,1)}, bf16[192,896]{1,0:T(8,128)(2,1)}, bf16[192,384]{1,0:T(8,128)(2,1)}) custom-call(bf16[192,1536]{1,0:T(8,128)(2,1)} %tiles.3, bf16[384,1024]{1,0:T(8,128)(2,1)} %w_gate.3, bf16[384,1024]{1,0:T(8,128)(2,1)} %w_up.3, f32[1536]{0:T(1024)} %gain.3), custom_call_target="tpu_custom_call" | custom-call | tf_op jit(solution)/shard_map/pallas_call | solution.py:151
  3.0 0.0 copy-start.5
  3.1 0.0 copy-start.6
  3.1 3.1 %collective-permute-start = (bf16[192,1408]{1,0:T(8,128)(2,1)}, bf16[192,1408]{1,0:T(8,128)(2,1)S(1)}, u32[]{:S(2)}, u32[]{:S(2)}) collective-permute-start(bf16[192,1408]{1,0:T(8,128)(2,1)} %get-tuple-element.44), channel_id=1, source_target_pairs={{0,4},{4,0},{8,12},{12,8},{1,5},{5,1},{9,13},{13,9},{2,6},{6,2},{1... | collective-permute-start | bytes 1622024 | tf_op jit(solution)/shard_map/ppermute | solution.py:139
  6.2 2.6 %collective-permute-start.1 = (bf16[192,896]{1,0:T(8,128)(2,1)}, bf16[192,896]{1,0:T(8,128)(2,1)S(1)}, u32[]{:S(2)}, u32[]{:S(2)}) collective-permute-start(bf16[192,896]{1,0:T(8,128)(2,1)} %get-tuple-element.45), channel_id=1, source_target_pairs={{0,8},{4,12},{8,0},{12,4},{1,9},{5,13},{9,1},{13,5},{2,10},{6,14},... | collective-permute-start | bytes 1032200 | tf_op jit(solution)/shard_map/ppermute | solution.py:139
  8.7 3.4 %shard_map.101 = (bf16[192,512]{1,0:T(8,128)(2,1)}, bf16[384,512]{1,0:T(8,128)(2,1)}, bf16[384,384]{1,0:T(8,128)(2,1)}, bf16[384,384]{1,0:T(8,128)(2,1)}, bf16[1...) custom-call(bf16[192,1536]{1,0:T(8,128)(2,1)} %tiles.3, bf16[384,1024]{1,0:T(8,128)(2,1)} %w_gate.3, ...), custom_call_target="tpu_custom_call" | custom-call | tf_op jit(solution)/shard_map/pallas_call | solution.py:151
  12.2 1.6 %collective-permute-start.3 = (bf16[384,384]{1,0:T(8,128)(2,1)}, bf16[384,384]{1,0:T(8,128)(2,1)S(1)}, u32[]{:S(2)}, u32[]{:S(2)}) collective-permute-start(bf16[384,384]{1,0:T(8,128)(2,1)} %get-tuple-element.47), channel_id=1, source_target_pairs={{0,2},{1,3},{2,0},{3,1},{4,6},{5,7},{6,4},{7,5},{8,10},{9,11},{10,... | collective-permute-start | bytes 884744 | tf_op jit(solution)/shard_map/ppermute | solution.py:139
  13.7 0.2 collective-permute-start.2
  14.0 0.1 copy.11.dest
  14.8 0.7 shard_map.102.routes
  15.4 15.9 %collective-permute-done.2.third = bf16[192,384]{1,0:T(8,128)(2,1)S(1)} collective-permute-done((bf16[192,384]{1,0:T(8,128)(2,1)S(1)}, bf16[192,384]{1,0:T(8,128)(2,1)S(1)}, u32[]{:S(2)}, u32[]{:S(2)}) %collective-permute-start.2) | collective-permute-done | bytes 147488 | tf_op jit(solution)/shard_map/ppermute | solution.py:139
  31.4 0.1 shard_map.103
  31.4 1.6 %collective-permute-start.6 = (bf16[3,192,384]{2,1,0:T(8,128)(2,1)S(1)}, bf16[3,192,384]{2,1,0:T(8,128)(2,1)S(1)}, u32[]{:S(2)}, u32[]{:S(2)}) collective-permute-start(bf16[3,192,384]{2,1,0:T(8,128)(2,1)S(1)} %get-tuple-element.54.own), channel_id=1, source_target_pairs={{0,2},{1,3},{2,0},{3,1},{4,6},{5,7},{6,4},{7,5},{8,10},{9,11},{10,... | collective-permute-start | bytes 1327112 | tf_op jit(solution)/shard_map/ppermute | solution.py:139
  33.0 1.6 %collective-permute-start.4 = (bf16[192,512]{1,0:T(8,128)(2,1)}, bf16[192,512]{1,0:T(8,128)(2,1)S(1)}, u32[]{:S(2)}, u32[]{:S(2)}) collective-permute-start(bf16[192,512]{1,0:T(8,128)(2,1)} %get-tuple-element.57), channel_id=1, source_target_pairs={{0,12},{4,8},{8,4},{12,0},{1,13},{5,9},{9,5},{13,1},{2,14},{6,10},... | collective-permute-start | bytes 589832 | tf_op jit(solution)/shard_map/ppermute | solution.py:139
  34.6 1.5 %collective-permute-start.5 = (bf16[192,512]{1,0:T(8,128)(2,1)S(1)}, bf16[192,512]{1,0:T(8,128)(2,1)S(1)}, u32[]{:S(2)}, u32[]{:S(2)}) collective-permute-start(bf16[192,512]{1,0:T(8,128)(2,1)S(1)} %get-tuple-element.58.refs_0_), channel_id=1, source_target_pairs={{0,16},{16,0},{1,17},{17,1},{2,18},{18,2},{3,19},{19,3},{4,20},{20... | collective-permute-start | bytes 589832 | tf_op jit(solution)/shard_map/ppermute | solution.py:139
  36.1 1.0 copy-done.3
  37.0 0.1 shard_map.104
  37.1 5.3 %collective-permute-done.4.refs_2_ = bf16[192,512]{1,0:T(8,128)(2,1)S(1)} collective-permute-done((bf16[192,512]{1,0:T(8,128)(2,1)}, bf16[192,512]{1,0:T(8,128)(2,1)S(1)}, u32[]{:S(2)}, u32[]{:S(2)}) %collective-permute-start.4) | collective-permute-done | bytes 196640 | tf_op jit(solution)/shard_map/ppermute | solution.py:139
  42.4 0.1 collective-permute-done.6.far
  42.5 0.7 collective-permute-start.9
  43.2 1.6 %collective-permute-start.10 = (bf16[192,512]{1,0:T(8,128)(2,1)S(1)}, bf16[192,512]{1,0:T(8,128)(2,1)S(1)}, u32[]{:S(2)}, u32[]{:S(2)}) collective-permute-start(bf16[192,512]{1,0:T(8,128)(2,1)S(1)} %collective-permute-done.4.refs_2_), channel_id=1, source_target_pairs={{0,16},{16,0},{1,17},{17,1},{2,18},{18,2},{3,19},{19,3},{4,20},{20... | collective-permute-start | bytes 589832 | tf_op jit(solution)/shard_map/ppermute | solution.py:139
  44.8 4.1 %collective-permute-done.10.refs_3_ = bf16[192,512]{1,0:T(8,128)(2,1)S(1)} collective-permute-done((bf16[192,512]{1,0:T(8,128)(2,1)S(1)}, bf16[192,512]{1,0:T(8,128)(2,1)S(1)}, u32[]{:S(2)}, u32[]{:S(2)}) %collective-permute-start.10) | collective-permute-done | bytes 196640 | tf_op jit(solution)/shard_map/ppermute | solution.py:139
  49.0 1.9 %shard_map.105.own = bf16[768,256]{1,0:T(8,128)(2,1)S(1)} custom-call(bf16[192,1536]{1,0:T(8,128)(2,1)S(1)} %copy-done.1, bf16[3,192,384]{2,1,0:T(8,128)(2,1)S(1)} %get-tuple-element.54.own, bf16[3,192,384]{2,1,0:T(8,128)(2,1)S(1)} %collective-permute-done.6.far, bf16[3,192,384]{2,1,0:T(8,128)(2,1)S(1)} %collective-permute-done.7.near, ...), custom_call_target="tpu_custom_call" | custom-call | tf_op jit(solution)/shard_map/pallas_call | solution.py:151
  50.9 5.0 %collective-permute-start.11 = (bf16[768,256]{1,0:T(8,128)(2,1)S(1)}, bf16[768,256]{1,0:T(8,128)(2,1)S(1)}, u32[]{:S(2)}, u32[]{:S(2)}) collective-permute-start(bf16[768,256]{1,0:T(8,128)(2,1)S(1)} %shard_map.105.own), channel_id=1, source_target_pairs={{0,2},{1,3},{2,0},{3,1},{4,6},{5,7},{6,4},{7,5},{8,10},{9,11},{10,... | collective-permute-start | bytes 1179656 | tf_op jit(solution)/shard_map/ppermute | solution.py:139
  55.9 1.5 %collective-permute-start.13 = (bf16[2,128,384]{2,1,0:T(8,128)(2,1)S(1)}, bf16[2,128,384]{2,1,0:T(8,128)(2,1)S(1)}, u32[]{:S(2)}, u32[]{:S(2)}) collective-permute-start(bf16[2,128,384]{2,1,0:T(8,128)(2,1)S(1)} %collective-permute-done.9.even), channel_id=1, source_target_pairs={{0,16},{16,0},{1,17},{17,1},{2,18},{18,2},{3,19},{19,3},{4,20},{20... | collective-permute-start | bytes 589832 | tf_op jit(solution)/shard_map/ppermute | solution.py:139
  57.4 0.6 collective-permute-start.15
  58.0 5.2 %collective-permute-done.13.even_other = bf16[2,128,384]{2,1,0:T(8,128)(2,1)S(1)} collective-permute-done((bf16[2,128,384]{2,1,0:T(8,128)(2,1)S(1)}, bf16[2,128,384]{2,1,0:T(8,128)(2,1)S(1)}, u32[]{:S(2)}, u32[]{:S(2)}) %collective-permute-start.13) | collective-permute-done | bytes 196640 | tf_op jit(solution)/shard_map/ppermute | solution.py:139
  63.2 2.5 %collective-permute-done.11.far = bf16[768,256]{1,0:T(8,128)(2,1)S(1)} collective-permute-done((bf16[768,256]{1,0:T(8,128)(2,1)S(1)}, bf16[768,256]{1,0:T(8,128)(2,1)S(1)}, u32[]{:S(2)}, u32[]{:S(2)}) %collective-permute-start.11) | collective-permute-done | bytes 393248 | tf_op jit(solution)/shard_map/ppermute | solution.py:139
  65.8 0.1 collective-permute-start.14
  65.9 1.6 %collective-permute-done.14.near_far = bf16[768,256]{1,0:T(8,128)(2,1)S(1)} collective-permute-done((bf16[768,256]{1,0:T(8,128)(2,1)S(1)}, bf16[768,256]{1,0:T(8,128)(2,1)S(1)}, u32[]{:S(2)}, u32[]{:S(2)}) %collective-permute-start.14) | collective-permute-done | bytes 393248 | tf_op jit(solution)/shard_map/ppermute | solution.py:139
  67.5 1.0 shard_map.106
  68.5 1.0 collective-permute-start.16
  69.5 3.5 %collective-permute-start.17 = (bf16[192,384]{1,0:T(8,128)(2,1)S(1)}, bf16[192,384]{1,0:T(8,128)(2,1)S(1)}, u32[]{:S(2)}, u32[]{:S(2)}) collective-permute-start(bf16[192,384]{1,0:T(8,128)(2,1)S(1)} %get-tuple-element.77), channel_id=1, source_target_pairs={{0,14},{1,15},{2,13},{3,12},{4,11},{5,10},{6,8},{7,9},{8,6},{9,7},... | collective-permute-start | bytes 442376 | tf_op jit(solution)/shard_map/ppermute | solution.py:541
  73.0 0.2 collective-permute-start.18
  73.1 7.9 %collective-permute-done.16.refs_0_ = bf16[192,384]{1,0:T(8,128)(2,1)S(1)} collective-permute-done((bf16[192,384]{1,0:T(8,128)(2,1)S(1)}, bf16[192,384]{1,0:T(8,128)(2,1)S(1)}, u32[]{:S(2)}, u32[]{:S(2)}) %collective-permute-start.16) | collective-permute-done | bytes 147488 | tf_op jit(solution)/shard_map/ppermute | solution.py:541
  81.0 4.6 %collective-permute-done.18.refs_2_ = bf16[192,384]{1,0:T(8,128)(2,1)S(1)} collective-permute-done((bf16[192,384]{1,0:T(8,128)(2,1)S(1)}, bf16[192,384]{1,0:T(8,128)(2,1)S(1)}, u32[]{:S(2)}, u32[]{:S(2)}) %collective-permute-start.18) | collective-permute-done | bytes 147488 | tf_op jit(solution)/shard_map/ppermute | solution.py:541
  85.6 0.1 shard_map.107.own
  85.7 0.1 collective-permute-start.19
  85.8 0.2 collective-permute-start.20
  86.0 5.7 %collective-permute-done.19.far = bf16[192,384]{1,0:T(8,128)(2,1)S(1)} collective-permute-done((bf16[192,384]{1,0:T(8,128)(2,1)S(1)}, bf16[192,384]{1,0:T(8,128)(2,1)S(1)}, u32[]{:S(2)}, u32[]{:S(2)}) %collective-permute-start.19) | collective-permute-done | bytes 147488 | tf_op jit(solution)/shard_map/ppermute | solution.py:139
  91.7 1.3 %collective-permute-done.21.near_far = bf16[192,384]{1,0:T(8,128)(2,1)S(1)} collective-permute-done((bf16[192,384]{1,0:T(8,128)(2,1)S(1)}, bf16[192,384]{1,0:T(8,128)(2,1)S(1)}, u32[]{:S(2)}, u32[]{:S(2)}) %collective-permute-start.21) | collective-permute-done | bytes 147488 | tf_op jit(solution)/shard_map/ppermute | solution.py:139
  93.0 1.3 %shard_map.108 = (bf16[64,768]{1,0:T(8,128)(2,1)S(1)}, bf16[64,768]{1,0:T(8,128)(2,1)S(1)}, bf16[64,768]{1,0:T(8,128)(2,1)S(1)}, bf16[64,768]{1,0:T(8,128)(2,1)S(1)}) custom-call(f32[1,1536]{1,0:T(1,128)S(1)} %broadcast_in_dim.3.gain, bf16[352,192]{1,0:T(8,128)(2,1)S(1)} %shard_map.102.routes, bf16[576,1536]{1,0:T(8,128)(2,1)S(1)} %bitcast.3, ...), custom_call_target="tpu_custom_call" | custom-call | tf_op jit(solution)/shard_map/pallas_call | solution.py:151
  94.3 1.2 %collective-permute-start.22 = (bf16[64,768]{1,0:T(8,128)(2,1)S(1)}, bf16[64,768]{1,0:T(8,128)(2,1)S(1)}, u32[]{:S(2)}, u32[]{:S(2)}) collective-permute-start(bf16[64,768]{1,0:T(8,128)(2,1)S(1)} %get-tuple-element.80), channel_id=1, source_target_pairs={{0,4},{4,0},{8,12},{12,8},{1,5},{5,1},{9,13},{13,9},{2,6},{6,2},{1... | collective-permute-start | bytes 294920 | tf_op jit(solution)/shard_map/ppermute | solution.py:139
  95.4 0.7 collective-permute-start.23
  96.1 2.6 %collective-permute-start.24 = (bf16[64,768]{1,0:T(8,128)(2,1)S(1)}, bf16[64,768]{1,0:T(8,128)(2,1)S(1)}, u32[]{:S(2)}, u32[]{:S(2)}) collective-permute-start(bf16[64,768]{1,0:T(8,128)(2,1)S(1)} %get-tuple-element.82), channel_id=1, source_target_pairs={{0,12},{4,8},{8,4},{12,0},{1,13},{5,9},{9,5},{13,1},{2,14},{6,10},... | collective-permute-start | bytes 294920 | tf_op jit(solution)/shard_map/ppermute | solution.py:139
  98.7 1.5 %collective-permute-done.22.refs_1_ = bf16[64,768]{1,0:T(8,128)(2,1)S(1)} collective-permute-done((bf16[64,768]{1,0:T(8,128)(2,1)S(1)}, bf16[64,768]{1,0:T(8,128)(2,1)S(1)}, u32[]{:S(2)}, u32[]{:S(2)}) %collective-permute-start.22) | collective-permute-done | bytes 98336 | tf_op jit(solution)/shard_map/ppermute | solution.py:139
  100.1 5.9 %collective-permute-done.23.refs_2_ = bf16[64,768]{1,0:T(8,128)(2,1)S(1)} collective-permute-done((bf16[64,768]{1,0:T(8,128)(2,1)S(1)}, bf16[64,768]{1,0:T(8,128)(2,1)S(1)}, u32[]{:S(2)}, u32[]{:S(2)}) %collective-permute-start.23) | collective-permute-done | bytes 98336 | tf_op jit(solution)/shard_map/ppermute | solution.py:139
  106.0 2.2 %shard_map.109 = bf16[192,256]{1,0:T(8,128)(2,1)} custom-call(s32[3]{0:T(128)S(1)} %copy-done.6, bf16[64,768]{1,0:T(8,128)(2,1)S(1)} %get-tuple-element.79.refs_0_, bf16[64,768]{1,0:T(8,128)(2,1)S(1)} %collective-permute-done.22.refs_1_, bf16[64,768]{1,0:T(8,128)(2,1)S(1)} %collective-permute-done.23.refs_2_, bf16[64,768]{1,0:T(8,128)(2,1)S(1)} %collective-permute-done.24.refs_3_), custom_call_target="tpu_custom_call" | custom-call | tf_op jit(solution)/shard_map/pallas_call | solution.py:151
  (32 shorter events, 0.1 us)
Async XLA Ops:
  3.0 10.7 %copy-start.8 = (bf16[192,384]{1,0:T(8,128)(2,1)S(1)}, bf16[192,384]{1,0:T(8,128)(2,1)}, u32[]{:S(2)}) copy-start(bf16[192,384]{1,0:T(8,128)(2,1)} %get-tuple-element.46) | copy-start | bytes 442372
  3.0 10.9 %copy-start.5 = (s32[192,1]{0,1:T(1,128)S(1)}, s32[192,1]{0,1:T(1,128)}, u32[]{:S(2)}) copy-start(s32[192,1]{0,1:T(1,128)} %param.12) | copy-start | bytes 2308
  3.1 11.7 %copy-start.6 = (s32[3]{0:T(128)S(1)}, s32[3]{0:T(128)}, u32[]{:S(2)}) copy-start(s32[3]{0:T(128)} %offsets.3) | copy-start | bytes 40
  3.1 28.3 %collective-permute-start = (bf16[192,1408]{1,0:T(8,128)(2,1)}, bf16[192,1408]{1,0:T(8,128)(2,1)S(1)}, u32[]{:S(2)}, u32[]{:S(2)}) collective-permute-start(bf16[192,1408]{1,0:T(8,128)(2,1)} %get-tuple-element.44), channel_id=1, source_target_pairs={{0,4},{4,0},{8,12},{12,8},{1,5},{5,1},{9,13},{13,9},{2,6},{6,2},{1... | collective-permute-start | bytes 1622024 | tf_op jit(solution)/shard_map/ppermute | solution.py:139
  6.2 25.2 %collective-permute-start.1 = (bf16[192,896]{1,0:T(8,128)(2,1)}, bf16[192,896]{1,0:T(8,128)(2,1)S(1)}, u32[]{:S(2)}, u32[]{:S(2)}) collective-permute-start(bf16[192,896]{1,0:T(8,128)(2,1)} %get-tuple-element.45), channel_id=1, source_target_pairs={{0,8},{4,12},{8,0},{12,4},{1,9},{5,13},{9,1},{13,5},{2,10},{6,14},... | collective-permute-start | bytes 1032200 | tf_op jit(solution)/shard_map/ppermute | solution.py:139
  12.2 36.8 %copy-start.1 = (bf16[192,1536]{1,0:T(8,128)(2,1)S(1)}, bf16[192,1536]{1,0:T(8,128)(2,1)}, u32[]{:S(2)}) copy-start(bf16[192,1536]{1,0:T(8,128)(2,1)} %get-tuple-element.50.normed) | copy-start | bytes 1769476
  12.2 36.8 %copy-start.2 = (bf16[384,512]{1,0:T(8,128)(2,1)S(1)}, bf16[384,512]{1,0:T(8,128)(2,1)}, u32[]{:S(2)}) copy-start(bf16[384,512]{1,0:T(8,128)(2,1)} %get-tuple-element.69.kept) | copy-start | bytes 1179652
  12.2 19.2 %collective-permute-start.3 = (bf16[384,384]{1,0:T(8,128)(2,1)}, bf16[384,384]{1,0:T(8,128)(2,1)S(1)}, u32[]{:S(2)}, u32[]{:S(2)}) collective-permute-start(bf16[384,384]{1,0:T(8,128)(2,1)} %get-tuple-element.47), channel_id=1, source_target_pairs={{0,2},{1,3},{2,0},{3,1},{4,6},{5,7},{6,4},{7,5},{8,10},{9,11},{10,... | collective-permute-start | bytes 884744 | tf_op jit(solution)/shard_map/ppermute | solution.py:139
  13.7 17.6 %collective-permute-start.2 = (bf16[192,384]{1,0:T(8,128)(2,1)S(1)}, bf16[192,384]{1,0:T(8,128)(2,1)S(1)}, u32[]{:S(2)}, u32[]{:S(2)}) collective-permute-start(bf16[192,384]{1,0:T(8,128)(2,1)S(1)} %copy-done.8), channel_id=1, source_target_pairs={{0,12},{4,8},{8,4},{12,0},{1,13},{5,9},{9,5},{13,1},{2,14},{6,10},... | collective-permute-start | bytes 442376 | tf_op jit(solution)/shard_map/ppermute | solution.py:139
  31.4 11.1 %collective-permute-start.6 = (bf16[3,192,384]{2,1,0:T(8,128)(2,1)S(1)}, bf16[3,192,384]{2,1,0:T(8,128)(2,1)S(1)}, u32[]{:S(2)}, u32[]{:S(2)}) collective-permute-start(bf16[3,192,384]{2,1,0:T(8,128)(2,1)S(1)} %get-tuple-element.54.own), channel_id=1, source_target_pairs={{0,2},{1,3},{2,0},{3,1},{4,6},{5,7},{6,4},{7,5},{8,10},{9,11},{10,... | collective-permute-start | bytes 1327112 | tf_op jit(solution)/shard_map/ppermute | solution.py:139
  33.0 9.5 %collective-permute-start.7 = (bf16[3,192,384]{2,1,0:T(8,128)(2,1)S(1)}, bf16[3,192,384]{2,1,0:T(8,128)(2,1)S(1)}, u32[]{:S(2)}, u32[]{:S(2)}) collective-permute-start(bf16[3,192,384]{2,1,0:T(8,128)(2,1)S(1)} %get-tuple-element.54.own), channel_id=1, source_target_pairs={{0,1},{1,0},{2,3},{3,2},{4,5},{5,4},{6,7},{7,6},{8,9},{9,8},{10,11... | collective-permute-start | bytes 1327112 | tf_op jit(solution)/shard_map/ppermute | solution.py:139
  33.0 9.4 %collective-permute-start.4 = (bf16[192,512]{1,0:T(8,128)(2,1)}, bf16[192,512]{1,0:T(8,128)(2,1)S(1)}, u32[]{:S(2)}, u32[]{:S(2)}) collective-permute-start(bf16[192,512]{1,0:T(8,128)(2,1)} %get-tuple-element.57), channel_id=1, source_target_pairs={{0,12},{4,8},{8,4},{12,0},{1,13},{5,9},{9,5},{13,1},{2,14},{6,10},... | collective-permute-start | bytes 589832 | tf_op jit(solution)/shard_map/ppermute | solution.py:139
  34.6 7.9 %collective-permute-start.5 = (bf16[192,512]{1,0:T(8,128)(2,1)S(1)}, bf16[192,512]{1,0:T(8,128)(2,1)S(1)}, u32[]{:S(2)}, u32[]{:S(2)}) collective-permute-start(bf16[192,512]{1,0:T(8,128)(2,1)S(1)} %get-tuple-element.58.refs_0_), channel_id=1, source_target_pairs={{0,16},{16,0},{1,17},{17,1},{2,18},{18,2},{3,19},{19,3},{4,20},{20... | collective-permute-start | bytes 589832 | tf_op jit(solution)/shard_map/ppermute | solution.py:139
  36.1 1.0 copy-start.3
  42.5 2.3 %collective-permute-start.8 = (bf16[3,192,384]{2,1,0:T(8,128)(2,1)S(1)}, bf16[3,192,384]{2,1,0:T(8,128)(2,1)S(1)}, u32[]{:S(2)}, u32[]{:S(2)}) collective-permute-start(bf16[3,192,384]{2,1,0:T(8,128)(2,1)S(1)} %collective-permute-done.6.far), channel_id=1, source_target_pairs={{0,1},{1,0},{2,3},{3,2},{4,5},{5,4},{6,7},{7,6},{8,9},{9,8},{10,11... | collective-permute-start | bytes 1327112 | tf_op jit(solution)/shard_map/ppermute | solution.py:139
  42.5 2.3 %collective-permute-start.9 = (bf16[2,128,384]{2,1,0:T(8,128)(2,1)S(1)}, bf16[2,128,384]{2,1,0:T(8,128)(2,1)S(1)}, u32[]{:S(2)}, u32[]{:S(2)}) collective-permute-start(bf16[2,128,384]{2,1,0:T(8,128)(2,1)S(1)} %get-tuple-element.65), channel_id=1, source_target_pairs={{0,0},{1,9},{2,14},{3,7},{4,4},{5,13},{6,2},{7,11},{8,8},{9,1},{10... | collective-permute-start | bytes 589832 | tf_op jit(solution)/shard_map/ppermute | solution.py:516
  43.2 5.7 %collective-permute-start.10 = (bf16[192,512]{1,0:T(8,128)(2,1)S(1)}, bf16[192,512]{1,0:T(8,128)(2,1)S(1)}, u32[]{:S(2)}, u32[]{:S(2)}) collective-permute-start(bf16[192,512]{1,0:T(8,128)(2,1)S(1)} %collective-permute-done.4.refs_2_), channel_id=1, source_target_pairs={{0,16},{16,0},{1,17},{17,1},{2,18},{18,2},{3,19},{19,3},{4,20},{20... | collective-permute-start | bytes 589832 | tf_op jit(solution)/shard_map/ppermute | solution.py:139
  49.0 18.6 %copy-start.4 = (bf16[192,384]{1,0:T(8,128)(2,1)S(1)}, bf16[192,384]{1,0:T(8,128)(2,1)}, u32[]{:S(2)}) copy-start(bf16[192,384]{1,0:T(8,128)(2,1)} %get-tuple-element.49.residual) | copy-start | bytes 442372
  50.9 40.8 %copy-start.7 = (f32[1536]{0:T(1024)S(1)}, f32[1536]{0:T(1024)}, u32[]{:S(2)}) copy-start(f32[1536]{0:T(1024)} %param.17) | copy-start | bytes 18436
  50.9 42.1 %copy-start = (bf16[1536,576]{0,1:T(8,128)(2,1)S(1)}, bf16[1536,576]{0,1:T(8,128)(2,1)}, u32[]{:S(2)}) copy-start(bf16[1536,576]{0,1:T(8,128)(2,1)} %param.18) | copy-start | bytes 5308420
  50.9 14.9 %collective-permute-start.11 = (bf16[768,256]{1,0:T(8,128)(2,1)S(1)}, bf16[768,256]{1,0:T(8,128)(2,1)S(1)}, u32[]{:S(2)}, u32[]{:S(2)}) collective-permute-start(bf16[768,256]{1,0:T(8,128)(2,1)S(1)} %shard_map.105.own), channel_id=1, source_target_pairs={{0,2},{1,3},{2,0},{3,1},{4,6},{5,7},{6,4},{7,5},{8,10},{9,11},{10,... | collective-permute-start | bytes 1179656 | tf_op jit(solution)/shard_map/ppermute | solution.py:139
  55.9 7.3 %collective-permute-start.13 = (bf16[2,128,384]{2,1,0:T(8,128)(2,1)S(1)}, bf16[2,128,384]{2,1,0:T(8,128)(2,1)S(1)}, u32[]{:S(2)}, u32[]{:S(2)}) collective-permute-start(bf16[2,128,384]{2,1,0:T(8,128)(2,1)S(1)} %collective-permute-done.9.even), channel_id=1, source_target_pairs={{0,16},{16,0},{1,17},{17,1},{2,18},{18,2},{3,19},{19,3},{4,20},{20... | collective-permute-start | bytes 589832 | tf_op jit(solution)/shard_map/ppermute | solution.py:139
  57.4 8.5 %collective-permute-start.15 = (bf16[2,256,384]{2,1,0:T(8,128)(2,1)S(1)}, bf16[2,256,384]{2,1,0:T(8,128)(2,1)S(1)}, u32[]{:S(2)}, u32[]{:S(2)}) collective-permute-start(bf16[2,256,384]{2,1,0:T(8,128)(2,1)S(1)} %get-tuple-element.74), channel_id=1, source_target_pairs={{0,9},{1,0},{2,7},{3,14},{4,13},{5,4},{6,11},{7,2},{8,1},{9,8},{10... | collective-permute-start | bytes 1179656 | tf_op jit(solution)/shard_map/ppermute | solution.py:516
  58.0 7.9 %collective-permute-start.12 = (bf16[768,256]{1,0:T(8,128)(2,1)S(1)}, bf16[768,256]{1,0:T(8,128)(2,1)S(1)}, u32[]{:S(2)}, u32[]{:S(2)}) collective-permute-start(bf16[768,256]{1,0:T(8,128)(2,1)S(1)} %shard_map.105.own), channel_id=1, source_target_pairs={{0,1},{1,0},{2,3},{3,2},{4,5},{5,4},{6,7},{7,6},{8,9},{9,8},{10,11... | collective-permute-start | bytes 1179656 | tf_op jit(solution)/shard_map/ppermute | solution.py:139
  65.8 1.7 %collective-permute-start.14 = (bf16[768,256]{1,0:T(8,128)(2,1)S(1)}, bf16[768,256]{1,0:T(8,128)(2,1)S(1)}, u32[]{:S(2)}, u32[]{:S(2)}) collective-permute-start(bf16[768,256]{1,0:T(8,128)(2,1)S(1)} %collective-permute-done.11.far), channel_id=1, source_target_pairs={{0,1},{1,0},{2,3},{3,2},{4,5},{5,4},{6,7},{7,6},{8,9},{9,8},{10,11... | collective-permute-start | bytes 1179656 | tf_op jit(solution)/shard_map/ppermute | solution.py:139
  68.5 12.5 %collective-permute-start.16 = (bf16[192,384]{1,0:T(8,128)(2,1)S(1)}, bf16[192,384]{1,0:T(8,128)(2,1)S(1)}, u32[]{:S(2)}, u32[]{:S(2)}) collective-permute-start(bf16[192,384]{1,0:T(8,128)(2,1)S(1)} %get-tuple-element.76), channel_id=1, source_target_pairs={{0,9},{1,8},{2,11},{3,10},{4,13},{5,12},{6,15},{7,14},{8,1},{9,0},... | collective-permute-start | bytes 442376 | tf_op jit(solution)/shard_map/ppermute | solution.py:541
  69.5 11.5 %collective-permute-start.17 = (bf16[192,384]{1,0:T(8,128)(2,1)S(1)}, bf16[192,384]{1,0:T(8,128)(2,1)S(1)}, u32[]{:S(2)}, u32[]{:S(2)}) collective-permute-start(bf16[192,384]{1,0:T(8,128)(2,1)S(1)} %get-tuple-element.77), channel_id=1, source_target_pairs={{0,14},{1,15},{2,13},{3,12},{4,11},{5,10},{6,8},{7,9},{8,6},{9,7},... | collective-permute-start | bytes 442376 | tf_op jit(solution)/shard_map/ppermute | solution.py:541
  73.0 12.7 %collective-permute-start.18 = (bf16[192,384]{1,0:T(8,128)(2,1)S(1)}, bf16[192,384]{1,0:T(8,128)(2,1)S(1)}, u32[]{:S(2)}, u32[]{:S(2)}) collective-permute-start(bf16[192,384]{1,0:T(8,128)(2,1)S(1)} %get-tuple-element.78), channel_id=1, source_target_pairs={{0,7},{1,6},{2,4},{3,5},{4,2},{5,3},{6,1},{7,0},{8,15},{9,14},{10,... | collective-permute-start | bytes 442376 | tf_op jit(solution)/shard_map/ppermute | solution.py:541
  85.7 5.9 %collective-permute-start.19 = (bf16[192,384]{1,0:T(8,128)(2,1)S(1)}, bf16[192,384]{1,0:T(8,128)(2,1)S(1)}, u32[]{:S(2)}, u32[]{:S(2)}) collective-permute-start(bf16[192,384]{1,0:T(8,128)(2,1)S(1)} %shard_map.107.own), channel_id=1, source_target_pairs={{0,2},{1,3},{2,0},{3,1},{4,6},{5,7},{6,4},{7,5},{8,10},{9,11},{10,... | collective-permute-start | bytes 442376 | tf_op jit(solution)/shard_map/ppermute | solution.py:139
  85.8 5.9 %collective-permute-start.20 = (bf16[192,384]{1,0:T(8,128)(2,1)S(1)}, bf16[192,384]{1,0:T(8,128)(2,1)S(1)}, u32[]{:S(2)}, u32[]{:S(2)}) collective-permute-start(bf16[192,384]{1,0:T(8,128)(2,1)S(1)} %shard_map.107.own), channel_id=1, source_target_pairs={{0,1},{1,0},{2,3},{3,2},{4,5},{5,4},{6,7},{7,6},{8,9},{9,8},{10,11... | collective-permute-start | bytes 442376 | tf_op jit(solution)/shard_map/ppermute | solution.py:139
  91.7 1.4 %collective-permute-start.21 = (bf16[192,384]{1,0:T(8,128)(2,1)S(1)}, bf16[192,384]{1,0:T(8,128)(2,1)S(1)}, u32[]{:S(2)}, u32[]{:S(2)}) collective-permute-start(bf16[192,384]{1,0:T(8,128)(2,1)S(1)} %collective-permute-done.19.far), channel_id=1, source_target_pairs={{0,1},{1,0},{2,3},{3,2},{4,5},{5,4},{6,7},{7,6},{8,9},{9,8},{10,11... | collective-permute-start | bytes 442376 | tf_op jit(solution)/shard_map/ppermute | solution.py:139
  94.3 5.9 %collective-permute-start.22 = (bf16[64,768]{1,0:T(8,128)(2,1)S(1)}, bf16[64,768]{1,0:T(8,128)(2,1)S(1)}, u32[]{:S(2)}, u32[]{:S(2)}) collective-permute-start(bf16[64,768]{1,0:T(8,128)(2,1)S(1)} %get-tuple-element.80), channel_id=1, source_target_pairs={{0,4},{4,0},{8,12},{12,8},{1,5},{5,1},{9,13},{13,9},{2,6},{6,2},{1... | collective-permute-start | bytes 294920 | tf_op jit(solution)/shard_map/ppermute | solution.py:139
  95.4 10.6 %collective-permute-start.23 = (bf16[64,768]{1,0:T(8,128)(2,1)S(1)}, bf16[64,768]{1,0:T(8,128)(2,1)S(1)}, u32[]{:S(2)}, u32[]{:S(2)}) collective-permute-start(bf16[64,768]{1,0:T(8,128)(2,1)S(1)} %get-tuple-element.81), channel_id=1, source_target_pairs={{0,8},{4,12},{8,0},{12,4},{1,9},{5,13},{9,1},{13,5},{2,10},{6,14},... | collective-permute-start | bytes 294920 | tf_op jit(solution)/shard_map/ppermute | solution.py:139
  96.1 9.9 %collective-permute-start.24 = (bf16[64,768]{1,0:T(8,128)(2,1)S(1)}, bf16[64,768]{1,0:T(8,128)(2,1)S(1)}, u32[]{:S(2)}, u32[]{:S(2)}) collective-permute-start(bf16[64,768]{1,0:T(8,128)(2,1)S(1)} %get-tuple-element.82), channel_id=1, source_target_pairs={{0,12},{4,8},{8,4},{12,0},{1,13},{5,9},{9,5},{13,1},{2,14},{6,10},... | collective-permute-start | bytes 294920 | tf_op jit(solution)/shard_map/ppermute | solution.py:139

commit v8 on v7

--- a/solution.py
+++ b/solution.py
@@ -11,6 +11,7 @@
 HEAD_WIDTH = 64
 DILATION_STEP = 8
 ENCODER_SLOTS = 256
+ORDER = (2, 3, 1, 0)
 
 
 epsilon = 1e-05
@@ -251,7 +252,7 @@
         started.wait()
 
 
-def restack_body(first, second, third, stacked, columns):
+def restack_body(second, third, first, stacked, columns):
     features = stacked.shape[2]
     stacked[0] = first[:, :features]
     stacked[1] = second[:, :features]
@@ -387,7 +388,7 @@
     capacity = packages[0].shape[0]
     heads = offsets.shape[0]
     width = heads * 3 * HEAD_WIDTH
-    for d, package in enumerate(packages):
+    for d, package in zip(ORDER, packages):
         rows[at(seq ^ d, capacity), :] = package[:, :width]
     far = [package[:, width:] for package in packages]
     half = capacity // 2
@@ -477,7 +478,7 @@
     )[0]
 
     second_in, third_in = swap(second_out, "seq", 2), swap(quarter, "seq", 3)
-    arrived = swap(first_out, "seq", 1), second_in, third_in
+    arrived = second_in, third_in, swap(first_out, "seq", 1)
     from_far = swap(down_far, "mp", 2)
     arrived, from_far, routes = lax.optimization_barrier((arrived, from_far, routes))
     own, columns = call(
@@ -505,6 +506,7 @@
     )
     halves = columns, others, third, swap(third, "groups", 1)
     spread = far, near, swap(far, "mp", 1)
+    down_send = lax.optimization_barrier((down_send[0], spread[2]))[0], down_send[1]
     parts = []
     for j in range(2):
         perm = []
@@ -514,11 +516,11 @@
                 user = (s ^ 2 * k) if k < 2 else (s + 2 * k - 5) % count
                 perm.append((s * mp_size + m, user * mp_size + k))
         parts.append(lax.ppermute(down_send[j], ("seq", "mp"), perm))
-    spread, parts[0] = lax.optimization_barrier((spread, parts[0]))
+    halves, spread, parts[0] = lax.optimization_barrier((halves, spread, parts[0]))
     hidden = call(
         functools.partial(hidden_body, count),
         [((count * tile_rows, units), bf16)],
-        (normed, own, *spread, kept, arrived[0], *halves),
+        (normed, own, *spread, kept, arrived[2], *halves),
         scratch=[
             pltpu.VMEM((2, count, depth, units), bf16),
         ],
@@ -550,7 +552,7 @@
         [((capacity, 4 * heads * HEAD_WIDTH), bf16)] * count,
         (gain_slide[None, :], routes, w_qkv.T, embedded_cols, *spread_mp(embedded_cols)),
     )
-    packages = [packages[0]] + [swap(packages[d], "seq", d) for d in range(1, count)]
+    packages = [swap(packages[d], "seq", d) for d in ORDER[:-1]] + [packages[0]]
     return call(
         functools.partial(attend_body, count),
         [((heads * HEAD_WIDTH, ENCODER_SLOTS), bf16)],

time: 108 us -> 108 us (level)
  waiting for transfers between devices: 61.8 us -> 60.6 us
    ppermute x20, starting transfers between devices: 25 us -> 26.2 us  [swap(): return lax.ppermute(array, axis, [(i, i ^ distance) for i in range(size)])]
  transfers between devices with their start and end apart: 25 -> 25, of which waited for: 13 -> 14; matrix products, arithmetic and copies ran while one was open for 0% -> 0% of each run, Pallas kernels for 4% -> 4%
where the time goes in v8:
time: 108 us
  waiting for transfers between devices  60.6 us (56%)
  starting transfers between devices  31.7 us (29%)
  Pallas kernels  13.6 us (13%)
  local copies, waits for them, and re-layouts  1.12 us (1%)
    ppermute x20, waiting for transfers between devices, swap(): return lax.ppermute(array, axis, [(i, i ^ distance) for i in range(size)])  48.3 us
    ppermute x20, starting transfers between devices, swap(): return lax.ppermute(array, axis, [(i, i ^ distance) for i in range(size)])  26.2 us
    pallas_call x10, Pallas kernels, call(): pl.pallas_call(body, out_shape=[jax.ShapeDtypeStruct(shape, kind) for sha...  13.6 us
    ppermute x3, waiting for transfers between devices, to_owner(): return lax.ppermute(part, ('seq', 'mp'), perm)  12.3 us
    ppermute x3, starting transfers between devices, to_owner(): return lax.ppermute(part, ('seq', 'mp'), perm)  3.96 us
  transfers between devices with their start and end apart: 25, of which 14 were waited for; matrix products, arithmetic and copies ran while one was open for 0% of the time, Pallas kernels for 4%

profile of v8, /device:TPU:0, one launch (start us, length us, event | category | flops | bytes accessed | tf_op | source)
XLA Modules:
  0.0 107.8 jit_solution(5557619373173332850)
XLA Ops:
  0.0 3.0 %shard_map.100 = (bf16[192,1408]{1,0:T(8,128)(2,1)}, bf16[192,896]{1,0:T(8,128)(2,1)}, bf16[192,384]{1,0:T(8,128)(2,1)}) custom-call(bf16[192,1536]{1,0:T(8,128)(2,1)} %tiles.3, bf16[384,1024]{1,0:T(8,128)(2,1)} %w_gate.3, bf16[384,1024]{1,0:T(8,128)(2,1)} %w_up.3, f32[1536]{0:T(1024)} %gain.3), custom_call_target="tpu_custom_call" | custom-call | tf_op jit(solution)/shard_map/pallas_call | solution.py:152
  3.0 0.0 copy-start.5
  3.1 0.0 copy-start.6
  3.1 3.1 %collective-permute-start.2 = (bf16[192,1408]{1,0:T(8,128)(2,1)}, bf16[192,1408]{1,0:T(8,128)(2,1)S(1)}, u32[]{:S(2)}, u32[]{:S(2)}) collective-permute-start(bf16[192,1408]{1,0:T(8,128)(2,1)} %get-tuple-element.51), channel_id=1, source_target_pairs={{0,4},{4,0},{8,12},{12,8},{1,5},{5,1},{9,13},{13,9},{2,6},{6,2},{1... | collective-permute-start | bytes 1622024 | tf_op jit(solution)/shard_map/ppermute | solution.py:140
  6.2 2.6 %collective-permute-start = (bf16[192,896]{1,0:T(8,128)(2,1)}, bf16[192,896]{1,0:T(8,128)(2,1)S(1)}, u32[]{:S(2)}, u32[]{:S(2)}) collective-permute-start(bf16[192,896]{1,0:T(8,128)(2,1)} %get-tuple-element.49), channel_id=1, source_target_pairs={{0,8},{4,12},{8,0},{12,4},{1,9},{5,13},{9,1},{13,5},{2,10},{6,14},... | collective-permute-start | bytes 1032200 | tf_op jit(solution)/shard_map/ppermute | solution.py:140
  8.7 3.4 %shard_map.101 = (bf16[192,512]{1,0:T(8,128)(2,1)}, bf16[384,512]{1,0:T(8,128)(2,1)}, bf16[384,384]{1,0:T(8,128)(2,1)}, bf16[384,384]{1,0:T(8,128)(2,1)}, bf16[1...) custom-call(bf16[192,1536]{1,0:T(8,128)(2,1)} %tiles.3, bf16[384,1024]{1,0:T(8,128)(2,1)} %w_gate.3, ...), custom_call_target="tpu_custom_call" | custom-call | tf_op jit(solution)/shard_map/pallas_call | solution.py:152
  12.2 1.6 %collective-permute-start.3 = (bf16[384,384]{1,0:T(8,128)(2,1)}, bf16[384,384]{1,0:T(8,128)(2,1)S(1)}, u32[]{:S(2)}, u32[]{:S(2)}) collective-permute-start(bf16[384,384]{1,0:T(8,128)(2,1)} %get-tuple-element.52), channel_id=1, source_target_pairs={{0,2},{1,3},{2,0},{3,1},{4,6},{5,7},{6,4},{7,5},{8,10},{9,11},{10,... | collective-permute-start | bytes 884744 | tf_op jit(solution)/shard_map/ppermute | solution.py:140
  13.7 0.2 collective-permute-start.1
  14.0 0.1 copy.11.dest
  14.8 0.7 shard_map.102.routes
  15.4 15.9 %collective-permute-done.1.third = bf16[192,384]{1,0:T(8,128)(2,1)S(1)} collective-permute-done((bf16[192,384]{1,0:T(8,128)(2,1)S(1)}, bf16[192,384]{1,0:T(8,128)(2,1)S(1)}, u32[]{:S(2)}, u32[]{:S(2)}) %collective-permute-start.1) | collective-permute-done | bytes 147488 | tf_op jit(solution)/shard_map/ppermute | solution.py:140
  31.4 0.1 shard_map.103
  31.4 1.6 %collective-permute-start.6 = (bf16[3,192,384]{2,1,0:T(8,128)(2,1)S(1)}, bf16[3,192,384]{2,1,0:T(8,128)(2,1)S(1)}, u32[]{:S(2)}, u32[]{:S(2)}) collective-permute-start(bf16[3,192,384]{2,1,0:T(8,128)(2,1)S(1)} %get-tuple-element.59.own), channel_id=1, source_target_pairs={{0,2},{1,3},{2,0},{3,1},{4,6},{5,7},{6,4},{7,5},{8,10},{9,11},{10,... | collective-permute-start | bytes 1327112 | tf_op jit(solution)/shard_map/ppermute | solution.py:140
  33.0 1.6 %collective-permute-start.4 = (bf16[192,512]{1,0:T(8,128)(2,1)}, bf16[192,512]{1,0:T(8,128)(2,1)S(1)}, u32[]{:S(2)}, u32[]{:S(2)}) collective-permute-start(bf16[192,512]{1,0:T(8,128)(2,1)} %get-tuple-element.63), channel_id=1, source_target_pairs={{0,12},{4,8},{8,4},{12,0},{1,13},{5,9},{9,5},{13,1},{2,14},{6,10},... | collective-permute-start | bytes 589832 | tf_op jit(solution)/shard_map/ppermute | solution.py:140
  34.6 1.5 %collective-permute-start.5 = (bf16[192,512]{1,0:T(8,128)(2,1)S(1)}, bf16[192,512]{1,0:T(8,128)(2,1)S(1)}, u32[]{:S(2)}, u32[]{:S(2)}) collective-permute-start(bf16[192,512]{1,0:T(8,128)(2,1)S(1)} %get-tuple-element.78.refs_0_), channel_id=1, source_target_pairs={{0,16},{16,0},{1,17},{17,1},{2,18},{18,2},{3,19},{19,3},{4,20},{20... | collective-permute-start | bytes 589832 | tf_op jit(solution)/shard_map/ppermute | solution.py:140
  36.1 1.0 copy-done.3
  37.0 0.1 shard_map.104
  37.1 5.3 %collective-permute-done.4.refs_2_ = bf16[192,512]{1,0:T(8,128)(2,1)S(1)} collective-permute-done((bf16[192,512]{1,0:T(8,128)(2,1)}, bf16[192,512]{1,0:T(8,128)(2,1)S(1)}, u32[]{:S(2)}, u32[]{:S(2)}) %collective-permute-start.4) | collective-permute-done | bytes 196640 | tf_op jit(solution)/shard_map/ppermute | solution.py:140
  42.4 0.1 collective-permute-done.6.far
  42.5 1.6 %collective-permute-start.8 = (bf16[192,512]{1,0:T(8,128)(2,1)S(1)}, bf16[192,512]{1,0:T(8,128)(2,1)S(1)}, u32[]{:S(2)}, u32[]{:S(2)}) collective-permute-start(bf16[192,512]{1,0:T(8,128)(2,1)S(1)} %collective-permute-done.4.refs_2_), channel_id=1, source_target_pairs={{0,16},{16,0},{1,17},{17,1},{2,18},{18,2},{3,19},{19,3},{4,20},{20... | collective-permute-start | bytes 589832 | tf_op jit(solution)/shard_map/ppermute | solution.py:140
  44.1 0.2 collective-permute-done.9.near_far
  44.3 0.7 collective-permute-start.10
  45.0 4.9 %collective-permute-done.8.refs_3_ = bf16[192,512]{1,0:T(8,128)(2,1)S(1)} collective-permute-done((bf16[192,512]{1,0:T(8,128)(2,1)S(1)}, bf16[192,512]{1,0:T(8,128)(2,1)S(1)}, u32[]{:S(2)}, u32[]{:S(2)}) %collective-permute-start.8) | collective-permute-done | bytes 196640 | tf_op jit(solution)/shard_map/ppermute | solution.py:140
  49.9 1.9 %shard_map.105.own = bf16[768,256]{1,0:T(8,128)(2,1)S(1)} custom-call(bf16[192,1536]{1,0:T(8,128)(2,1)S(1)} %copy-done.1, bf16[3,192,384]{2,1,0:T(8,128)(2,1)S(1)} %get-tuple-element.59.own, bf16[3,192,384]{2,1,0:T(8,128)(2,1)S(1)} %collective-permute-done.6.far, bf16[3,192,384]{2,1,0:T(8,128)(2,1)S(1)} %collective-permute-done.7.near, ...), custom_call_target="tpu_custom_call" | custom-call | tf_op jit(solution)/shard_map/pallas_call | solution.py:152
  51.8 0.0 copy-start.7
  51.8 5.2 %collective-permute-start.11 = (bf16[768,256]{1,0:T(8,128)(2,1)S(1)}, bf16[768,256]{1,0:T(8,128)(2,1)S(1)}, u32[]{:S(2)}, u32[]{:S(2)}) collective-permute-start(bf16[768,256]{1,0:T(8,128)(2,1)S(1)} %shard_map.105.own), channel_id=1, source_target_pairs={{0,2},{1,3},{2,0},{3,1},{4,6},{5,7},{6,4},{7,5},{8,10},{9,11},{10,... | collective-permute-start | bytes 1179656 | tf_op jit(solution)/shard_map/ppermute | solution.py:140
  57.0 1.5 %collective-permute-start.13 = (bf16[2,128,384]{2,1,0:T(8,128)(2,1)S(1)}, bf16[2,128,384]{2,1,0:T(8,128)(2,1)S(1)}, u32[]{:S(2)}, u32[]{:S(2)}) collective-permute-start(bf16[2,128,384]{2,1,0:T(8,128)(2,1)S(1)} %collective-permute-done.10.even), channel_id=1, source_target_pairs={{0,16},{16,0},{1,17},{17,1},{2,18},{18,2},{3,19},{19,3},{4,20},{20... | collective-permute-start | bytes 589832 | tf_op jit(solution)/shard_map/ppermute | solution.py:140
  58.5 0.9 collective-permute-start.15
  59.4 5.0 %collective-permute-done.13.even_other = bf16[2,128,384]{2,1,0:T(8,128)(2,1)S(1)} collective-permute-done((bf16[2,128,384]{2,1,0:T(8,128)(2,1)S(1)}, bf16[2,128,384]{2,1,0:T(8,128)(2,1)S(1)}, u32[]{:S(2)}, u32[]{:S(2)}) %collective-permute-start.13) | collective-permute-done | bytes 196640 | tf_op jit(solution)/shard_map/ppermute | solution.py:140
  64.4 2.2 %collective-permute-done.11.far = bf16[768,256]{1,0:T(8,128)(2,1)S(1)} collective-permute-done((bf16[768,256]{1,0:T(8,128)(2,1)S(1)}, bf16[768,256]{1,0:T(8,128)(2,1)S(1)}, u32[]{:S(2)}, u32[]{:S(2)}) %collective-permute-start.11) | collective-permute-done | bytes 393248 | tf_op jit(solution)/shard_map/ppermute | solution.py:140
  66.6 0.2 collective-permute-start.14
  66.8 1.6 %collective-permute-done.14.near_far = bf16[768,256]{1,0:T(8,128)(2,1)S(1)} collective-permute-done((bf16[768,256]{1,0:T(8,128)(2,1)S(1)}, bf16[768,256]{1,0:T(8,128)(2,1)S(1)}, u32[]{:S(2)}, u32[]{:S(2)}) %collective-permute-start.14) | collective-permute-done | bytes 393248 | tf_op jit(solution)/shard_map/ppermute | solution.py:140
  68.3 1.0 shard_map.106
  69.3 1.3 %collective-permute-start.16 = (bf16[192,384]{1,0:T(8,128)(2,1)S(1)}, bf16[192,384]{1,0:T(8,128)(2,1)S(1)}, u32[]{:S(2)}, u32[]{:S(2)}) collective-permute-start(bf16[192,384]{1,0:T(8,128)(2,1)S(1)} %get-tuple-element.86), channel_id=1, source_target_pairs={{0,9},{1,8},{2,11},{3,10},{4,13},{5,12},{6,15},{7,14},{8,1},{9,0},... | collective-permute-start | bytes 442376 | tf_op jit(solution)/shard_map/ppermute | solution.py:543
  70.6 2.4 %collective-permute-start.17 = (bf16[192,384]{1,0:T(8,128)(2,1)S(1)}, bf16[192,384]{1,0:T(8,128)(2,1)S(1)}, u32[]{:S(2)}, u32[]{:S(2)}) collective-permute-start(bf16[192,384]{1,0:T(8,128)(2,1)S(1)} %get-tuple-element.87), channel_id=1, source_target_pairs={{0,14},{1,15},{2,13},{3,12},{4,11},{5,10},{6,8},{7,9},{8,6},{9,7},... | collective-permute-start | bytes 442376 | tf_op jit(solution)/shard_map/ppermute | solution.py:543
  73.1 0.2 collective-permute-start.18
  73.3 9.4 %collective-permute-done.16.refs_0_ = bf16[192,384]{1,0:T(8,128)(2,1)S(1)} collective-permute-done((bf16[192,384]{1,0:T(8,128)(2,1)S(1)}, bf16[192,384]{1,0:T(8,128)(2,1)S(1)}, u32[]{:S(2)}, u32[]{:S(2)}) %collective-permute-start.16) | collective-permute-done | bytes 147488 | tf_op jit(solution)/shard_map/ppermute | solution.py:543
  82.6 2.9 %collective-permute-done.18.refs_2_ = bf16[192,384]{1,0:T(8,128)(2,1)S(1)} collective-permute-done((bf16[192,384]{1,0:T(8,128)(2,1)S(1)}, bf16[192,384]{1,0:T(8,128)(2,1)S(1)}, u32[]{:S(2)}, u32[]{:S(2)}) %collective-permute-start.18) | collective-permute-done | bytes 147488 | tf_op jit(solution)/shard_map/ppermute | solution.py:543
  85.6 0.1 shard_map.107.own
  85.6 1.2 %collective-permute-start.19 = (bf16[192,384]{1,0:T(8,128)(2,1)S(1)}, bf16[192,384]{1,0:T(8,128)(2,1)S(1)}, u32[]{:S(2)}, u32[]{:S(2)}) collective-permute-start(bf16[192,384]{1,0:T(8,128)(2,1)S(1)} %shard_map.107.own), channel_id=1, source_target_pairs={{0,2},{1,3},{2,0},{3,1},{4,6},{5,7},{6,4},{7,5},{8,10},{9,11},{10,... | collective-permute-start | bytes 442376 | tf_op jit(solution)/shard_map/ppermute | solution.py:140
  86.9 4.7 %collective-permute-done.19.far = bf16[192,384]{1,0:T(8,128)(2,1)S(1)} collective-permute-done((bf16[192,384]{1,0:T(8,128)(2,1)S(1)}, bf16[192,384]{1,0:T(8,128)(2,1)S(1)}, u32[]{:S(2)}, u32[]{:S(2)}) %collective-permute-start.19) | collective-permute-done | bytes 147488 | tf_op jit(solution)/shard_map/ppermute | solution.py:140
  91.6 1.3 %collective-permute-done.21.near_far = bf16[192,384]{1,0:T(8,128)(2,1)S(1)} collective-permute-done((bf16[192,384]{1,0:T(8,128)(2,1)S(1)}, bf16[192,384]{1,0:T(8,128)(2,1)S(1)}, u32[]{:S(2)}, u32[]{:S(2)}) %collective-permute-start.21) | collective-permute-done | bytes 147488 | tf_op jit(solution)/shard_map/ppermute | solution.py:140
  92.9 1.2 %shard_map.108 = (bf16[64,768]{1,0:T(8,128)(2,1)S(1)}, bf16[64,768]{1,0:T(8,128)(2,1)S(1)}, bf16[64,768]{1,0:T(8,128)(2,1)S(1)}, bf16[64,768]{1,0:T(8,128)(2,1)S(1)}) custom-call(f32[1,1536]{1,0:T(1,128)S(1)} %broadcast_in_dim.3.gain, bf16[352,192]{1,0:T(8,128)(2,1)S(1)} %shard_map.102.routes, bf16[576,1536]{1,0:T(8,128)(2,1)S(1)} %bitcast.3, ...), custom_call_target="tpu_custom_call" | custom-call | tf_op jit(solution)/shard_map/pallas_call | solution.py:152
  94.2 1.1 %collective-permute-start.22 = (bf16[64,768]{1,0:T(8,128)(2,1)S(1)}, bf16[64,768]{1,0:T(8,128)(2,1)S(1)}, u32[]{:S(2)}, u32[]{:S(2)}) collective-permute-start(bf16[64,768]{1,0:T(8,128)(2,1)S(1)} %get-tuple-element.89), channel_id=1, source_target_pairs={{0,8},{4,12},{8,0},{12,4},{1,9},{5,13},{9,1},{13,5},{2,10},{6,14},... | collective-permute-start | bytes 294920 | tf_op jit(solution)/shard_map/ppermute | solution.py:140
  95.3 3.3 %collective-permute-start.23 = (bf16[64,768]{1,0:T(8,128)(2,1)S(1)}, bf16[64,768]{1,0:T(8,128)(2,1)S(1)}, u32[]{:S(2)}, u32[]{:S(2)}) collective-permute-start(bf16[64,768]{1,0:T(8,128)(2,1)S(1)} %get-tuple-element.90), channel_id=1, source_target_pairs={{0,12},{4,8},{8,4},{12,0},{1,13},{5,9},{9,5},{13,1},{2,14},{6,10},... | collective-permute-start | bytes 294920 | tf_op jit(solution)/shard_map/ppermute | solution.py:140
  98.6 6.3 %collective-permute-done.22.refs_0_ = bf16[64,768]{1,0:T(8,128)(2,1)S(1)} collective-permute-done((bf16[64,768]{1,0:T(8,128)(2,1)S(1)}, bf16[64,768]{1,0:T(8,128)(2,1)S(1)}, u32[]{:S(2)}, u32[]{:S(2)}) %collective-permute-start.22) | collective-permute-done | bytes 98336 | tf_op jit(solution)/shard_map/ppermute | solution.py:140
  105.0 0.7 collective-permute-done.24.refs_2_
  105.7 2.2 %shard_map.109 = bf16[192,256]{1,0:T(8,128)(2,1)} custom-call(s32[3]{0:T(128)S(1)} %copy-done.6, bf16[64,768]{1,0:T(8,128)(2,1)S(1)} %collective-permute-done.22.refs_0_, bf16[64,768]{1,0:T(8,128)(2,1)S(1)} %collective-permute-done.23.refs_1_, bf16[64,768]{1,0:T(8,128)(2,1)S(1)} %collective-permute-done.24.refs_2_, bf16[64,768]{1,0:T(8,128)(2,1)S(1)} %get-tuple-element.92.refs_3_), custom_call_target="tpu_custom_call" | custom-call | tf_op jit(solution)/shard_map/pallas_call | solution.py:152
  (32 shorter events, 0.1 us)
Async XLA Ops:
  3.0 10.7 %copy-start.8 = (bf16[192,384]{1,0:T(8,128)(2,1)S(1)}, bf16[192,384]{1,0:T(8,128)(2,1)}, u32[]{:S(2)}) copy-start(bf16[192,384]{1,0:T(8,128)(2,1)} %get-tuple-element.50) | copy-start | bytes 442372
  3.0 10.9 %copy-start.5 = (s32[192,1]{0,1:T(1,128)S(1)}, s32[192,1]{0,1:T(1,128)}, u32[]{:S(2)}) copy-start(s32[192,1]{0,1:T(1,128)} %param.12) | copy-start | bytes 2308
  3.1 11.7 %copy-start.6 = (s32[3]{0:T(128)S(1)}, s32[3]{0:T(128)}, u32[]{:S(2)}) copy-start(s32[3]{0:T(128)} %offsets.3) | copy-start | bytes 40
  3.1 28.3 %collective-permute-start.2 = (bf16[192,1408]{1,0:T(8,128)(2,1)}, bf16[192,1408]{1,0:T(8,128)(2,1)S(1)}, u32[]{:S(2)}, u32[]{:S(2)}) collective-permute-start(bf16[192,1408]{1,0:T(8,128)(2,1)} %get-tuple-element.51), channel_id=1, source_target_pairs={{0,4},{4,0},{8,12},{12,8},{1,5},{5,1},{9,13},{13,9},{2,6},{6,2},{1... | collective-permute-start | bytes 1622024 | tf_op jit(solution)/shard_map/ppermute | solution.py:140
  6.2 25.2 %collective-permute-start = (bf16[192,896]{1,0:T(8,128)(2,1)}, bf16[192,896]{1,0:T(8,128)(2,1)S(1)}, u32[]{:S(2)}, u32[]{:S(2)}) collective-permute-start(bf16[192,896]{1,0:T(8,128)(2,1)} %get-tuple-element.49), channel_id=1, source_target_pairs={{0,8},{4,12},{8,0},{12,4},{1,9},{5,13},{9,1},{13,5},{2,10},{6,14},... | collective-permute-start | bytes 1032200 | tf_op jit(solution)/shard_map/ppermute | solution.py:140
  12.2 37.7 %copy-start.1 = (bf16[192,1536]{1,0:T(8,128)(2,1)S(1)}, bf16[192,1536]{1,0:T(8,128)(2,1)}, u32[]{:S(2)}) copy-start(bf16[192,1536]{1,0:T(8,128)(2,1)} %get-tuple-element.55.normed) | copy-start | bytes 1769476
  12.2 37.7 %copy-start.2 = (bf16[384,512]{1,0:T(8,128)(2,1)S(1)}, bf16[384,512]{1,0:T(8,128)(2,1)}, u32[]{:S(2)}) copy-start(bf16[384,512]{1,0:T(8,128)(2,1)} %get-tuple-element.77.kept) | copy-start | bytes 1179652
  12.2 19.2 %collective-permute-start.3 = (bf16[384,384]{1,0:T(8,128)(2,1)}, bf16[384,384]{1,0:T(8,128)(2,1)S(1)}, u32[]{:S(2)}, u32[]{:S(2)}) collective-permute-start(bf16[384,384]{1,0:T(8,128)(2,1)} %get-tuple-element.52), channel_id=1, source_target_pairs={{0,2},{1,3},{2,0},{3,1},{4,6},{5,7},{6,4},{7,5},{8,10},{9,11},{10,... | collective-permute-start | bytes 884744 | tf_op jit(solution)/shard_map/ppermute | solution.py:140
  13.7 17.6 %collective-permute-start.1 = (bf16[192,384]{1,0:T(8,128)(2,1)S(1)}, bf16[192,384]{1,0:T(8,128)(2,1)S(1)}, u32[]{:S(2)}, u32[]{:S(2)}) collective-permute-start(bf16[192,384]{1,0:T(8,128)(2,1)S(1)} %copy-done.8), channel_id=1, source_target_pairs={{0,12},{4,8},{8,4},{12,0},{1,13},{5,9},{9,5},{13,1},{2,14},{6,10},... | collective-permute-start | bytes 442376 | tf_op jit(solution)/shard_map/ppermute | solution.py:140
  31.4 11.1 %collective-permute-start.6 = (bf16[3,192,384]{2,1,0:T(8,128)(2,1)S(1)}, bf16[3,192,384]{2,1,0:T(8,128)(2,1)S(1)}, u32[]{:S(2)}, u32[]{:S(2)}) collective-permute-start(bf16[3,192,384]{2,1,0:T(8,128)(2,1)S(1)} %get-tuple-element.59.own), channel_id=1, source_target_pairs={{0,2},{1,3},{2,0},{3,1},{4,6},{5,7},{6,4},{7,5},{8,10},{9,11},{10,... | collective-permute-start | bytes 1327112 | tf_op jit(solution)/shard_map/ppermute | solution.py:140
  33.0 9.5 %collective-permute-start.7 = (bf16[3,192,384]{2,1,0:T(8,128)(2,1)S(1)}, bf16[3,192,384]{2,1,0:T(8,128)(2,1)S(1)}, u32[]{:S(2)}, u32[]{:S(2)}) collective-permute-start(bf16[3,192,384]{2,1,0:T(8,128)(2,1)S(1)} %get-tuple-element.59.own), channel_id=1, source_target_pairs={{0,1},{1,0},{2,3},{3,2},{4,5},{5,4},{6,7},{7,6},{8,9},{9,8},{10,11... | collective-permute-start | bytes 1327112 | tf_op jit(solution)/shard_map/ppermute | solution.py:140
  33.0 9.4 %collective-permute-start.4 = (bf16[192,512]{1,0:T(8,128)(2,1)}, bf16[192,512]{1,0:T(8,128)(2,1)S(1)}, u32[]{:S(2)}, u32[]{:S(2)}) collective-permute-start(bf16[192,512]{1,0:T(8,128)(2,1)} %get-tuple-element.63), channel_id=1, source_target_pairs={{0,12},{4,8},{8,4},{12,0},{1,13},{5,9},{9,5},{13,1},{2,14},{6,10},... | collective-permute-start | bytes 589832 | tf_op jit(solution)/shard_map/ppermute | solution.py:140
  34.6 7.9 %collective-permute-start.5 = (bf16[192,512]{1,0:T(8,128)(2,1)S(1)}, bf16[192,512]{1,0:T(8,128)(2,1)S(1)}, u32[]{:S(2)}, u32[]{:S(2)}) collective-permute-start(bf16[192,512]{1,0:T(8,128)(2,1)S(1)} %get-tuple-element.78.refs_0_), channel_id=1, source_target_pairs={{0,16},{16,0},{1,17},{17,1},{2,18},{18,2},{3,19},{19,3},{4,20},{20... | collective-permute-start | bytes 589832 | tf_op jit(solution)/shard_map/ppermute | solution.py:140
  36.1 1.0 copy-start.3
  42.5 1.8 %collective-permute-start.9 = (bf16[3,192,384]{2,1,0:T(8,128)(2,1)S(1)}, bf16[3,192,384]{2,1,0:T(8,128)(2,1)S(1)}, u32[]{:S(2)}, u32[]{:S(2)}) collective-permute-start(bf16[3,192,384]{2,1,0:T(8,128)(2,1)S(1)} %collective-permute-done.6.far), channel_id=1, source_target_pairs={{0,1},{1,0},{2,3},{3,2},{4,5},{5,4},{6,7},{7,6},{8,9},{9,8},{10,11... | collective-permute-start | bytes 1327112 | tf_op jit(solution)/shard_map/ppermute | solution.py:140
  42.5 7.3 %collective-permute-start.8 = (bf16[192,512]{1,0:T(8,128)(2,1)S(1)}, bf16[192,512]{1,0:T(8,128)(2,1)S(1)}, u32[]{:S(2)}, u32[]{:S(2)}) collective-permute-start(bf16[192,512]{1,0:T(8,128)(2,1)S(1)} %collective-permute-done.4.refs_2_), channel_id=1, source_target_pairs={{0,16},{16,0},{1,17},{17,1},{2,18},{18,2},{3,19},{19,3},{4,20},{20... | collective-permute-start | bytes 589832 | tf_op jit(solution)/shard_map/ppermute | solution.py:140
  44.3 5.5 %collective-permute-start.10 = (bf16[2,128,384]{2,1,0:T(8,128)(2,1)S(1)}, bf16[2,128,384]{2,1,0:T(8,128)(2,1)S(1)}, u32[]{:S(2)}, u32[]{:S(2)}) collective-permute-start(bf16[2,128,384]{2,1,0:T(8,128)(2,1)S(1)} %get-tuple-element.73), channel_id=1, source_target_pairs={{0,0},{1,9},{2,14},{3,7},{4,4},{5,13},{6,2},{7,11},{8,8},{9,1},{10... | collective-permute-start | bytes 589832 | tf_op jit(solution)/shard_map/ppermute | solution.py:518
  49.9 18.5 %copy-start.4 = (bf16[192,384]{1,0:T(8,128)(2,1)S(1)}, bf16[192,384]{1,0:T(8,128)(2,1)}, u32[]{:S(2)}) copy-start(bf16[192,384]{1,0:T(8,128)(2,1)} %get-tuple-element.54.residual) | copy-start | bytes 442372
  51.8 39.8 %copy-start.7 = (f32[1536]{0:T(1024)S(1)}, f32[1536]{0:T(1024)}, u32[]{:S(2)}) copy-start(f32[1536]{0:T(1024)} %param.17) | copy-start | bytes 18436
  51.8 41.1 %copy-start = (bf16[1536,576]{0,1:T(8,128)(2,1)S(1)}, bf16[1536,576]{0,1:T(8,128)(2,1)}, u32[]{:S(2)}) copy-start(bf16[1536,576]{0,1:T(8,128)(2,1)} %param.18) | copy-start | bytes 5308420
  51.8 14.8 %collective-permute-start.11 = (bf16[768,256]{1,0:T(8,128)(2,1)S(1)}, bf16[768,256]{1,0:T(8,128)(2,1)S(1)}, u32[]{:S(2)}, u32[]{:S(2)}) collective-permute-start(bf16[768,256]{1,0:T(8,128)(2,1)S(1)} %shard_map.105.own), channel_id=1, source_target_pairs={{0,2},{1,3},{2,0},{3,1},{4,6},{5,7},{6,4},{7,5},{8,10},{9,11},{10,... | collective-permute-start | bytes 1179656 | tf_op jit(solution)/shard_map/ppermute | solution.py:140
  57.0 7.4 %collective-permute-start.13 = (bf16[2,128,384]{2,1,0:T(8,128)(2,1)S(1)}, bf16[2,128,384]{2,1,0:T(8,128)(2,1)S(1)}, u32[]{:S(2)}, u32[]{:S(2)}) collective-permute-start(bf16[2,128,384]{2,1,0:T(8,128)(2,1)S(1)} %collective-permute-done.10.even), channel_id=1, source_target_pairs={{0,16},{16,0},{1,17},{17,1},{2,18},{18,2},{3,19},{19,3},{4,20},{20... | collective-permute-start | bytes 589832 | tf_op jit(solution)/shard_map/ppermute | solution.py:140
  58.5 8.3 %collective-permute-start.15 = (bf16[2,256,384]{2,1,0:T(8,128)(2,1)S(1)}, bf16[2,256,384]{2,1,0:T(8,128)(2,1)S(1)}, u32[]{:S(2)}, u32[]{:S(2)}) collective-permute-start(bf16[2,256,384]{2,1,0:T(8,128)(2,1)S(1)} %get-tuple-element.84), channel_id=1, source_target_pairs={{0,9},{1,0},{2,7},{3,14},{4,13},{5,4},{6,11},{7,2},{8,1},{9,8},{10... | collective-permute-start | bytes 1179656 | tf_op jit(solution)/shard_map/ppermute | solution.py:518
  59.4 7.4 %collective-permute-start.12 = (bf16[768,256]{1,0:T(8,128)(2,1)S(1)}, bf16[768,256]{1,0:T(8,128)(2,1)S(1)}, u32[]{:S(2)}, u32[]{:S(2)}) collective-permute-start(bf16[768,256]{1,0:T(8,128)(2,1)S(1)} %shard_map.105.own), channel_id=1, source_target_pairs={{0,1},{1,0},{2,3},{3,2},{4,5},{5,4},{6,7},{7,6},{8,9},{9,8},{10,11... | collective-permute-start | bytes 1179656 | tf_op jit(solution)/shard_map/ppermute | solution.py:140
  66.6 1.7 %collective-permute-start.14 = (bf16[768,256]{1,0:T(8,128)(2,1)S(1)}, bf16[768,256]{1,0:T(8,128)(2,1)S(1)}, u32[]{:S(2)}, u32[]{:S(2)}) collective-permute-start(bf16[768,256]{1,0:T(8,128)(2,1)S(1)} %collective-permute-done.11.far), channel_id=1, source_target_pairs={{0,1},{1,0},{2,3},{3,2},{4,5},{5,4},{6,7},{7,6},{8,9},{9,8},{10,11... | collective-permute-start | bytes 1179656 | tf_op jit(solution)/shard_map/ppermute | solution.py:140
  69.3 13.3 %collective-permute-start.16 = (bf16[192,384]{1,0:T(8,128)(2,1)S(1)}, bf16[192,384]{1,0:T(8,128)(2,1)S(1)}, u32[]{:S(2)}, u32[]{:S(2)}) collective-permute-start(bf16[192,384]{1,0:T(8,128)(2,1)S(1)} %get-tuple-element.86), channel_id=1, source_target_pairs={{0,9},{1,8},{2,11},{3,10},{4,13},{5,12},{6,15},{7,14},{8,1},{9,0},... | collective-permute-start | bytes 442376 | tf_op jit(solution)/shard_map/ppermute | solution.py:543
  70.6 12.0 %collective-permute-start.17 = (bf16[192,384]{1,0:T(8,128)(2,1)S(1)}, bf16[192,384]{1,0:T(8,128)(2,1)S(1)}, u32[]{:S(2)}, u32[]{:S(2)}) collective-permute-start(bf16[192,384]{1,0:T(8,128)(2,1)S(1)} %get-tuple-element.87), channel_id=1, source_target_pairs={{0,14},{1,15},{2,13},{3,12},{4,11},{5,10},{6,8},{7,9},{8,6},{9,7},... | collective-permute-start | bytes 442376 | tf_op jit(solution)/shard_map/ppermute | solution.py:543
  73.1 12.5 %collective-permute-start.18 = (bf16[192,384]{1,0:T(8,128)(2,1)S(1)}, bf16[192,384]{1,0:T(8,128)(2,1)S(1)}, u32[]{:S(2)}, u32[]{:S(2)}) collective-permute-start(bf16[192,384]{1,0:T(8,128)(2,1)S(1)} %get-tuple-element.88), channel_id=1, source_target_pairs={{0,7},{1,6},{2,4},{3,5},{4,2},{5,3},{6,1},{7,0},{8,15},{9,14},{10,... | collective-permute-start | bytes 442376 | tf_op jit(solution)/shard_map/ppermute | solution.py:543
  85.6 5.9 %collective-permute-start.19 = (bf16[192,384]{1,0:T(8,128)(2,1)S(1)}, bf16[192,384]{1,0:T(8,128)(2,1)S(1)}, u32[]{:S(2)}, u32[]{:S(2)}) collective-permute-start(bf16[192,384]{1,0:T(8,128)(2,1)S(1)} %shard_map.107.own), channel_id=1, source_target_pairs={{0,2},{1,3},{2,0},{3,1},{4,6},{5,7},{6,4},{7,5},{8,10},{9,11},{10,... | collective-permute-start | bytes 442376 | tf_op jit(solution)/shard_map/ppermute | solution.py:140
  86.9 4.7 %collective-permute-start.20 = (bf16[192,384]{1,0:T(8,128)(2,1)S(1)}, bf16[192,384]{1,0:T(8,128)(2,1)S(1)}, u32[]{:S(2)}, u32[]{:S(2)}) collective-permute-start(bf16[192,384]{1,0:T(8,128)(2,1)S(1)} %shard_map.107.own), channel_id=1, source_target_pairs={{0,1},{1,0},{2,3},{3,2},{4,5},{5,4},{6,7},{7,6},{8,9},{9,8},{10,11... | collective-permute-start | bytes 442376 | tf_op jit(solution)/shard_map/ppermute | solution.py:140
  91.6 1.4 %collective-permute-start.21 = (bf16[192,384]{1,0:T(8,128)(2,1)S(1)}, bf16[192,384]{1,0:T(8,128)(2,1)S(1)}, u32[]{:S(2)}, u32[]{:S(2)}) collective-permute-start(bf16[192,384]{1,0:T(8,128)(2,1)S(1)} %collective-permute-done.19.far), channel_id=1, source_target_pairs={{0,1},{1,0},{2,3},{3,2},{4,5},{5,4},{6,7},{7,6},{8,9},{9,8},{10,11... | collective-permute-start | bytes 442376 | tf_op jit(solution)/shard_map/ppermute | solution.py:140
  94.2 10.8 %collective-permute-start.22 = (bf16[64,768]{1,0:T(8,128)(2,1)S(1)}, bf16[64,768]{1,0:T(8,128)(2,1)S(1)}, u32[]{:S(2)}, u32[]{:S(2)}) collective-permute-start(bf16[64,768]{1,0:T(8,128)(2,1)S(1)} %get-tuple-element.89), channel_id=1, source_target_pairs={{0,8},{4,12},{8,0},{12,4},{1,9},{5,13},{9,1},{13,5},{2,10},{6,14},... | collective-permute-start | bytes 294920 | tf_op jit(solution)/shard_map/ppermute | solution.py:140
  95.3 9.7 %collective-permute-start.23 = (bf16[64,768]{1,0:T(8,128)(2,1)S(1)}, bf16[64,768]{1,0:T(8,128)(2,1)S(1)}, u32[]{:S(2)}, u32[]{:S(2)}) collective-permute-start(bf16[64,768]{1,0:T(8,128)(2,1)S(1)} %get-tuple-element.90), channel_id=1, source_target_pairs={{0,12},{4,8},{8,4},{12,0},{1,13},{5,9},{9,5},{13,1},{2,14},{6,10},... | collective-permute-start | bytes 294920 | tf_op jit(solution)/shard_map/ppermute | solution.py:140
  98.6 7.0 %collective-permute-start.24 = (bf16[64,768]{1,0:T(8,128)(2,1)S(1)}, bf16[64,768]{1,0:T(8,128)(2,1)S(1)}, u32[]{:S(2)}, u32[]{:S(2)}) collective-permute-start(bf16[64,768]{1,0:T(8,128)(2,1)S(1)} %get-tuple-element.91), channel_id=1, source_target_pairs={{0,4},{4,0},{8,12},{12,8},{1,5},{5,1},{9,13},{13,9},{2,6},{6,2},{1... | collective-permute-start | bytes 294920 | tf_op jit(solution)/shard_map/ppermute | solution.py:140

commit v9 on v8

--- a/solution.py
+++ b/solution.py
@@ -202,47 +202,41 @@
 
 
 def cut_first_body(
-    count, tiles, w_gate, w_up, gain, first_out, second_out, quarter, held, sems
+    count, tiles, w_gate, w_up, w_down, gain, first_out, second_out, third_out, near, far, held, sems
 ):
     seq, mp, group = place()
     copies, copy = copier(sems, group)
     half, units = w_gate.shape[0] // 2, w_gate.shape[1] // count
-    features = quarter.shape[1]
+    features = D_ENC // count
     copy(tiles, held)
     for i in range(2):
-        span = pl.ds(i * half, half), at(seq ^ 2, units)
-        columns = pl.ds(features + i * units, units)
-        copy(w_gate.at[span], second_out.at[:, columns], w_up.at[span])
+        for d, target in ((2, second_out), (3, third_out)):
+            span = pl.ds(i * half, half), at(seq ^ d, units)
+            columns = pl.ds(features + i * units, units)
+            copy(w_gate.at[span], target.at[:, columns], w_up.at[span])
         span = pl.ds(i * half, half), at(seq ^ 1, units)
         for k, weight in enumerate((w_gate, w_up)):
             columns = pl.ds(features + (2 * i + k) * units, units)
             copy(weight.at[span], first_out.at[:, columns])
+    for j in range(4):
+        rows = at(column_user(seq, mp ^ j), units)
+        copy(w_down.at[rows, :], (far if j >= 2 else near).at[j % 2])
     copies.pop(0).wait()
     columns = at(mp, features)
     own_columns = normalise(held, held[:, columns], gain[columns])
-    second_out[:, :features] = own_columns
-    first_out[:, :features] = own_columns
-    quarter[...] = own_columns
+    for target in (second_out, third_out, first_out):
+        target[:, :features] = own_columns
     for started in copies:
         started.wait()
 
 
 def cut_second_body(
-    count, tiles, w_gate, w_up, w_down, gain, third_out, kept, near, far, normed, residual, held, sems
+    count, tiles, w_gate, w_up, gain, kept, normed, residual, held, sems
 ):
     seq, mp, group = place()
     copies, copy = copier(sems, group)
-    half, units = w_gate.shape[0] // 2, w_gate.shape[1] // count
+    units = w_gate.shape[1] // count
     copy(tiles, held)
-    part = units // 2
-    for j, target in ((2, far), (0, near)):
-        rows = at(column_user(seq, mp ^ j) * 2 + group, part)
-        copy(w_down.at[rows, :], target.at[pl.ds(0, part), :])
-        rows = at(column_user(seq, mp ^ (j + 1)), units)
-        copy(w_down.at[rows, :], target.at[pl.ds(part, units), :])
-    for i in range(2):
-        span = pl.ds(i * half, half), at(seq ^ 3, units)
-        copy(w_gate.at[span], third_out.at[:, pl.ds(i * units, units)], w_up.at[span])
     for i, weight in enumerate((w_gate, w_up)):
         copy(weight.at[:, at(seq, units)], kept.at[:, pl.ds(i * units, units)])
     copies.pop(0).wait()
@@ -252,18 +246,19 @@
         started.wait()
 
 
-def restack_body(second, third, first, stacked, columns):
+def restack_body(first, second, third, stacked, columns):
     features = stacked.shape[2]
     stacked[0] = first[:, :features]
     stacked[1] = second[:, :features]
-    stacked[2] = third[...]
-    columns[...] = second[:, features:]
+    stacked[2] = third[:, :features]
+    columns[0] = second[:, features:]
+    columns[1] = third[:, features:]
 
 
 def pair_body(near, far, even, odd):
     for i, rows in enumerate((near, far)):
-        even[i] = rows[: even.shape[1], :]
-        odd[i] = rows[even.shape[1] :, :]
+        even[i] = rows[0]
+        odd[i] = rows[1]
 
 
 def routes_body(count, counts, offsets, dest, dest_row, routes):
@@ -292,7 +287,7 @@
 
 
 def hidden_body(count, normed, own, far, near, near_far, kept, next_in, *refs):
-    (second, second_other, third, third_other), (out, weights) = refs[:4], refs[4:]
+    columns, others, out, weights = refs
     seq, mp, group = place()
     depth, units = weights.shape[2:]
     half = depth // 2
@@ -303,11 +298,11 @@
             start = own.shape[2] + (2 * i + k) * units
             span = pl.ds(i * half, half)
             weights[k, seq ^ 1, span, :] = next_in[:, start : start + units]
-    for d, mine, other in ((2, second, second_other), (3, third, third_other)):
+    for j in range(2):
         for i in range(2):
-            span, columns = pl.ds(i * half, half), slice(i * units, (i + 1) * units)
-            weights[group, seq ^ d, span, :] = mine[:, columns]
-            weights[1 - group, seq ^ d, span, :] = other[:, columns]
+            span, half_columns = pl.ds(i * half, half), slice(i * units, (i + 1) * units)
+            weights[group, seq ^ (2 + j), span, :] = columns[j, :, half_columns]
+            weights[1 - group, seq ^ (2 + j), span, :] = others[j, :, half_columns]
     for d in range(count):
         if d == 0:
             pieces = [(normed[:, q * depth : (q + 1) * depth], q) for q in range(count)]
@@ -325,14 +320,9 @@
         out[pl.ds(d * rows, rows), :] = gated.astype(jnp.bfloat16)
 
 
-def down_body(residual, own, far, near, near_far, even, even_other, odd, *outs):
-    _, _, group = place()
+def down_body(residual, own, far, near, near_far, even, odd, *outs):
     rows = outs[0].shape[0]
-    weights = [None, odd[0], None, odd[1]]
-    for j in range(2):
-        mine, other = even[j], even_other[j]
-        low, high = jnp.where(group == 0, mine, other), jnp.where(group == 0, other, mine)
-        weights[2 * j] = jnp.concatenate([low, high], axis=0)
+    weights = [even[0], odd[0], even[1], odd[1]]
     for i, out in enumerate(outs):
         total = residual[...].astype(jnp.float32) if i == 0 else 0.0
         for j, piece in enumerate((own, near, far, near_far)):
@@ -441,33 +431,32 @@
     bf16 = jnp.bfloat16
     vmem, smem = pltpu.VMEM, pltpu.SMEM
 
-    first_out, second_out, quarter = call(
+    *outgoing, down_near, down_far = call(
         functools.partial(cut_first_body, count),
         [
             ((tile_rows, features + 4 * units), bf16),
             ((tile_rows, features + 2 * units), bf16),
+            ((tile_rows, features + 2 * units), bf16),
+            ((2, units, features), bf16),
+            ((2, units, features), bf16),
+        ],
+        (tiles, w_gate, w_up, w_down, gain_enc),
+        spaces=[pltpu.HBM] * 4 + [vmem],
+        copies=13,
+        scratch=[pltpu.VMEM((tile_rows, D_ENC), bf16)],
+        megabytes=57,
+    )
+    kept, normed, residual = call(
+        functools.partial(cut_second_body, count),
+        [
+            ((depth, 2 * units), bf16),
+            ((tile_rows, D_ENC), bf16),
             ((tile_rows, features), bf16),
         ],
         (tiles, w_gate, w_up, gain_enc),
         spaces=[pltpu.HBM] * 3 + [vmem],
-        copies=7,
         scratch=[pltpu.VMEM((tile_rows, D_ENC), bf16)],
-        megabytes=57,
-    )
-    third_out, kept, down_near, down_far, normed, residual = call(
-        functools.partial(cut_second_body, count),
-        [
-            ((tile_rows, 2 * units), bf16),
-            ((depth, 2 * units), bf16),
-            ((3 * units // 2, features), bf16),
-            ((3 * units // 2, features), bf16),
-            ((tile_rows, D_ENC), bf16),
-            ((tile_rows, features), bf16),
-        ],
-        (tiles, w_gate, w_up, w_down, gain_enc),
-        spaces=[pltpu.HBM] * 4 + [vmem],
-        scratch=[pltpu.VMEM((tile_rows, D_ENC), bf16)],
-        copies=9,
+        copies=3,
         megabytes=57,
     )
     routes = call(
@@ -477,36 +466,22 @@
         spaces=[smem, smem, vmem, vmem],
     )[0]
 
-    second_in, third_in = swap(second_out, "seq", 2), swap(quarter, "seq", 3)
-    arrived = second_in, third_in, swap(first_out, "seq", 1)
+    arrived = [swap(outgoing[d - 1], "seq", d) for d in (1, 2, 3)]
     from_far = swap(down_far, "mp", 2)
-    arrived, from_far, routes = lax.optimization_barrier((arrived, from_far, routes))
+    down_send = call(pair_body, [((2, units, features), bf16)] * 2, (down_near, from_far))
+    arrived, down_send, routes, kept, normed, residual = lax.optimization_barrier(
+        (arrived, down_send, routes, kept, normed, residual)
+    )
     own, columns = call(
         restack_body,
         [
             ((count - 1, tile_rows, features), bf16),
-            ((tile_rows, 2 * units), bf16),
+            ((count - 2, tile_rows, 2 * units), bf16),
         ],
         arrived,
     )
-    third_out, down_near, _ = lax.optimization_barrier((third_out, down_near, own))
-    down_send = call(
-        pair_body,
-        [((2, units // 2, features), bf16), ((2, units, features), bf16)],
-        (down_near, from_far),
-    )
-    third, others, far, near, down_send = lax.optimization_barrier(
-        (
-            swap(third_out, "seq", 3),
-            swap(columns, "groups", 1),
-            swap(own, "mp", 2),
-            swap(own, "mp", 1),
-            down_send,
-        )
-    )
-    halves = columns, others, third, swap(third, "groups", 1)
-    spread = far, near, swap(far, "mp", 1)
-    down_send = lax.optimization_barrier((down_send[0], spread[2]))[0], down_send[1]
+    others = swap(columns, "groups", 1)
+    down_send, _ = lax.optimization_barrier((down_send, own))
     parts = []
     for j in range(2):
         perm = []
@@ -516,21 +491,20 @@
                 user = (s ^ 2 * k) if k < 2 else (s + 2 * k - 5) % count
                 perm.append((s * mp_size + m, user * mp_size + k))
         parts.append(lax.ppermute(down_send[j], ("seq", "mp"), perm))
-    halves, spread, parts[0] = lax.optimization_barrier((halves, spread, parts[0]))
+    even, odd = parts
+    spread = spread_mp(own, (others, even))
     hidden = call(
         functools.partial(hidden_body, count),
         [((count * tile_rows, units), bf16)],
-        (normed, own, *spread, kept, arrived[2], *halves),
+        (normed, own, *spread, kept, arrived[0], columns, others),
         scratch=[
             pltpu.VMEM((2, count, depth, units), bf16),
         ],
     )[0]
-    even, odd = parts
-    even_other = swap(even, "groups", 1)
     sums = call(
         down_body,
         [((tile_rows, features), kind) for kind in (jnp.float32, bf16, bf16, bf16)],
-        (residual, hidden, *spread_mp(hidden, even_other), even, even_other, odd),
+        (residual, hidden, *spread_mp(hidden), even, odd),
     )
     holder = [0, 2, 1, 3]
 

time: 108 us -> 109 us (level)
  starting transfers between devices: 31.7 us -> 33.4 us
    ppermute x3, starting transfers between devices: 3.96 us -> 5.54 us  [to_owner(): return lax.ppermute(part, ('seq', 'mp'), perm)]
    ppermute x20 -> x17, waiting for transfers between devices: 48.3 us -> 49.3 us  [swap(): return lax.ppermute(array, axis, [(i, i ^ distance) for i in range(size)])]
    ppermute x20 -> x17, starting transfers between devices: 26.2 us -> 25.6 us  [swap(): return lax.ppermute(array, axis, [(i, i ^ distance) for i in range(size)])]
  transfers between devices with their start and end apart: 25 -> 22, of which waited for: 14 -> 14; matrix products, arithmetic and copies ran while one was open for 0% -> 0% of each run, Pallas kernels for 4% -> 3%
where the time goes in v9:
time: 109 us
  waiting for transfers between devices  60.5 us (56%)
  starting transfers between devices  33.4 us (31%)
  Pallas kernels  13.9 us (13%)
    ppermute x17, waiting for transfers between devices, swap(): return lax.ppermute(array, axis, [(i, i ^ distance) for i in range(size)])  49.3 us
    ppermute x17, starting transfers between devices, swap(): return lax.ppermute(array, axis, [(i, i ^ distance) for i in range(size)])  25.6 us
    pallas_call x10, Pallas kernels, call(): pl.pallas_call(body, out_shape=[jax.ShapeDtypeStruct(shape, kind) for sha...  13.9 us
    ppermute x3, waiting for transfers between devices, to_owner(): return lax.ppermute(part, ('seq', 'mp'), perm)  11.2 us
    ppermute x3, starting transfers between devices, to_owner(): return lax.ppermute(part, ('seq', 'mp'), perm)  5.54 us
    ppermute x2, starting transfers between devices, split_hidden_plan(): parts.append(lax.ppermute(down_send[j], ('seq', 'mp'), perm))  2.26 us
  transfers between devices with their start and end apart: 22, of which 14 were waited for; matrix products, arithmetic and copies ran while one was open for 0% of the time, Pallas kernels for 3%

profile of v9, /device:TPU:0, one launch (start us, length us, event | category | flops | bytes accessed | tf_op | source)
XLA Modules:
  0.0 108.9 jit_solution(17922986442696377234)
XLA Ops:
  0.0 3.6 %shard_map.100 = (bf16[192,1408]{1,0:T(8,128)(2,1)}, bf16[192,896]{1,0:T(8,128)(2,1)}, bf16[192,896]{1,0:T(8,128)(2,1)}, bf16[2,256,384]{2,1,0:T(8,128)(2,1)}, bf16[2,256,384]{2,1,0:T(8,128)(2,1)}) custom-call(bf16[192,1536]{1,0:T(8,128)(2,1)} %tiles.3, bf16[384,1024]{1,0:T(8,128)(2,1)} %w_gate.3, bf16[384,1024]{1,0:T(8,128)(2,1)} %w_up.3, ...), custom_call_target="tpu_custom_call" | custom-call | tf_op jit(solution)/shard_map/pallas_call | solution.py:152
  3.7 0.0 copy-start.5
  3.7 0.0 copy-start.6
  3.7 3.1 %collective-permute-start = (bf16[192,1408]{1,0:T(8,128)(2,1)}, bf16[192,1408]{1,0:T(8,128)(2,1)S(1)}, u32[]{:S(2)}, u32[]{:S(2)}) collective-permute-start(bf16[192,1408]{1,0:T(8,128)(2,1)} %get-tuple-element.37), channel_id=1, source_target_pairs={{0,4},{4,0},{8,12},{12,8},{1,5},{5,1},{9,13},{13,9},{2,6},{6,2},{1... | collective-permute-start | bytes 1622024 | tf_op jit(solution)/shard_map/ppermute | solution.py:140
  6.8 1.5 %collective-permute-start.3 = (bf16[2,256,384]{2,1,0:T(8,128)(2,1)}, bf16[2,256,384]{2,1,0:T(8,128)(2,1)S(1)}, u32[]{:S(2)}, u32[]{:S(2)}) collective-permute-start(bf16[2,256,384]{2,1,0:T(8,128)(2,1)} %get-tuple-element.41), channel_id=1, source_target_pairs={{0,2},{1,3},{2,0},{3,1},{4,6},{5,7},{6,4},{7,5},{8,10},{9,11},{10,... | collective-permute-start | bytes 1179656 | tf_op jit(solution)/shard_map/ppermute | solution.py:140
  8.3 2.6 %collective-permute-start.1 = (bf16[192,896]{1,0:T(8,128)(2,1)}, bf16[192,896]{1,0:T(8,128)(2,1)S(1)}, u32[]{:S(2)}, u32[]{:S(2)}) collective-permute-start(bf16[192,896]{1,0:T(8,128)(2,1)} %get-tuple-element.38), channel_id=1, source_target_pairs={{0,8},{4,12},{8,0},{12,4},{1,9},{5,13},{9,1},{13,5},{2,10},{6,14},... | collective-permute-start | bytes 1032200 | tf_op jit(solution)/shard_map/ppermute | solution.py:140
  10.9 0.2 collective-permute-start.2
  11.1 3.0 %shard_map.103 = (bf16[384,512]{1,0:T(8,128)(2,1)}, bf16[192,1536]{1,0:T(8,128)(2,1)}, bf16[192,384]{1,0:T(8,128)(2,1)}) custom-call(bf16[192,1536]{1,0:T(8,128)(2,1)} %tiles.3, bf16[384,1024]{1,0:T(8,128)(2,1)} %w_gate.3, bf16[384,1024]{1,0:T(8,128)(2,1)} %w_up.3, f32[1536]{0:T(1024)} %gain.3), custom_call_target="tpu_custom_call" | custom-call | tf_op jit(solution)/shard_map/pallas_call | solution.py:152
  14.1 0.1 copy.11.dest
  15.0 0.7 shard_map.102.routes
  15.7 1.9 %collective-permute-done.3.far = bf16[2,256,384]{2,1,0:T(8,128)(2,1)S(1)} collective-permute-done((bf16[2,256,384]{2,1,0:T(8,128)(2,1)}, bf16[2,256,384]{2,1,0:T(8,128)(2,1)S(1)}, u32[]{:S(2)}, u32[]{:S(2)}) %collective-permute-start.3) | collective-permute-done | bytes 393248 | tf_op jit(solution)/shard_map/ppermute | solution.py:140
  17.6 0.1 shard_map.101
  17.6 9.6 %collective-permute-done.1.second = bf16[192,896]{1,0:T(8,128)(2,1)S(1)} collective-permute-done((bf16[192,896]{1,0:T(8,128)(2,1)}, bf16[192,896]{1,0:T(8,128)(2,1)S(1)}, u32[]{:S(2)}, u32[]{:S(2)}) %collective-permute-start.1) | collective-permute-done | bytes 344096 | tf_op jit(solution)/shard_map/ppermute | solution.py:140
  27.2 9.1 %collective-permute-done.2.third = bf16[192,896]{1,0:T(8,128)(2,1)S(1)} collective-permute-done((bf16[192,896]{1,0:T(8,128)(2,1)}, bf16[192,896]{1,0:T(8,128)(2,1)S(1)}, u32[]{:S(2)}, u32[]{:S(2)}) %collective-permute-start.2) | collective-permute-done | bytes 344096 | tf_op jit(solution)/shard_map/ppermute | solution.py:140
  36.3 0.1 shard_map.104
  36.4 1.6 %collective-permute-start.4 = (bf16[3,192,384]{2,1,0:T(8,128)(2,1)S(1)}, bf16[3,192,384]{2,1,0:T(8,128)(2,1)S(1)}, u32[]{:S(2)}, u32[]{:S(2)}) collective-permute-start(bf16[3,192,384]{2,1,0:T(8,128)(2,1)S(1)} %get-tuple-element.53.own), channel_id=1, source_target_pairs={{0,2},{1,3},{2,0},{3,1},{4,6},{5,7},{6,4},{7,5},{8,10},{9,11},{10,... | collective-permute-start | bytes 1327112 | tf_op jit(solution)/shard_map/ppermute | solution.py:140
  37.9 0.7 collective-permute-start.7
  38.6 1.6 %collective-permute-start.6 = (bf16[2,192,512]{2,1,0:T(8,128)(2,1)S(1)}, bf16[2,192,512]{2,1,0:T(8,128)(2,1)S(1)}, u32[]{:S(2)}, u32[]{:S(2)}) collective-permute-start(bf16[2,192,512]{2,1,0:T(8,128)(2,1)S(1)} %get-tuple-element.54.refs_0_), channel_id=1, source_target_pairs={{0,16},{16,0},{1,17},{17,1},{2,18},{18,2},{3,19},{19,3},{4,20},{20... | collective-permute-start | bytes 1179656 | tf_op jit(solution)/shard_map/ppermute | solution.py:140
  40.2 3.9 %collective-permute-start.5 = (bf16[3,192,384]{2,1,0:T(8,128)(2,1)S(1)}, bf16[3,192,384]{2,1,0:T(8,128)(2,1)S(1)}, u32[]{:S(2)}, u32[]{:S(2)}) collective-permute-start(bf16[3,192,384]{2,1,0:T(8,128)(2,1)S(1)} %get-tuple-element.53.own), channel_id=1, source_target_pairs={{0,1},{1,0},{2,3},{3,2},{4,5},{5,4},{6,7},{7,6},{8,9},{9,8},{10,11... | collective-permute-start | bytes 1327112 | tf_op jit(solution)/shard_map/ppermute | solution.py:140
  44.1 3.3 %collective-permute-done.6.refs_1_ = bf16[2,192,512]{2,1,0:T(8,128)(2,1)S(1)} collective-permute-done((bf16[2,192,512]{2,1,0:T(8,128)(2,1)S(1)}, bf16[2,192,512]{2,1,0:T(8,128)(2,1)S(1)}, u32[]{:S(2)}, u32[]{:S(2)}) %collective-permute-start.6) | collective-permute-done | bytes 393248 | tf_op jit(solution)/shard_map/ppermute | solution.py:140
  47.4 4.7 %collective-permute-start.8 = (bf16[3,192,384]{2,1,0:T(8,128)(2,1)S(1)}, bf16[3,192,384]{2,1,0:T(8,128)(2,1)S(1)}, u32[]{:S(2)}, u32[]{:S(2)}) collective-permute-start(bf16[3,192,384]{2,1,0:T(8,128)(2,1)S(1)} %collective-permute-done.4.far), channel_id=1, source_target_pairs={{0,1},{1,0},{2,3},{3,2},{4,5},{5,4},{6,7},{7,6},{8,9},{9,8},{10,11... | collective-permute-start | bytes 1327112 | tf_op jit(solution)/shard_map/ppermute | solution.py:140
  52.2 1.4 %collective-permute-done.8.near_far = bf16[3,192,384]{2,1,0:T(8,128)(2,1)S(1)} collective-permute-done((bf16[3,192,384]{2,1,0:T(8,128)(2,1)S(1)}, bf16[3,192,384]{2,1,0:T(8,128)(2,1)S(1)}, u32[]{:S(2)}, u32[]{:S(2)}) %collective-permute-start.8) | collective-permute-done | bytes 442400 | tf_op jit(solution)/shard_map/ppermute | solution.py:140
  53.6 1.9 %shard_map.105.own = bf16[768,256]{1,0:T(8,128)(2,1)S(1)} custom-call(bf16[192,1536]{1,0:T(8,128)(2,1)S(1)} %copy-done.1, bf16[3,192,384]{2,1,0:T(8,128)(2,1)S(1)} %get-tuple-element.53.own, bf16[3,192,384]{2,1,0:T(8,128)(2,1)S(1)} %collective-permute-done.4.far, bf16[3,192,384]{2,1,0:T(8,128)(2,1)S(1)} %collective-permute-done.5.near, ...), custom_call_target="tpu_custom_call" | custom-call | tf_op jit(solution)/shard_map/pallas_call | solution.py:152
  55.5 0.0 copy-start.7
  55.5 0.0 copy-start
  55.5 1.8 %collective-permute-start.9 = (bf16[768,256]{1,0:T(8,128)(2,1)S(1)}, bf16[768,256]{1,0:T(8,128)(2,1)S(1)}, u32[]{:S(2)}, u32[]{:S(2)}) collective-permute-start(bf16[768,256]{1,0:T(8,128)(2,1)S(1)} %shard_map.105.own), channel_id=1, source_target_pairs={{0,2},{1,3},{2,0},{3,1},{4,6},{5,7},{6,4},{7,5},{8,10},{9,11},{10,... | collective-permute-start | bytes 1179656 | tf_op jit(solution)/shard_map/ppermute | solution.py:140
  57.3 1.6 %collective-permute-start.12 = (bf16[2,256,384]{2,1,0:T(8,128)(2,1)S(1)}, bf16[2,256,384]{2,1,0:T(8,128)(2,1)S(1)}, u32[]{:S(2)}, u32[]{:S(2)}) collective-permute-start(bf16[2,256,384]{2,1,0:T(8,128)(2,1)S(1)} %get-tuple-element.60), channel_id=1, source_target_pairs={{0,9},{1,0},{2,7},{3,14},{4,13},{5,4},{6,11},{7,2},{8,1},{9,8},{10... | collective-permute-start | bytes 1179656 | tf_op jit(solution)/shard_map/ppermute | solution.py:493
  58.9 8.0 %collective-permute-done.9.far = bf16[768,256]{1,0:T(8,128)(2,1)S(1)} collective-permute-done((bf16[768,256]{1,0:T(8,128)(2,1)S(1)}, bf16[768,256]{1,0:T(8,128)(2,1)S(1)}, u32[]{:S(2)}, u32[]{:S(2)}) %collective-permute-start.9) | collective-permute-done | bytes 393248 | tf_op jit(solution)/shard_map/ppermute | solution.py:140
  67.0 1.7 %collective-permute-done.11.near_far = bf16[768,256]{1,0:T(8,128)(2,1)S(1)} collective-permute-done((bf16[768,256]{1,0:T(8,128)(2,1)S(1)}, bf16[768,256]{1,0:T(8,128)(2,1)S(1)}, u32[]{:S(2)}, u32[]{:S(2)}) %collective-permute-start.11) | collective-permute-done | bytes 393248 | tf_op jit(solution)/shard_map/ppermute | solution.py:140
  68.7 1.0 shard_map.106
  69.7 2.0 %collective-permute-start.13 = (bf16[192,384]{1,0:T(8,128)(2,1)S(1)}, bf16[192,384]{1,0:T(8,128)(2,1)S(1)}, u32[]{:S(2)}, u32[]{:S(2)}) collective-permute-start(bf16[192,384]{1,0:T(8,128)(2,1)S(1)} %get-tuple-element.62), channel_id=1, source_target_pairs={{0,9},{1,8},{2,11},{3,10},{4,13},{5,12},{6,15},{7,14},{8,1},{9,0},... | collective-permute-start | bytes 442376 | tf_op jit(solution)/shard_map/ppermute | solution.py:517
  71.6 3.6 %collective-permute-start.14 = (bf16[192,384]{1,0:T(8,128)(2,1)S(1)}, bf16[192,384]{1,0:T(8,128)(2,1)S(1)}, u32[]{:S(2)}, u32[]{:S(2)}) collective-permute-start(bf16[192,384]{1,0:T(8,128)(2,1)S(1)} %get-tuple-element.63), channel_id=1, source_target_pairs={{0,14},{1,15},{2,13},{3,12},{4,11},{5,10},{6,8},{7,9},{8,6},{9,7},... | collective-permute-start | bytes 442376 | tf_op jit(solution)/shard_map/ppermute | solution.py:517
  75.2 0.0 collective-permute-start.15
  75.2 6.9 %collective-permute-done.13.refs_0_ = bf16[192,384]{1,0:T(8,128)(2,1)S(1)} collective-permute-done((bf16[192,384]{1,0:T(8,128)(2,1)S(1)}, bf16[192,384]{1,0:T(8,128)(2,1)S(1)}, u32[]{:S(2)}, u32[]{:S(2)}) %collective-permute-start.13) | collective-permute-done | bytes 147488 | tf_op jit(solution)/shard_map/ppermute | solution.py:517
  82.1 1.1 collective-permute-done.14.refs_1_
  83.2 3.2 %collective-permute-done.15.refs_2_ = bf16[192,384]{1,0:T(8,128)(2,1)S(1)} collective-permute-done((bf16[192,384]{1,0:T(8,128)(2,1)S(1)}, bf16[192,384]{1,0:T(8,128)(2,1)S(1)}, u32[]{:S(2)}, u32[]{:S(2)}) %collective-permute-start.15) | collective-permute-done | bytes 147488 | tf_op jit(solution)/shard_map/ppermute | solution.py:517
  86.4 0.1 shard_map.107.own
  86.5 0.5 collective-permute-start.16
  87.0 5.4 %collective-permute-done.16.far = bf16[192,384]{1,0:T(8,128)(2,1)S(1)} collective-permute-done((bf16[192,384]{1,0:T(8,128)(2,1)S(1)}, bf16[192,384]{1,0:T(8,128)(2,1)S(1)}, u32[]{:S(2)}, u32[]{:S(2)}) %collective-permute-start.16) | collective-permute-done | bytes 147488 | tf_op jit(solution)/shard_map/ppermute | solution.py:140
  92.5 0.0 collective-permute-start.18
  92.5 0.0 collective-permute-done.17.near
  92.5 1.3 %collective-permute-done.18.near_far = bf16[192,384]{1,0:T(8,128)(2,1)S(1)} collective-permute-done((bf16[192,384]{1,0:T(8,128)(2,1)S(1)}, bf16[192,384]{1,0:T(8,128)(2,1)S(1)}, u32[]{:S(2)}, u32[]{:S(2)}) %collective-permute-start.18) | collective-permute-done | bytes 147488 | tf_op jit(solution)/shard_map/ppermute | solution.py:140
  93.8 1.2 %shard_map.108 = (bf16[64,768]{1,0:T(8,128)(2,1)S(1)}, bf16[64,768]{1,0:T(8,128)(2,1)S(1)}, bf16[64,768]{1,0:T(8,128)(2,1)S(1)}, bf16[64,768]{1,0:T(8,128)(2,1)S(1)}) custom-call(f32[1,1536]{1,0:T(1,128)S(1)} %broadcast_in_dim.3.gain, bf16[352,192]{1,0:T(8,128)(2,1)S(1)} %shard_map.102.routes, bf16[576,1536]{1,0:T(8,128)(2,1)S(1)} %bitcast.3, ...), custom_call_target="tpu_custom_call" | custom-call | tf_op jit(solution)/shard_map/pallas_call | solution.py:152
  95.1 2.9 %collective-permute-start.19 = (bf16[64,768]{1,0:T(8,128)(2,1)S(1)}, bf16[64,768]{1,0:T(8,128)(2,1)S(1)}, u32[]{:S(2)}, u32[]{:S(2)}) collective-permute-start(bf16[64,768]{1,0:T(8,128)(2,1)S(1)} %get-tuple-element.65), channel_id=1, source_target_pairs={{0,8},{4,12},{8,0},{12,4},{1,9},{5,13},{9,1},{13,5},{2,10},{6,14},... | collective-permute-start | bytes 294920 | tf_op jit(solution)/shard_map/ppermute | solution.py:140
  98.0 1.2 %collective-permute-start.20 = (bf16[64,768]{1,0:T(8,128)(2,1)S(1)}, bf16[64,768]{1,0:T(8,128)(2,1)S(1)}, u32[]{:S(2)}, u32[]{:S(2)}) collective-permute-start(bf16[64,768]{1,0:T(8,128)(2,1)S(1)} %get-tuple-element.66), channel_id=1, source_target_pairs={{0,12},{4,8},{8,4},{12,0},{1,13},{5,9},{9,5},{13,1},{2,14},{6,10},... | collective-permute-start | bytes 294920 | tf_op jit(solution)/shard_map/ppermute | solution.py:140
  99.3 6.6 %collective-permute-done.19.refs_0_ = bf16[64,768]{1,0:T(8,128)(2,1)S(1)} collective-permute-done((bf16[64,768]{1,0:T(8,128)(2,1)S(1)}, bf16[64,768]{1,0:T(8,128)(2,1)S(1)}, u32[]{:S(2)}, u32[]{:S(2)}) %collective-permute-start.19) | collective-permute-done | bytes 98336 | tf_op jit(solution)/shard_map/ppermute | solution.py:140
  105.9 0.8 collective-permute-done.21.refs_2_
  106.7 2.2 %shard_map.109 = bf16[192,256]{1,0:T(8,128)(2,1)} custom-call(s32[3]{0:T(128)S(1)} %copy-done.6, bf16[64,768]{1,0:T(8,128)(2,1)S(1)} %collective-permute-done.19.refs_0_, bf16[64,768]{1,0:T(8,128)(2,1)S(1)} %collective-permute-done.20.refs_1_, bf16[64,768]{1,0:T(8,128)(2,1)S(1)} %collective-permute-done.21.refs_2_, bf16[64,768]{1,0:T(8,128)(2,1)S(1)} %get-tuple-element.68.refs_3_), custom_call_target="tpu_custom_call" | custom-call | tf_op jit(solution)/shard_map/pallas_call | solution.py:152
  (24 shorter events, 0.1 us)
Async XLA Ops:
  3.7 10.5 %copy-start.5 = (s32[192,1]{0,1:T(1,128)S(1)}, s32[192,1]{0,1:T(1,128)}, u32[]{:S(2)}) copy-start(s32[192,1]{0,1:T(1,128)} %param.12) | copy-start | bytes 2308
  3.7 11.3 %copy-start.6 = (s32[3]{0:T(128)S(1)}, s32[3]{0:T(128)}, u32[]{:S(2)}) copy-start(s32[3]{0:T(128)} %offsets.3) | copy-start | bytes 40
  3.7 13.9 %copy-start.3 = (bf16[2,256,384]{2,1,0:T(8,128)(2,1)S(1)}, bf16[2,256,384]{2,1,0:T(8,128)(2,1)}, u32[]{:S(2)}) copy-start(bf16[2,256,384]{2,1,0:T(8,128)(2,1)} %get-tuple-element.40.near) | copy-start | bytes 1179652
  3.7 32.6 %collective-permute-start = (bf16[192,1408]{1,0:T(8,128)(2,1)}, bf16[192,1408]{1,0:T(8,128)(2,1)S(1)}, u32[]{:S(2)}, u32[]{:S(2)}) collective-permute-start(bf16[192,1408]{1,0:T(8,128)(2,1)} %get-tuple-element.37), channel_id=1, source_target_pairs={{0,4},{4,0},{8,12},{12,8},{1,5},{5,1},{9,13},{13,9},{2,6},{6,2},{1... | collective-permute-start | bytes 1622024 | tf_op jit(solution)/shard_map/ppermute | solution.py:140
  6.8 10.8 %collective-permute-start.3 = (bf16[2,256,384]{2,1,0:T(8,128)(2,1)}, bf16[2,256,384]{2,1,0:T(8,128)(2,1)S(1)}, u32[]{:S(2)}, u32[]{:S(2)}) collective-permute-start(bf16[2,256,384]{2,1,0:T(8,128)(2,1)} %get-tuple-element.41), channel_id=1, source_target_pairs={{0,2},{1,3},{2,0},{3,1},{4,6},{5,7},{6,4},{7,5},{8,10},{9,11},{10,... | collective-permute-start | bytes 1179656 | tf_op jit(solution)/shard_map/ppermute | solution.py:140
  8.3 18.9 %collective-permute-start.1 = (bf16[192,896]{1,0:T(8,128)(2,1)}, bf16[192,896]{1,0:T(8,128)(2,1)S(1)}, u32[]{:S(2)}, u32[]{:S(2)}) collective-permute-start(bf16[192,896]{1,0:T(8,128)(2,1)} %get-tuple-element.38), channel_id=1, source_target_pairs={{0,8},{4,12},{8,0},{12,4},{1,9},{5,13},{9,1},{13,5},{2,10},{6,14},... | collective-permute-start | bytes 1032200 | tf_op jit(solution)/shard_map/ppermute | solution.py:140
  10.9 25.4 %collective-permute-start.2 = (bf16[192,896]{1,0:T(8,128)(2,1)}, bf16[192,896]{1,0:T(8,128)(2,1)S(1)}, u32[]{:S(2)}, u32[]{:S(2)}) collective-permute-start(bf16[192,896]{1,0:T(8,128)(2,1)} %get-tuple-element.39), channel_id=1, source_target_pairs={{0,12},{4,8},{8,4},{12,0},{1,13},{5,9},{9,5},{13,1},{2,14},{6,10},... | collective-permute-start | bytes 1032200 | tf_op jit(solution)/shard_map/ppermute | solution.py:140
  14.1 39.4 %copy-start.1 = (bf16[192,1536]{1,0:T(8,128)(2,1)S(1)}, bf16[192,1536]{1,0:T(8,128)(2,1)}, u32[]{:S(2)}) copy-start(bf16[192,1536]{1,0:T(8,128)(2,1)} %get-tuple-element.49.normed) | copy-start | bytes 1769476
  14.1 39.4 %copy-start.2 = (bf16[384,512]{1,0:T(8,128)(2,1)S(1)}, bf16[384,512]{1,0:T(8,128)(2,1)}, u32[]{:S(2)}) copy-start(bf16[384,512]{1,0:T(8,128)(2,1)} %get-tuple-element.59.kept) | copy-start | bytes 1179652
  36.4 11.0 %collective-permute-start.4 = (bf16[3,192,384]{2,1,0:T(8,128)(2,1)S(1)}, bf16[3,192,384]{2,1,0:T(8,128)(2,1)S(1)}, u32[]{:S(2)}, u32[]{:S(2)}) collective-permute-start(bf16[3,192,384]{2,1,0:T(8,128)(2,1)S(1)} %get-tuple-element.53.own), channel_id=1, source_target_pairs={{0,2},{1,3},{2,0},{3,1},{4,6},{5,7},{6,4},{7,5},{8,10},{9,11},{10,... | collective-permute-start | bytes 1327112 | tf_op jit(solution)/shard_map/ppermute | solution.py:140
  37.9 6.2 %collective-permute-start.7 = (bf16[2,256,384]{2,1,0:T(8,128)(2,1)S(1)}, bf16[2,256,384]{2,1,0:T(8,128)(2,1)S(1)}, u32[]{:S(2)}, u32[]{:S(2)}) collective-permute-start(bf16[2,256,384]{2,1,0:T(8,128)(2,1)S(1)} %get-tuple-element.57), channel_id=1, source_target_pairs={{0,0},{1,9},{2,14},{3,7},{4,4},{5,13},{6,2},{7,11},{8,8},{9,1},{10... | collective-permute-start | bytes 1179656 | tf_op jit(solution)/shard_map/ppermute | solution.py:493
  38.6 30.1 %copy-start.4 = (bf16[192,384]{1,0:T(8,128)(2,1)S(1)}, bf16[192,384]{1,0:T(8,128)(2,1)}, u32[]{:S(2)}) copy-start(bf16[192,384]{1,0:T(8,128)(2,1)} %get-tuple-element.48.residual) | copy-start | bytes 442372
  38.6 8.8 %collective-permute-start.6 = (bf16[2,192,512]{2,1,0:T(8,128)(2,1)S(1)}, bf16[2,192,512]{2,1,0:T(8,128)(2,1)S(1)}, u32[]{:S(2)}, u32[]{:S(2)}) collective-permute-start(bf16[2,192,512]{2,1,0:T(8,128)(2,1)S(1)} %get-tuple-element.54.refs_0_), channel_id=1, source_target_pairs={{0,16},{16,0},{1,17},{17,1},{2,18},{18,2},{3,19},{19,3},{4,20},{20... | collective-permute-start | bytes 1179656 | tf_op jit(solution)/shard_map/ppermute | solution.py:140
  40.2 11.9 %collective-permute-start.5 = (bf16[3,192,384]{2,1,0:T(8,128)(2,1)S(1)}, bf16[3,192,384]{2,1,0:T(8,128)(2,1)S(1)}, u32[]{:S(2)}, u32[]{:S(2)}) collective-permute-start(bf16[3,192,384]{2,1,0:T(8,128)(2,1)S(1)} %get-tuple-element.53.own), channel_id=1, source_target_pairs={{0,1},{1,0},{2,3},{3,2},{4,5},{5,4},{6,7},{7,6},{8,9},{9,8},{10,11... | collective-permute-start | bytes 1327112 | tf_op jit(solution)/shard_map/ppermute | solution.py:140
  47.4 6.1 %collective-permute-start.8 = (bf16[3,192,384]{2,1,0:T(8,128)(2,1)S(1)}, bf16[3,192,384]{2,1,0:T(8,128)(2,1)S(1)}, u32[]{:S(2)}, u32[]{:S(2)}) collective-permute-start(bf16[3,192,384]{2,1,0:T(8,128)(2,1)S(1)} %collective-permute-done.4.far), channel_id=1, source_target_pairs={{0,1},{1,0},{2,3},{3,2},{4,5},{5,4},{6,7},{7,6},{8,9},{9,8},{10,11... | collective-permute-start | bytes 1327112 | tf_op jit(solution)/shard_map/ppermute | solution.py:140
  55.5 37.0 %copy-start.7 = (f32[1536]{0:T(1024)S(1)}, f32[1536]{0:T(1024)}, u32[]{:S(2)}) copy-start(f32[1536]{0:T(1024)} %param.17) | copy-start | bytes 18436
  55.5 38.3 %copy-start = (bf16[1536,576]{0,1:T(8,128)(2,1)S(1)}, bf16[1536,576]{0,1:T(8,128)(2,1)}, u32[]{:S(2)}) copy-start(bf16[1536,576]{0,1:T(8,128)(2,1)} %param.18) | copy-start | bytes 5308420
  55.5 11.5 %collective-permute-start.9 = (bf16[768,256]{1,0:T(8,128)(2,1)S(1)}, bf16[768,256]{1,0:T(8,128)(2,1)S(1)}, u32[]{:S(2)}, u32[]{:S(2)}) collective-permute-start(bf16[768,256]{1,0:T(8,128)(2,1)S(1)} %shard_map.105.own), channel_id=1, source_target_pairs={{0,2},{1,3},{2,0},{3,1},{4,6},{5,7},{6,4},{7,5},{8,10},{9,11},{10,... | collective-permute-start | bytes 1179656 | tf_op jit(solution)/shard_map/ppermute | solution.py:140
  57.3 9.6 %collective-permute-start.12 = (bf16[2,256,384]{2,1,0:T(8,128)(2,1)S(1)}, bf16[2,256,384]{2,1,0:T(8,128)(2,1)S(1)}, u32[]{:S(2)}, u32[]{:S(2)}) collective-permute-start(bf16[2,256,384]{2,1,0:T(8,128)(2,1)S(1)} %get-tuple-element.60), channel_id=1, source_target_pairs={{0,9},{1,0},{2,7},{3,14},{4,13},{5,4},{6,11},{7,2},{8,1},{9,8},{10... | collective-permute-start | bytes 1179656 | tf_op jit(solution)/shard_map/ppermute | solution.py:493
  58.9 8.1 %collective-permute-start.10 = (bf16[768,256]{1,0:T(8,128)(2,1)S(1)}, bf16[768,256]{1,0:T(8,128)(2,1)S(1)}, u32[]{:S(2)}, u32[]{:S(2)}) collective-permute-start(bf16[768,256]{1,0:T(8,128)(2,1)S(1)} %shard_map.105.own), channel_id=1, source_target_pairs={{0,1},{1,0},{2,3},{3,2},{4,5},{5,4},{6,7},{7,6},{8,9},{9,8},{10,11... | collective-permute-start | bytes 1179656 | tf_op jit(solution)/shard_map/ppermute | solution.py:140
  67.0 1.7 %collective-permute-start.11 = (bf16[768,256]{1,0:T(8,128)(2,1)S(1)}, bf16[768,256]{1,0:T(8,128)(2,1)S(1)}, u32[]{:S(2)}, u32[]{:S(2)}) collective-permute-start(bf16[768,256]{1,0:T(8,128)(2,1)S(1)} %collective-permute-done.9.far), channel_id=1, source_target_pairs={{0,1},{1,0},{2,3},{3,2},{4,5},{5,4},{6,7},{7,6},{8,9},{9,8},{10,11... | collective-permute-start | bytes 1179656 | tf_op jit(solution)/shard_map/ppermute | solution.py:140
  69.7 12.5 %collective-permute-start.13 = (bf16[192,384]{1,0:T(8,128)(2,1)S(1)}, bf16[192,384]{1,0:T(8,128)(2,1)S(1)}, u32[]{:S(2)}, u32[]{:S(2)}) collective-permute-start(bf16[192,384]{1,0:T(8,128)(2,1)S(1)} %get-tuple-element.62), channel_id=1, source_target_pairs={{0,9},{1,8},{2,11},{3,10},{4,13},{5,12},{6,15},{7,14},{8,1},{9,0},... | collective-permute-start | bytes 442376 | tf_op jit(solution)/shard_map/ppermute | solution.py:517
  71.6 11.6 %collective-permute-start.14 = (bf16[192,384]{1,0:T(8,128)(2,1)S(1)}, bf16[192,384]{1,0:T(8,128)(2,1)S(1)}, u32[]{:S(2)}, u32[]{:S(2)}) collective-permute-start(bf16[192,384]{1,0:T(8,128)(2,1)S(1)} %get-tuple-element.63), channel_id=1, source_target_pairs={{0,14},{1,15},{2,13},{3,12},{4,11},{5,10},{6,8},{7,9},{8,6},{9,7},... | collective-permute-start | bytes 442376 | tf_op jit(solution)/shard_map/ppermute | solution.py:517
  75.2 11.2 %collective-permute-start.15 = (bf16[192,384]{1,0:T(8,128)(2,1)S(1)}, bf16[192,384]{1,0:T(8,128)(2,1)S(1)}, u32[]{:S(2)}, u32[]{:S(2)}) collective-permute-start(bf16[192,384]{1,0:T(8,128)(2,1)S(1)} %get-tuple-element.64), channel_id=1, source_target_pairs={{0,7},{1,6},{2,4},{3,5},{4,2},{5,3},{6,1},{7,0},{8,15},{9,14},{10,... | collective-permute-start | bytes 442376 | tf_op jit(solution)/shard_map/ppermute | solution.py:517
  86.5 5.9 %collective-permute-start.16 = (bf16[192,384]{1,0:T(8,128)(2,1)S(1)}, bf16[192,384]{1,0:T(8,128)(2,1)S(1)}, u32[]{:S(2)}, u32[]{:S(2)}) collective-permute-start(bf16[192,384]{1,0:T(8,128)(2,1)S(1)} %shard_map.107.own), channel_id=1, source_target_pairs={{0,2},{1,3},{2,0},{3,1},{4,6},{5,7},{6,4},{7,5},{8,10},{9,11},{10,... | collective-permute-start | bytes 442376 | tf_op jit(solution)/shard_map/ppermute | solution.py:140
  87.0 5.5 %collective-permute-start.17 = (bf16[192,384]{1,0:T(8,128)(2,1)S(1)}, bf16[192,384]{1,0:T(8,128)(2,1)S(1)}, u32[]{:S(2)}, u32[]{:S(2)}) collective-permute-start(bf16[192,384]{1,0:T(8,128)(2,1)S(1)} %shard_map.107.own), channel_id=1, source_target_pairs={{0,1},{1,0},{2,3},{3,2},{4,5},{5,4},{6,7},{7,6},{8,9},{9,8},{10,11... | collective-permute-start | bytes 442376 | tf_op jit(solution)/shard_map/ppermute | solution.py:140
  92.5 1.4 %collective-permute-start.18 = (bf16[192,384]{1,0:T(8,128)(2,1)S(1)}, bf16[192,384]{1,0:T(8,128)(2,1)S(1)}, u32[]{:S(2)}, u32[]{:S(2)}) collective-permute-start(bf16[192,384]{1,0:T(8,128)(2,1)S(1)} %collective-permute-done.16.far), channel_id=1, source_target_pairs={{0,1},{1,0},{2,3},{3,2},{4,5},{5,4},{6,7},{7,6},{8,9},{9,8},{10,11... | collective-permute-start | bytes 442376 | tf_op jit(solution)/shard_map/ppermute | solution.py:140
  95.1 10.8 %collective-permute-start.19 = (bf16[64,768]{1,0:T(8,128)(2,1)S(1)}, bf16[64,768]{1,0:T(8,128)(2,1)S(1)}, u32[]{:S(2)}, u32[]{:S(2)}) collective-permute-start(bf16[64,768]{1,0:T(8,128)(2,1)S(1)} %get-tuple-element.65), channel_id=1, source_target_pairs={{0,8},{4,12},{8,0},{12,4},{1,9},{5,13},{9,1},{13,5},{2,10},{6,14},... | collective-permute-start | bytes 294920 | tf_op jit(solution)/shard_map/ppermute | solution.py:140
  98.0 7.9 %collective-permute-start.20 = (bf16[64,768]{1,0:T(8,128)(2,1)S(1)}, bf16[64,768]{1,0:T(8,128)(2,1)S(1)}, u32[]{:S(2)}, u32[]{:S(2)}) collective-permute-start(bf16[64,768]{1,0:T(8,128)(2,1)S(1)} %get-tuple-element.66), channel_id=1, source_target_pairs={{0,12},{4,8},{8,4},{12,0},{1,13},{5,9},{9,5},{13,1},{2,14},{6,10},... | collective-permute-start | bytes 294920 | tf_op jit(solution)/shard_map/ppermute | solution.py:140
  99.2 7.4 %collective-permute-start.21 = (bf16[64,768]{1,0:T(8,128)(2,1)S(1)}, bf16[64,768]{1,0:T(8,128)(2,1)S(1)}, u32[]{:S(2)}, u32[]{:S(2)}) collective-permute-start(bf16[64,768]{1,0:T(8,128)(2,1)S(1)} %get-tuple-element.67), channel_id=1, source_target_pairs={{0,4},{4,0},{8,12},{12,8},{1,5},{5,1},{9,13},{13,9},{2,6},{6,2},{1... | collective-permute-start | bytes 294920 | tf_op jit(solution)/shard_map/ppermute | solution.py:140

commit v10 on v8

--- a/solution.py
+++ b/solution.py
@@ -506,7 +506,6 @@
     )
     halves = columns, others, third, swap(third, "groups", 1)
     spread = far, near, swap(far, "mp", 1)
-    down_send = lax.optimization_barrier((down_send[0], spread[2]))[0], down_send[1]
     parts = []
     for j in range(2):
         perm = []
@@ -516,7 +515,6 @@
                 user = (s ^ 2 * k) if k < 2 else (s + 2 * k - 5) % count
                 perm.append((s * mp_size + m, user * mp_size + k))
         parts.append(lax.ppermute(down_send[j], ("seq", "mp"), perm))
-    halves, spread, parts[0] = lax.optimization_barrier((halves, spread, parts[0]))
     hidden = call(
         functools.partial(hidden_body, count),
         [((count * tile_rows, units), bf16)],

time: 108 us -> 106 us (0.981)
  starting transfers between devices: 31.7 us -> 28.9 us
    ppermute x20, starting transfers between devices: 26.2 us -> 22.1 us  [swap(): return lax.ppermute(array, axis, [(i, i ^ distance) for i in range(size)])]
    ppermute x3, starting transfers between devices: 3.96 us -> 5.39 us  [to_owner(): return lax.ppermute(part, ('seq', 'mp'), perm)]
  transfers between devices with their start and end apart: 25 -> 25, of which waited for: 14 -> 14; matrix products, arithmetic and copies ran while one was open for 0% -> 0% of each run, Pallas kernels for 4% -> 6%
where the time goes in v10:
time: 106 us; the launch traced here: 105 us
  waiting for transfers between devices  60.9 us (57%)
  starting transfers between devices  28.9 us (27%)
  Pallas kernels  13.6 us (13%)
  local copies, waits for them, and re-layouts  1.12 us (1%)
    ppermute x20, waiting for transfers between devices, swap(): return lax.ppermute(array, axis, [(i, i ^ distance) for i in range(size)])  48.7 us
    ppermute x20, starting transfers between devices, swap(): return lax.ppermute(array, axis, [(i, i ^ distance) for i in range(size)])  22.1 us
    pallas_call x10, Pallas kernels, call(): pl.pallas_call(body, out_shape=[jax.ShapeDtypeStruct(shape, kind) for sha...  13.6 us
    ppermute x3, waiting for transfers between devices, to_owner(): return lax.ppermute(part, ('seq', 'mp'), perm)  12.2 us
    ppermute x3, starting transfers between devices, to_owner(): return lax.ppermute(part, ('seq', 'mp'), perm)  5.39 us
  transfers between devices with their start and end apart: 25, of which 14 were waited for; matrix products, arithmetic and copies ran while one was open for 0% of the time, Pallas kernels for 6%

profile of v10, /device:TPU:0, one launch (start us, length us, event | category | flops | bytes accessed | tf_op | source)
XLA Modules:
  0.0 105.4 jit_solution(14316630809915889372)
XLA Ops:
  0.0 3.0 %shard_map.100 = (bf16[192,1408]{1,0:T(8,128)(2,1)}, bf16[192,896]{1,0:T(8,128)(2,1)}, bf16[192,384]{1,0:T(8,128)(2,1)}) custom-call(bf16[192,1536]{1,0:T(8,128)(2,1)} %tiles.3, bf16[384,1024]{1,0:T(8,128)(2,1)} %w_gate.3, bf16[384,1024]{1,0:T(8,128)(2,1)} %w_up.3, f32[1536]{0:T(1024)} %gain.3), custom_call_target="tpu_custom_call" | custom-call | tf_op jit(solution)/shard_map/pallas_call | solution.py:152
  3.0 0.0 copy-start.5
  3.1 0.0 copy-start.6
  3.1 3.1 %collective-permute-start.2 = (bf16[192,1408]{1,0:T(8,128)(2,1)}, bf16[192,1408]{1,0:T(8,128)(2,1)S(1)}, u32[]{:S(2)}, u32[]{:S(2)}) collective-permute-start(bf16[192,1408]{1,0:T(8,128)(2,1)} %get-tuple-element.42), channel_id=1, source_target_pairs={{0,4},{4,0},{8,12},{12,8},{1,5},{5,1},{9,13},{13,9},{2,6},{6,2},{1... | collective-permute-start | bytes 1622024 | tf_op jit(solution)/shard_map/ppermute | solution.py:140
  6.2 2.6 %collective-permute-start = (bf16[192,896]{1,0:T(8,128)(2,1)}, bf16[192,896]{1,0:T(8,128)(2,1)S(1)}, u32[]{:S(2)}, u32[]{:S(2)}) collective-permute-start(bf16[192,896]{1,0:T(8,128)(2,1)} %get-tuple-element.40), channel_id=1, source_target_pairs={{0,8},{4,12},{8,0},{12,4},{1,9},{5,13},{9,1},{13,5},{2,10},{6,14},... | collective-permute-start | bytes 1032200 | tf_op jit(solution)/shard_map/ppermute | solution.py:140
  8.7 3.4 %shard_map.101 = (bf16[192,512]{1,0:T(8,128)(2,1)}, bf16[384,512]{1,0:T(8,128)(2,1)}, bf16[384,384]{1,0:T(8,128)(2,1)}, bf16[384,384]{1,0:T(8,128)(2,1)}, bf16[1...) custom-call(bf16[192,1536]{1,0:T(8,128)(2,1)} %tiles.3, bf16[384,1024]{1,0:T(8,128)(2,1)} %w_gate.3, ...), custom_call_target="tpu_custom_call" | custom-call | tf_op jit(solution)/shard_map/pallas_call | solution.py:152
  12.2 1.6 %collective-permute-start.3 = (bf16[384,384]{1,0:T(8,128)(2,1)}, bf16[384,384]{1,0:T(8,128)(2,1)S(1)}, u32[]{:S(2)}, u32[]{:S(2)}) collective-permute-start(bf16[384,384]{1,0:T(8,128)(2,1)} %get-tuple-element.43), channel_id=1, source_target_pairs={{0,2},{1,3},{2,0},{3,1},{4,6},{5,7},{6,4},{7,5},{8,10},{9,11},{10,... | collective-permute-start | bytes 884744 | tf_op jit(solution)/shard_map/ppermute | solution.py:140
  13.7 0.2 collective-permute-start.1
  14.0 0.1 copy.11.dest
  14.8 0.7 shard_map.102.routes
  15.4 15.9 %collective-permute-done.1.third = bf16[192,384]{1,0:T(8,128)(2,1)S(1)} collective-permute-done((bf16[192,384]{1,0:T(8,128)(2,1)S(1)}, bf16[192,384]{1,0:T(8,128)(2,1)S(1)}, u32[]{:S(2)}, u32[]{:S(2)}) %collective-permute-start.1) | collective-permute-done | bytes 147488 | tf_op jit(solution)/shard_map/ppermute | solution.py:140
  31.4 0.1 shard_map.103
  31.4 1.6 %collective-permute-start.6 = (bf16[3,192,384]{2,1,0:T(8,128)(2,1)S(1)}, bf16[3,192,384]{2,1,0:T(8,128)(2,1)S(1)}, u32[]{:S(2)}, u32[]{:S(2)}) collective-permute-start(bf16[3,192,384]{2,1,0:T(8,128)(2,1)S(1)} %get-tuple-element.50.own), channel_id=1, source_target_pairs={{0,2},{1,3},{2,0},{3,1},{4,6},{5,7},{6,4},{7,5},{8,10},{9,11},{10,... | collective-permute-start | bytes 1327112 | tf_op jit(solution)/shard_map/ppermute | solution.py:140
  33.0 1.6 %collective-permute-start.4 = (bf16[192,512]{1,0:T(8,128)(2,1)}, bf16[192,512]{1,0:T(8,128)(2,1)S(1)}, u32[]{:S(2)}, u32[]{:S(2)}) collective-permute-start(bf16[192,512]{1,0:T(8,128)(2,1)} %get-tuple-element.53), channel_id=1, source_target_pairs={{0,12},{4,8},{8,4},{12,0},{1,13},{5,9},{9,5},{13,1},{2,14},{6,10},... | collective-permute-start | bytes 589832 | tf_op jit(solution)/shard_map/ppermute | solution.py:140
  34.6 1.5 %collective-permute-start.5 = (bf16[192,512]{1,0:T(8,128)(2,1)S(1)}, bf16[192,512]{1,0:T(8,128)(2,1)S(1)}, u32[]{:S(2)}, u32[]{:S(2)}) collective-permute-start(bf16[192,512]{1,0:T(8,128)(2,1)S(1)} %get-tuple-element.54.refs_0_), channel_id=1, source_target_pairs={{0,16},{16,0},{1,17},{17,1},{2,18},{18,2},{3,19},{19,3},{4,20},{20... | collective-permute-start | bytes 589832 | tf_op jit(solution)/shard_map/ppermute | solution.py:140
  36.1 1.0 copy-done.3
  37.0 0.1 shard_map.104
  37.1 5.3 %collective-permute-done.4.refs_2_ = bf16[192,512]{1,0:T(8,128)(2,1)S(1)} collective-permute-done((bf16[192,512]{1,0:T(8,128)(2,1)}, bf16[192,512]{1,0:T(8,128)(2,1)S(1)}, u32[]{:S(2)}, u32[]{:S(2)}) %collective-permute-start.4) | collective-permute-done | bytes 196640 | tf_op jit(solution)/shard_map/ppermute | solution.py:140
  42.4 0.1 collective-permute-done.6.far
  42.5 1.6 %collective-permute-start.9 = (bf16[192,512]{1,0:T(8,128)(2,1)S(1)}, bf16[192,512]{1,0:T(8,128)(2,1)S(1)}, u32[]{:S(2)}, u32[]{:S(2)}) collective-permute-start(bf16[192,512]{1,0:T(8,128)(2,1)S(1)} %collective-permute-done.4.refs_2_), channel_id=1, source_target_pairs={{0,16},{16,0},{1,17},{17,1},{2,18},{18,2},{3,19},{19,3},{4,20},{20... | collective-permute-start | bytes 589832 | tf_op jit(solution)/shard_map/ppermute | solution.py:140
  44.1 0.7 collective-permute-start.12
  44.8 5.1 %collective-permute-done.9.refs_3_ = bf16[192,512]{1,0:T(8,128)(2,1)S(1)} collective-permute-done((bf16[192,512]{1,0:T(8,128)(2,1)S(1)}, bf16[192,512]{1,0:T(8,128)(2,1)S(1)}, u32[]{:S(2)}, u32[]{:S(2)}) %collective-permute-start.9) | collective-permute-done | bytes 196640 | tf_op jit(solution)/shard_map/ppermute | solution.py:140
  49.9 1.9 %shard_map.105.own = bf16[768,256]{1,0:T(8,128)(2,1)S(1)} custom-call(bf16[192,1536]{1,0:T(8,128)(2,1)S(1)} %copy-done.1, bf16[3,192,384]{2,1,0:T(8,128)(2,1)S(1)} %get-tuple-element.50.own, bf16[3,192,384]{2,1,0:T(8,128)(2,1)S(1)} %collective-permute-done.6.far, bf16[3,192,384]{2,1,0:T(8,128)(2,1)S(1)} %collective-permute-done.7.near, ...), custom_call_target="tpu_custom_call" | custom-call | tf_op jit(solution)/shard_map/pallas_call | solution.py:152
  51.8 0.0 copy-start.7
  51.8 0.0 copy-start
  51.8 1.6 %collective-permute-start.10 = (bf16[768,256]{1,0:T(8,128)(2,1)S(1)}, bf16[768,256]{1,0:T(8,128)(2,1)S(1)}, u32[]{:S(2)}, u32[]{:S(2)}) collective-permute-start(bf16[768,256]{1,0:T(8,128)(2,1)S(1)} %shard_map.105.own), channel_id=1, source_target_pairs={{0,2},{1,3},{2,0},{3,1},{4,6},{5,7},{6,4},{7,5},{8,10},{9,11},{10,... | collective-permute-start | bytes 1179656 | tf_op jit(solution)/shard_map/ppermute | solution.py:140
  53.4 1.5 %collective-permute-start.13 = (bf16[2,128,384]{2,1,0:T(8,128)(2,1)S(1)}, bf16[2,128,384]{2,1,0:T(8,128)(2,1)S(1)}, u32[]{:S(2)}, u32[]{:S(2)}) collective-permute-start(bf16[2,128,384]{2,1,0:T(8,128)(2,1)S(1)} %collective-permute-done.12.even), channel_id=1, source_target_pairs={{0,16},{16,0},{1,17},{17,1},{2,18},{18,2},{3,19},{19,3},{4,20},{20... | collective-permute-start | bytes 589832 | tf_op jit(solution)/shard_map/ppermute | solution.py:140
  54.9 0.8 collective-permute-start.15
  55.7 5.2 %collective-permute-done.13.even_other = bf16[2,128,384]{2,1,0:T(8,128)(2,1)S(1)} collective-permute-done((bf16[2,128,384]{2,1,0:T(8,128)(2,1)S(1)}, bf16[2,128,384]{2,1,0:T(8,128)(2,1)S(1)}, u32[]{:S(2)}, u32[]{:S(2)}) %collective-permute-start.13) | collective-permute-done | bytes 196640 | tf_op jit(solution)/shard_map/ppermute | solution.py:140
  60.9 1.7 %collective-permute-done.10.far = bf16[768,256]{1,0:T(8,128)(2,1)S(1)} collective-permute-done((bf16[768,256]{1,0:T(8,128)(2,1)S(1)}, bf16[768,256]{1,0:T(8,128)(2,1)S(1)}, u32[]{:S(2)}, u32[]{:S(2)}) %collective-permute-start.10) | collective-permute-done | bytes 393248 | tf_op jit(solution)/shard_map/ppermute | solution.py:140
  62.6 1.7 %collective-permute-done.14.near_far = bf16[768,256]{1,0:T(8,128)(2,1)S(1)} collective-permute-done((bf16[768,256]{1,0:T(8,128)(2,1)S(1)}, bf16[768,256]{1,0:T(8,128)(2,1)S(1)}, u32[]{:S(2)}, u32[]{:S(2)}) %collective-permute-start.14) | collective-permute-done | bytes 393248 | tf_op jit(solution)/shard_map/ppermute | solution.py:140
  64.3 1.0 shard_map.106
  65.3 2.8 %collective-permute-start.16 = (bf16[192,384]{1,0:T(8,128)(2,1)S(1)}, bf16[192,384]{1,0:T(8,128)(2,1)S(1)}, u32[]{:S(2)}, u32[]{:S(2)}) collective-permute-start(bf16[192,384]{1,0:T(8,128)(2,1)S(1)} %get-tuple-element.68), channel_id=1, source_target_pairs={{0,9},{1,8},{2,11},{3,10},{4,13},{5,12},{6,15},{7,14},{8,1},{9,0},... | collective-permute-start | bytes 442376 | tf_op jit(solution)/shard_map/ppermute | solution.py:541
  68.1 2.4 %collective-permute-start.17 = (bf16[192,384]{1,0:T(8,128)(2,1)S(1)}, bf16[192,384]{1,0:T(8,128)(2,1)S(1)}, u32[]{:S(2)}, u32[]{:S(2)}) collective-permute-start(bf16[192,384]{1,0:T(8,128)(2,1)S(1)} %get-tuple-element.69), channel_id=1, source_target_pairs={{0,14},{1,15},{2,13},{3,12},{4,11},{5,10},{6,8},{7,9},{8,6},{9,7},... | collective-permute-start | bytes 442376 | tf_op jit(solution)/shard_map/ppermute | solution.py:541
  70.5 0.2 collective-permute-start.18
  70.7 5.9 %collective-permute-done.16.refs_0_ = bf16[192,384]{1,0:T(8,128)(2,1)S(1)} collective-permute-done((bf16[192,384]{1,0:T(8,128)(2,1)S(1)}, bf16[192,384]{1,0:T(8,128)(2,1)S(1)}, u32[]{:S(2)}, u32[]{:S(2)}) %collective-permute-start.16) | collective-permute-done | bytes 147488 | tf_op jit(solution)/shard_map/ppermute | solution.py:541
  76.6 1.8 %collective-permute-done.17.refs_1_ = bf16[192,384]{1,0:T(8,128)(2,1)S(1)} collective-permute-done((bf16[192,384]{1,0:T(8,128)(2,1)S(1)}, bf16[192,384]{1,0:T(8,128)(2,1)S(1)}, u32[]{:S(2)}, u32[]{:S(2)}) %collective-permute-start.17) | collective-permute-done | bytes 147488 | tf_op jit(solution)/shard_map/ppermute | solution.py:541
  78.3 4.6 %collective-permute-done.18.refs_2_ = bf16[192,384]{1,0:T(8,128)(2,1)S(1)} collective-permute-done((bf16[192,384]{1,0:T(8,128)(2,1)S(1)}, bf16[192,384]{1,0:T(8,128)(2,1)S(1)}, u32[]{:S(2)}, u32[]{:S(2)}) %collective-permute-start.18) | collective-permute-done | bytes 147488 | tf_op jit(solution)/shard_map/ppermute | solution.py:541
  82.9 0.1 shard_map.107.own
  83.0 0.5 collective-permute-start.19
  83.4 5.4 %collective-permute-done.19.far = bf16[192,384]{1,0:T(8,128)(2,1)S(1)} collective-permute-done((bf16[192,384]{1,0:T(8,128)(2,1)S(1)}, bf16[192,384]{1,0:T(8,128)(2,1)S(1)}, u32[]{:S(2)}, u32[]{:S(2)}) %collective-permute-start.19) | collective-permute-done | bytes 147488 | tf_op jit(solution)/shard_map/ppermute | solution.py:140
  88.9 1.3 %collective-permute-done.21.near_far = bf16[192,384]{1,0:T(8,128)(2,1)S(1)} collective-permute-done((bf16[192,384]{1,0:T(8,128)(2,1)S(1)}, bf16[192,384]{1,0:T(8,128)(2,1)S(1)}, u32[]{:S(2)}, u32[]{:S(2)}) %collective-permute-start.21) | collective-permute-done | bytes 147488 | tf_op jit(solution)/shard_map/ppermute | solution.py:140
  90.3 1.3 %shard_map.108 = (bf16[64,768]{1,0:T(8,128)(2,1)S(1)}, bf16[64,768]{1,0:T(8,128)(2,1)S(1)}, bf16[64,768]{1,0:T(8,128)(2,1)S(1)}, bf16[64,768]{1,0:T(8,128)(2,1)S(1)}) custom-call(f32[1,1536]{1,0:T(1,128)S(1)} %broadcast_in_dim.3.gain, bf16[352,192]{1,0:T(8,128)(2,1)S(1)} %shard_map.102.routes, bf16[576,1536]{1,0:T(8,128)(2,1)S(1)} %bitcast.3, ...), custom_call_target="tpu_custom_call" | custom-call | tf_op jit(solution)/shard_map/pallas_call | solution.py:152
  91.5 2.2 %collective-permute-start.22 = (bf16[64,768]{1,0:T(8,128)(2,1)S(1)}, bf16[64,768]{1,0:T(8,128)(2,1)S(1)}, u32[]{:S(2)}, u32[]{:S(2)}) collective-permute-start(bf16[64,768]{1,0:T(8,128)(2,1)S(1)} %get-tuple-element.71), channel_id=1, source_target_pairs={{0,8},{4,12},{8,0},{12,4},{1,9},{5,13},{9,1},{13,5},{2,10},{6,14},... | collective-permute-start | bytes 294920 | tf_op jit(solution)/shard_map/ppermute | solution.py:140
  93.7 2.7 %collective-permute-start.23 = (bf16[64,768]{1,0:T(8,128)(2,1)S(1)}, bf16[64,768]{1,0:T(8,128)(2,1)S(1)}, u32[]{:S(2)}, u32[]{:S(2)}) collective-permute-start(bf16[64,768]{1,0:T(8,128)(2,1)S(1)} %get-tuple-element.72), channel_id=1, source_target_pairs={{0,12},{4,8},{8,4},{12,0},{1,13},{5,9},{9,5},{13,1},{2,14},{6,10},... | collective-permute-start | bytes 294920 | tf_op jit(solution)/shard_map/ppermute | solution.py:140
  96.4 5.9 %collective-permute-done.22.refs_0_ = bf16[64,768]{1,0:T(8,128)(2,1)S(1)} collective-permute-done((bf16[64,768]{1,0:T(8,128)(2,1)S(1)}, bf16[64,768]{1,0:T(8,128)(2,1)S(1)}, u32[]{:S(2)}, u32[]{:S(2)}) %collective-permute-start.22) | collective-permute-done | bytes 98336 | tf_op jit(solution)/shard_map/ppermute | solution.py:140
  102.3 0.9 collective-permute-done.24.refs_2_
  103.2 2.2 %shard_map.109 = bf16[192,256]{1,0:T(8,128)(2,1)} custom-call(s32[3]{0:T(128)S(1)} %copy-done.6, bf16[64,768]{1,0:T(8,128)(2,1)S(1)} %collective-permute-done.22.refs_0_, bf16[64,768]{1,0:T(8,128)(2,1)S(1)} %collective-permute-done.23.refs_1_, bf16[64,768]{1,0:T(8,128)(2,1)S(1)} %collective-permute-done.24.refs_2_, bf16[64,768]{1,0:T(8,128)(2,1)S(1)} %get-tuple-element.74.refs_3_), custom_call_target="tpu_custom_call" | custom-call | tf_op jit(solution)/shard_map/pallas_call | solution.py:152
  (32 shorter events, 0.1 us)
Async XLA Ops:
  3.0 10.7 %copy-start.8 = (bf16[192,384]{1,0:T(8,128)(2,1)S(1)}, bf16[192,384]{1,0:T(8,128)(2,1)}, u32[]{:S(2)}) copy-start(bf16[192,384]{1,0:T(8,128)(2,1)} %get-tuple-element.41) | copy-start | bytes 442372
  3.0 10.9 %copy-start.5 = (s32[192,1]{0,1:T(1,128)S(1)}, s32[192,1]{0,1:T(1,128)}, u32[]{:S(2)}) copy-start(s32[192,1]{0,1:T(1,128)} %param.12) | copy-start | bytes 2308
  3.1 11.7 %copy-start.6 = (s32[3]{0:T(128)S(1)}, s32[3]{0:T(128)}, u32[]{:S(2)}) copy-start(s32[3]{0:T(128)} %offsets.3) | copy-start | bytes 40
  3.1 28.3 %collective-permute-start.2 = (bf16[192,1408]{1,0:T(8,128)(2,1)}, bf16[192,1408]{1,0:T(8,128)(2,1)S(1)}, u32[]{:S(2)}, u32[]{:S(2)}) collective-permute-start(bf16[192,1408]{1,0:T(8,128)(2,1)} %get-tuple-element.42), channel_id=1, source_target_pairs={{0,4},{4,0},{8,12},{12,8},{1,5},{5,1},{9,13},{13,9},{2,6},{6,2},{1... | collective-permute-start | bytes 1622024 | tf_op jit(solution)/shard_map/ppermute | solution.py:140
  6.2 25.2 %collective-permute-start = (bf16[192,896]{1,0:T(8,128)(2,1)}, bf16[192,896]{1,0:T(8,128)(2,1)S(1)}, u32[]{:S(2)}, u32[]{:S(2)}) collective-permute-start(bf16[192,896]{1,0:T(8,128)(2,1)} %get-tuple-element.40), channel_id=1, source_target_pairs={{0,8},{4,12},{8,0},{12,4},{1,9},{5,13},{9,1},{13,5},{2,10},{6,14},... | collective-permute-start | bytes 1032200 | tf_op jit(solution)/shard_map/ppermute | solution.py:140
  12.2 37.7 %copy-start.1 = (bf16[192,1536]{1,0:T(8,128)(2,1)S(1)}, bf16[192,1536]{1,0:T(8,128)(2,1)}, u32[]{:S(2)}) copy-start(bf16[192,1536]{1,0:T(8,128)(2,1)} %get-tuple-element.46.normed) | copy-start | bytes 1769476
  12.2 37.7 %copy-start.2 = (bf16[384,512]{1,0:T(8,128)(2,1)S(1)}, bf16[384,512]{1,0:T(8,128)(2,1)}, u32[]{:S(2)}) copy-start(bf16[384,512]{1,0:T(8,128)(2,1)} %get-tuple-element.61.kept) | copy-start | bytes 1179652
  12.2 19.2 %collective-permute-start.3 = (bf16[384,384]{1,0:T(8,128)(2,1)}, bf16[384,384]{1,0:T(8,128)(2,1)S(1)}, u32[]{:S(2)}, u32[]{:S(2)}) collective-permute-start(bf16[384,384]{1,0:T(8,128)(2,1)} %get-tuple-element.43), channel_id=1, source_target_pairs={{0,2},{1,3},{2,0},{3,1},{4,6},{5,7},{6,4},{7,5},{8,10},{9,11},{10,... | collective-permute-start | bytes 884744 | tf_op jit(solution)/shard_map/ppermute | solution.py:140
  13.7 17.6 %collective-permute-start.1 = (bf16[192,384]{1,0:T(8,128)(2,1)S(1)}, bf16[192,384]{1,0:T(8,128)(2,1)S(1)}, u32[]{:S(2)}, u32[]{:S(2)}) collective-permute-start(bf16[192,384]{1,0:T(8,128)(2,1)S(1)} %copy-done.8), channel_id=1, source_target_pairs={{0,12},{4,8},{8,4},{12,0},{1,13},{5,9},{9,5},{13,1},{2,14},{6,10},... | collective-permute-start | bytes 442376 | tf_op jit(solution)/shard_map/ppermute | solution.py:140
  31.4 11.1 %collective-permute-start.6 = (bf16[3,192,384]{2,1,0:T(8,128)(2,1)S(1)}, bf16[3,192,384]{2,1,0:T(8,128)(2,1)S(1)}, u32[]{:S(2)}, u32[]{:S(2)}) collective-permute-start(bf16[3,192,384]{2,1,0:T(8,128)(2,1)S(1)} %get-tuple-element.50.own), channel_id=1, source_target_pairs={{0,2},{1,3},{2,0},{3,1},{4,6},{5,7},{6,4},{7,5},{8,10},{9,11},{10,... | collective-permute-start | bytes 1327112 | tf_op jit(solution)/shard_map/ppermute | solution.py:140
  33.0 9.5 %collective-permute-start.7 = (bf16[3,192,384]{2,1,0:T(8,128)(2,1)S(1)}, bf16[3,192,384]{2,1,0:T(8,128)(2,1)S(1)}, u32[]{:S(2)}, u32[]{:S(2)}) collective-permute-start(bf16[3,192,384]{2,1,0:T(8,128)(2,1)S(1)} %get-tuple-element.50.own), channel_id=1, source_target_pairs={{0,1},{1,0},{2,3},{3,2},{4,5},{5,4},{6,7},{7,6},{8,9},{9,8},{10,11... | collective-permute-start | bytes 1327112 | tf_op jit(solution)/shard_map/ppermute | solution.py:140
  33.0 9.4 %collective-permute-start.4 = (bf16[192,512]{1,0:T(8,128)(2,1)}, bf16[192,512]{1,0:T(8,128)(2,1)S(1)}, u32[]{:S(2)}, u32[]{:S(2)}) collective-permute-start(bf16[192,512]{1,0:T(8,128)(2,1)} %get-tuple-element.53), channel_id=1, source_target_pairs={{0,12},{4,8},{8,4},{12,0},{1,13},{5,9},{9,5},{13,1},{2,14},{6,10},... | collective-permute-start | bytes 589832 | tf_op jit(solution)/shard_map/ppermute | solution.py:140
  34.6 7.9 %collective-permute-start.5 = (bf16[192,512]{1,0:T(8,128)(2,1)S(1)}, bf16[192,512]{1,0:T(8,128)(2,1)S(1)}, u32[]{:S(2)}, u32[]{:S(2)}) collective-permute-start(bf16[192,512]{1,0:T(8,128)(2,1)S(1)} %get-tuple-element.54.refs_0_), channel_id=1, source_target_pairs={{0,16},{16,0},{1,17},{17,1},{2,18},{18,2},{3,19},{19,3},{4,20},{20... | collective-permute-start | bytes 589832 | tf_op jit(solution)/shard_map/ppermute | solution.py:140
  36.1 1.0 copy-start.3
  42.5 7.3 %collective-permute-start.8 = (bf16[3,192,384]{2,1,0:T(8,128)(2,1)S(1)}, bf16[3,192,384]{2,1,0:T(8,128)(2,1)S(1)}, u32[]{:S(2)}, u32[]{:S(2)}) collective-permute-start(bf16[3,192,384]{2,1,0:T(8,128)(2,1)S(1)} %collective-permute-done.6.far), channel_id=1, source_target_pairs={{0,1},{1,0},{2,3},{3,2},{4,5},{5,4},{6,7},{7,6},{8,9},{9,8},{10,11... | collective-permute-start | bytes 1327112 | tf_op jit(solution)/shard_map/ppermute | solution.py:140
  42.5 7.3 %collective-permute-start.9 = (bf16[192,512]{1,0:T(8,128)(2,1)S(1)}, bf16[192,512]{1,0:T(8,128)(2,1)S(1)}, u32[]{:S(2)}, u32[]{:S(2)}) collective-permute-start(bf16[192,512]{1,0:T(8,128)(2,1)S(1)} %collective-permute-done.4.refs_2_), channel_id=1, source_target_pairs={{0,16},{16,0},{1,17},{17,1},{2,18},{18,2},{3,19},{19,3},{4,20},{20... | collective-permute-start | bytes 589832 | tf_op jit(solution)/shard_map/ppermute | solution.py:140
  44.1 9.3 %collective-permute-start.12 = (bf16[2,128,384]{2,1,0:T(8,128)(2,1)S(1)}, bf16[2,128,384]{2,1,0:T(8,128)(2,1)S(1)}, u32[]{:S(2)}, u32[]{:S(2)}) collective-permute-start(bf16[2,128,384]{2,1,0:T(8,128)(2,1)S(1)} %get-tuple-element.64), channel_id=1, source_target_pairs={{0,0},{1,9},{2,14},{3,7},{4,4},{5,13},{6,2},{7,11},{8,8},{9,1},{10... | collective-permute-start | bytes 589832 | tf_op jit(solution)/shard_map/ppermute | solution.py:517
  49.9 14.4 %copy-start.4 = (bf16[192,384]{1,0:T(8,128)(2,1)S(1)}, bf16[192,384]{1,0:T(8,128)(2,1)}, u32[]{:S(2)}) copy-start(bf16[192,384]{1,0:T(8,128)(2,1)} %get-tuple-element.45.residual) | copy-start | bytes 442372
  51.8 37.1 %copy-start.7 = (f32[1536]{0:T(1024)S(1)}, f32[1536]{0:T(1024)}, u32[]{:S(2)}) copy-start(f32[1536]{0:T(1024)} %param.17) | copy-start | bytes 18436
  51.8 38.5 %copy-start = (bf16[1536,576]{0,1:T(8,128)(2,1)S(1)}, bf16[1536,576]{0,1:T(8,128)(2,1)}, u32[]{:S(2)}) copy-start(bf16[1536,576]{0,1:T(8,128)(2,1)} %param.18) | copy-start | bytes 5308420
  51.8 10.8 %collective-permute-start.10 = (bf16[768,256]{1,0:T(8,128)(2,1)S(1)}, bf16[768,256]{1,0:T(8,128)(2,1)S(1)}, u32[]{:S(2)}, u32[]{:S(2)}) collective-permute-start(bf16[768,256]{1,0:T(8,128)(2,1)S(1)} %shard_map.105.own), channel_id=1, source_target_pairs={{0,2},{1,3},{2,0},{3,1},{4,6},{5,7},{6,4},{7,5},{8,10},{9,11},{10,... | collective-permute-start | bytes 1179656 | tf_op jit(solution)/shard_map/ppermute | solution.py:140
  53.4 7.5 %collective-permute-start.13 = (bf16[2,128,384]{2,1,0:T(8,128)(2,1)S(1)}, bf16[2,128,384]{2,1,0:T(8,128)(2,1)S(1)}, u32[]{:S(2)}, u32[]{:S(2)}) collective-permute-start(bf16[2,128,384]{2,1,0:T(8,128)(2,1)S(1)} %collective-permute-done.12.even), channel_id=1, source_target_pairs={{0,16},{16,0},{1,17},{17,1},{2,18},{18,2},{3,19},{19,3},{4,20},{20... | collective-permute-start | bytes 589832 | tf_op jit(solution)/shard_map/ppermute | solution.py:140
  54.9 7.7 %collective-permute-start.15 = (bf16[2,256,384]{2,1,0:T(8,128)(2,1)S(1)}, bf16[2,256,384]{2,1,0:T(8,128)(2,1)S(1)}, u32[]{:S(2)}, u32[]{:S(2)}) collective-permute-start(bf16[2,256,384]{2,1,0:T(8,128)(2,1)S(1)} %get-tuple-element.66), channel_id=1, source_target_pairs={{0,9},{1,0},{2,7},{3,14},{4,13},{5,4},{6,11},{7,2},{8,1},{9,8},{10... | collective-permute-start | bytes 1179656 | tf_op jit(solution)/shard_map/ppermute | solution.py:517
  55.7 6.9 %collective-permute-start.11 = (bf16[768,256]{1,0:T(8,128)(2,1)S(1)}, bf16[768,256]{1,0:T(8,128)(2,1)S(1)}, u32[]{:S(2)}, u32[]{:S(2)}) collective-permute-start(bf16[768,256]{1,0:T(8,128)(2,1)S(1)} %shard_map.105.own), channel_id=1, source_target_pairs={{0,1},{1,0},{2,3},{3,2},{4,5},{5,4},{6,7},{7,6},{8,9},{9,8},{10,11... | collective-permute-start | bytes 1179656 | tf_op jit(solution)/shard_map/ppermute | solution.py:140
  62.6 1.7 %collective-permute-start.14 = (bf16[768,256]{1,0:T(8,128)(2,1)S(1)}, bf16[768,256]{1,0:T(8,128)(2,1)S(1)}, u32[]{:S(2)}, u32[]{:S(2)}) collective-permute-start(bf16[768,256]{1,0:T(8,128)(2,1)S(1)} %collective-permute-done.10.far), channel_id=1, source_target_pairs={{0,1},{1,0},{2,3},{3,2},{4,5},{5,4},{6,7},{7,6},{8,9},{9,8},{10,11... | collective-permute-start | bytes 1179656 | tf_op jit(solution)/shard_map/ppermute | solution.py:140
  65.3 11.3 %collective-permute-start.16 = (bf16[192,384]{1,0:T(8,128)(2,1)S(1)}, bf16[192,384]{1,0:T(8,128)(2,1)S(1)}, u32[]{:S(2)}, u32[]{:S(2)}) collective-permute-start(bf16[192,384]{1,0:T(8,128)(2,1)S(1)} %get-tuple-element.68), channel_id=1, source_target_pairs={{0,9},{1,8},{2,11},{3,10},{4,13},{5,12},{6,15},{7,14},{8,1},{9,0},... | collective-permute-start | bytes 442376 | tf_op jit(solution)/shard_map/ppermute | solution.py:541
  68.1 10.2 %collective-permute-start.17 = (bf16[192,384]{1,0:T(8,128)(2,1)S(1)}, bf16[192,384]{1,0:T(8,128)(2,1)S(1)}, u32[]{:S(2)}, u32[]{:S(2)}) collective-permute-start(bf16[192,384]{1,0:T(8,128)(2,1)S(1)} %get-tuple-element.69), channel_id=1, source_target_pairs={{0,14},{1,15},{2,13},{3,12},{4,11},{5,10},{6,8},{7,9},{8,6},{9,7},... | collective-permute-start | bytes 442376 | tf_op jit(solution)/shard_map/ppermute | solution.py:541
  70.5 12.4 %collective-permute-start.18 = (bf16[192,384]{1,0:T(8,128)(2,1)S(1)}, bf16[192,384]{1,0:T(8,128)(2,1)S(1)}, u32[]{:S(2)}, u32[]{:S(2)}) collective-permute-start(bf16[192,384]{1,0:T(8,128)(2,1)S(1)} %get-tuple-element.70), channel_id=1, source_target_pairs={{0,7},{1,6},{2,4},{3,5},{4,2},{5,3},{6,1},{7,0},{8,15},{9,14},{10,... | collective-permute-start | bytes 442376 | tf_op jit(solution)/shard_map/ppermute | solution.py:541
  83.0 5.9 %collective-permute-start.19 = (bf16[192,384]{1,0:T(8,128)(2,1)S(1)}, bf16[192,384]{1,0:T(8,128)(2,1)S(1)}, u32[]{:S(2)}, u32[]{:S(2)}) collective-permute-start(bf16[192,384]{1,0:T(8,128)(2,1)S(1)} %shard_map.107.own), channel_id=1, source_target_pairs={{0,2},{1,3},{2,0},{3,1},{4,6},{5,7},{6,4},{7,5},{8,10},{9,11},{10,... | collective-permute-start | bytes 442376 | tf_op jit(solution)/shard_map/ppermute | solution.py:140
  83.4 5.5 %collective-permute-start.20 = (bf16[192,384]{1,0:T(8,128)(2,1)S(1)}, bf16[192,384]{1,0:T(8,128)(2,1)S(1)}, u32[]{:S(2)}, u32[]{:S(2)}) collective-permute-start(bf16[192,384]{1,0:T(8,128)(2,1)S(1)} %shard_map.107.own), channel_id=1, source_target_pairs={{0,1},{1,0},{2,3},{3,2},{4,5},{5,4},{6,7},{7,6},{8,9},{9,8},{10,11... | collective-permute-start | bytes 442376 | tf_op jit(solution)/shard_map/ppermute | solution.py:140
  88.9 1.4 %collective-permute-start.21 = (bf16[192,384]{1,0:T(8,128)(2,1)S(1)}, bf16[192,384]{1,0:T(8,128)(2,1)S(1)}, u32[]{:S(2)}, u32[]{:S(2)}) collective-permute-start(bf16[192,384]{1,0:T(8,128)(2,1)S(1)} %collective-permute-done.19.far), channel_id=1, source_target_pairs={{0,1},{1,0},{2,3},{3,2},{4,5},{5,4},{6,7},{7,6},{8,9},{9,8},{10,11... | collective-permute-start | bytes 442376 | tf_op jit(solution)/shard_map/ppermute | solution.py:140
  91.5 10.8 %collective-permute-start.22 = (bf16[64,768]{1,0:T(8,128)(2,1)S(1)}, bf16[64,768]{1,0:T(8,128)(2,1)S(1)}, u32[]{:S(2)}, u32[]{:S(2)}) collective-permute-start(bf16[64,768]{1,0:T(8,128)(2,1)S(1)} %get-tuple-element.71), channel_id=1, source_target_pairs={{0,8},{4,12},{8,0},{12,4},{1,9},{5,13},{9,1},{13,5},{2,10},{6,14},... | collective-permute-start | bytes 294920 | tf_op jit(solution)/shard_map/ppermute | solution.py:140
  93.7 8.6 %collective-permute-start.23 = (bf16[64,768]{1,0:T(8,128)(2,1)S(1)}, bf16[64,768]{1,0:T(8,128)(2,1)S(1)}, u32[]{:S(2)}, u32[]{:S(2)}) collective-permute-start(bf16[64,768]{1,0:T(8,128)(2,1)S(1)} %get-tuple-element.72), channel_id=1, source_target_pairs={{0,12},{4,8},{8,4},{12,0},{1,13},{5,9},{9,5},{13,1},{2,14},{6,10},... | collective-permute-start | bytes 294920 | tf_op jit(solution)/shard_map/ppermute | solution.py:140
  96.4 6.8 %collective-permute-start.24 = (bf16[64,768]{1,0:T(8,128)(2,1)S(1)}, bf16[64,768]{1,0:T(8,128)(2,1)S(1)}, u32[]{:S(2)}, u32[]{:S(2)}) collective-permute-start(bf16[64,768]{1,0:T(8,128)(2,1)S(1)} %get-tuple-element.73), channel_id=1, source_target_pairs={{0,4},{4,0},{8,12},{12,8},{1,5},{5,1},{9,13},{13,9},{2,6},{6,2},{1... | collective-permute-start | bytes 294920 | tf_op jit(solution)/shard_map/ppermute | solution.py:140

commit v11 on v10

--- a/solution.py
+++ b/solution.py
@@ -11,7 +11,7 @@
 HEAD_WIDTH = 64
 DILATION_STEP = 8
 ENCODER_SLOTS = 256
-ORDER = (2, 3, 1, 0)
+ORDER = (2, 1, 3, 0)
 
 
 epsilon = 1e-05
@@ -540,7 +540,7 @@
                 perm.append((s * mp_size + m, owner * mp_size + holder[(s + holder[m] - owner) % count]))
         return lax.ppermute(part, ("seq", "mp"), perm)
 
-    arrived = [to_owner(sums[d], d) for d in (2, 3, 1)]
+    arrived = [to_owner(sums[d], d) for d in (2, 1, 3)]
     embedded_cols = call(
         sum_body, [((tile_rows, features), bf16)], (sums[0], *arrived)
     )[0]

time: 106 us -> 104 us (0.981)
  waiting for transfers between devices: 60.9 us -> 57.5 us
  starting transfers between devices: 28.9 us -> 30.9 us
    ppermute x20, starting transfers between devices: 22.1 us -> 24.1 us  [swap(): return lax.ppermute(array, axis, [(i, i ^ distance) for i in range(size)])]
    ppermute x3, waiting for transfers between devices: 12.2 us -> 10.4 us  [to_owner(): return lax.ppermute(part, ('seq', 'mp'), perm)]
    ppermute x20, waiting for transfers between devices: 48.7 us -> 47.1 us  [swap(): return lax.ppermute(array, axis, [(i, i ^ distance) for i in range(size)])]
  transfers between devices with their start and end apart: 25 -> 25, of which waited for: 14 -> 15; matrix products, arithmetic and copies ran while one was open for 0% -> 0% of each run, Pallas kernels for 6% -> 6%
where the time goes in v11:
time: 104 us
  waiting for transfers between devices  57.5 us (55%)
  starting transfers between devices  30.9 us (30%)
  Pallas kernels  13.6 us (13%)
  local copies, waits for them, and re-layouts  1.12 us (1%)
    ppermute x20, waiting for transfers between devices, swap(): return lax.ppermute(array, axis, [(i, i ^ distance) for i in range(size)])  47.1 us
    ppermute x20, starting transfers between devices, swap(): return lax.ppermute(array, axis, [(i, i ^ distance) for i in range(size)])  24.1 us
    pallas_call x10, Pallas kernels, call(): pl.pallas_call(body, out_shape=[jax.ShapeDtypeStruct(shape, kind) for sha...  13.6 us
    ppermute x3, waiting for transfers between devices, to_owner(): return lax.ppermute(part, ('seq', 'mp'), perm)  10.4 us
    ppermute x3, starting transfers between devices, to_owner(): return lax.ppermute(part, ('seq', 'mp'), perm)  5.39 us
  transfers between devices with their start and end apart: 25, of which 15 were waited for; matrix products, arithmetic and copies ran while one was open for 0% of the time, Pallas kernels for 6%

profile of v11, /device:TPU:0, one launch (start us, length us, event | category | flops | bytes accessed | tf_op | source)
XLA Modules:
  0.0 104.0 jit_solution(14891012514299824056)
XLA Ops:
  0.0 3.0 %shard_map.100 = (bf16[192,1408]{1,0:T(8,128)(2,1)}, bf16[192,896]{1,0:T(8,128)(2,1)}, bf16[192,384]{1,0:T(8,128)(2,1)}) custom-call(bf16[192,1536]{1,0:T(8,128)(2,1)} %tiles.3, bf16[384,1024]{1,0:T(8,128)(2,1)} %w_gate.3, bf16[384,1024]{1,0:T(8,128)(2,1)} %w_up.3, f32[1536]{0:T(1024)} %gain.3), custom_call_target="tpu_custom_call" | custom-call | tf_op jit(solution)/shard_map/pallas_call | solution.py:152
  3.0 0.0 copy-start.5
  3.1 0.0 copy-start.6
  3.1 3.1 %collective-permute-start.2 = (bf16[192,1408]{1,0:T(8,128)(2,1)}, bf16[192,1408]{1,0:T(8,128)(2,1)S(1)}, u32[]{:S(2)}, u32[]{:S(2)}) collective-permute-start(bf16[192,1408]{1,0:T(8,128)(2,1)} %get-tuple-element.42), channel_id=1, source_target_pairs={{0,4},{4,0},{8,12},{12,8},{1,5},{5,1},{9,13},{13,9},{2,6},{6,2},{1... | collective-permute-start | bytes 1622024 | tf_op jit(solution)/shard_map/ppermute | solution.py:140
  6.2 2.6 %collective-permute-start = (bf16[192,896]{1,0:T(8,128)(2,1)}, bf16[192,896]{1,0:T(8,128)(2,1)S(1)}, u32[]{:S(2)}, u32[]{:S(2)}) collective-permute-start(bf16[192,896]{1,0:T(8,128)(2,1)} %get-tuple-element.40), channel_id=1, source_target_pairs={{0,8},{4,12},{8,0},{12,4},{1,9},{5,13},{9,1},{13,5},{2,10},{6,14},... | collective-permute-start | bytes 1032200 | tf_op jit(solution)/shard_map/ppermute | solution.py:140
  8.7 3.4 %shard_map.101 = (bf16[192,512]{1,0:T(8,128)(2,1)}, bf16[384,512]{1,0:T(8,128)(2,1)}, bf16[384,384]{1,0:T(8,128)(2,1)}, bf16[384,384]{1,0:T(8,128)(2,1)}, bf16[1...) custom-call(bf16[192,1536]{1,0:T(8,128)(2,1)} %tiles.3, bf16[384,1024]{1,0:T(8,128)(2,1)} %w_gate.3, ...), custom_call_target="tpu_custom_call" | custom-call | tf_op jit(solution)/shard_map/pallas_call | solution.py:152
  12.2 1.6 %collective-permute-start.3 = (bf16[384,384]{1,0:T(8,128)(2,1)}, bf16[384,384]{1,0:T(8,128)(2,1)S(1)}, u32[]{:S(2)}, u32[]{:S(2)}) collective-permute-start(bf16[384,384]{1,0:T(8,128)(2,1)} %get-tuple-element.43), channel_id=1, source_target_pairs={{0,2},{1,3},{2,0},{3,1},{4,6},{5,7},{6,4},{7,5},{8,10},{9,11},{10,... | collective-permute-start | bytes 884744 | tf_op jit(solution)/shard_map/ppermute | solution.py:140
  13.7 0.2 collective-permute-start.1
  14.0 0.1 copy.11.dest
  14.8 0.7 shard_map.102.routes
  15.4 15.9 %collective-permute-done.1.third = bf16[192,384]{1,0:T(8,128)(2,1)S(1)} collective-permute-done((bf16[192,384]{1,0:T(8,128)(2,1)S(1)}, bf16[192,384]{1,0:T(8,128)(2,1)S(1)}, u32[]{:S(2)}, u32[]{:S(2)}) %collective-permute-start.1) | collective-permute-done | bytes 147488 | tf_op jit(solution)/shard_map/ppermute | solution.py:140
  31.4 0.1 shard_map.103
  31.4 1.6 %collective-permute-start.6 = (bf16[3,192,384]{2,1,0:T(8,128)(2,1)S(1)}, bf16[3,192,384]{2,1,0:T(8,128)(2,1)S(1)}, u32[]{:S(2)}, u32[]{:S(2)}) collective-permute-start(bf16[3,192,384]{2,1,0:T(8,128)(2,1)S(1)} %get-tuple-element.50.own), channel_id=1, source_target_pairs={{0,2},{1,3},{2,0},{3,1},{4,6},{5,7},{6,4},{7,5},{8,10},{9,11},{10,... | collective-permute-start | bytes 1327112 | tf_op jit(solution)/shard_map/ppermute | solution.py:140
  33.0 1.6 %collective-permute-start.4 = (bf16[192,512]{1,0:T(8,128)(2,1)}, bf16[192,512]{1,0:T(8,128)(2,1)S(1)}, u32[]{:S(2)}, u32[]{:S(2)}) collective-permute-start(bf16[192,512]{1,0:T(8,128)(2,1)} %get-tuple-element.53), channel_id=1, source_target_pairs={{0,12},{4,8},{8,4},{12,0},{1,13},{5,9},{9,5},{13,1},{2,14},{6,10},... | collective-permute-start | bytes 589832 | tf_op jit(solution)/shard_map/ppermute | solution.py:140
  34.6 1.5 %collective-permute-start.5 = (bf16[192,512]{1,0:T(8,128)(2,1)S(1)}, bf16[192,512]{1,0:T(8,128)(2,1)S(1)}, u32[]{:S(2)}, u32[]{:S(2)}) collective-permute-start(bf16[192,512]{1,0:T(8,128)(2,1)S(1)} %get-tuple-element.54.refs_0_), channel_id=1, source_target_pairs={{0,16},{16,0},{1,17},{17,1},{2,18},{18,2},{3,19},{19,3},{4,20},{20... | collective-permute-start | bytes 589832 | tf_op jit(solution)/shard_map/ppermute | solution.py:140
  36.1 1.0 copy-done.3
  37.0 0.1 shard_map.104
  37.1 5.3 %collective-permute-done.4.refs_2_ = bf16[192,512]{1,0:T(8,128)(2,1)S(1)} collective-permute-done((bf16[192,512]{1,0:T(8,128)(2,1)}, bf16[192,512]{1,0:T(8,128)(2,1)S(1)}, u32[]{:S(2)}, u32[]{:S(2)}) %collective-permute-start.4) | collective-permute-done | bytes 196640 | tf_op jit(solution)/shard_map/ppermute | solution.py:140
  42.4 0.1 collective-permute-done.6.far
  42.5 1.6 %collective-permute-start.9 = (bf16[192,512]{1,0:T(8,128)(2,1)S(1)}, bf16[192,512]{1,0:T(8,128)(2,1)S(1)}, u32[]{:S(2)}, u32[]{:S(2)}) collective-permute-start(bf16[192,512]{1,0:T(8,128)(2,1)S(1)} %collective-permute-done.4.refs_2_), channel_id=1, source_target_pairs={{0,16},{16,0},{1,17},{17,1},{2,18},{18,2},{3,19},{19,3},{4,20},{20... | collective-permute-start | bytes 589832 | tf_op jit(solution)/shard_map/ppermute | solution.py:140
  44.1 0.7 collective-permute-start.12
  44.8 5.1 %collective-permute-done.9.refs_3_ = bf16[192,512]{1,0:T(8,128)(2,1)S(1)} collective-permute-done((bf16[192,512]{1,0:T(8,128)(2,1)S(1)}, bf16[192,512]{1,0:T(8,128)(2,1)S(1)}, u32[]{:S(2)}, u32[]{:S(2)}) %collective-permute-start.9) | collective-permute-done | bytes 196640 | tf_op jit(solution)/shard_map/ppermute | solution.py:140
  49.9 1.9 %shard_map.105.own = bf16[768,256]{1,0:T(8,128)(2,1)S(1)} custom-call(bf16[192,1536]{1,0:T(8,128)(2,1)S(1)} %copy-done.1, bf16[3,192,384]{2,1,0:T(8,128)(2,1)S(1)} %get-tuple-element.50.own, bf16[3,192,384]{2,1,0:T(8,128)(2,1)S(1)} %collective-permute-done.6.far, bf16[3,192,384]{2,1,0:T(8,128)(2,1)S(1)} %collective-permute-done.7.near, ...), custom_call_target="tpu_custom_call" | custom-call | tf_op jit(solution)/shard_map/pallas_call | solution.py:152
  51.8 0.0 copy-start
  51.8 1.6 %collective-permute-start.10 = (bf16[768,256]{1,0:T(8,128)(2,1)S(1)}, bf16[768,256]{1,0:T(8,128)(2,1)S(1)}, u32[]{:S(2)}, u32[]{:S(2)}) collective-permute-start(bf16[768,256]{1,0:T(8,128)(2,1)S(1)} %shard_map.105.own), channel_id=1, source_target_pairs={{0,2},{1,3},{2,0},{3,1},{4,6},{5,7},{6,4},{7,5},{8,10},{9,11},{10,... | collective-permute-start | bytes 1179656 | tf_op jit(solution)/shard_map/ppermute | solution.py:140
  53.4 1.5 %collective-permute-start.13 = (bf16[2,128,384]{2,1,0:T(8,128)(2,1)S(1)}, bf16[2,128,384]{2,1,0:T(8,128)(2,1)S(1)}, u32[]{:S(2)}, u32[]{:S(2)}) collective-permute-start(bf16[2,128,384]{2,1,0:T(8,128)(2,1)S(1)} %collective-permute-done.12.even), channel_id=1, source_target_pairs={{0,16},{16,0},{1,17},{17,1},{2,18},{18,2},{3,19},{19,3},{4,20},{20... | collective-permute-start | bytes 589832 | tf_op jit(solution)/shard_map/ppermute | solution.py:140
  54.9 0.8 collective-permute-start.15
  55.7 5.2 %collective-permute-done.13.even_other = bf16[2,128,384]{2,1,0:T(8,128)(2,1)S(1)} collective-permute-done((bf16[2,128,384]{2,1,0:T(8,128)(2,1)S(1)}, bf16[2,128,384]{2,1,0:T(8,128)(2,1)S(1)}, u32[]{:S(2)}, u32[]{:S(2)}) %collective-permute-start.13) | collective-permute-done | bytes 196640 | tf_op jit(solution)/shard_map/ppermute | solution.py:140
  60.9 1.7 %collective-permute-done.10.far = bf16[768,256]{1,0:T(8,128)(2,1)S(1)} collective-permute-done((bf16[768,256]{1,0:T(8,128)(2,1)S(1)}, bf16[768,256]{1,0:T(8,128)(2,1)S(1)}, u32[]{:S(2)}, u32[]{:S(2)}) %collective-permute-start.10) | collective-permute-done | bytes 393248 | tf_op jit(solution)/shard_map/ppermute | solution.py:140
  62.6 1.7 %collective-permute-done.14.near_far = bf16[768,256]{1,0:T(8,128)(2,1)S(1)} collective-permute-done((bf16[768,256]{1,0:T(8,128)(2,1)S(1)}, bf16[768,256]{1,0:T(8,128)(2,1)S(1)}, u32[]{:S(2)}, u32[]{:S(2)}) %collective-permute-start.14) | collective-permute-done | bytes 393248 | tf_op jit(solution)/shard_map/ppermute | solution.py:140
  64.3 1.0 shard_map.106
  65.3 2.8 %collective-permute-start.16 = (bf16[192,384]{1,0:T(8,128)(2,1)S(1)}, bf16[192,384]{1,0:T(8,128)(2,1)S(1)}, u32[]{:S(2)}, u32[]{:S(2)}) collective-permute-start(bf16[192,384]{1,0:T(8,128)(2,1)S(1)} %get-tuple-element.68), channel_id=1, source_target_pairs={{0,9},{1,8},{2,11},{3,10},{4,13},{5,12},{6,15},{7,14},{8,1},{9,0},... | collective-permute-start | bytes 442376 | tf_op jit(solution)/shard_map/ppermute | solution.py:541
  68.1 2.6 %collective-permute-start.17 = (bf16[192,384]{1,0:T(8,128)(2,1)S(1)}, bf16[192,384]{1,0:T(8,128)(2,1)S(1)}, u32[]{:S(2)}, u32[]{:S(2)}) collective-permute-start(bf16[192,384]{1,0:T(8,128)(2,1)S(1)} %get-tuple-element.69), channel_id=1, source_target_pairs={{0,7},{1,6},{2,4},{3,5},{4,2},{5,3},{6,1},{7,0},{8,15},{9,14},{10,... | collective-permute-start | bytes 442376 | tf_op jit(solution)/shard_map/ppermute | solution.py:541
  70.7 3.8 %collective-permute-done.16.refs_0_ = bf16[192,384]{1,0:T(8,128)(2,1)S(1)} collective-permute-done((bf16[192,384]{1,0:T(8,128)(2,1)S(1)}, bf16[192,384]{1,0:T(8,128)(2,1)S(1)}, u32[]{:S(2)}, u32[]{:S(2)}) %collective-permute-start.16) | collective-permute-done | bytes 147488 | tf_op jit(solution)/shard_map/ppermute | solution.py:541
  74.5 1.8 %collective-permute-done.17.refs_1_ = bf16[192,384]{1,0:T(8,128)(2,1)S(1)} collective-permute-done((bf16[192,384]{1,0:T(8,128)(2,1)S(1)}, bf16[192,384]{1,0:T(8,128)(2,1)S(1)}, u32[]{:S(2)}, u32[]{:S(2)}) %collective-permute-start.17) | collective-permute-done | bytes 147488 | tf_op jit(solution)/shard_map/ppermute | solution.py:541
  76.2 4.8 %collective-permute-done.18.refs_2_ = bf16[192,384]{1,0:T(8,128)(2,1)S(1)} collective-permute-done((bf16[192,384]{1,0:T(8,128)(2,1)S(1)}, bf16[192,384]{1,0:T(8,128)(2,1)S(1)}, u32[]{:S(2)}, u32[]{:S(2)}) %collective-permute-start.18) | collective-permute-done | bytes 147488 | tf_op jit(solution)/shard_map/ppermute | solution.py:541
  81.0 0.1 shard_map.107.own
  81.1 1.5 %collective-permute-start.19 = (bf16[192,384]{1,0:T(8,128)(2,1)S(1)}, bf16[192,384]{1,0:T(8,128)(2,1)S(1)}, u32[]{:S(2)}, u32[]{:S(2)}) collective-permute-start(bf16[192,384]{1,0:T(8,128)(2,1)S(1)} %shard_map.107.own), channel_id=1, source_target_pairs={{0,2},{1,3},{2,0},{3,1},{4,6},{5,7},{6,4},{7,5},{8,10},{9,11},{10,... | collective-permute-start | bytes 442376 | tf_op jit(solution)/shard_map/ppermute | solution.py:140
  82.7 4.1 %collective-permute-done.19.far = bf16[192,384]{1,0:T(8,128)(2,1)S(1)} collective-permute-done((bf16[192,384]{1,0:T(8,128)(2,1)S(1)}, bf16[192,384]{1,0:T(8,128)(2,1)S(1)}, u32[]{:S(2)}, u32[]{:S(2)}) %collective-permute-start.19) | collective-permute-done | bytes 147488 | tf_op jit(solution)/shard_map/ppermute | solution.py:140
  86.8 1.3 %collective-permute-done.21.near_far = bf16[192,384]{1,0:T(8,128)(2,1)S(1)} collective-permute-done((bf16[192,384]{1,0:T(8,128)(2,1)S(1)}, bf16[192,384]{1,0:T(8,128)(2,1)S(1)}, u32[]{:S(2)}, u32[]{:S(2)}) %collective-permute-start.21) | collective-permute-done | bytes 147488 | tf_op jit(solution)/shard_map/ppermute | solution.py:140
  88.2 1.2 %shard_map.108 = (bf16[64,768]{1,0:T(8,128)(2,1)S(1)}, bf16[64,768]{1,0:T(8,128)(2,1)S(1)}, bf16[64,768]{1,0:T(8,128)(2,1)S(1)}, bf16[64,768]{1,0:T(8,128)(2,1)S(1)}) custom-call(f32[1,1536]{1,0:T(1,128)S(1)} %broadcast_in_dim.3.gain, bf16[352,192]{1,0:T(8,128)(2,1)S(1)} %shard_map.102.routes, bf16[576,1536]{1,0:T(8,128)(2,1)S(1)} %bitcast.3, ...), custom_call_target="tpu_custom_call" | custom-call | tf_op jit(solution)/shard_map/pallas_call | solution.py:152
  89.4 4.3 %collective-permute-start.22 = (bf16[64,768]{1,0:T(8,128)(2,1)S(1)}, bf16[64,768]{1,0:T(8,128)(2,1)S(1)}, u32[]{:S(2)}, u32[]{:S(2)}) collective-permute-start(bf16[64,768]{1,0:T(8,128)(2,1)S(1)} %get-tuple-element.71), channel_id=1, source_target_pairs={{0,8},{4,12},{8,0},{12,4},{1,9},{5,13},{9,1},{13,5},{2,10},{6,14},... | collective-permute-start | bytes 294920 | tf_op jit(solution)/shard_map/ppermute | solution.py:140
  93.7 0.3 collective-permute-start.23
  93.9 1.3 %collective-permute-start.24 = (bf16[64,768]{1,0:T(8,128)(2,1)S(1)}, bf16[64,768]{1,0:T(8,128)(2,1)S(1)}, u32[]{:S(2)}, u32[]{:S(2)}) collective-permute-start(bf16[64,768]{1,0:T(8,128)(2,1)S(1)} %get-tuple-element.73), channel_id=1, source_target_pairs={{0,12},{4,8},{8,4},{12,0},{1,13},{5,9},{9,5},{13,1},{2,14},{6,10},... | collective-permute-start | bytes 294920 | tf_op jit(solution)/shard_map/ppermute | solution.py:140
  95.2 4.8 %collective-permute-done.22.refs_0_ = bf16[64,768]{1,0:T(8,128)(2,1)S(1)} collective-permute-done((bf16[64,768]{1,0:T(8,128)(2,1)S(1)}, bf16[64,768]{1,0:T(8,128)(2,1)S(1)}, u32[]{:S(2)}, u32[]{:S(2)}) %collective-permute-start.22) | collective-permute-done | bytes 98336 | tf_op jit(solution)/shard_map/ppermute | solution.py:140
  100.0 0.9 collective-permute-done.23.refs_1_
  100.9 0.9 collective-permute-done.24.refs_2_
  101.8 2.2 %shard_map.109 = bf16[192,256]{1,0:T(8,128)(2,1)} custom-call(s32[3]{0:T(128)S(1)} %copy-done.6, bf16[64,768]{1,0:T(8,128)(2,1)S(1)} %collective-permute-done.22.refs_0_, bf16[64,768]{1,0:T(8,128)(2,1)S(1)} %collective-permute-done.23.refs_1_, bf16[64,768]{1,0:T(8,128)(2,1)S(1)} %collective-permute-done.24.refs_2_, bf16[64,768]{1,0:T(8,128)(2,1)S(1)} %get-tuple-element.74.refs_3_), custom_call_target="tpu_custom_call" | custom-call | tf_op jit(solution)/shard_map/pallas_call | solution.py:152
  (32 shorter events, 0.1 us)
Async XLA Ops:
  3.0 10.7 %copy-start.8 = (bf16[192,384]{1,0:T(8,128)(2,1)S(1)}, bf16[192,384]{1,0:T(8,128)(2,1)}, u32[]{:S(2)}) copy-start(bf16[192,384]{1,0:T(8,128)(2,1)} %get-tuple-element.41) | copy-start | bytes 442372
  3.0 10.9 %copy-start.5 = (s32[192,1]{0,1:T(1,128)S(1)}, s32[192,1]{0,1:T(1,128)}, u32[]{:S(2)}) copy-start(s32[192,1]{0,1:T(1,128)} %param.12) | copy-start | bytes 2308
  3.1 11.7 %copy-start.6 = (s32[3]{0:T(128)S(1)}, s32[3]{0:T(128)}, u32[]{:S(2)}) copy-start(s32[3]{0:T(128)} %offsets.3) | copy-start | bytes 40
  3.1 28.3 %collective-permute-start.2 = (bf16[192,1408]{1,0:T(8,128)(2,1)}, bf16[192,1408]{1,0:T(8,128)(2,1)S(1)}, u32[]{:S(2)}, u32[]{:S(2)}) collective-permute-start(bf16[192,1408]{1,0:T(8,128)(2,1)} %get-tuple-element.42), channel_id=1, source_target_pairs={{0,4},{4,0},{8,12},{12,8},{1,5},{5,1},{9,13},{13,9},{2,6},{6,2},{1... | collective-permute-start | bytes 1622024 | tf_op jit(solution)/shard_map/ppermute | solution.py:140
  6.2 25.2 %collective-permute-start = (bf16[192,896]{1,0:T(8,128)(2,1)}, bf16[192,896]{1,0:T(8,128)(2,1)S(1)}, u32[]{:S(2)}, u32[]{:S(2)}) collective-permute-start(bf16[192,896]{1,0:T(8,128)(2,1)} %get-tuple-element.40), channel_id=1, source_target_pairs={{0,8},{4,12},{8,0},{12,4},{1,9},{5,13},{9,1},{13,5},{2,10},{6,14},... | collective-permute-start | bytes 1032200 | tf_op jit(solution)/shard_map/ppermute | solution.py:140
  12.2 37.7 %copy-start.1 = (bf16[192,1536]{1,0:T(8,128)(2,1)S(1)}, bf16[192,1536]{1,0:T(8,128)(2,1)}, u32[]{:S(2)}) copy-start(bf16[192,1536]{1,0:T(8,128)(2,1)} %get-tuple-element.46.normed) | copy-start | bytes 1769476
  12.2 37.7 %copy-start.2 = (bf16[384,512]{1,0:T(8,128)(2,1)S(1)}, bf16[384,512]{1,0:T(8,128)(2,1)}, u32[]{:S(2)}) copy-start(bf16[384,512]{1,0:T(8,128)(2,1)} %get-tuple-element.61.kept) | copy-start | bytes 1179652
  12.2 19.2 %collective-permute-start.3 = (bf16[384,384]{1,0:T(8,128)(2,1)}, bf16[384,384]{1,0:T(8,128)(2,1)S(1)}, u32[]{:S(2)}, u32[]{:S(2)}) collective-permute-start(bf16[384,384]{1,0:T(8,128)(2,1)} %get-tuple-element.43), channel_id=1, source_target_pairs={{0,2},{1,3},{2,0},{3,1},{4,6},{5,7},{6,4},{7,5},{8,10},{9,11},{10,... | collective-permute-start | bytes 884744 | tf_op jit(solution)/shard_map/ppermute | solution.py:140
  13.7 17.6 %collective-permute-start.1 = (bf16[192,384]{1,0:T(8,128)(2,1)S(1)}, bf16[192,384]{1,0:T(8,128)(2,1)S(1)}, u32[]{:S(2)}, u32[]{:S(2)}) collective-permute-start(bf16[192,384]{1,0:T(8,128)(2,1)S(1)} %copy-done.8), channel_id=1, source_target_pairs={{0,12},{4,8},{8,4},{12,0},{1,13},{5,9},{9,5},{13,1},{2,14},{6,10},... | collective-permute-start | bytes 442376 | tf_op jit(solution)/shard_map/ppermute | solution.py:140
  31.4 11.1 %collective-permute-start.6 = (bf16[3,192,384]{2,1,0:T(8,128)(2,1)S(1)}, bf16[3,192,384]{2,1,0:T(8,128)(2,1)S(1)}, u32[]{:S(2)}, u32[]{:S(2)}) collective-permute-start(bf16[3,192,384]{2,1,0:T(8,128)(2,1)S(1)} %get-tuple-element.50.own), channel_id=1, source_target_pairs={{0,2},{1,3},{2,0},{3,1},{4,6},{5,7},{6,4},{7,5},{8,10},{9,11},{10,... | collective-permute-start | bytes 1327112 | tf_op jit(solution)/shard_map/ppermute | solution.py:140
  33.0 9.5 %collective-permute-start.7 = (bf16[3,192,384]{2,1,0:T(8,128)(2,1)S(1)}, bf16[3,192,384]{2,1,0:T(8,128)(2,1)S(1)}, u32[]{:S(2)}, u32[]{:S(2)}) collective-permute-start(bf16[3,192,384]{2,1,0:T(8,128)(2,1)S(1)} %get-tuple-element.50.own), channel_id=1, source_target_pairs={{0,1},{1,0},{2,3},{3,2},{4,5},{5,4},{6,7},{7,6},{8,9},{9,8},{10,11... | collective-permute-start | bytes 1327112 | tf_op jit(solution)/shard_map/ppermute | solution.py:140
  33.0 9.4 %collective-permute-start.4 = (bf16[192,512]{1,0:T(8,128)(2,1)}, bf16[192,512]{1,0:T(8,128)(2,1)S(1)}, u32[]{:S(2)}, u32[]{:S(2)}) collective-permute-start(bf16[192,512]{1,0:T(8,128)(2,1)} %get-tuple-element.53), channel_id=1, source_target_pairs={{0,12},{4,8},{8,4},{12,0},{1,13},{5,9},{9,5},{13,1},{2,14},{6,10},... | collective-permute-start | bytes 589832 | tf_op jit(solution)/shard_map/ppermute | solution.py:140
  34.6 7.9 %collective-permute-start.5 = (bf16[192,512]{1,0:T(8,128)(2,1)S(1)}, bf16[192,512]{1,0:T(8,128)(2,1)S(1)}, u32[]{:S(2)}, u32[]{:S(2)}) collective-permute-start(bf16[192,512]{1,0:T(8,128)(2,1)S(1)} %get-tuple-element.54.refs_0_), channel_id=1, source_target_pairs={{0,16},{16,0},{1,17},{17,1},{2,18},{18,2},{3,19},{19,3},{4,20},{20... | collective-permute-start | bytes 589832 | tf_op jit(solution)/shard_map/ppermute | solution.py:140
  36.1 1.0 copy-start.3
  42.5 7.3 %collective-permute-start.8 = (bf16[3,192,384]{2,1,0:T(8,128)(2,1)S(1)}, bf16[3,192,384]{2,1,0:T(8,128)(2,1)S(1)}, u32[]{:S(2)}, u32[]{:S(2)}) collective-permute-start(bf16[3,192,384]{2,1,0:T(8,128)(2,1)S(1)} %collective-permute-done.6.far), channel_id=1, source_target_pairs={{0,1},{1,0},{2,3},{3,2},{4,5},{5,4},{6,7},{7,6},{8,9},{9,8},{10,11... | collective-permute-start | bytes 1327112 | tf_op jit(solution)/shard_map/ppermute | solution.py:140
  42.5 7.3 %collective-permute-start.9 = (bf16[192,512]{1,0:T(8,128)(2,1)S(1)}, bf16[192,512]{1,0:T(8,128)(2,1)S(1)}, u32[]{:S(2)}, u32[]{:S(2)}) collective-permute-start(bf16[192,512]{1,0:T(8,128)(2,1)S(1)} %collective-permute-done.4.refs_2_), channel_id=1, source_target_pairs={{0,16},{16,0},{1,17},{17,1},{2,18},{18,2},{3,19},{19,3},{4,20},{20... | collective-permute-start | bytes 589832 | tf_op jit(solution)/shard_map/ppermute | solution.py:140
  44.1 9.3 %collective-permute-start.12 = (bf16[2,128,384]{2,1,0:T(8,128)(2,1)S(1)}, bf16[2,128,384]{2,1,0:T(8,128)(2,1)S(1)}, u32[]{:S(2)}, u32[]{:S(2)}) collective-permute-start(bf16[2,128,384]{2,1,0:T(8,128)(2,1)S(1)} %get-tuple-element.64), channel_id=1, source_target_pairs={{0,0},{1,9},{2,14},{3,7},{4,4},{5,13},{6,2},{7,11},{8,8},{9,1},{10... | collective-permute-start | bytes 589832 | tf_op jit(solution)/shard_map/ppermute | solution.py:517
  49.9 14.4 %copy-start.4 = (bf16[192,384]{1,0:T(8,128)(2,1)S(1)}, bf16[192,384]{1,0:T(8,128)(2,1)}, u32[]{:S(2)}) copy-start(bf16[192,384]{1,0:T(8,128)(2,1)} %get-tuple-element.45.residual) | copy-start | bytes 442372
  51.8 35.0 %copy-start.7 = (f32[1536]{0:T(1024)S(1)}, f32[1536]{0:T(1024)}, u32[]{:S(2)}) copy-start(f32[1536]{0:T(1024)} %param.17) | copy-start | bytes 18436
  51.8 36.4 %copy-start = (bf16[1536,576]{0,1:T(8,128)(2,1)S(1)}, bf16[1536,576]{0,1:T(8,128)(2,1)}, u32[]{:S(2)}) copy-start(bf16[1536,576]{0,1:T(8,128)(2,1)} %param.18) | copy-start | bytes 5308420
  51.8 10.8 %collective-permute-start.10 = (bf16[768,256]{1,0:T(8,128)(2,1)S(1)}, bf16[768,256]{1,0:T(8,128)(2,1)S(1)}, u32[]{:S(2)}, u32[]{:S(2)}) collective-permute-start(bf16[768,256]{1,0:T(8,128)(2,1)S(1)} %shard_map.105.own), channel_id=1, source_target_pairs={{0,2},{1,3},{2,0},{3,1},{4,6},{5,7},{6,4},{7,5},{8,10},{9,11},{10,... | collective-permute-start | bytes 1179656 | tf_op jit(solution)/shard_map/ppermute | solution.py:140
  53.4 7.5 %collective-permute-start.13 = (bf16[2,128,384]{2,1,0:T(8,128)(2,1)S(1)}, bf16[2,128,384]{2,1,0:T(8,128)(2,1)S(1)}, u32[]{:S(2)}, u32[]{:S(2)}) collective-permute-start(bf16[2,128,384]{2,1,0:T(8,128)(2,1)S(1)} %collective-permute-done.12.even), channel_id=1, source_target_pairs={{0,16},{16,0},{1,17},{17,1},{2,18},{18,2},{3,19},{19,3},{4,20},{20... | collective-permute-start | bytes 589832 | tf_op jit(solution)/shard_map/ppermute | solution.py:140
  54.9 7.7 %collective-permute-start.15 = (bf16[2,256,384]{2,1,0:T(8,128)(2,1)S(1)}, bf16[2,256,384]{2,1,0:T(8,128)(2,1)S(1)}, u32[]{:S(2)}, u32[]{:S(2)}) collective-permute-start(bf16[2,256,384]{2,1,0:T(8,128)(2,1)S(1)} %get-tuple-element.66), channel_id=1, source_target_pairs={{0,9},{1,0},{2,7},{3,14},{4,13},{5,4},{6,11},{7,2},{8,1},{9,8},{10... | collective-permute-start | bytes 1179656 | tf_op jit(solution)/shard_map/ppermute | solution.py:517
  55.7 6.9 %collective-permute-start.11 = (bf16[768,256]{1,0:T(8,128)(2,1)S(1)}, bf16[768,256]{1,0:T(8,128)(2,1)S(1)}, u32[]{:S(2)}, u32[]{:S(2)}) collective-permute-start(bf16[768,256]{1,0:T(8,128)(2,1)S(1)} %shard_map.105.own), channel_id=1, source_target_pairs={{0,1},{1,0},{2,3},{3,2},{4,5},{5,4},{6,7},{7,6},{8,9},{9,8},{10,11... | collective-permute-start | bytes 1179656 | tf_op jit(solution)/shard_map/ppermute | solution.py:140
  62.6 1.7 %collective-permute-start.14 = (bf16[768,256]{1,0:T(8,128)(2,1)S(1)}, bf16[768,256]{1,0:T(8,128)(2,1)S(1)}, u32[]{:S(2)}, u32[]{:S(2)}) collective-permute-start(bf16[768,256]{1,0:T(8,128)(2,1)S(1)} %collective-permute-done.10.far), channel_id=1, source_target_pairs={{0,1},{1,0},{2,3},{3,2},{4,5},{5,4},{6,7},{7,6},{8,9},{9,8},{10,11... | collective-permute-start | bytes 1179656 | tf_op jit(solution)/shard_map/ppermute | solution.py:140
  65.3 9.2 %collective-permute-start.16 = (bf16[192,384]{1,0:T(8,128)(2,1)S(1)}, bf16[192,384]{1,0:T(8,128)(2,1)S(1)}, u32[]{:S(2)}, u32[]{:S(2)}) collective-permute-start(bf16[192,384]{1,0:T(8,128)(2,1)S(1)} %get-tuple-element.68), channel_id=1, source_target_pairs={{0,9},{1,8},{2,11},{3,10},{4,13},{5,12},{6,15},{7,14},{8,1},{9,0},... | collective-permute-start | bytes 442376 | tf_op jit(solution)/shard_map/ppermute | solution.py:541
  68.1 8.1 %collective-permute-start.17 = (bf16[192,384]{1,0:T(8,128)(2,1)S(1)}, bf16[192,384]{1,0:T(8,128)(2,1)S(1)}, u32[]{:S(2)}, u32[]{:S(2)}) collective-permute-start(bf16[192,384]{1,0:T(8,128)(2,1)S(1)} %get-tuple-element.69), channel_id=1, source_target_pairs={{0,7},{1,6},{2,4},{3,5},{4,2},{5,3},{6,1},{7,0},{8,15},{9,14},{10,... | collective-permute-start | bytes 442376 | tf_op jit(solution)/shard_map/ppermute | solution.py:541
  70.7 10.4 %collective-permute-start.18 = (bf16[192,384]{1,0:T(8,128)(2,1)S(1)}, bf16[192,384]{1,0:T(8,128)(2,1)S(1)}, u32[]{:S(2)}, u32[]{:S(2)}) collective-permute-start(bf16[192,384]{1,0:T(8,128)(2,1)S(1)} %get-tuple-element.70), channel_id=1, source_target_pairs={{0,14},{1,15},{2,13},{3,12},{4,11},{5,10},{6,8},{7,9},{8,6},{9,7},... | collective-permute-start | bytes 442376 | tf_op jit(solution)/shard_map/ppermute | solution.py:541
  81.1 5.7 %collective-permute-start.19 = (bf16[192,384]{1,0:T(8,128)(2,1)S(1)}, bf16[192,384]{1,0:T(8,128)(2,1)S(1)}, u32[]{:S(2)}, u32[]{:S(2)}) collective-permute-start(bf16[192,384]{1,0:T(8,128)(2,1)S(1)} %shard_map.107.own), channel_id=1, source_target_pairs={{0,2},{1,3},{2,0},{3,1},{4,6},{5,7},{6,4},{7,5},{8,10},{9,11},{10,... | collective-permute-start | bytes 442376 | tf_op jit(solution)/shard_map/ppermute | solution.py:140
  82.7 4.1 %collective-permute-start.20 = (bf16[192,384]{1,0:T(8,128)(2,1)S(1)}, bf16[192,384]{1,0:T(8,128)(2,1)S(1)}, u32[]{:S(2)}, u32[]{:S(2)}) collective-permute-start(bf16[192,384]{1,0:T(8,128)(2,1)S(1)} %shard_map.107.own), channel_id=1, source_target_pairs={{0,1},{1,0},{2,3},{3,2},{4,5},{5,4},{6,7},{7,6},{8,9},{9,8},{10,11... | collective-permute-start | bytes 442376 | tf_op jit(solution)/shard_map/ppermute | solution.py:140
  86.8 1.4 %collective-permute-start.21 = (bf16[192,384]{1,0:T(8,128)(2,1)S(1)}, bf16[192,384]{1,0:T(8,128)(2,1)S(1)}, u32[]{:S(2)}, u32[]{:S(2)}) collective-permute-start(bf16[192,384]{1,0:T(8,128)(2,1)S(1)} %collective-permute-done.19.far), channel_id=1, source_target_pairs={{0,1},{1,0},{2,3},{3,2},{4,5},{5,4},{6,7},{7,6},{8,9},{9,8},{10,11... | collective-permute-start | bytes 442376 | tf_op jit(solution)/shard_map/ppermute | solution.py:140
  89.4 10.6 %collective-permute-start.22 = (bf16[64,768]{1,0:T(8,128)(2,1)S(1)}, bf16[64,768]{1,0:T(8,128)(2,1)S(1)}, u32[]{:S(2)}, u32[]{:S(2)}) collective-permute-start(bf16[64,768]{1,0:T(8,128)(2,1)S(1)} %get-tuple-element.71), channel_id=1, source_target_pairs={{0,8},{4,12},{8,0},{12,4},{1,9},{5,13},{9,1},{13,5},{2,10},{6,14},... | collective-permute-start | bytes 294920 | tf_op jit(solution)/shard_map/ppermute | solution.py:140
  93.7 7.2 %collective-permute-start.23 = (bf16[64,768]{1,0:T(8,128)(2,1)S(1)}, bf16[64,768]{1,0:T(8,128)(2,1)S(1)}, u32[]{:S(2)}, u32[]{:S(2)}) collective-permute-start(bf16[64,768]{1,0:T(8,128)(2,1)S(1)} %get-tuple-element.72), channel_id=1, source_target_pairs={{0,4},{4,0},{8,12},{12,8},{1,5},{5,1},{9,13},{13,9},{2,6},{6,2},{1... | collective-permute-start | bytes 294920 | tf_op jit(solution)/shard_map/ppermute | solution.py:140
  93.9 7.8 %collective-permute-start.24 = (bf16[64,768]{1,0:T(8,128)(2,1)S(1)}, bf16[64,768]{1,0:T(8,128)(2,1)S(1)}, u32[]{:S(2)}, u32[]{:S(2)}) collective-permute-start(bf16[64,768]{1,0:T(8,128)(2,1)S(1)} %get-tuple-element.73), channel_id=1, source_target_pairs={{0,12},{4,8},{8,4},{12,0},{1,13},{5,9},{9,5},{13,1},{2,14},{6,10},... | collective-permute-start | bytes 294920 | tf_op jit(solution)/shard_map/ppermute | solution.py:140

commit v12 on v11

--- a/solution.py
+++ b/solution.py
@@ -489,7 +489,8 @@
         ],
         arrived,
     )
-    third_out, down_near, _ = lax.optimization_barrier((third_out, down_near, own))
+    third_out, _ = lax.optimization_barrier((third_out, arrived[0]))
+    down_near, _ = lax.optimization_barrier((down_near, own))
     down_send = call(
         pair_body,
         [((2, units // 2, features), bf16), ((2, units, features), bf16)],

time: 104 us -> 104 us (level)
  waiting for transfers between devices: 57.5 us -> 60.7 us
  starting transfers between devices: 30.9 us -> 27.8 us
    ppermute x20, waiting for transfers between devices: 47.1 us -> 51.3 us  [swap(): return lax.ppermute(array, axis, [(i, i ^ distance) for i in range(size)])]
    ppermute x20, starting transfers between devices: 24.1 us -> 20.9 us  [swap(): return lax.ppermute(array, axis, [(i, i ^ distance) for i in range(size)])]
where the time goes in v12:
time: 104 us
  waiting for transfers between devices  60.7 us (58%)
  starting transfers between devices  27.8 us (27%)
  Pallas kernels  13.6 us (13%)
  local copies, waits for them, and re-layouts  1.12 us (1%)
    ppermute x20, waiting for transfers between devices, swap(): return lax.ppermute(array, axis, [(i, i ^ distance) for i in range(size)])  51.3 us
    ppermute x20, starting transfers between devices, swap(): return lax.ppermute(array, axis, [(i, i ^ distance) for i in range(size)])  20.9 us
    pallas_call x10, Pallas kernels, call(): pl.pallas_call(body, out_shape=[jax.ShapeDtypeStruct(shape, kind) for sha...  13.6 us
    ppermute x3, waiting for transfers between devices, to_owner(): return lax.ppermute(part, ('seq', 'mp'), perm)  9.38 us
    ppermute x3, starting transfers between devices, to_owner(): return lax.ppermute(part, ('seq', 'mp'), perm)  5.29 us
  transfers between devices with their start and end apart: 25, of which 15 were waited for; matrix products, arithmetic and copies ran while one was open for 0% of the time, Pallas kernels for 6%

profile of v12, /device:TPU:0, one launch (start us, length us, event | category | flops | bytes accessed | tf_op | source)
XLA Modules:
  0.0 104.1 jit_solution(7800860392111622137)
XLA Ops:
  0.0 3.0 %shard_map.100 = (bf16[192,1408]{1,0:T(8,128)(2,1)}, bf16[192,896]{1,0:T(8,128)(2,1)}, bf16[192,384]{1,0:T(8,128)(2,1)}) custom-call(bf16[192,1536]{1,0:T(8,128)(2,1)} %tiles.3, bf16[384,1024]{1,0:T(8,128)(2,1)} %w_gate.3, bf16[384,1024]{1,0:T(8,128)(2,1)} %w_up.3, f32[1536]{0:T(1024)} %gain.3), custom_call_target="tpu_custom_call" | custom-call | tf_op jit(solution)/shard_map/pallas_call | solution.py:152
  3.1 0.0 copy-start.6
  3.1 3.1 %collective-permute-start.2 = (bf16[192,1408]{1,0:T(8,128)(2,1)}, bf16[192,1408]{1,0:T(8,128)(2,1)S(1)}, u32[]{:S(2)}, u32[]{:S(2)}) collective-permute-start(bf16[192,1408]{1,0:T(8,128)(2,1)} %get-tuple-element.42), channel_id=1, source_target_pairs={{0,4},{4,0},{8,12},{12,8},{1,5},{5,1},{9,13},{13,9},{2,6},{6,2},{1... | collective-permute-start | bytes 1622024 | tf_op jit(solution)/shard_map/ppermute | solution.py:140
  6.2 2.6 %collective-permute-start = (bf16[192,896]{1,0:T(8,128)(2,1)}, bf16[192,896]{1,0:T(8,128)(2,1)S(1)}, u32[]{:S(2)}, u32[]{:S(2)}) collective-permute-start(bf16[192,896]{1,0:T(8,128)(2,1)} %get-tuple-element.40), channel_id=1, source_target_pairs={{0,8},{4,12},{8,0},{12,4},{1,9},{5,13},{9,1},{13,5},{2,10},{6,14},... | collective-permute-start | bytes 1032200 | tf_op jit(solution)/shard_map/ppermute | solution.py:140
  8.7 3.4 %shard_map.101 = (bf16[192,512]{1,0:T(8,128)(2,1)}, bf16[384,512]{1,0:T(8,128)(2,1)}, bf16[384,384]{1,0:T(8,128)(2,1)}, bf16[384,384]{1,0:T(8,128)(2,1)}, bf16[1...) custom-call(bf16[192,1536]{1,0:T(8,128)(2,1)} %tiles.3, bf16[384,1024]{1,0:T(8,128)(2,1)} %w_gate.3, ...), custom_call_target="tpu_custom_call" | custom-call | tf_op jit(solution)/shard_map/pallas_call | solution.py:152
  12.2 1.6 %collective-permute-start.3 = (bf16[384,384]{1,0:T(8,128)(2,1)}, bf16[384,384]{1,0:T(8,128)(2,1)S(1)}, u32[]{:S(2)}, u32[]{:S(2)}) collective-permute-start(bf16[384,384]{1,0:T(8,128)(2,1)} %get-tuple-element.43), channel_id=1, source_target_pairs={{0,2},{1,3},{2,0},{3,1},{4,6},{5,7},{6,4},{7,5},{8,10},{9,11},{10,... | collective-permute-start | bytes 884744 | tf_op jit(solution)/shard_map/ppermute | solution.py:140
  13.7 0.2 collective-permute-start.1
  14.0 0.1 copy.11.dest
  14.8 0.7 shard_map.102.routes
  15.4 15.9 %collective-permute-done.1.third = bf16[192,384]{1,0:T(8,128)(2,1)S(1)} collective-permute-done((bf16[192,384]{1,0:T(8,128)(2,1)S(1)}, bf16[192,384]{1,0:T(8,128)(2,1)S(1)}, u32[]{:S(2)}, u32[]{:S(2)}) %collective-permute-start.1) | collective-permute-done | bytes 147488 | tf_op jit(solution)/shard_map/ppermute | solution.py:140
  31.4 0.1 shard_map.103
  31.4 1.6 %collective-permute-start.6 = (bf16[3,192,384]{2,1,0:T(8,128)(2,1)S(1)}, bf16[3,192,384]{2,1,0:T(8,128)(2,1)S(1)}, u32[]{:S(2)}, u32[]{:S(2)}) collective-permute-start(bf16[3,192,384]{2,1,0:T(8,128)(2,1)S(1)} %get-tuple-element.50.own), channel_id=1, source_target_pairs={{0,2},{1,3},{2,0},{3,1},{4,6},{5,7},{6,4},{7,5},{8,10},{9,11},{10,... | collective-permute-start | bytes 1327112 | tf_op jit(solution)/shard_map/ppermute | solution.py:140
  33.0 1.5 %collective-permute-start.5 = (bf16[192,512]{1,0:T(8,128)(2,1)S(1)}, bf16[192,512]{1,0:T(8,128)(2,1)S(1)}, u32[]{:S(2)}, u32[]{:S(2)}) collective-permute-start(bf16[192,512]{1,0:T(8,128)(2,1)S(1)} %get-tuple-element.53.refs_0_), channel_id=1, source_target_pairs={{0,16},{16,0},{1,17},{17,1},{2,18},{18,2},{3,19},{19,3},{4,20},{20... | collective-permute-start | bytes 589832 | tf_op jit(solution)/shard_map/ppermute | solution.py:140
  34.5 1.6 %collective-permute-start.4 = (bf16[192,512]{1,0:T(8,128)(2,1)}, bf16[192,512]{1,0:T(8,128)(2,1)S(1)}, u32[]{:S(2)}, u32[]{:S(2)}) collective-permute-start(bf16[192,512]{1,0:T(8,128)(2,1)} %get-tuple-element.52), channel_id=1, source_target_pairs={{0,12},{4,8},{8,4},{12,0},{1,13},{5,9},{9,5},{13,1},{2,14},{6,10},... | collective-permute-start | bytes 589832 | tf_op jit(solution)/shard_map/ppermute | solution.py:140
  36.1 1.0 copy-done.3
  37.0 0.1 shard_map.104
  37.1 3.2 %collective-permute-done.5.refs_1_ = bf16[192,512]{1,0:T(8,128)(2,1)S(1)} collective-permute-done((bf16[192,512]{1,0:T(8,128)(2,1)S(1)}, bf16[192,512]{1,0:T(8,128)(2,1)S(1)}, u32[]{:S(2)}, u32[]{:S(2)}) %collective-permute-start.5) | collective-permute-done | bytes 196640 | tf_op jit(solution)/shard_map/ppermute | solution.py:140
  40.3 3.4 %collective-permute-done.4.refs_2_ = bf16[192,512]{1,0:T(8,128)(2,1)S(1)} collective-permute-done((bf16[192,512]{1,0:T(8,128)(2,1)}, bf16[192,512]{1,0:T(8,128)(2,1)S(1)}, u32[]{:S(2)}, u32[]{:S(2)}) %collective-permute-start.4) | collective-permute-done | bytes 196640 | tf_op jit(solution)/shard_map/ppermute | solution.py:140
  43.7 0.6 collective-permute-start.9
  44.3 0.7 collective-permute-start.12
  44.9 6.1 %collective-permute-done.9.refs_3_ = bf16[192,512]{1,0:T(8,128)(2,1)S(1)} collective-permute-done((bf16[192,512]{1,0:T(8,128)(2,1)S(1)}, bf16[192,512]{1,0:T(8,128)(2,1)S(1)}, u32[]{:S(2)}, u32[]{:S(2)}) %collective-permute-start.9) | collective-permute-done | bytes 196640 | tf_op jit(solution)/shard_map/ppermute | solution.py:140
  51.0 1.9 %shard_map.105.own = bf16[768,256]{1,0:T(8,128)(2,1)S(1)} custom-call(bf16[192,1536]{1,0:T(8,128)(2,1)S(1)} %copy-done.1, bf16[3,192,384]{2,1,0:T(8,128)(2,1)S(1)} %get-tuple-element.50.own, bf16[3,192,384]{2,1,0:T(8,128)(2,1)S(1)} %collective-permute-done.6.far, bf16[3,192,384]{2,1,0:T(8,128)(2,1)S(1)} %collective-permute-done.7.near, ...), custom_call_target="tpu_custom_call" | custom-call | tf_op jit(solution)/shard_map/pallas_call | solution.py:152
  52.9 0.0 copy-start
  53.0 0.6 collective-permute-start.10
  53.6 1.3 %collective-permute-start.13 = (bf16[2,128,384]{2,1,0:T(8,128)(2,1)S(1)}, bf16[2,128,384]{2,1,0:T(8,128)(2,1)S(1)}, u32[]{:S(2)}, u32[]{:S(2)}) collective-permute-start(bf16[2,128,384]{2,1,0:T(8,128)(2,1)S(1)} %collective-permute-done.12.even), channel_id=1, source_target_pairs={{0,16},{16,0},{1,17},{17,1},{2,18},{18,2},{3,19},{19,3},{4,20},{20... | collective-permute-start | bytes 589832 | tf_op jit(solution)/shard_map/ppermute | solution.py:140
  54.9 0.9 collective-permute-start.15
  55.8 5.2 %collective-permute-done.13.even_other = bf16[2,128,384]{2,1,0:T(8,128)(2,1)S(1)} collective-permute-done((bf16[2,128,384]{2,1,0:T(8,128)(2,1)S(1)}, bf16[2,128,384]{2,1,0:T(8,128)(2,1)S(1)}, u32[]{:S(2)}, u32[]{:S(2)}) %collective-permute-start.13) | collective-permute-done | bytes 196640 | tf_op jit(solution)/shard_map/ppermute | solution.py:140
  61.0 2.7 %collective-permute-done.10.far = bf16[768,256]{1,0:T(8,128)(2,1)S(1)} collective-permute-done((bf16[768,256]{1,0:T(8,128)(2,1)S(1)}, bf16[768,256]{1,0:T(8,128)(2,1)S(1)}, u32[]{:S(2)}, u32[]{:S(2)}) %collective-permute-start.10) | collective-permute-done | bytes 393248 | tf_op jit(solution)/shard_map/ppermute | solution.py:140
  63.7 1.7 %collective-permute-done.14.near_far = bf16[768,256]{1,0:T(8,128)(2,1)S(1)} collective-permute-done((bf16[768,256]{1,0:T(8,128)(2,1)S(1)}, bf16[768,256]{1,0:T(8,128)(2,1)S(1)}, u32[]{:S(2)}, u32[]{:S(2)}) %collective-permute-start.14) | collective-permute-done | bytes 393248 | tf_op jit(solution)/shard_map/ppermute | solution.py:140
  65.4 1.0 shard_map.106
  66.4 2.9 %collective-permute-start.16 = (bf16[192,384]{1,0:T(8,128)(2,1)S(1)}, bf16[192,384]{1,0:T(8,128)(2,1)S(1)}, u32[]{:S(2)}, u32[]{:S(2)}) collective-permute-start(bf16[192,384]{1,0:T(8,128)(2,1)S(1)} %get-tuple-element.68), channel_id=1, source_target_pairs={{0,9},{1,8},{2,11},{3,10},{4,13},{5,12},{6,15},{7,14},{8,1},{9,0},... | collective-permute-start | bytes 442376 | tf_op jit(solution)/shard_map/ppermute | solution.py:542
  69.3 1.6 %collective-permute-start.17 = (bf16[192,384]{1,0:T(8,128)(2,1)S(1)}, bf16[192,384]{1,0:T(8,128)(2,1)S(1)}, u32[]{:S(2)}, u32[]{:S(2)}) collective-permute-start(bf16[192,384]{1,0:T(8,128)(2,1)S(1)} %get-tuple-element.69), channel_id=1, source_target_pairs={{0,7},{1,6},{2,4},{3,5},{4,2},{5,3},{6,1},{7,0},{8,15},{9,14},{10,... | collective-permute-start | bytes 442376 | tf_op jit(solution)/shard_map/ppermute | solution.py:542
  70.8 0.9 collective-permute-start.18
  71.7 3.9 %collective-permute-done.16.refs_0_ = bf16[192,384]{1,0:T(8,128)(2,1)S(1)} collective-permute-done((bf16[192,384]{1,0:T(8,128)(2,1)S(1)}, bf16[192,384]{1,0:T(8,128)(2,1)S(1)}, u32[]{:S(2)}, u32[]{:S(2)}) %collective-permute-start.16) | collective-permute-done | bytes 147488 | tf_op jit(solution)/shard_map/ppermute | solution.py:542
  75.6 1.9 %collective-permute-done.17.refs_1_ = bf16[192,384]{1,0:T(8,128)(2,1)S(1)} collective-permute-done((bf16[192,384]{1,0:T(8,128)(2,1)S(1)}, bf16[192,384]{1,0:T(8,128)(2,1)S(1)}, u32[]{:S(2)}, u32[]{:S(2)}) %collective-permute-start.17) | collective-permute-done | bytes 147488 | tf_op jit(solution)/shard_map/ppermute | solution.py:542
  77.5 3.6 %collective-permute-done.18.refs_2_ = bf16[192,384]{1,0:T(8,128)(2,1)S(1)} collective-permute-done((bf16[192,384]{1,0:T(8,128)(2,1)S(1)}, bf16[192,384]{1,0:T(8,128)(2,1)S(1)}, u32[]{:S(2)}, u32[]{:S(2)}) %collective-permute-start.18) | collective-permute-done | bytes 147488 | tf_op jit(solution)/shard_map/ppermute | solution.py:542
  81.1 0.1 shard_map.107.own
  81.2 1.7 %collective-permute-start.19 = (bf16[192,384]{1,0:T(8,128)(2,1)S(1)}, bf16[192,384]{1,0:T(8,128)(2,1)S(1)}, u32[]{:S(2)}, u32[]{:S(2)}) collective-permute-start(bf16[192,384]{1,0:T(8,128)(2,1)S(1)} %shard_map.107.own), channel_id=1, source_target_pairs={{0,2},{1,3},{2,0},{3,1},{4,6},{5,7},{6,4},{7,5},{8,10},{9,11},{10,... | collective-permute-start | bytes 442376 | tf_op jit(solution)/shard_map/ppermute | solution.py:140
  82.8 4.6 %collective-permute-done.19.far = bf16[192,384]{1,0:T(8,128)(2,1)S(1)} collective-permute-done((bf16[192,384]{1,0:T(8,128)(2,1)S(1)}, bf16[192,384]{1,0:T(8,128)(2,1)S(1)}, u32[]{:S(2)}, u32[]{:S(2)}) %collective-permute-start.19) | collective-permute-done | bytes 147488 | tf_op jit(solution)/shard_map/ppermute | solution.py:140
  87.5 1.3 %collective-permute-done.21.near_far = bf16[192,384]{1,0:T(8,128)(2,1)S(1)} collective-permute-done((bf16[192,384]{1,0:T(8,128)(2,1)S(1)}, bf16[192,384]{1,0:T(8,128)(2,1)S(1)}, u32[]{:S(2)}, u32[]{:S(2)}) %collective-permute-start.21) | collective-permute-done | bytes 147488 | tf_op jit(solution)/shard_map/ppermute | solution.py:140
  88.8 1.3 %shard_map.108 = (bf16[64,768]{1,0:T(8,128)(2,1)S(1)}, bf16[64,768]{1,0:T(8,128)(2,1)S(1)}, bf16[64,768]{1,0:T(8,128)(2,1)S(1)}, bf16[64,768]{1,0:T(8,128)(2,1)S(1)}) custom-call(f32[1,1536]{1,0:T(1,128)S(1)} %broadcast_in_dim.3.gain, bf16[352,192]{1,0:T(8,128)(2,1)S(1)} %shard_map.102.routes, bf16[576,1536]{1,0:T(8,128)(2,1)S(1)} %bitcast.3, ...), custom_call_target="tpu_custom_call" | custom-call | tf_op jit(solution)/shard_map/pallas_call | solution.py:152
  90.1 2.3 %collective-permute-start.22 = (bf16[64,768]{1,0:T(8,128)(2,1)S(1)}, bf16[64,768]{1,0:T(8,128)(2,1)S(1)}, u32[]{:S(2)}, u32[]{:S(2)}) collective-permute-start(bf16[64,768]{1,0:T(8,128)(2,1)S(1)} %get-tuple-element.71), channel_id=1, source_target_pairs={{0,8},{4,12},{8,0},{12,4},{1,9},{5,13},{9,1},{13,5},{2,10},{6,14},... | collective-permute-start | bytes 294920 | tf_op jit(solution)/shard_map/ppermute | solution.py:140
  92.3 2.0 %collective-permute-start.23 = (bf16[64,768]{1,0:T(8,128)(2,1)S(1)}, bf16[64,768]{1,0:T(8,128)(2,1)S(1)}, u32[]{:S(2)}, u32[]{:S(2)}) collective-permute-start(bf16[64,768]{1,0:T(8,128)(2,1)S(1)} %get-tuple-element.72), channel_id=1, source_target_pairs={{0,4},{4,0},{8,12},{12,8},{1,5},{5,1},{9,13},{13,9},{2,6},{6,2},{1... | collective-permute-start | bytes 294920 | tf_op jit(solution)/shard_map/ppermute | solution.py:140
  94.3 0.4 collective-permute-start.24
  94.7 3.1 %collective-permute-done.22.refs_0_ = bf16[64,768]{1,0:T(8,128)(2,1)S(1)} collective-permute-done((bf16[64,768]{1,0:T(8,128)(2,1)S(1)}, bf16[64,768]{1,0:T(8,128)(2,1)S(1)}, u32[]{:S(2)}, u32[]{:S(2)}) %collective-permute-start.22) | collective-permute-done | bytes 98336 | tf_op jit(solution)/shard_map/ppermute | solution.py:140
  97.9 0.1 collective-permute-done.23.refs_1_
  97.9 4.0 %collective-permute-done.24.refs_2_ = bf16[64,768]{1,0:T(8,128)(2,1)S(1)} collective-permute-done((bf16[64,768]{1,0:T(8,128)(2,1)S(1)}, bf16[64,768]{1,0:T(8,128)(2,1)S(1)}, u32[]{:S(2)}, u32[]{:S(2)}) %collective-permute-start.24) | collective-permute-done | bytes 98336 | tf_op jit(solution)/shard_map/ppermute | solution.py:140
  101.9 2.2 %shard_map.109 = bf16[192,256]{1,0:T(8,128)(2,1)} custom-call(s32[3]{0:T(128)S(1)} %copy-done.6, bf16[64,768]{1,0:T(8,128)(2,1)S(1)} %collective-permute-done.22.refs_0_, bf16[64,768]{1,0:T(8,128)(2,1)S(1)} %collective-permute-done.23.refs_1_, bf16[64,768]{1,0:T(8,128)(2,1)S(1)} %collective-permute-done.24.refs_2_, bf16[64,768]{1,0:T(8,128)(2,1)S(1)} %get-tuple-element.74.refs_3_), custom_call_target="tpu_custom_call" | custom-call | tf_op jit(solution)/shard_map/pallas_call | solution.py:152
  (32 shorter events, 0.1 us)
Async XLA Ops:
  3.0 10.7 %copy-start.8 = (bf16[192,384]{1,0:T(8,128)(2,1)S(1)}, bf16[192,384]{1,0:T(8,128)(2,1)}, u32[]{:S(2)}) copy-start(bf16[192,384]{1,0:T(8,128)(2,1)} %get-tuple-element.41) | copy-start | bytes 442372
  3.0 10.9 %copy-start.5 = (s32[192,1]{0,1:T(1,128)S(1)}, s32[192,1]{0,1:T(1,128)}, u32[]{:S(2)}) copy-start(s32[192,1]{0,1:T(1,128)} %param.12) | copy-start | bytes 2308
  3.1 11.7 %copy-start.6 = (s32[3]{0:T(128)S(1)}, s32[3]{0:T(128)}, u32[]{:S(2)}) copy-start(s32[3]{0:T(128)} %offsets.3) | copy-start | bytes 40
  3.1 28.3 %collective-permute-start.2 = (bf16[192,1408]{1,0:T(8,128)(2,1)}, bf16[192,1408]{1,0:T(8,128)(2,1)S(1)}, u32[]{:S(2)}, u32[]{:S(2)}) collective-permute-start(bf16[192,1408]{1,0:T(8,128)(2,1)} %get-tuple-element.42), channel_id=1, source_target_pairs={{0,4},{4,0},{8,12},{12,8},{1,5},{5,1},{9,13},{13,9},{2,6},{6,2},{1... | collective-permute-start | bytes 1622024 | tf_op jit(solution)/shard_map/ppermute | solution.py:140
  6.2 25.2 %collective-permute-start = (bf16[192,896]{1,0:T(8,128)(2,1)}, bf16[192,896]{1,0:T(8,128)(2,1)S(1)}, u32[]{:S(2)}, u32[]{:S(2)}) collective-permute-start(bf16[192,896]{1,0:T(8,128)(2,1)} %get-tuple-element.40), channel_id=1, source_target_pairs={{0,8},{4,12},{8,0},{12,4},{1,9},{5,13},{9,1},{13,5},{2,10},{6,14},... | collective-permute-start | bytes 1032200 | tf_op jit(solution)/shard_map/ppermute | solution.py:140
  12.2 38.8 %copy-start.1 = (bf16[192,1536]{1,0:T(8,128)(2,1)S(1)}, bf16[192,1536]{1,0:T(8,128)(2,1)}, u32[]{:S(2)}) copy-start(bf16[192,1536]{1,0:T(8,128)(2,1)} %get-tuple-element.46.normed) | copy-start | bytes 1769476
  12.2 38.8 %copy-start.2 = (bf16[384,512]{1,0:T(8,128)(2,1)S(1)}, bf16[384,512]{1,0:T(8,128)(2,1)}, u32[]{:S(2)}) copy-start(bf16[384,512]{1,0:T(8,128)(2,1)} %get-tuple-element.61.kept) | copy-start | bytes 1179652
  12.2 19.2 %collective-permute-start.3 = (bf16[384,384]{1,0:T(8,128)(2,1)}, bf16[384,384]{1,0:T(8,128)(2,1)S(1)}, u32[]{:S(2)}, u32[]{:S(2)}) collective-permute-start(bf16[384,384]{1,0:T(8,128)(2,1)} %get-tuple-element.43), channel_id=1, source_target_pairs={{0,2},{1,3},{2,0},{3,1},{4,6},{5,7},{6,4},{7,5},{8,10},{9,11},{10,... | collective-permute-start | bytes 884744 | tf_op jit(solution)/shard_map/ppermute | solution.py:140
  13.7 17.6 %collective-permute-start.1 = (bf16[192,384]{1,0:T(8,128)(2,1)S(1)}, bf16[192,384]{1,0:T(8,128)(2,1)S(1)}, u32[]{:S(2)}, u32[]{:S(2)}) collective-permute-start(bf16[192,384]{1,0:T(8,128)(2,1)S(1)} %copy-done.8), channel_id=1, source_target_pairs={{0,12},{4,8},{8,4},{12,0},{1,13},{5,9},{9,5},{13,1},{2,14},{6,10},... | collective-permute-start | bytes 442376 | tf_op jit(solution)/shard_map/ppermute | solution.py:140
  31.4 12.2 %collective-permute-start.6 = (bf16[3,192,384]{2,1,0:T(8,128)(2,1)S(1)}, bf16[3,192,384]{2,1,0:T(8,128)(2,1)S(1)}, u32[]{:S(2)}, u32[]{:S(2)}) collective-permute-start(bf16[3,192,384]{2,1,0:T(8,128)(2,1)S(1)} %get-tuple-element.50.own), channel_id=1, source_target_pairs={{0,2},{1,3},{2,0},{3,1},{4,6},{5,7},{6,4},{7,5},{8,10},{9,11},{10,... | collective-permute-start | bytes 1327112 | tf_op jit(solution)/shard_map/ppermute | solution.py:140
  33.0 10.7 %collective-permute-start.7 = (bf16[3,192,384]{2,1,0:T(8,128)(2,1)S(1)}, bf16[3,192,384]{2,1,0:T(8,128)(2,1)S(1)}, u32[]{:S(2)}, u32[]{:S(2)}) collective-permute-start(bf16[3,192,384]{2,1,0:T(8,128)(2,1)S(1)} %get-tuple-element.50.own), channel_id=1, source_target_pairs={{0,1},{1,0},{2,3},{3,2},{4,5},{5,4},{6,7},{7,6},{8,9},{9,8},{10,11... | collective-permute-start | bytes 1327112 | tf_op jit(solution)/shard_map/ppermute | solution.py:140
  33.0 7.3 %collective-permute-start.5 = (bf16[192,512]{1,0:T(8,128)(2,1)S(1)}, bf16[192,512]{1,0:T(8,128)(2,1)S(1)}, u32[]{:S(2)}, u32[]{:S(2)}) collective-permute-start(bf16[192,512]{1,0:T(8,128)(2,1)S(1)} %get-tuple-element.53.refs_0_), channel_id=1, source_target_pairs={{0,16},{16,0},{1,17},{17,1},{2,18},{18,2},{3,19},{19,3},{4,20},{20... | collective-permute-start | bytes 589832 | tf_op jit(solution)/shard_map/ppermute | solution.py:140
  34.5 9.2 %collective-permute-start.4 = (bf16[192,512]{1,0:T(8,128)(2,1)}, bf16[192,512]{1,0:T(8,128)(2,1)S(1)}, u32[]{:S(2)}, u32[]{:S(2)}) collective-permute-start(bf16[192,512]{1,0:T(8,128)(2,1)} %get-tuple-element.52), channel_id=1, source_target_pairs={{0,12},{4,8},{8,4},{12,0},{1,13},{5,9},{9,5},{13,1},{2,14},{6,10},... | collective-permute-start | bytes 589832 | tf_op jit(solution)/shard_map/ppermute | solution.py:140
  36.1 1.0 copy-start.3
  43.7 7.3 %collective-permute-start.8 = (bf16[3,192,384]{2,1,0:T(8,128)(2,1)S(1)}, bf16[3,192,384]{2,1,0:T(8,128)(2,1)S(1)}, u32[]{:S(2)}, u32[]{:S(2)}) collective-permute-start(bf16[3,192,384]{2,1,0:T(8,128)(2,1)S(1)} %collective-permute-done.6.far), channel_id=1, source_target_pairs={{0,1},{1,0},{2,3},{3,2},{4,5},{5,4},{6,7},{7,6},{8,9},{9,8},{10,11... | collective-permute-start | bytes 1327112 | tf_op jit(solution)/shard_map/ppermute | solution.py:140
  43.7 7.3 %collective-permute-start.9 = (bf16[192,512]{1,0:T(8,128)(2,1)S(1)}, bf16[192,512]{1,0:T(8,128)(2,1)S(1)}, u32[]{:S(2)}, u32[]{:S(2)}) collective-permute-start(bf16[192,512]{1,0:T(8,128)(2,1)S(1)} %collective-permute-done.4.refs_2_), channel_id=1, source_target_pairs={{0,16},{16,0},{1,17},{17,1},{2,18},{18,2},{3,19},{19,3},{4,20},{20... | collective-permute-start | bytes 589832 | tf_op jit(solution)/shard_map/ppermute | solution.py:140
  44.3 9.3 %collective-permute-start.12 = (bf16[2,128,384]{2,1,0:T(8,128)(2,1)S(1)}, bf16[2,128,384]{2,1,0:T(8,128)(2,1)S(1)}, u32[]{:S(2)}, u32[]{:S(2)}) collective-permute-start(bf16[2,128,384]{2,1,0:T(8,128)(2,1)S(1)} %get-tuple-element.64), channel_id=1, source_target_pairs={{0,0},{1,9},{2,14},{3,7},{4,4},{5,13},{6,2},{7,11},{8,8},{9,1},{10... | collective-permute-start | bytes 589832 | tf_op jit(solution)/shard_map/ppermute | solution.py:518
  51.0 14.4 %copy-start.4 = (bf16[192,384]{1,0:T(8,128)(2,1)S(1)}, bf16[192,384]{1,0:T(8,128)(2,1)}, u32[]{:S(2)}) copy-start(bf16[192,384]{1,0:T(8,128)(2,1)} %get-tuple-element.45.residual) | copy-start | bytes 442372
  52.9 34.5 %copy-start.7 = (f32[1536]{0:T(1024)S(1)}, f32[1536]{0:T(1024)}, u32[]{:S(2)}) copy-start(f32[1536]{0:T(1024)} %param.17) | copy-start | bytes 18436
  52.9 35.9 %copy-start = (bf16[1536,576]{0,1:T(8,128)(2,1)S(1)}, bf16[1536,576]{0,1:T(8,128)(2,1)}, u32[]{:S(2)}) copy-start(bf16[1536,576]{0,1:T(8,128)(2,1)} %param.18) | copy-start | bytes 5308420
  53.0 10.7 %collective-permute-start.10 = (bf16[768,256]{1,0:T(8,128)(2,1)S(1)}, bf16[768,256]{1,0:T(8,128)(2,1)S(1)}, u32[]{:S(2)}, u32[]{:S(2)}) collective-permute-start(bf16[768,256]{1,0:T(8,128)(2,1)S(1)} %shard_map.105.own), channel_id=1, source_target_pairs={{0,2},{1,3},{2,0},{3,1},{4,6},{5,7},{6,4},{7,5},{8,10},{9,11},{10,... | collective-permute-start | bytes 1179656 | tf_op jit(solution)/shard_map/ppermute | solution.py:140
  53.6 7.5 %collective-permute-start.13 = (bf16[2,128,384]{2,1,0:T(8,128)(2,1)S(1)}, bf16[2,128,384]{2,1,0:T(8,128)(2,1)S(1)}, u32[]{:S(2)}, u32[]{:S(2)}) collective-permute-start(bf16[2,128,384]{2,1,0:T(8,128)(2,1)S(1)} %collective-permute-done.12.even), channel_id=1, source_target_pairs={{0,16},{16,0},{1,17},{17,1},{2,18},{18,2},{3,19},{19,3},{4,20},{20... | collective-permute-start | bytes 589832 | tf_op jit(solution)/shard_map/ppermute | solution.py:140
  54.9 8.8 %collective-permute-start.15 = (bf16[2,256,384]{2,1,0:T(8,128)(2,1)S(1)}, bf16[2,256,384]{2,1,0:T(8,128)(2,1)S(1)}, u32[]{:S(2)}, u32[]{:S(2)}) collective-permute-start(bf16[2,256,384]{2,1,0:T(8,128)(2,1)S(1)} %get-tuple-element.66), channel_id=1, source_target_pairs={{0,9},{1,0},{2,7},{3,14},{4,13},{5,4},{6,11},{7,2},{8,1},{9,8},{10... | collective-permute-start | bytes 1179656 | tf_op jit(solution)/shard_map/ppermute | solution.py:518
  55.8 7.9 %collective-permute-start.11 = (bf16[768,256]{1,0:T(8,128)(2,1)S(1)}, bf16[768,256]{1,0:T(8,128)(2,1)S(1)}, u32[]{:S(2)}, u32[]{:S(2)}) collective-permute-start(bf16[768,256]{1,0:T(8,128)(2,1)S(1)} %shard_map.105.own), channel_id=1, source_target_pairs={{0,1},{1,0},{2,3},{3,2},{4,5},{5,4},{6,7},{7,6},{8,9},{9,8},{10,11... | collective-permute-start | bytes 1179656 | tf_op jit(solution)/shard_map/ppermute | solution.py:140
  63.7 1.7 %collective-permute-start.14 = (bf16[768,256]{1,0:T(8,128)(2,1)S(1)}, bf16[768,256]{1,0:T(8,128)(2,1)S(1)}, u32[]{:S(2)}, u32[]{:S(2)}) collective-permute-start(bf16[768,256]{1,0:T(8,128)(2,1)S(1)} %collective-permute-done.10.far), channel_id=1, source_target_pairs={{0,1},{1,0},{2,3},{3,2},{4,5},{5,4},{6,7},{7,6},{8,9},{9,8},{10,11... | collective-permute-start | bytes 1179656 | tf_op jit(solution)/shard_map/ppermute | solution.py:140
  66.4 9.2 %collective-permute-start.16 = (bf16[192,384]{1,0:T(8,128)(2,1)S(1)}, bf16[192,384]{1,0:T(8,128)(2,1)S(1)}, u32[]{:S(2)}, u32[]{:S(2)}) collective-permute-start(bf16[192,384]{1,0:T(8,128)(2,1)S(1)} %get-tuple-element.68), channel_id=1, source_target_pairs={{0,9},{1,8},{2,11},{3,10},{4,13},{5,12},{6,15},{7,14},{8,1},{9,0},... | collective-permute-start | bytes 442376 | tf_op jit(solution)/shard_map/ppermute | solution.py:542
  69.3 8.3 %collective-permute-start.17 = (bf16[192,384]{1,0:T(8,128)(2,1)S(1)}, bf16[192,384]{1,0:T(8,128)(2,1)S(1)}, u32[]{:S(2)}, u32[]{:S(2)}) collective-permute-start(bf16[192,384]{1,0:T(8,128)(2,1)S(1)} %get-tuple-element.69), channel_id=1, source_target_pairs={{0,7},{1,6},{2,4},{3,5},{4,2},{5,3},{6,1},{7,0},{8,15},{9,14},{10,... | collective-permute-start | bytes 442376 | tf_op jit(solution)/shard_map/ppermute | solution.py:542
  70.8 10.2 %collective-permute-start.18 = (bf16[192,384]{1,0:T(8,128)(2,1)S(1)}, bf16[192,384]{1,0:T(8,128)(2,1)S(1)}, u32[]{:S(2)}, u32[]{:S(2)}) collective-permute-start(bf16[192,384]{1,0:T(8,128)(2,1)S(1)} %get-tuple-element.70), channel_id=1, source_target_pairs={{0,14},{1,15},{2,13},{3,12},{4,11},{5,10},{6,8},{7,9},{8,6},{9,7},... | collective-permute-start | bytes 442376 | tf_op jit(solution)/shard_map/ppermute | solution.py:542
  81.2 6.3 %collective-permute-start.19 = (bf16[192,384]{1,0:T(8,128)(2,1)S(1)}, bf16[192,384]{1,0:T(8,128)(2,1)S(1)}, u32[]{:S(2)}, u32[]{:S(2)}) collective-permute-start(bf16[192,384]{1,0:T(8,128)(2,1)S(1)} %shard_map.107.own), channel_id=1, source_target_pairs={{0,2},{1,3},{2,0},{3,1},{4,6},{5,7},{6,4},{7,5},{8,10},{9,11},{10,... | collective-permute-start | bytes 442376 | tf_op jit(solution)/shard_map/ppermute | solution.py:140
  82.8 4.6 %collective-permute-start.20 = (bf16[192,384]{1,0:T(8,128)(2,1)S(1)}, bf16[192,384]{1,0:T(8,128)(2,1)S(1)}, u32[]{:S(2)}, u32[]{:S(2)}) collective-permute-start(bf16[192,384]{1,0:T(8,128)(2,1)S(1)} %shard_map.107.own), channel_id=1, source_target_pairs={{0,1},{1,0},{2,3},{3,2},{4,5},{5,4},{6,7},{7,6},{8,9},{9,8},{10,11... | collective-permute-start | bytes 442376 | tf_op jit(solution)/shard_map/ppermute | solution.py:140
  87.4 1.4 %collective-permute-start.21 = (bf16[192,384]{1,0:T(8,128)(2,1)S(1)}, bf16[192,384]{1,0:T(8,128)(2,1)S(1)}, u32[]{:S(2)}, u32[]{:S(2)}) collective-permute-start(bf16[192,384]{1,0:T(8,128)(2,1)S(1)} %collective-permute-done.19.far), channel_id=1, source_target_pairs={{0,1},{1,0},{2,3},{3,2},{4,5},{5,4},{6,7},{7,6},{8,9},{9,8},{10,11... | collective-permute-start | bytes 442376 | tf_op jit(solution)/shard_map/ppermute | solution.py:140
  90.1 7.8 %collective-permute-start.22 = (bf16[64,768]{1,0:T(8,128)(2,1)S(1)}, bf16[64,768]{1,0:T(8,128)(2,1)S(1)}, u32[]{:S(2)}, u32[]{:S(2)}) collective-permute-start(bf16[64,768]{1,0:T(8,128)(2,1)S(1)} %get-tuple-element.71), channel_id=1, source_target_pairs={{0,8},{4,12},{8,0},{12,4},{1,9},{5,13},{9,1},{13,5},{2,10},{6,14},... | collective-permute-start | bytes 294920 | tf_op jit(solution)/shard_map/ppermute | solution.py:140
  92.3 5.6 %collective-permute-start.23 = (bf16[64,768]{1,0:T(8,128)(2,1)S(1)}, bf16[64,768]{1,0:T(8,128)(2,1)S(1)}, u32[]{:S(2)}, u32[]{:S(2)}) collective-permute-start(bf16[64,768]{1,0:T(8,128)(2,1)S(1)} %get-tuple-element.72), channel_id=1, source_target_pairs={{0,4},{4,0},{8,12},{12,8},{1,5},{5,1},{9,13},{13,9},{2,6},{6,2},{1... | collective-permute-start | bytes 294920 | tf_op jit(solution)/shard_map/ppermute | solution.py:140
  94.3 7.6 %collective-permute-start.24 = (bf16[64,768]{1,0:T(8,128)(2,1)S(1)}, bf16[64,768]{1,0:T(8,128)(2,1)S(1)}, u32[]{:S(2)}, u32[]{:S(2)}) collective-permute-start(bf16[64,768]{1,0:T(8,128)(2,1)S(1)} %get-tuple-element.73), channel_id=1, source_target_pairs={{0,12},{4,8},{8,4},{12,0},{1,13},{5,9},{9,5},{13,1},{2,14},{6,10},... | collective-permute-start | bytes 294920 | tf_op jit(solution)/shard_map/ppermute | solution.py:140

commit v13 on v12

--- a/solution.py
+++ b/solution.py
@@ -529,7 +529,7 @@
     sums = call(
         down_body,
         [((tile_rows, features), kind) for kind in (jnp.float32, bf16, bf16, bf16)],
-        (residual, hidden, *spread_mp(hidden, even_other), even, even_other, odd),
+        (residual, hidden, *spread_mp(hidden, (even_other, odd)), even, even_other, odd),
     )
     holder = [0, 2, 1, 3]
 

time: 104 us -> 104 us (level)
  waiting for transfers between devices: 60.7 us -> 51.6 us
  starting transfers between devices: 27.8 us -> 36.6 us
    ppermute x20, waiting for transfers between devices: 51.3 us -> 42 us  [swap(): return lax.ppermute(array, axis, [(i, i ^ distance) for i in range(size)])]
    ppermute x20, starting transfers between devices: 20.9 us -> 26.6 us  [swap(): return lax.ppermute(array, axis, [(i, i ^ distance) for i in range(size)])]
    ppermute x2, starting transfers between devices: 1.56 us -> 4.77 us  [split_hidden_plan(): parts.append(lax.ppermute(down_send[j], ('seq', 'mp'), perm))]
  transfers between devices with their start and end apart: 25 -> 25, of which waited for: 15 -> 13; matrix products, arithmetic and copies ran while one was open for 0% -> 0% of each run, Pallas kernels for 6% -> 6%
where the time goes in v13:
time: 104 us
  waiting for transfers between devices  51.6 us (50%)
  starting transfers between devices  36.6 us (35%)
  Pallas kernels  13.6 us (13%)
  local copies, waits for them, and re-layouts  1.12 us (1%)
    ppermute x20, waiting for transfers between devices, swap(): return lax.ppermute(array, axis, [(i, i ^ distance) for i in range(size)])  42 us
    ppermute x20, starting transfers between devices, swap(): return lax.ppermute(array, axis, [(i, i ^ distance) for i in range(size)])  26.6 us
    pallas_call x10, Pallas kernels, call(): pl.pallas_call(body, out_shape=[jax.ShapeDtypeStruct(shape, kind) for sha...  13.6 us
    ppermute x3, waiting for transfers between devices, to_owner(): return lax.ppermute(part, ('seq', 'mp'), perm)  9.64 us
    ppermute x3, starting transfers between devices, to_owner(): return lax.ppermute(part, ('seq', 'mp'), perm)  5.3 us
    ppermute x2, starting transfers between devices, split_hidden_plan(): parts.append(lax.ppermute(down_send[j], ('seq', 'mp'), perm))  4.77 us
  transfers between devices with their start and end apart: 25, of which 13 were waited for; matrix products, arithmetic and copies ran while one was open for 0% of the time, Pallas kernels for 6%

profile of v13, /device:TPU:0, one launch (start us, length us, event | category | flops | bytes accessed | tf_op | source)
XLA Modules:
  0.0 103.9 jit_solution(3927036895931513824)
XLA Ops:
  0.0 3.0 %shard_map.100 = (bf16[192,1408]{1,0:T(8,128)(2,1)}, bf16[192,896]{1,0:T(8,128)(2,1)}, bf16[192,384]{1,0:T(8,128)(2,1)}) custom-call(bf16[192,1536]{1,0:T(8,128)(2,1)} %tiles.3, bf16[384,1024]{1,0:T(8,128)(2,1)} %w_gate.3, bf16[384,1024]{1,0:T(8,128)(2,1)} %w_up.3, f32[1536]{0:T(1024)} %gain.3), custom_call_target="tpu_custom_call" | custom-call | tf_op jit(solution)/shard_map/pallas_call | solution.py:152
  3.0 0.0 copy-start.5
  3.1 0.0 copy-start.6
  3.1 3.1 %collective-permute-start.2 = (bf16[192,1408]{1,0:T(8,128)(2,1)}, bf16[192,1408]{1,0:T(8,128)(2,1)S(1)}, u32[]{:S(2)}, u32[]{:S(2)}) collective-permute-start(bf16[192,1408]{1,0:T(8,128)(2,1)} %get-tuple-element.42), channel_id=1, source_target_pairs={{0,4},{4,0},{8,12},{12,8},{1,5},{5,1},{9,13},{13,9},{2,6},{6,2},{1... | collective-permute-start | bytes 1622024 | tf_op jit(solution)/shard_map/ppermute | solution.py:140
  6.2 2.6 %collective-permute-start = (bf16[192,896]{1,0:T(8,128)(2,1)}, bf16[192,896]{1,0:T(8,128)(2,1)S(1)}, u32[]{:S(2)}, u32[]{:S(2)}) collective-permute-start(bf16[192,896]{1,0:T(8,128)(2,1)} %get-tuple-element.40), channel_id=1, source_target_pairs={{0,8},{4,12},{8,0},{12,4},{1,9},{5,13},{9,1},{13,5},{2,10},{6,14},... | collective-permute-start | bytes 1032200 | tf_op jit(solution)/shard_map/ppermute | solution.py:140
  8.7 3.4 %shard_map.101 = (bf16[192,512]{1,0:T(8,128)(2,1)}, bf16[384,512]{1,0:T(8,128)(2,1)}, bf16[384,384]{1,0:T(8,128)(2,1)}, bf16[384,384]{1,0:T(8,128)(2,1)}, bf16[1...) custom-call(bf16[192,1536]{1,0:T(8,128)(2,1)} %tiles.3, bf16[384,1024]{1,0:T(8,128)(2,1)} %w_gate.3, ...), custom_call_target="tpu_custom_call" | custom-call | tf_op jit(solution)/shard_map/pallas_call | solution.py:152
  12.2 1.6 %collective-permute-start.3 = (bf16[384,384]{1,0:T(8,128)(2,1)}, bf16[384,384]{1,0:T(8,128)(2,1)S(1)}, u32[]{:S(2)}, u32[]{:S(2)}) collective-permute-start(bf16[384,384]{1,0:T(8,128)(2,1)} %get-tuple-element.43), channel_id=1, source_target_pairs={{0,2},{1,3},{2,0},{3,1},{4,6},{5,7},{6,4},{7,5},{8,10},{9,11},{10,... | collective-permute-start | bytes 884744 | tf_op jit(solution)/shard_map/ppermute | solution.py:140
  13.7 0.2 collective-permute-start.1
  14.0 0.1 copy.11.dest
  14.8 0.7 shard_map.102.routes
  15.4 15.9 %collective-permute-done.1.third = bf16[192,384]{1,0:T(8,128)(2,1)S(1)} collective-permute-done((bf16[192,384]{1,0:T(8,128)(2,1)S(1)}, bf16[192,384]{1,0:T(8,128)(2,1)S(1)}, u32[]{:S(2)}, u32[]{:S(2)}) %collective-permute-start.1) | collective-permute-done | bytes 147488 | tf_op jit(solution)/shard_map/ppermute | solution.py:140
  31.4 0.1 shard_map.103
  31.4 1.6 %collective-permute-start.6 = (bf16[3,192,384]{2,1,0:T(8,128)(2,1)S(1)}, bf16[3,192,384]{2,1,0:T(8,128)(2,1)S(1)}, u32[]{:S(2)}, u32[]{:S(2)}) collective-permute-start(bf16[3,192,384]{2,1,0:T(8,128)(2,1)S(1)} %get-tuple-element.50.own), channel_id=1, source_target_pairs={{0,2},{1,3},{2,0},{3,1},{4,6},{5,7},{6,4},{7,5},{8,10},{9,11},{10,... | collective-permute-start | bytes 1327112 | tf_op jit(solution)/shard_map/ppermute | solution.py:140
  33.0 1.5 %collective-permute-start.5 = (bf16[192,512]{1,0:T(8,128)(2,1)S(1)}, bf16[192,512]{1,0:T(8,128)(2,1)S(1)}, u32[]{:S(2)}, u32[]{:S(2)}) collective-permute-start(bf16[192,512]{1,0:T(8,128)(2,1)S(1)} %get-tuple-element.53.refs_0_), channel_id=1, source_target_pairs={{0,16},{16,0},{1,17},{17,1},{2,18},{18,2},{3,19},{19,3},{4,20},{20... | collective-permute-start | bytes 589832 | tf_op jit(solution)/shard_map/ppermute | solution.py:140
  34.5 1.6 %collective-permute-start.4 = (bf16[192,512]{1,0:T(8,128)(2,1)}, bf16[192,512]{1,0:T(8,128)(2,1)S(1)}, u32[]{:S(2)}, u32[]{:S(2)}) collective-permute-start(bf16[192,512]{1,0:T(8,128)(2,1)} %get-tuple-element.52), channel_id=1, source_target_pairs={{0,12},{4,8},{8,4},{12,0},{1,13},{5,9},{9,5},{13,1},{2,14},{6,10},... | collective-permute-start | bytes 589832 | tf_op jit(solution)/shard_map/ppermute | solution.py:140
  36.1 1.0 copy-done.3
  37.0 0.1 shard_map.104
  37.1 3.2 %collective-permute-done.5.refs_1_ = bf16[192,512]{1,0:T(8,128)(2,1)S(1)} collective-permute-done((bf16[192,512]{1,0:T(8,128)(2,1)S(1)}, bf16[192,512]{1,0:T(8,128)(2,1)S(1)}, u32[]{:S(2)}, u32[]{:S(2)}) %collective-permute-start.5) | collective-permute-done | bytes 196640 | tf_op jit(solution)/shard_map/ppermute | solution.py:140
  40.3 3.4 %collective-permute-done.4.refs_2_ = bf16[192,512]{1,0:T(8,128)(2,1)S(1)} collective-permute-done((bf16[192,512]{1,0:T(8,128)(2,1)}, bf16[192,512]{1,0:T(8,128)(2,1)S(1)}, u32[]{:S(2)}, u32[]{:S(2)}) %collective-permute-start.4) | collective-permute-done | bytes 196640 | tf_op jit(solution)/shard_map/ppermute | solution.py:140
  43.7 0.6 collective-permute-start.9
  44.3 0.7 collective-permute-start.12
  44.9 4.1 %collective-permute-start.14 = (bf16[2,256,384]{2,1,0:T(8,128)(2,1)S(1)}, bf16[2,256,384]{2,1,0:T(8,128)(2,1)S(1)}, u32[]{:S(2)}, u32[]{:S(2)}) collective-permute-start(bf16[2,256,384]{2,1,0:T(8,128)(2,1)S(1)} %get-tuple-element.65), channel_id=1, source_target_pairs={{0,9},{1,0},{2,7},{3,14},{4,13},{5,4},{6,11},{7,2},{8,1},{9,8},{10... | collective-permute-start | bytes 1179656 | tf_op jit(solution)/shard_map/ppermute | solution.py:518
  49.0 2.0 %collective-permute-done.9.refs_3_ = bf16[192,512]{1,0:T(8,128)(2,1)S(1)} collective-permute-done((bf16[192,512]{1,0:T(8,128)(2,1)S(1)}, bf16[192,512]{1,0:T(8,128)(2,1)S(1)}, u32[]{:S(2)}, u32[]{:S(2)}) %collective-permute-start.9) | collective-permute-done | bytes 196640 | tf_op jit(solution)/shard_map/ppermute | solution.py:140
  51.0 1.9 %shard_map.105.own = bf16[768,256]{1,0:T(8,128)(2,1)S(1)} custom-call(bf16[192,1536]{1,0:T(8,128)(2,1)S(1)} %copy-done.1, bf16[3,192,384]{2,1,0:T(8,128)(2,1)S(1)} %get-tuple-element.50.own, bf16[3,192,384]{2,1,0:T(8,128)(2,1)S(1)} %collective-permute-done.6.far, bf16[3,192,384]{2,1,0:T(8,128)(2,1)S(1)} %collective-permute-done.7.near, ...), custom_call_target="tpu_custom_call" | custom-call | tf_op jit(solution)/shard_map/pallas_call | solution.py:152
  52.9 0.0 copy-start.7
  53.0 0.6 collective-permute-start.10
  53.6 1.3 %collective-permute-start.13 = (bf16[2,128,384]{2,1,0:T(8,128)(2,1)S(1)}, bf16[2,128,384]{2,1,0:T(8,128)(2,1)S(1)}, u32[]{:S(2)}, u32[]{:S(2)}) collective-permute-start(bf16[2,128,384]{2,1,0:T(8,128)(2,1)S(1)} %collective-permute-done.12.even), channel_id=1, source_target_pairs={{0,16},{16,0},{1,17},{17,1},{2,18},{18,2},{3,19},{19,3},{4,20},{20... | collective-permute-start | bytes 589832 | tf_op jit(solution)/shard_map/ppermute | solution.py:140
  54.9 5.8 %collective-permute-start.11 = (bf16[768,256]{1,0:T(8,128)(2,1)S(1)}, bf16[768,256]{1,0:T(8,128)(2,1)S(1)}, u32[]{:S(2)}, u32[]{:S(2)}) collective-permute-start(bf16[768,256]{1,0:T(8,128)(2,1)S(1)} %shard_map.105.own), channel_id=1, source_target_pairs={{0,1},{1,0},{2,3},{3,2},{4,5},{5,4},{6,7},{7,6},{8,9},{9,8},{10,11... | collective-permute-start | bytes 1179656 | tf_op jit(solution)/shard_map/ppermute | solution.py:140
  60.7 3.0 %collective-permute-done.10.far = bf16[768,256]{1,0:T(8,128)(2,1)S(1)} collective-permute-done((bf16[768,256]{1,0:T(8,128)(2,1)S(1)}, bf16[768,256]{1,0:T(8,128)(2,1)S(1)}, u32[]{:S(2)}, u32[]{:S(2)}) %collective-permute-start.10) | collective-permute-done | bytes 393248 | tf_op jit(solution)/shard_map/ppermute | solution.py:140
  63.7 0.3 collective-permute-start.15
  64.0 1.4 %collective-permute-done.15.near_far = bf16[768,256]{1,0:T(8,128)(2,1)S(1)} collective-permute-done((bf16[768,256]{1,0:T(8,128)(2,1)S(1)}, bf16[768,256]{1,0:T(8,128)(2,1)S(1)}, u32[]{:S(2)}, u32[]{:S(2)}) %collective-permute-start.15) | collective-permute-done | bytes 393248 | tf_op jit(solution)/shard_map/ppermute | solution.py:140
  65.4 1.0 shard_map.106
  66.4 2.9 %collective-permute-start.16 = (bf16[192,384]{1,0:T(8,128)(2,1)S(1)}, bf16[192,384]{1,0:T(8,128)(2,1)S(1)}, u32[]{:S(2)}, u32[]{:S(2)}) collective-permute-start(bf16[192,384]{1,0:T(8,128)(2,1)S(1)} %get-tuple-element.68), channel_id=1, source_target_pairs={{0,9},{1,8},{2,11},{3,10},{4,13},{5,12},{6,15},{7,14},{8,1},{9,0},... | collective-permute-start | bytes 442376 | tf_op jit(solution)/shard_map/ppermute | solution.py:542
  69.3 2.5 %collective-permute-start.18 = (bf16[192,384]{1,0:T(8,128)(2,1)S(1)}, bf16[192,384]{1,0:T(8,128)(2,1)S(1)}, u32[]{:S(2)}, u32[]{:S(2)}) collective-permute-start(bf16[192,384]{1,0:T(8,128)(2,1)S(1)} %get-tuple-element.70), channel_id=1, source_target_pairs={{0,14},{1,15},{2,13},{3,12},{4,11},{5,10},{6,8},{7,9},{8,6},{9,7},... | collective-permute-start | bytes 442376 | tf_op jit(solution)/shard_map/ppermute | solution.py:542
  71.7 4.7 %collective-permute-done.16.refs_0_ = bf16[192,384]{1,0:T(8,128)(2,1)S(1)} collective-permute-done((bf16[192,384]{1,0:T(8,128)(2,1)S(1)}, bf16[192,384]{1,0:T(8,128)(2,1)S(1)}, u32[]{:S(2)}, u32[]{:S(2)}) %collective-permute-start.16) | collective-permute-done | bytes 147488 | tf_op jit(solution)/shard_map/ppermute | solution.py:542
  76.4 1.4 %collective-permute-done.17.refs_1_ = bf16[192,384]{1,0:T(8,128)(2,1)S(1)} collective-permute-done((bf16[192,384]{1,0:T(8,128)(2,1)S(1)}, bf16[192,384]{1,0:T(8,128)(2,1)S(1)}, u32[]{:S(2)}, u32[]{:S(2)}) %collective-permute-start.17) | collective-permute-done | bytes 147488 | tf_op jit(solution)/shard_map/ppermute | solution.py:542
  77.8 3.5 %collective-permute-done.18.refs_2_ = bf16[192,384]{1,0:T(8,128)(2,1)S(1)} collective-permute-done((bf16[192,384]{1,0:T(8,128)(2,1)S(1)}, bf16[192,384]{1,0:T(8,128)(2,1)S(1)}, u32[]{:S(2)}, u32[]{:S(2)}) %collective-permute-start.18) | collective-permute-done | bytes 147488 | tf_op jit(solution)/shard_map/ppermute | solution.py:542
  81.3 0.1 shard_map.107.own
  81.4 1.2 %collective-permute-start.19 = (bf16[192,384]{1,0:T(8,128)(2,1)S(1)}, bf16[192,384]{1,0:T(8,128)(2,1)S(1)}, u32[]{:S(2)}, u32[]{:S(2)}) collective-permute-start(bf16[192,384]{1,0:T(8,128)(2,1)S(1)} %shard_map.107.own), channel_id=1, source_target_pairs={{0,2},{1,3},{2,0},{3,1},{4,6},{5,7},{6,4},{7,5},{8,10},{9,11},{10,... | collective-permute-start | bytes 442376 | tf_op jit(solution)/shard_map/ppermute | solution.py:140
  82.7 4.6 %collective-permute-done.19.far = bf16[192,384]{1,0:T(8,128)(2,1)S(1)} collective-permute-done((bf16[192,384]{1,0:T(8,128)(2,1)S(1)}, bf16[192,384]{1,0:T(8,128)(2,1)S(1)}, u32[]{:S(2)}, u32[]{:S(2)}) %collective-permute-start.19) | collective-permute-done | bytes 147488 | tf_op jit(solution)/shard_map/ppermute | solution.py:140
  87.3 1.3 %collective-permute-done.21.near_far = bf16[192,384]{1,0:T(8,128)(2,1)S(1)} collective-permute-done((bf16[192,384]{1,0:T(8,128)(2,1)S(1)}, bf16[192,384]{1,0:T(8,128)(2,1)S(1)}, u32[]{:S(2)}, u32[]{:S(2)}) %collective-permute-start.21) | collective-permute-done | bytes 147488 | tf_op jit(solution)/shard_map/ppermute | solution.py:140
  88.7 1.3 %shard_map.108 = (bf16[64,768]{1,0:T(8,128)(2,1)S(1)}, bf16[64,768]{1,0:T(8,128)(2,1)S(1)}, bf16[64,768]{1,0:T(8,128)(2,1)S(1)}, bf16[64,768]{1,0:T(8,128)(2,1)S(1)}) custom-call(f32[1,1536]{1,0:T(1,128)S(1)} %broadcast_in_dim.3.gain, bf16[352,192]{1,0:T(8,128)(2,1)S(1)} %shard_map.102.routes, bf16[576,1536]{1,0:T(8,128)(2,1)S(1)} %bitcast.3, ...), custom_call_target="tpu_custom_call" | custom-call | tf_op jit(solution)/shard_map/pallas_call | solution.py:152
  89.9 2.7 %collective-permute-start.22 = (bf16[64,768]{1,0:T(8,128)(2,1)S(1)}, bf16[64,768]{1,0:T(8,128)(2,1)S(1)}, u32[]{:S(2)}, u32[]{:S(2)}) collective-permute-start(bf16[64,768]{1,0:T(8,128)(2,1)S(1)} %get-tuple-element.71), channel_id=1, source_target_pairs={{0,8},{4,12},{8,0},{12,4},{1,9},{5,13},{9,1},{13,5},{2,10},{6,14},... | collective-permute-start | bytes 294920 | tf_op jit(solution)/shard_map/ppermute | solution.py:140
  92.6 0.4 collective-permute-start.23
  93.0 1.5 %collective-permute-start.24 = (bf16[64,768]{1,0:T(8,128)(2,1)S(1)}, bf16[64,768]{1,0:T(8,128)(2,1)S(1)}, u32[]{:S(2)}, u32[]{:S(2)}) collective-permute-start(bf16[64,768]{1,0:T(8,128)(2,1)S(1)} %get-tuple-element.73), channel_id=1, source_target_pairs={{0,12},{4,8},{8,4},{12,0},{1,13},{5,9},{9,5},{13,1},{2,14},{6,10},... | collective-permute-start | bytes 294920 | tf_op jit(solution)/shard_map/ppermute | solution.py:140
  94.5 3.7 %collective-permute-done.22.refs_0_ = bf16[64,768]{1,0:T(8,128)(2,1)S(1)} collective-permute-done((bf16[64,768]{1,0:T(8,128)(2,1)S(1)}, bf16[64,768]{1,0:T(8,128)(2,1)S(1)}, u32[]{:S(2)}, u32[]{:S(2)}) %collective-permute-start.22) | collective-permute-done | bytes 98336 | tf_op jit(solution)/shard_map/ppermute | solution.py:140
  98.2 3.5 %collective-permute-done.24.refs_2_ = bf16[64,768]{1,0:T(8,128)(2,1)S(1)} collective-permute-done((bf16[64,768]{1,0:T(8,128)(2,1)S(1)}, bf16[64,768]{1,0:T(8,128)(2,1)S(1)}, u32[]{:S(2)}, u32[]{:S(2)}) %collective-permute-start.24) | collective-permute-done | bytes 98336 | tf_op jit(solution)/shard_map/ppermute | solution.py:140
  101.7 2.2 %shard_map.109 = bf16[192,256]{1,0:T(8,128)(2,1)} custom-call(s32[3]{0:T(128)S(1)} %copy-done.6, bf16[64,768]{1,0:T(8,128)(2,1)S(1)} %collective-permute-done.22.refs_0_, bf16[64,768]{1,0:T(8,128)(2,1)S(1)} %collective-permute-done.23.refs_1_, bf16[64,768]{1,0:T(8,128)(2,1)S(1)} %collective-permute-done.24.refs_2_, bf16[64,768]{1,0:T(8,128)(2,1)S(1)} %get-tuple-element.74.refs_3_), custom_call_target="tpu_custom_call" | custom-call | tf_op jit(solution)/shard_map/pallas_call | solution.py:152
  (32 shorter events, 0.1 us)
Async XLA Ops:
  3.0 10.7 %copy-start.8 = (bf16[192,384]{1,0:T(8,128)(2,1)S(1)}, bf16[192,384]{1,0:T(8,128)(2,1)}, u32[]{:S(2)}) copy-start(bf16[192,384]{1,0:T(8,128)(2,1)} %get-tuple-element.41) | copy-start | bytes 442372
  3.0 10.9 %copy-start.5 = (s32[192,1]{0,1:T(1,128)S(1)}, s32[192,1]{0,1:T(1,128)}, u32[]{:S(2)}) copy-start(s32[192,1]{0,1:T(1,128)} %param.12) | copy-start | bytes 2308
  3.1 11.7 %copy-start.6 = (s32[3]{0:T(128)S(1)}, s32[3]{0:T(128)}, u32[]{:S(2)}) copy-start(s32[3]{0:T(128)} %offsets.3) | copy-start | bytes 40
  3.1 28.3 %collective-permute-start.2 = (bf16[192,1408]{1,0:T(8,128)(2,1)}, bf16[192,1408]{1,0:T(8,128)(2,1)S(1)}, u32[]{:S(2)}, u32[]{:S(2)}) collective-permute-start(bf16[192,1408]{1,0:T(8,128)(2,1)} %get-tuple-element.42), channel_id=1, source_target_pairs={{0,4},{4,0},{8,12},{12,8},{1,5},{5,1},{9,13},{13,9},{2,6},{6,2},{1... | collective-permute-start | bytes 1622024 | tf_op jit(solution)/shard_map/ppermute | solution.py:140
  6.2 25.2 %collective-permute-start = (bf16[192,896]{1,0:T(8,128)(2,1)}, bf16[192,896]{1,0:T(8,128)(2,1)S(1)}, u32[]{:S(2)}, u32[]{:S(2)}) collective-permute-start(bf16[192,896]{1,0:T(8,128)(2,1)} %get-tuple-element.40), channel_id=1, source_target_pairs={{0,8},{4,12},{8,0},{12,4},{1,9},{5,13},{9,1},{13,5},{2,10},{6,14},... | collective-permute-start | bytes 1032200 | tf_op jit(solution)/shard_map/ppermute | solution.py:140
  12.2 38.8 %copy-start.1 = (bf16[192,1536]{1,0:T(8,128)(2,1)S(1)}, bf16[192,1536]{1,0:T(8,128)(2,1)}, u32[]{:S(2)}) copy-start(bf16[192,1536]{1,0:T(8,128)(2,1)} %get-tuple-element.46.normed) | copy-start | bytes 1769476
  12.2 38.8 %copy-start.2 = (bf16[384,512]{1,0:T(8,128)(2,1)S(1)}, bf16[384,512]{1,0:T(8,128)(2,1)}, u32[]{:S(2)}) copy-start(bf16[384,512]{1,0:T(8,128)(2,1)} %get-tuple-element.61.kept) | copy-start | bytes 1179652
  12.2 19.2 %collective-permute-start.3 = (bf16[384,384]{1,0:T(8,128)(2,1)}, bf16[384,384]{1,0:T(8,128)(2,1)S(1)}, u32[]{:S(2)}, u32[]{:S(2)}) collective-permute-start(bf16[384,384]{1,0:T(8,128)(2,1)} %get-tuple-element.43), channel_id=1, source_target_pairs={{0,2},{1,3},{2,0},{3,1},{4,6},{5,7},{6,4},{7,5},{8,10},{9,11},{10,... | collective-permute-start | bytes 884744 | tf_op jit(solution)/shard_map/ppermute | solution.py:140
  13.7 17.6 %collective-permute-start.1 = (bf16[192,384]{1,0:T(8,128)(2,1)S(1)}, bf16[192,384]{1,0:T(8,128)(2,1)S(1)}, u32[]{:S(2)}, u32[]{:S(2)}) collective-permute-start(bf16[192,384]{1,0:T(8,128)(2,1)S(1)} %copy-done.8), channel_id=1, source_target_pairs={{0,12},{4,8},{8,4},{12,0},{1,13},{5,9},{9,5},{13,1},{2,14},{6,10},... | collective-permute-start | bytes 442376 | tf_op jit(solution)/shard_map/ppermute | solution.py:140
  31.4 12.2 %collective-permute-start.6 = (bf16[3,192,384]{2,1,0:T(8,128)(2,1)S(1)}, bf16[3,192,384]{2,1,0:T(8,128)(2,1)S(1)}, u32[]{:S(2)}, u32[]{:S(2)}) collective-permute-start(bf16[3,192,384]{2,1,0:T(8,128)(2,1)S(1)} %get-tuple-element.50.own), channel_id=1, source_target_pairs={{0,2},{1,3},{2,0},{3,1},{4,6},{5,7},{6,4},{7,5},{8,10},{9,11},{10,... | collective-permute-start | bytes 1327112 | tf_op jit(solution)/shard_map/ppermute | solution.py:140
  33.0 10.7 %collective-permute-start.7 = (bf16[3,192,384]{2,1,0:T(8,128)(2,1)S(1)}, bf16[3,192,384]{2,1,0:T(8,128)(2,1)S(1)}, u32[]{:S(2)}, u32[]{:S(2)}) collective-permute-start(bf16[3,192,384]{2,1,0:T(8,128)(2,1)S(1)} %get-tuple-element.50.own), channel_id=1, source_target_pairs={{0,1},{1,0},{2,3},{3,2},{4,5},{5,4},{6,7},{7,6},{8,9},{9,8},{10,11... | collective-permute-start | bytes 1327112 | tf_op jit(solution)/shard_map/ppermute | solution.py:140
  33.0 7.3 %collective-permute-start.5 = (bf16[192,512]{1,0:T(8,128)(2,1)S(1)}, bf16[192,512]{1,0:T(8,128)(2,1)S(1)}, u32[]{:S(2)}, u32[]{:S(2)}) collective-permute-start(bf16[192,512]{1,0:T(8,128)(2,1)S(1)} %get-tuple-element.53.refs_0_), channel_id=1, source_target_pairs={{0,16},{16,0},{1,17},{17,1},{2,18},{18,2},{3,19},{19,3},{4,20},{20... | collective-permute-start | bytes 589832 | tf_op jit(solution)/shard_map/ppermute | solution.py:140
  34.5 9.2 %collective-permute-start.4 = (bf16[192,512]{1,0:T(8,128)(2,1)}, bf16[192,512]{1,0:T(8,128)(2,1)S(1)}, u32[]{:S(2)}, u32[]{:S(2)}) collective-permute-start(bf16[192,512]{1,0:T(8,128)(2,1)} %get-tuple-element.52), channel_id=1, source_target_pairs={{0,12},{4,8},{8,4},{12,0},{1,13},{5,9},{9,5},{13,1},{2,14},{6,10},... | collective-permute-start | bytes 589832 | tf_op jit(solution)/shard_map/ppermute | solution.py:140
  36.1 1.0 copy-start.3
  43.7 7.3 %collective-permute-start.8 = (bf16[3,192,384]{2,1,0:T(8,128)(2,1)S(1)}, bf16[3,192,384]{2,1,0:T(8,128)(2,1)S(1)}, u32[]{:S(2)}, u32[]{:S(2)}) collective-permute-start(bf16[3,192,384]{2,1,0:T(8,128)(2,1)S(1)} %collective-permute-done.6.far), channel_id=1, source_target_pairs={{0,1},{1,0},{2,3},{3,2},{4,5},{5,4},{6,7},{7,6},{8,9},{9,8},{10,11... | collective-permute-start | bytes 1327112 | tf_op jit(solution)/shard_map/ppermute | solution.py:140
  43.7 7.3 %collective-permute-start.9 = (bf16[192,512]{1,0:T(8,128)(2,1)S(1)}, bf16[192,512]{1,0:T(8,128)(2,1)S(1)}, u32[]{:S(2)}, u32[]{:S(2)}) collective-permute-start(bf16[192,512]{1,0:T(8,128)(2,1)S(1)} %collective-permute-done.4.refs_2_), channel_id=1, source_target_pairs={{0,16},{16,0},{1,17},{17,1},{2,18},{18,2},{3,19},{19,3},{4,20},{20... | collective-permute-start | bytes 589832 | tf_op jit(solution)/shard_map/ppermute | solution.py:140
  44.3 9.3 %collective-permute-start.12 = (bf16[2,128,384]{2,1,0:T(8,128)(2,1)S(1)}, bf16[2,128,384]{2,1,0:T(8,128)(2,1)S(1)}, u32[]{:S(2)}, u32[]{:S(2)}) collective-permute-start(bf16[2,128,384]{2,1,0:T(8,128)(2,1)S(1)} %get-tuple-element.64), channel_id=1, source_target_pairs={{0,0},{1,9},{2,14},{3,7},{4,4},{5,13},{6,2},{7,11},{8,8},{9,1},{10... | collective-permute-start | bytes 589832 | tf_op jit(solution)/shard_map/ppermute | solution.py:518
  44.9 15.8 %collective-permute-start.14 = (bf16[2,256,384]{2,1,0:T(8,128)(2,1)S(1)}, bf16[2,256,384]{2,1,0:T(8,128)(2,1)S(1)}, u32[]{:S(2)}, u32[]{:S(2)}) collective-permute-start(bf16[2,256,384]{2,1,0:T(8,128)(2,1)S(1)} %get-tuple-element.65), channel_id=1, source_target_pairs={{0,9},{1,0},{2,7},{3,14},{4,13},{5,4},{6,11},{7,2},{8,1},{9,8},{10... | collective-permute-start | bytes 1179656 | tf_op jit(solution)/shard_map/ppermute | solution.py:518
  51.0 14.4 %copy-start.4 = (bf16[192,384]{1,0:T(8,128)(2,1)S(1)}, bf16[192,384]{1,0:T(8,128)(2,1)}, u32[]{:S(2)}) copy-start(bf16[192,384]{1,0:T(8,128)(2,1)} %get-tuple-element.45.residual) | copy-start | bytes 442372
  52.9 34.4 %copy-start.7 = (f32[1536]{0:T(1024)S(1)}, f32[1536]{0:T(1024)}, u32[]{:S(2)}) copy-start(f32[1536]{0:T(1024)} %param.17) | copy-start | bytes 18436
  52.9 35.7 %copy-start = (bf16[1536,576]{0,1:T(8,128)(2,1)S(1)}, bf16[1536,576]{0,1:T(8,128)(2,1)}, u32[]{:S(2)}) copy-start(bf16[1536,576]{0,1:T(8,128)(2,1)} %param.18) | copy-start | bytes 5308420
  53.0 10.7 %collective-permute-start.10 = (bf16[768,256]{1,0:T(8,128)(2,1)S(1)}, bf16[768,256]{1,0:T(8,128)(2,1)S(1)}, u32[]{:S(2)}, u32[]{:S(2)}) collective-permute-start(bf16[768,256]{1,0:T(8,128)(2,1)S(1)} %shard_map.105.own), channel_id=1, source_target_pairs={{0,2},{1,3},{2,0},{3,1},{4,6},{5,7},{6,4},{7,5},{8,10},{9,11},{10,... | collective-permute-start | bytes 1179656 | tf_op jit(solution)/shard_map/ppermute | solution.py:140
  53.6 7.2 %collective-permute-start.13 = (bf16[2,128,384]{2,1,0:T(8,128)(2,1)S(1)}, bf16[2,128,384]{2,1,0:T(8,128)(2,1)S(1)}, u32[]{:S(2)}, u32[]{:S(2)}) collective-permute-start(bf16[2,128,384]{2,1,0:T(8,128)(2,1)S(1)} %collective-permute-done.12.even), channel_id=1, source_target_pairs={{0,16},{16,0},{1,17},{17,1},{2,18},{18,2},{3,19},{19,3},{4,20},{20... | collective-permute-start | bytes 589832 | tf_op jit(solution)/shard_map/ppermute | solution.py:140
  54.9 9.1 %collective-permute-start.11 = (bf16[768,256]{1,0:T(8,128)(2,1)S(1)}, bf16[768,256]{1,0:T(8,128)(2,1)S(1)}, u32[]{:S(2)}, u32[]{:S(2)}) collective-permute-start(bf16[768,256]{1,0:T(8,128)(2,1)S(1)} %shard_map.105.own), channel_id=1, source_target_pairs={{0,1},{1,0},{2,3},{3,2},{4,5},{5,4},{6,7},{7,6},{8,9},{9,8},{10,11... | collective-permute-start | bytes 1179656 | tf_op jit(solution)/shard_map/ppermute | solution.py:140
  63.7 1.7 %collective-permute-start.15 = (bf16[768,256]{1,0:T(8,128)(2,1)S(1)}, bf16[768,256]{1,0:T(8,128)(2,1)S(1)}, u32[]{:S(2)}, u32[]{:S(2)}) collective-permute-start(bf16[768,256]{1,0:T(8,128)(2,1)S(1)} %collective-permute-done.10.far), channel_id=1, source_target_pairs={{0,1},{1,0},{2,3},{3,2},{4,5},{5,4},{6,7},{7,6},{8,9},{9,8},{10,11... | collective-permute-start | bytes 1179656 | tf_op jit(solution)/shard_map/ppermute | solution.py:140
  66.4 10.0 %collective-permute-start.16 = (bf16[192,384]{1,0:T(8,128)(2,1)S(1)}, bf16[192,384]{1,0:T(8,128)(2,1)S(1)}, u32[]{:S(2)}, u32[]{:S(2)}) collective-permute-start(bf16[192,384]{1,0:T(8,128)(2,1)S(1)} %get-tuple-element.68), channel_id=1, source_target_pairs={{0,9},{1,8},{2,11},{3,10},{4,13},{5,12},{6,15},{7,14},{8,1},{9,0},... | collective-permute-start | bytes 442376 | tf_op jit(solution)/shard_map/ppermute | solution.py:542
  69.3 8.6 %collective-permute-start.17 = (bf16[192,384]{1,0:T(8,128)(2,1)S(1)}, bf16[192,384]{1,0:T(8,128)(2,1)S(1)}, u32[]{:S(2)}, u32[]{:S(2)}) collective-permute-start(bf16[192,384]{1,0:T(8,128)(2,1)S(1)} %get-tuple-element.69), channel_id=1, source_target_pairs={{0,7},{1,6},{2,4},{3,5},{4,2},{5,3},{6,1},{7,0},{8,15},{9,14},{10,... | collective-permute-start | bytes 442376 | tf_op jit(solution)/shard_map/ppermute | solution.py:542
  69.3 12.1 %collective-permute-start.18 = (bf16[192,384]{1,0:T(8,128)(2,1)S(1)}, bf16[192,384]{1,0:T(8,128)(2,1)S(1)}, u32[]{:S(2)}, u32[]{:S(2)}) collective-permute-start(bf16[192,384]{1,0:T(8,128)(2,1)S(1)} %get-tuple-element.70), channel_id=1, source_target_pairs={{0,14},{1,15},{2,13},{3,12},{4,11},{5,10},{6,8},{7,9},{8,6},{9,7},... | collective-permute-start | bytes 442376 | tf_op jit(solution)/shard_map/ppermute | solution.py:542
  81.4 5.9 %collective-permute-start.19 = (bf16[192,384]{1,0:T(8,128)(2,1)S(1)}, bf16[192,384]{1,0:T(8,128)(2,1)S(1)}, u32[]{:S(2)}, u32[]{:S(2)}) collective-permute-start(bf16[192,384]{1,0:T(8,128)(2,1)S(1)} %shard_map.107.own), channel_id=1, source_target_pairs={{0,2},{1,3},{2,0},{3,1},{4,6},{5,7},{6,4},{7,5},{8,10},{9,11},{10,... | collective-permute-start | bytes 442376 | tf_op jit(solution)/shard_map/ppermute | solution.py:140
  82.7 4.7 %collective-permute-start.20 = (bf16[192,384]{1,0:T(8,128)(2,1)S(1)}, bf16[192,384]{1,0:T(8,128)(2,1)S(1)}, u32[]{:S(2)}, u32[]{:S(2)}) collective-permute-start(bf16[192,384]{1,0:T(8,128)(2,1)S(1)} %shard_map.107.own), channel_id=1, source_target_pairs={{0,1},{1,0},{2,3},{3,2},{4,5},{5,4},{6,7},{7,6},{8,9},{9,8},{10,11... | collective-permute-start | bytes 442376 | tf_op jit(solution)/shard_map/ppermute | solution.py:140
  87.3 1.4 %collective-permute-start.21 = (bf16[192,384]{1,0:T(8,128)(2,1)S(1)}, bf16[192,384]{1,0:T(8,128)(2,1)S(1)}, u32[]{:S(2)}, u32[]{:S(2)}) collective-permute-start(bf16[192,384]{1,0:T(8,128)(2,1)S(1)} %collective-permute-done.19.far), channel_id=1, source_target_pairs={{0,1},{1,0},{2,3},{3,2},{4,5},{5,4},{6,7},{7,6},{8,9},{9,8},{10,11... | collective-permute-start | bytes 442376 | tf_op jit(solution)/shard_map/ppermute | solution.py:140
  89.9 8.2 %collective-permute-start.22 = (bf16[64,768]{1,0:T(8,128)(2,1)S(1)}, bf16[64,768]{1,0:T(8,128)(2,1)S(1)}, u32[]{:S(2)}, u32[]{:S(2)}) collective-permute-start(bf16[64,768]{1,0:T(8,128)(2,1)S(1)} %get-tuple-element.71), channel_id=1, source_target_pairs={{0,8},{4,12},{8,0},{12,4},{1,9},{5,13},{9,1},{13,5},{2,10},{6,14},... | collective-permute-start | bytes 294920 | tf_op jit(solution)/shard_map/ppermute | solution.py:140
  92.6 5.5 %collective-permute-start.23 = (bf16[64,768]{1,0:T(8,128)(2,1)S(1)}, bf16[64,768]{1,0:T(8,128)(2,1)S(1)}, u32[]{:S(2)}, u32[]{:S(2)}) collective-permute-start(bf16[64,768]{1,0:T(8,128)(2,1)S(1)} %get-tuple-element.72), channel_id=1, source_target_pairs={{0,4},{4,0},{8,12},{12,8},{1,5},{5,1},{9,13},{13,9},{2,6},{6,2},{1... | collective-permute-start | bytes 294920 | tf_op jit(solution)/shard_map/ppermute | solution.py:140
  93.0 8.7 %collective-permute-start.24 = (bf16[64,768]{1,0:T(8,128)(2,1)S(1)}, bf16[64,768]{1,0:T(8,128)(2,1)S(1)}, u32[]{:S(2)}, u32[]{:S(2)}) collective-permute-start(bf16[64,768]{1,0:T(8,128)(2,1)S(1)} %get-tuple-element.73), channel_id=1, source_target_pairs={{0,12},{4,8},{8,4},{12,0},{1,13},{5,9},{9,5},{13,1},{2,14},{6,10},... | collective-permute-start | bytes 294920 | tf_op jit(solution)/shard_map/ppermute | solution.py:140

commit v14 on v13

--- a/solution.py
+++ b/solution.py
@@ -11,7 +11,7 @@
 HEAD_WIDTH = 64
 DILATION_STEP = 8
 ENCODER_SLOTS = 256
-ORDER = (2, 1, 3, 0)
+ORDER = (1, 2, 3, 0)
 
 
 epsilon = 1e-05
@@ -541,7 +541,7 @@
                 perm.append((s * mp_size + m, owner * mp_size + holder[(s + holder[m] - owner) % count]))
         return lax.ppermute(part, ("seq", "mp"), perm)
 
-    arrived = [to_owner(sums[d], d) for d in (2, 1, 3)]
+    arrived = [to_owner(sums[d], d) for d in (1, 2, 3)]
     embedded_cols = call(
         sum_body, [((tile_rows, features), bf16)], (sums[0], *arrived)
     )[0]

time: 104 us -> 108 us (1.038)
  waiting for transfers between devices: 51.6 us -> 53.8 us
  starting transfers between devices: 36.6 us -> 38.3 us
    ppermute x20, starting transfers between devices: 26.6 us -> 28.3 us  [swap(): return lax.ppermute(array, axis, [(i, i ^ distance) for i in range(size)])]
    ppermute x3, waiting for transfers between devices: 9.64 us -> 10.8 us  [to_owner(): return lax.ppermute(part, ('seq', 'mp'), perm)]
where the time goes in v14:
time: 108 us
  waiting for transfers between devices  53.8 us (50%)
  starting transfers between devices  38.3 us (35%)
  Pallas kernels  13.6 us (13%)
  local copies, waits for them, and re-layouts  1.12 us (1%)
    ppermute x20, waiting for transfers between devices, swap(): return lax.ppermute(array, axis, [(i, i ^ distance) for i in range(size)])  43 us
    ppermute x20, starting transfers between devices, swap(): return lax.ppermute(array, axis, [(i, i ^ distance) for i in range(size)])  28.3 us
    pallas_call x10, Pallas kernels, call(): pl.pallas_call(body, out_shape=[jax.ShapeDtypeStruct(shape, kind) for sha...  13.6 us
    ppermute x3, waiting for transfers between devices, to_owner(): return lax.ppermute(part, ('seq', 'mp'), perm)  10.8 us
    ppermute x3, starting transfers between devices, to_owner(): return lax.ppermute(part, ('seq', 'mp'), perm)  5.23 us
    ppermute x2, starting transfers between devices, split_hidden_plan(): parts.append(lax.ppermute(down_send[j], ('seq', 'mp'), perm))  4.77 us
  transfers between devices with their start and end apart: 25, of which 13 were waited for; matrix products, arithmetic and copies ran while one was open for 0% of the time, Pallas kernels for 6%

profile of v14, /device:TPU:0, one launch (start us, length us, event | category | flops | bytes accessed | tf_op | source)
XLA Modules:
  0.0 107.7 jit_solution(9885629153014813382)
XLA Ops:
  0.0 3.0 %shard_map.100 = (bf16[192,1408]{1,0:T(8,128)(2,1)}, bf16[192,896]{1,0:T(8,128)(2,1)}, bf16[192,384]{1,0:T(8,128)(2,1)}) custom-call(bf16[192,1536]{1,0:T(8,128)(2,1)} %tiles.3, bf16[384,1024]{1,0:T(8,128)(2,1)} %w_gate.3, bf16[384,1024]{1,0:T(8,128)(2,1)} %w_up.3, f32[1536]{0:T(1024)} %gain.3), custom_call_target="tpu_custom_call" | custom-call | tf_op jit(solution)/shard_map/pallas_call | solution.py:152
  3.0 0.0 copy-start.5
  3.1 3.1 %collective-permute-start.2 = (bf16[192,1408]{1,0:T(8,128)(2,1)}, bf16[192,1408]{1,0:T(8,128)(2,1)S(1)}, u32[]{:S(2)}, u32[]{:S(2)}) collective-permute-start(bf16[192,1408]{1,0:T(8,128)(2,1)} %get-tuple-element.42), channel_id=1, source_target_pairs={{0,4},{4,0},{8,12},{12,8},{1,5},{5,1},{9,13},{13,9},{2,6},{6,2},{1... | collective-permute-start | bytes 1622024 | tf_op jit(solution)/shard_map/ppermute | solution.py:140
  6.2 2.6 %collective-permute-start = (bf16[192,896]{1,0:T(8,128)(2,1)}, bf16[192,896]{1,0:T(8,128)(2,1)S(1)}, u32[]{:S(2)}, u32[]{:S(2)}) collective-permute-start(bf16[192,896]{1,0:T(8,128)(2,1)} %get-tuple-element.40), channel_id=1, source_target_pairs={{0,8},{4,12},{8,0},{12,4},{1,9},{5,13},{9,1},{13,5},{2,10},{6,14},... | collective-permute-start | bytes 1032200 | tf_op jit(solution)/shard_map/ppermute | solution.py:140
  8.7 3.4 %shard_map.101 = (bf16[192,512]{1,0:T(8,128)(2,1)}, bf16[384,512]{1,0:T(8,128)(2,1)}, bf16[384,384]{1,0:T(8,128)(2,1)}, bf16[384,384]{1,0:T(8,128)(2,1)}, bf16[1...) custom-call(bf16[192,1536]{1,0:T(8,128)(2,1)} %tiles.3, bf16[384,1024]{1,0:T(8,128)(2,1)} %w_gate.3, ...), custom_call_target="tpu_custom_call" | custom-call | tf_op jit(solution)/shard_map/pallas_call | solution.py:152
  12.2 1.6 %collective-permute-start.3 = (bf16[384,384]{1,0:T(8,128)(2,1)}, bf16[384,384]{1,0:T(8,128)(2,1)S(1)}, u32[]{:S(2)}, u32[]{:S(2)}) collective-permute-start(bf16[384,384]{1,0:T(8,128)(2,1)} %get-tuple-element.43), channel_id=1, source_target_pairs={{0,2},{1,3},{2,0},{3,1},{4,6},{5,7},{6,4},{7,5},{8,10},{9,11},{10,... | collective-permute-start | bytes 884744 | tf_op jit(solution)/shard_map/ppermute | solution.py:140
  13.7 0.2 collective-permute-start.1
  14.0 0.1 copy.11.dest
  14.8 0.7 shard_map.102.routes
  15.4 15.9 %collective-permute-done.1.third = bf16[192,384]{1,0:T(8,128)(2,1)S(1)} collective-permute-done((bf16[192,384]{1,0:T(8,128)(2,1)S(1)}, bf16[192,384]{1,0:T(8,128)(2,1)S(1)}, u32[]{:S(2)}, u32[]{:S(2)}) %collective-permute-start.1) | collective-permute-done | bytes 147488 | tf_op jit(solution)/shard_map/ppermute | solution.py:140
  31.4 0.1 shard_map.103
  31.4 1.6 %collective-permute-start.6 = (bf16[3,192,384]{2,1,0:T(8,128)(2,1)S(1)}, bf16[3,192,384]{2,1,0:T(8,128)(2,1)S(1)}, u32[]{:S(2)}, u32[]{:S(2)}) collective-permute-start(bf16[3,192,384]{2,1,0:T(8,128)(2,1)S(1)} %get-tuple-element.50.own), channel_id=1, source_target_pairs={{0,2},{1,3},{2,0},{3,1},{4,6},{5,7},{6,4},{7,5},{8,10},{9,11},{10,... | collective-permute-start | bytes 1327112 | tf_op jit(solution)/shard_map/ppermute | solution.py:140
  33.0 1.5 %collective-permute-start.5 = (bf16[192,512]{1,0:T(8,128)(2,1)S(1)}, bf16[192,512]{1,0:T(8,128)(2,1)S(1)}, u32[]{:S(2)}, u32[]{:S(2)}) collective-permute-start(bf16[192,512]{1,0:T(8,128)(2,1)S(1)} %get-tuple-element.53.refs_0_), channel_id=1, source_target_pairs={{0,16},{16,0},{1,17},{17,1},{2,18},{18,2},{3,19},{19,3},{4,20},{20... | collective-permute-start | bytes 589832 | tf_op jit(solution)/shard_map/ppermute | solution.py:140
  34.5 1.6 %collective-permute-start.4 = (bf16[192,512]{1,0:T(8,128)(2,1)}, bf16[192,512]{1,0:T(8,128)(2,1)S(1)}, u32[]{:S(2)}, u32[]{:S(2)}) collective-permute-start(bf16[192,512]{1,0:T(8,128)(2,1)} %get-tuple-element.52), channel_id=1, source_target_pairs={{0,12},{4,8},{8,4},{12,0},{1,13},{5,9},{9,5},{13,1},{2,14},{6,10},... | collective-permute-start | bytes 589832 | tf_op jit(solution)/shard_map/ppermute | solution.py:140
  36.1 1.0 copy-done.3
  37.0 0.1 shard_map.104
  37.1 3.2 %collective-permute-done.5.refs_1_ = bf16[192,512]{1,0:T(8,128)(2,1)S(1)} collective-permute-done((bf16[192,512]{1,0:T(8,128)(2,1)S(1)}, bf16[192,512]{1,0:T(8,128)(2,1)S(1)}, u32[]{:S(2)}, u32[]{:S(2)}) %collective-permute-start.5) | collective-permute-done | bytes 196640 | tf_op jit(solution)/shard_map/ppermute | solution.py:140
  40.3 3.4 %collective-permute-done.4.refs_2_ = bf16[192,512]{1,0:T(8,128)(2,1)S(1)} collective-permute-done((bf16[192,512]{1,0:T(8,128)(2,1)}, bf16[192,512]{1,0:T(8,128)(2,1)S(1)}, u32[]{:S(2)}, u32[]{:S(2)}) %collective-permute-start.4) | collective-permute-done | bytes 196640 | tf_op jit(solution)/shard_map/ppermute | solution.py:140
  43.7 0.6 collective-permute-start.9
  44.3 0.7 collective-permute-start.12
  44.9 4.1 %collective-permute-start.14 = (bf16[2,256,384]{2,1,0:T(8,128)(2,1)S(1)}, bf16[2,256,384]{2,1,0:T(8,128)(2,1)S(1)}, u32[]{:S(2)}, u32[]{:S(2)}) collective-permute-start(bf16[2,256,384]{2,1,0:T(8,128)(2,1)S(1)} %get-tuple-element.65), channel_id=1, source_target_pairs={{0,9},{1,0},{2,7},{3,14},{4,13},{5,4},{6,11},{7,2},{8,1},{9,8},{10... | collective-permute-start | bytes 1179656 | tf_op jit(solution)/shard_map/ppermute | solution.py:518
  49.0 2.0 %collective-permute-done.9.refs_3_ = bf16[192,512]{1,0:T(8,128)(2,1)S(1)} collective-permute-done((bf16[192,512]{1,0:T(8,128)(2,1)S(1)}, bf16[192,512]{1,0:T(8,128)(2,1)S(1)}, u32[]{:S(2)}, u32[]{:S(2)}) %collective-permute-start.9) | collective-permute-done | bytes 196640 | tf_op jit(solution)/shard_map/ppermute | solution.py:140
  51.0 1.9 %shard_map.105.own = bf16[768,256]{1,0:T(8,128)(2,1)S(1)} custom-call(bf16[192,1536]{1,0:T(8,128)(2,1)S(1)} %copy-done.1, bf16[3,192,384]{2,1,0:T(8,128)(2,1)S(1)} %get-tuple-element.50.own, bf16[3,192,384]{2,1,0:T(8,128)(2,1)S(1)} %collective-permute-done.6.far, bf16[3,192,384]{2,1,0:T(8,128)(2,1)S(1)} %collective-permute-done.7.near, ...), custom_call_target="tpu_custom_call" | custom-call | tf_op jit(solution)/shard_map/pallas_call | solution.py:152
  52.9 0.0 copy-start.7
  53.0 0.6 collective-permute-start.10
  53.6 1.3 %collective-permute-start.13 = (bf16[2,128,384]{2,1,0:T(8,128)(2,1)S(1)}, bf16[2,128,384]{2,1,0:T(8,128)(2,1)S(1)}, u32[]{:S(2)}, u32[]{:S(2)}) collective-permute-start(bf16[2,128,384]{2,1,0:T(8,128)(2,1)S(1)} %collective-permute-done.12.even), channel_id=1, source_target_pairs={{0,16},{16,0},{1,17},{17,1},{2,18},{18,2},{3,19},{19,3},{4,20},{20... | collective-permute-start | bytes 589832 | tf_op jit(solution)/shard_map/ppermute | solution.py:140
  54.9 5.8 %collective-permute-start.11 = (bf16[768,256]{1,0:T(8,128)(2,1)S(1)}, bf16[768,256]{1,0:T(8,128)(2,1)S(1)}, u32[]{:S(2)}, u32[]{:S(2)}) collective-permute-start(bf16[768,256]{1,0:T(8,128)(2,1)S(1)} %shard_map.105.own), channel_id=1, source_target_pairs={{0,1},{1,0},{2,3},{3,2},{4,5},{5,4},{6,7},{7,6},{8,9},{9,8},{10,11... | collective-permute-start | bytes 1179656 | tf_op jit(solution)/shard_map/ppermute | solution.py:140
  60.7 3.0 %collective-permute-done.10.far = bf16[768,256]{1,0:T(8,128)(2,1)S(1)} collective-permute-done((bf16[768,256]{1,0:T(8,128)(2,1)S(1)}, bf16[768,256]{1,0:T(8,128)(2,1)S(1)}, u32[]{:S(2)}, u32[]{:S(2)}) %collective-permute-start.10) | collective-permute-done | bytes 393248 | tf_op jit(solution)/shard_map/ppermute | solution.py:140
  63.7 0.3 collective-permute-start.15
  64.0 1.4 %collective-permute-done.15.near_far = bf16[768,256]{1,0:T(8,128)(2,1)S(1)} collective-permute-done((bf16[768,256]{1,0:T(8,128)(2,1)S(1)}, bf16[768,256]{1,0:T(8,128)(2,1)S(1)}, u32[]{:S(2)}, u32[]{:S(2)}) %collective-permute-start.15) | collective-permute-done | bytes 393248 | tf_op jit(solution)/shard_map/ppermute | solution.py:140
  65.4 1.0 shard_map.106
  66.4 1.6 %collective-permute-start.16 = (bf16[192,384]{1,0:T(8,128)(2,1)S(1)}, bf16[192,384]{1,0:T(8,128)(2,1)S(1)}, u32[]{:S(2)}, u32[]{:S(2)}) collective-permute-start(bf16[192,384]{1,0:T(8,128)(2,1)S(1)} %get-tuple-element.68), channel_id=1, source_target_pairs={{0,7},{1,6},{2,4},{3,5},{4,2},{5,3},{6,1},{7,0},{8,15},{9,14},{10,... | collective-permute-start | bytes 442376 | tf_op jit(solution)/shard_map/ppermute | solution.py:542
  68.0 1.3 %collective-permute-start.17 = (bf16[192,384]{1,0:T(8,128)(2,1)S(1)}, bf16[192,384]{1,0:T(8,128)(2,1)S(1)}, u32[]{:S(2)}, u32[]{:S(2)}) collective-permute-start(bf16[192,384]{1,0:T(8,128)(2,1)S(1)} %get-tuple-element.69), channel_id=1, source_target_pairs={{0,9},{1,8},{2,11},{3,10},{4,13},{5,12},{6,15},{7,14},{8,1},{9,0},... | collective-permute-start | bytes 442376 | tf_op jit(solution)/shard_map/ppermute | solution.py:542
  69.3 2.3 %collective-permute-start.18 = (bf16[192,384]{1,0:T(8,128)(2,1)S(1)}, bf16[192,384]{1,0:T(8,128)(2,1)S(1)}, u32[]{:S(2)}, u32[]{:S(2)}) collective-permute-start(bf16[192,384]{1,0:T(8,128)(2,1)S(1)} %get-tuple-element.70), channel_id=1, source_target_pairs={{0,14},{1,15},{2,13},{3,12},{4,11},{5,10},{6,8},{7,9},{8,6},{9,7},... | collective-permute-start | bytes 442376 | tf_op jit(solution)/shard_map/ppermute | solution.py:542
  71.6 1.4 %collective-permute-done.16.refs_0_ = bf16[192,384]{1,0:T(8,128)(2,1)S(1)} collective-permute-done((bf16[192,384]{1,0:T(8,128)(2,1)S(1)}, bf16[192,384]{1,0:T(8,128)(2,1)S(1)}, u32[]{:S(2)}, u32[]{:S(2)}) %collective-permute-start.16) | collective-permute-done | bytes 147488 | tf_op jit(solution)/shard_map/ppermute | solution.py:542
  73.1 2.4 %collective-permute-done.17.refs_1_ = bf16[192,384]{1,0:T(8,128)(2,1)S(1)} collective-permute-done((bf16[192,384]{1,0:T(8,128)(2,1)S(1)}, bf16[192,384]{1,0:T(8,128)(2,1)S(1)}, u32[]{:S(2)}, u32[]{:S(2)}) %collective-permute-start.17) | collective-permute-done | bytes 147488 | tf_op jit(solution)/shard_map/ppermute | solution.py:542
  75.5 6.9 %collective-permute-done.18.refs_2_ = bf16[192,384]{1,0:T(8,128)(2,1)S(1)} collective-permute-done((bf16[192,384]{1,0:T(8,128)(2,1)S(1)}, bf16[192,384]{1,0:T(8,128)(2,1)S(1)}, u32[]{:S(2)}, u32[]{:S(2)}) %collective-permute-start.18) | collective-permute-done | bytes 147488 | tf_op jit(solution)/shard_map/ppermute | solution.py:542
  82.4 0.1 shard_map.107.own
  82.5 0.8 collective-permute-start.19
  83.3 4.7 %collective-permute-done.19.far = bf16[192,384]{1,0:T(8,128)(2,1)S(1)} collective-permute-done((bf16[192,384]{1,0:T(8,128)(2,1)S(1)}, bf16[192,384]{1,0:T(8,128)(2,1)S(1)}, u32[]{:S(2)}, u32[]{:S(2)}) %collective-permute-start.19) | collective-permute-done | bytes 147488 | tf_op jit(solution)/shard_map/ppermute | solution.py:140
  88.1 1.3 %collective-permute-done.21.near_far = bf16[192,384]{1,0:T(8,128)(2,1)S(1)} collective-permute-done((bf16[192,384]{1,0:T(8,128)(2,1)S(1)}, bf16[192,384]{1,0:T(8,128)(2,1)S(1)}, u32[]{:S(2)}, u32[]{:S(2)}) %collective-permute-start.21) | collective-permute-done | bytes 147488 | tf_op jit(solution)/shard_map/ppermute | solution.py:140
  89.4 1.3 %shard_map.108 = (bf16[64,768]{1,0:T(8,128)(2,1)S(1)}, bf16[64,768]{1,0:T(8,128)(2,1)S(1)}, bf16[64,768]{1,0:T(8,128)(2,1)S(1)}, bf16[64,768]{1,0:T(8,128)(2,1)S(1)}) custom-call(f32[1,1536]{1,0:T(1,128)S(1)} %broadcast_in_dim.3.gain, bf16[352,192]{1,0:T(8,128)(2,1)S(1)} %shard_map.102.routes, bf16[576,1536]{1,0:T(8,128)(2,1)S(1)} %bitcast.3, ...), custom_call_target="tpu_custom_call" | custom-call | tf_op jit(solution)/shard_map/pallas_call | solution.py:152
  90.7 4.3 %collective-permute-start.22 = (bf16[64,768]{1,0:T(8,128)(2,1)S(1)}, bf16[64,768]{1,0:T(8,128)(2,1)S(1)}, u32[]{:S(2)}, u32[]{:S(2)}) collective-permute-start(bf16[64,768]{1,0:T(8,128)(2,1)S(1)} %get-tuple-element.71), channel_id=1, source_target_pairs={{0,4},{4,0},{8,12},{12,8},{1,5},{5,1},{9,13},{13,9},{2,6},{6,2},{1... | collective-permute-start | bytes 294920 | tf_op jit(solution)/shard_map/ppermute | solution.py:140
  95.0 0.6 collective-permute-start.23
  95.5 1.9 %collective-permute-start.24 = (bf16[64,768]{1,0:T(8,128)(2,1)S(1)}, bf16[64,768]{1,0:T(8,128)(2,1)S(1)}, u32[]{:S(2)}, u32[]{:S(2)}) collective-permute-start(bf16[64,768]{1,0:T(8,128)(2,1)S(1)} %get-tuple-element.73), channel_id=1, source_target_pairs={{0,12},{4,8},{8,4},{12,0},{1,13},{5,9},{9,5},{13,1},{2,14},{6,10},... | collective-permute-start | bytes 294920 | tf_op jit(solution)/shard_map/ppermute | solution.py:140
  97.4 0.7 collective-permute-done.22.refs_0_
  98.1 7.4 %collective-permute-done.23.refs_1_ = bf16[64,768]{1,0:T(8,128)(2,1)S(1)} collective-permute-done((bf16[64,768]{1,0:T(8,128)(2,1)S(1)}, bf16[64,768]{1,0:T(8,128)(2,1)S(1)}, u32[]{:S(2)}, u32[]{:S(2)}) %collective-permute-start.23) | collective-permute-done | bytes 98336 | tf_op jit(solution)/shard_map/ppermute | solution.py:140
  105.5 2.2 %shard_map.109 = bf16[192,256]{1,0:T(8,128)(2,1)} custom-call(s32[3]{0:T(128)S(1)} %copy-done.6, bf16[64,768]{1,0:T(8,128)(2,1)S(1)} %collective-permute-done.22.refs_0_, bf16[64,768]{1,0:T(8,128)(2,1)S(1)} %collective-permute-done.23.refs_1_, bf16[64,768]{1,0:T(8,128)(2,1)S(1)} %collective-permute-done.24.refs_2_, bf16[64,768]{1,0:T(8,128)(2,1)S(1)} %get-tuple-element.74.refs_3_), custom_call_target="tpu_custom_call" | custom-call | tf_op jit(solution)/shard_map/pallas_call | solution.py:152
  (32 shorter events, 0.1 us)
Async XLA Ops:
  3.0 10.7 %copy-start.8 = (bf16[192,384]{1,0:T(8,128)(2,1)S(1)}, bf16[192,384]{1,0:T(8,128)(2,1)}, u32[]{:S(2)}) copy-start(bf16[192,384]{1,0:T(8,128)(2,1)} %get-tuple-element.41) | copy-start | bytes 442372
  3.0 10.9 %copy-start.5 = (s32[192,1]{0,1:T(1,128)S(1)}, s32[192,1]{0,1:T(1,128)}, u32[]{:S(2)}) copy-start(s32[192,1]{0,1:T(1,128)} %param.12) | copy-start | bytes 2308
  3.1 11.7 %copy-start.6 = (s32[3]{0:T(128)S(1)}, s32[3]{0:T(128)}, u32[]{:S(2)}) copy-start(s32[3]{0:T(128)} %offsets.3) | copy-start | bytes 40
  3.1 28.3 %collective-permute-start.2 = (bf16[192,1408]{1,0:T(8,128)(2,1)}, bf16[192,1408]{1,0:T(8,128)(2,1)S(1)}, u32[]{:S(2)}, u32[]{:S(2)}) collective-permute-start(bf16[192,1408]{1,0:T(8,128)(2,1)} %get-tuple-element.42), channel_id=1, source_target_pairs={{0,4},{4,0},{8,12},{12,8},{1,5},{5,1},{9,13},{13,9},{2,6},{6,2},{1... | collective-permute-start | bytes 1622024 | tf_op jit(solution)/shard_map/ppermute | solution.py:140
  6.2 25.2 %collective-permute-start = (bf16[192,896]{1,0:T(8,128)(2,1)}, bf16[192,896]{1,0:T(8,128)(2,1)S(1)}, u32[]{:S(2)}, u32[]{:S(2)}) collective-permute-start(bf16[192,896]{1,0:T(8,128)(2,1)} %get-tuple-element.40), channel_id=1, source_target_pairs={{0,8},{4,12},{8,0},{12,4},{1,9},{5,13},{9,1},{13,5},{2,10},{6,14},... | collective-permute-start | bytes 1032200 | tf_op jit(solution)/shard_map/ppermute | solution.py:140
  12.2 38.8 %copy-start.1 = (bf16[192,1536]{1,0:T(8,128)(2,1)S(1)}, bf16[192,1536]{1,0:T(8,128)(2,1)}, u32[]{:S(2)}) copy-start(bf16[192,1536]{1,0:T(8,128)(2,1)} %get-tuple-element.46.normed) | copy-start | bytes 1769476
  12.2 38.8 %copy-start.2 = (bf16[384,512]{1,0:T(8,128)(2,1)S(1)}, bf16[384,512]{1,0:T(8,128)(2,1)}, u32[]{:S(2)}) copy-start(bf16[384,512]{1,0:T(8,128)(2,1)} %get-tuple-element.61.kept) | copy-start | bytes 1179652
  12.2 19.2 %collective-permute-start.3 = (bf16[384,384]{1,0:T(8,128)(2,1)}, bf16[384,384]{1,0:T(8,128)(2,1)S(1)}, u32[]{:S(2)}, u32[]{:S(2)}) collective-permute-start(bf16[384,384]{1,0:T(8,128)(2,1)} %get-tuple-element.43), channel_id=1, source_target_pairs={{0,2},{1,3},{2,0},{3,1},{4,6},{5,7},{6,4},{7,5},{8,10},{9,11},{10,... | collective-permute-start | bytes 884744 | tf_op jit(solution)/shard_map/ppermute | solution.py:140
  13.7 17.6 %collective-permute-start.1 = (bf16[192,384]{1,0:T(8,128)(2,1)S(1)}, bf16[192,384]{1,0:T(8,128)(2,1)S(1)}, u32[]{:S(2)}, u32[]{:S(2)}) collective-permute-start(bf16[192,384]{1,0:T(8,128)(2,1)S(1)} %copy-done.8), channel_id=1, source_target_pairs={{0,12},{4,8},{8,4},{12,0},{1,13},{5,9},{9,5},{13,1},{2,14},{6,10},... | collective-permute-start | bytes 442376 | tf_op jit(solution)/shard_map/ppermute | solution.py:140
  31.4 12.2 %collective-permute-start.6 = (bf16[3,192,384]{2,1,0:T(8,128)(2,1)S(1)}, bf16[3,192,384]{2,1,0:T(8,128)(2,1)S(1)}, u32[]{:S(2)}, u32[]{:S(2)}) collective-permute-start(bf16[3,192,384]{2,1,0:T(8,128)(2,1)S(1)} %get-tuple-element.50.own), channel_id=1, source_target_pairs={{0,2},{1,3},{2,0},{3,1},{4,6},{5,7},{6,4},{7,5},{8,10},{9,11},{10,... | collective-permute-start | bytes 1327112 | tf_op jit(solution)/shard_map/ppermute | solution.py:140
  33.0 10.7 %collective-permute-start.7 = (bf16[3,192,384]{2,1,0:T(8,128)(2,1)S(1)}, bf16[3,192,384]{2,1,0:T(8,128)(2,1)S(1)}, u32[]{:S(2)}, u32[]{:S(2)}) collective-permute-start(bf16[3,192,384]{2,1,0:T(8,128)(2,1)S(1)} %get-tuple-element.50.own), channel_id=1, source_target_pairs={{0,1},{1,0},{2,3},{3,2},{4,5},{5,4},{6,7},{7,6},{8,9},{9,8},{10,11... | collective-permute-start | bytes 1327112 | tf_op jit(solution)/shard_map/ppermute | solution.py:140
  33.0 7.3 %collective-permute-start.5 = (bf16[192,512]{1,0:T(8,128)(2,1)S(1)}, bf16[192,512]{1,0:T(8,128)(2,1)S(1)}, u32[]{:S(2)}, u32[]{:S(2)}) collective-permute-start(bf16[192,512]{1,0:T(8,128)(2,1)S(1)} %get-tuple-element.53.refs_0_), channel_id=1, source_target_pairs={{0,16},{16,0},{1,17},{17,1},{2,18},{18,2},{3,19},{19,3},{4,20},{20... | collective-permute-start | bytes 589832 | tf_op jit(solution)/shard_map/ppermute | solution.py:140
  34.5 9.2 %collective-permute-start.4 = (bf16[192,512]{1,0:T(8,128)(2,1)}, bf16[192,512]{1,0:T(8,128)(2,1)S(1)}, u32[]{:S(2)}, u32[]{:S(2)}) collective-permute-start(bf16[192,512]{1,0:T(8,128)(2,1)} %get-tuple-element.52), channel_id=1, source_target_pairs={{0,12},{4,8},{8,4},{12,0},{1,13},{5,9},{9,5},{13,1},{2,14},{6,10},... | collective-permute-start | bytes 589832 | tf_op jit(solution)/shard_map/ppermute | solution.py:140
  36.1 1.0 copy-start.3
  43.7 7.3 %collective-permute-start.8 = (bf16[3,192,384]{2,1,0:T(8,128)(2,1)S(1)}, bf16[3,192,384]{2,1,0:T(8,128)(2,1)S(1)}, u32[]{:S(2)}, u32[]{:S(2)}) collective-permute-start(bf16[3,192,384]{2,1,0:T(8,128)(2,1)S(1)} %collective-permute-done.6.far), channel_id=1, source_target_pairs={{0,1},{1,0},{2,3},{3,2},{4,5},{5,4},{6,7},{7,6},{8,9},{9,8},{10,11... | collective-permute-start | bytes 1327112 | tf_op jit(solution)/shard_map/ppermute | solution.py:140
  43.7 7.3 %collective-permute-start.9 = (bf16[192,512]{1,0:T(8,128)(2,1)S(1)}, bf16[192,512]{1,0:T(8,128)(2,1)S(1)}, u32[]{:S(2)}, u32[]{:S(2)}) collective-permute-start(bf16[192,512]{1,0:T(8,128)(2,1)S(1)} %collective-permute-done.4.refs_2_), channel_id=1, source_target_pairs={{0,16},{16,0},{1,17},{17,1},{2,18},{18,2},{3,19},{19,3},{4,20},{20... | collective-permute-start | bytes 589832 | tf_op jit(solution)/shard_map/ppermute | solution.py:140
  44.3 9.3 %collective-permute-start.12 = (bf16[2,128,384]{2,1,0:T(8,128)(2,1)S(1)}, bf16[2,128,384]{2,1,0:T(8,128)(2,1)S(1)}, u32[]{:S(2)}, u32[]{:S(2)}) collective-permute-start(bf16[2,128,384]{2,1,0:T(8,128)(2,1)S(1)} %get-tuple-element.64), channel_id=1, source_target_pairs={{0,0},{1,9},{2,14},{3,7},{4,4},{5,13},{6,2},{7,11},{8,8},{9,1},{10... | collective-permute-start | bytes 589832 | tf_op jit(solution)/shard_map/ppermute | solution.py:518
  44.9 15.8 %collective-permute-start.14 = (bf16[2,256,384]{2,1,0:T(8,128)(2,1)S(1)}, bf16[2,256,384]{2,1,0:T(8,128)(2,1)S(1)}, u32[]{:S(2)}, u32[]{:S(2)}) collective-permute-start(bf16[2,256,384]{2,1,0:T(8,128)(2,1)S(1)} %get-tuple-element.65), channel_id=1, source_target_pairs={{0,9},{1,0},{2,7},{3,14},{4,13},{5,4},{6,11},{7,2},{8,1},{9,8},{10... | collective-permute-start | bytes 1179656 | tf_op jit(solution)/shard_map/ppermute | solution.py:518
  51.0 14.4 %copy-start.4 = (bf16[192,384]{1,0:T(8,128)(2,1)S(1)}, bf16[192,384]{1,0:T(8,128)(2,1)}, u32[]{:S(2)}) copy-start(bf16[192,384]{1,0:T(8,128)(2,1)} %get-tuple-element.45.residual) | copy-start | bytes 442372
  52.9 35.1 %copy-start.7 = (f32[1536]{0:T(1024)S(1)}, f32[1536]{0:T(1024)}, u32[]{:S(2)}) copy-start(f32[1536]{0:T(1024)} %param.17) | copy-start | bytes 18436
  52.9 36.5 %copy-start = (bf16[1536,576]{0,1:T(8,128)(2,1)S(1)}, bf16[1536,576]{0,1:T(8,128)(2,1)}, u32[]{:S(2)}) copy-start(bf16[1536,576]{0,1:T(8,128)(2,1)} %param.18) | copy-start | bytes 5308420
  53.0 10.7 %collective-permute-start.10 = (bf16[768,256]{1,0:T(8,128)(2,1)S(1)}, bf16[768,256]{1,0:T(8,128)(2,1)S(1)}, u32[]{:S(2)}, u32[]{:S(2)}) collective-permute-start(bf16[768,256]{1,0:T(8,128)(2,1)S(1)} %shard_map.105.own), channel_id=1, source_target_pairs={{0,2},{1,3},{2,0},{3,1},{4,6},{5,7},{6,4},{7,5},{8,10},{9,11},{10,... | collective-permute-start | bytes 1179656 | tf_op jit(solution)/shard_map/ppermute | solution.py:140
  53.6 7.2 %collective-permute-start.13 = (bf16[2,128,384]{2,1,0:T(8,128)(2,1)S(1)}, bf16[2,128,384]{2,1,0:T(8,128)(2,1)S(1)}, u32[]{:S(2)}, u32[]{:S(2)}) collective-permute-start(bf16[2,128,384]{2,1,0:T(8,128)(2,1)S(1)} %collective-permute-done.12.even), channel_id=1, source_target_pairs={{0,16},{16,0},{1,17},{17,1},{2,18},{18,2},{3,19},{19,3},{4,20},{20... | collective-permute-start | bytes 589832 | tf_op jit(solution)/shard_map/ppermute | solution.py:140
  54.9 9.1 %collective-permute-start.11 = (bf16[768,256]{1,0:T(8,128)(2,1)S(1)}, bf16[768,256]{1,0:T(8,128)(2,1)S(1)}, u32[]{:S(2)}, u32[]{:S(2)}) collective-permute-start(bf16[768,256]{1,0:T(8,128)(2,1)S(1)} %shard_map.105.own), channel_id=1, source_target_pairs={{0,1},{1,0},{2,3},{3,2},{4,5},{5,4},{6,7},{7,6},{8,9},{9,8},{10,11... | collective-permute-start | bytes 1179656 | tf_op jit(solution)/shard_map/ppermute | solution.py:140
  63.7 1.7 %collective-permute-start.15 = (bf16[768,256]{1,0:T(8,128)(2,1)S(1)}, bf16[768,256]{1,0:T(8,128)(2,1)S(1)}, u32[]{:S(2)}, u32[]{:S(2)}) collective-permute-start(bf16[768,256]{1,0:T(8,128)(2,1)S(1)} %collective-permute-done.10.far), channel_id=1, source_target_pairs={{0,1},{1,0},{2,3},{3,2},{4,5},{5,4},{6,7},{7,6},{8,9},{9,8},{10,11... | collective-permute-start | bytes 1179656 | tf_op jit(solution)/shard_map/ppermute | solution.py:140
  66.4 6.7 %collective-permute-start.16 = (bf16[192,384]{1,0:T(8,128)(2,1)S(1)}, bf16[192,384]{1,0:T(8,128)(2,1)S(1)}, u32[]{:S(2)}, u32[]{:S(2)}) collective-permute-start(bf16[192,384]{1,0:T(8,128)(2,1)S(1)} %get-tuple-element.68), channel_id=1, source_target_pairs={{0,7},{1,6},{2,4},{3,5},{4,2},{5,3},{6,1},{7,0},{8,15},{9,14},{10,... | collective-permute-start | bytes 442376 | tf_op jit(solution)/shard_map/ppermute | solution.py:542
  68.0 7.4 %collective-permute-start.17 = (bf16[192,384]{1,0:T(8,128)(2,1)S(1)}, bf16[192,384]{1,0:T(8,128)(2,1)S(1)}, u32[]{:S(2)}, u32[]{:S(2)}) collective-permute-start(bf16[192,384]{1,0:T(8,128)(2,1)S(1)} %get-tuple-element.69), channel_id=1, source_target_pairs={{0,9},{1,8},{2,11},{3,10},{4,13},{5,12},{6,15},{7,14},{8,1},{9,0},... | collective-permute-start | bytes 442376 | tf_op jit(solution)/shard_map/ppermute | solution.py:542
  69.3 13.1 %collective-permute-start.18 = (bf16[192,384]{1,0:T(8,128)(2,1)S(1)}, bf16[192,384]{1,0:T(8,128)(2,1)S(1)}, u32[]{:S(2)}, u32[]{:S(2)}) collective-permute-start(bf16[192,384]{1,0:T(8,128)(2,1)S(1)} %get-tuple-element.70), channel_id=1, source_target_pairs={{0,14},{1,15},{2,13},{3,12},{4,11},{5,10},{6,8},{7,9},{8,6},{9,7},... | collective-permute-start | bytes 442376 | tf_op jit(solution)/shard_map/ppermute | solution.py:542
  82.5 5.6 %collective-permute-start.19 = (bf16[192,384]{1,0:T(8,128)(2,1)S(1)}, bf16[192,384]{1,0:T(8,128)(2,1)S(1)}, u32[]{:S(2)}, u32[]{:S(2)}) collective-permute-start(bf16[192,384]{1,0:T(8,128)(2,1)S(1)} %shard_map.107.own), channel_id=1, source_target_pairs={{0,2},{1,3},{2,0},{3,1},{4,6},{5,7},{6,4},{7,5},{8,10},{9,11},{10,... | collective-permute-start | bytes 442376 | tf_op jit(solution)/shard_map/ppermute | solution.py:140
  83.3 4.8 %collective-permute-start.20 = (bf16[192,384]{1,0:T(8,128)(2,1)S(1)}, bf16[192,384]{1,0:T(8,128)(2,1)S(1)}, u32[]{:S(2)}, u32[]{:S(2)}) collective-permute-start(bf16[192,384]{1,0:T(8,128)(2,1)S(1)} %shard_map.107.own), channel_id=1, source_target_pairs={{0,1},{1,0},{2,3},{3,2},{4,5},{5,4},{6,7},{7,6},{8,9},{9,8},{10,11... | collective-permute-start | bytes 442376 | tf_op jit(solution)/shard_map/ppermute | solution.py:140
  88.1 1.4 %collective-permute-start.21 = (bf16[192,384]{1,0:T(8,128)(2,1)S(1)}, bf16[192,384]{1,0:T(8,128)(2,1)S(1)}, u32[]{:S(2)}, u32[]{:S(2)}) collective-permute-start(bf16[192,384]{1,0:T(8,128)(2,1)S(1)} %collective-permute-done.19.far), channel_id=1, source_target_pairs={{0,1},{1,0},{2,3},{3,2},{4,5},{5,4},{6,7},{7,6},{8,9},{9,8},{10,11... | collective-permute-start | bytes 442376 | tf_op jit(solution)/shard_map/ppermute | solution.py:140
  90.7 7.4 %collective-permute-start.22 = (bf16[64,768]{1,0:T(8,128)(2,1)S(1)}, bf16[64,768]{1,0:T(8,128)(2,1)S(1)}, u32[]{:S(2)}, u32[]{:S(2)}) collective-permute-start(bf16[64,768]{1,0:T(8,128)(2,1)S(1)} %get-tuple-element.71), channel_id=1, source_target_pairs={{0,4},{4,0},{8,12},{12,8},{1,5},{5,1},{9,13},{13,9},{2,6},{6,2},{1... | collective-permute-start | bytes 294920 | tf_op jit(solution)/shard_map/ppermute | solution.py:140
  95.0 10.5 %collective-permute-start.23 = (bf16[64,768]{1,0:T(8,128)(2,1)S(1)}, bf16[64,768]{1,0:T(8,128)(2,1)S(1)}, u32[]{:S(2)}, u32[]{:S(2)}) collective-permute-start(bf16[64,768]{1,0:T(8,128)(2,1)S(1)} %get-tuple-element.72), channel_id=1, source_target_pairs={{0,8},{4,12},{8,0},{12,4},{1,9},{5,13},{9,1},{13,5},{2,10},{6,14},... | collective-permute-start | bytes 294920 | tf_op jit(solution)/shard_map/ppermute | solution.py:140
  95.5 10.0 %collective-permute-start.24 = (bf16[64,768]{1,0:T(8,128)(2,1)S(1)}, bf16[64,768]{1,0:T(8,128)(2,1)S(1)}, u32[]{:S(2)}, u32[]{:S(2)}) collective-permute-start(bf16[64,768]{1,0:T(8,128)(2,1)S(1)} %get-tuple-element.73), channel_id=1, source_target_pairs={{0,12},{4,8},{8,4},{12,0},{1,13},{5,9},{9,5},{13,1},{2,14},{6,10},... | collective-permute-start | bytes 294920 | tf_op jit(solution)/shard_map/ppermute | solution.py:140
